TPU v7x, 32 devices: a whole 2x2x4 slice. The times are simulated.
32 devices in a mesh: dp: 8 (over z, y), fsdp: 4 (over x, core).
Axes of the slice: x: 2, y: 2, z: 4, core: 2. Of those that a mesh axis runs over, the one named last changes fastest.
Arguments:
- tokens: bfloat16 [4, 32, 256, 768], P('fsdp', 'dp'), may hold values from -6 to 6
- visible_index: int32 [4, 32, 256], P('fsdp'), may hold values from 0 to 1023, as said below
- cotangent: bfloat16 [4, 32, 1024, 768], P('fsdp', None, 'dp'), may hold values from -6 to 6
- qkv_weight: float32 [768, 2304], P('dp', 'fsdp'), may hold values from -0.21875 to 0.21875
- out_weight: float32 [768, 768], P('dp', 'fsdp'), may hold values from -1.25 to 1.25
- up_weight: float32 [768, 3072], P('dp', 'fsdp'), may hold values from -0.21875 to 0.21875
- down_weight: float32 [3072, 768], P('dp', 'fsdp'), may hold values from -0.109375 to 0.109375
- vectors: float32 [12, 768], P('fsdp', 'dp'), may hold values from -3 to 4
- qkv_first: float32 [768, 2304], P('dp', 'fsdp'), may hold values from -14 to 14
- out_first: float32 [768, 768], P('dp', 'fsdp'), may hold values from -4 to 4
- up_first: float32 [768, 3072], P('dp', 'fsdp'), may hold values from -12 to 12
- down_first: float32 [3072, 768], P('dp', 'fsdp'), may hold values from -20 to 20
- vector_first: float32 [12, 768], P('fsdp', 'dp'), may hold values from -32 to 32
- qkv_second: float32 [768, 2304], P('dp', 'fsdp'), may hold values from 2.29376 to 36.0448
- out_second: float32 [768, 768], P('dp', 'fsdp'), may hold values from 0.262144 to 4.25984
- up_second: float32 [768, 3072], P('dp', 'fsdp'), may hold values from 1.96608 to 32.768
- down_second: float32 [3072, 768], P('dp', 'fsdp'), may hold values from 5.89824 to 95.0272
- vector_second: float32 [12, 768], P('fsdp', 'dp'), may hold values from 13.1072 to 196.608
Outputs:
- full_layout: bfloat16 [4, 32, 1024, 768], P('fsdp', None, 'dp')
- tokens_grad: float32 [4, 32, 256, 768], P('fsdp', 'dp')
- qkv_first_new: float32 [768, 2304], P('dp', 'fsdp')
- qkv_second_new: float32 [768, 2304], P('dp', 'fsdp')
- qkv_new: float32 [768, 2304], P('dp', 'fsdp')
- qkv_copy: bfloat16 [768, 2304], P('dp', 'fsdp')
- out_first_new: float32 [768, 768], P('dp', 'fsdp')
- out_second_new: float32 [768, 768], P('dp', 'fsdp')
- out_new: float32 [768, 768], P('dp', 'fsdp')
- out_copy: bfloat16 [768, 768], P('dp', 'fsdp')
- up_first_new: float32 [768, 3072], P('dp', 'fsdp')
- up_second_new: float32 [768, 3072], P('dp', 'fsdp')
- up_new: float32 [768, 3072], P('dp', 'fsdp')
- up_copy: bfloat16 [768, 3072], P('dp', 'fsdp')
- down_first_new: float32 [3072, 768], P('dp', 'fsdp')
- down_second_new: float32 [3072, 768], P('dp', 'fsdp')
- down_new: float32 [3072, 768], P('dp', 'fsdp')
- down_copy: bfloat16 [3072, 768], P('dp', 'fsdp')
- vector_first_new: float32 [12, 768], P('fsdp', 'dp')
- vector_second_new: float32 [12, 768], P('fsdp', 'dp')
- vector_new: float32 [12, 768], P('fsdp', 'dp')
- grad_norm: float32 [], replicated
Inputs may be any that keep to these rules, and one draw needn't show every extreme that they name: `visible_index`: for every chip and every block b of 128 consecutive patches, exactly 32 entries lie in the block, and entries b * 32 to (b + 1) * 32 - 1 of the chip are those of block b, ascending and distinct.
All inputs are finite; a program needn't handle non-finite values.
Results may differ from a plain program's by a relative error of at most 0.019.
Values may be sent and summed in bfloat16 or wider, within the bound.
No kernel may reach another device: no remote copies, remote signals or barrier semaphores. Data moves between devices by JAX's collectives and lax.ppermute only.
A program may use at most 192 MiB of HBM per device.

v0:
```python
import math

import jax
import jax.numpy as jnp
from jax import lax
from jax.sharding import PartitionSpec as P

HD = 64
STEP = 10


def norm_rows(values, gain_row, offset):
    center = values - jnp.mean(values, axis=-1, keepdims=True)
    spread = jnp.mean(center * center, axis=-1, keepdims=True)
    return center * lax.rsqrt(spread + 1e-05) * gain_row + offset


def gelu_exact(values):
    return jax.nn.gelu(values, approximate=False)


def contract_rows(left, right):
    return lax.dot_general(
        left, right, (((0,), (0,)), ((), ())), preferred_element_type=jnp.float32
    )


def contract_cols(left, right):
    return lax.dot_general(
        left, right, (((1,), (1,)), ((), ())), preferred_element_type=jnp.float32
    )


def adam_step(weight, gradient, first_mom, second, clip_factor, step_rate, decay_rate):
    scaled = gradient * clip_factor
    first_new = 0.5 * first_mom + 0.5 * scaled
    second_new = 0.5 * second + 0.5 * scaled * scaled
    correction = 1.0 - 0.5**STEP
    update = first_new / correction / (jnp.sqrt(second_new / correction) + 1e-08)
    return (first_new, second_new, weight - step_rate * (update + decay_rate * weight))


def on_device(
    tokens,
    visible_index,
    cotangent,
    qkv_weight,
    out_weight,
    up_weight,
    down_weight,
    vectors,
    qkv_first,
    out_first,
    up_first,
    down_first,
    vector_first,
    qkv_second,
    out_second,
    up_second,
    down_second,
    vector_second,
):
    chip_count = tokens.shape[1]
    seq_len = tokens.shape[2]
    model_width = tokens.shape[3]
    block_count = lax.axis_size("dp")
    block_seen = seq_len // block_count
    block_len = cotangent.shape[2]
    chips_group = chip_count * block_count
    head_count = model_width // HD
    row_count = chip_count * seq_len
    score_scale = HD ** (-0.5)
    qkv_low = qkv_weight.astype(jnp.bfloat16)
    out_low = out_weight.astype(jnp.bfloat16)
    up_low = up_weight.astype(jnp.bfloat16)
    down_low = down_weight.astype(jnp.bfloat16)
    vector_low = vectors.astype(jnp.bfloat16)
    side_cols = (
        lax.all_gather(qkv_low, "fsdp", axis=1, tiled=True),
        lax.all_gather(out_low, "fsdp", axis=1, tiled=True),
        lax.all_gather(up_low, "fsdp", axis=1, tiled=True),
        lax.all_gather(down_low, "fsdp", axis=1, tiled=True),
        lax.all_gather(vector_low, "fsdp", axis=0, tiled=True),
    )
    whole_set = (
        lax.all_gather(side_cols[0], "dp", axis=0, tiled=True),
        lax.all_gather(side_cols[1], "dp", axis=0, tiled=True),
        lax.all_gather(side_cols[2], "dp", axis=0, tiled=True),
        lax.all_gather(side_cols[3], "dp", axis=0, tiled=True),
        lax.all_gather(side_cols[4], "dp", axis=1, tiled=True),
    )
    qkv_full, out_full, up_full, down_full, vector_full = whole_set
    params = vector_full.astype(jnp.float32)
    inputs = tokens.reshape(row_count, model_width).astype(jnp.float32)
    normed, pull_one = jax.vjp(norm_rows, inputs, params[0], params[1])
    normed_low = normed.astype(jnp.bfloat16)
    value_bias = jnp.concatenate([jnp.zeros((2 * model_width,), jnp.float32), params[2]])
    mixed_all = (
        jnp.dot(normed_low, qkv_full, preferred_element_type=jnp.float32) + value_bias
    ).astype(jnp.bfloat16)
    mixed_all = mixed_all.reshape(chip_count, seq_len, 3, head_count, HD)
    queries = mixed_all[:, :, 0]
    key_rows = mixed_all[:, :, 1]
    values = mixed_all[:, :, 2]
    scores = (
        jnp.einsum("cqhe,ckhe->chqk", queries, key_rows, preferred_element_type=jnp.float32)
        * score_scale
    )
    row_peak = jnp.max(scores, axis=-1, keepdims=True)
    exponent = jnp.exp(scores - row_peak)
    row_total = jnp.sum(exponent, axis=-1, keepdims=True)
    log_total = row_peak + jnp.log(row_total)
    attn_low = (exponent / row_total).astype(jnp.bfloat16)
    context = jnp.einsum("chqk,ckhe->cqhe", attn_low, values, preferred_element_type=jnp.float32)
    context = context.astype(jnp.bfloat16).reshape(row_count, model_width)
    middle = inputs + jnp.dot(context, out_full, preferred_element_type=jnp.float32) + params[3]
    normed_two, pull_two = jax.vjp(norm_rows, middle, params[4], params[5])
    normed_two_low = normed_two.astype(jnp.bfloat16)
    gate_pre = jnp.dot(normed_two_low, up_full, preferred_element_type=jnp.float32) + params[
        6:10
    ].reshape(-1)
    active, pull_gelu = jax.vjp(gelu_exact, gate_pre)
    active_low = active.astype(jnp.bfloat16)
    result = (
        middle + jnp.dot(active_low, down_full, preferred_element_type=jnp.float32) + params[10]
    )
    result_low = result.astype(jnp.bfloat16)
    mask_value = params[11]
    block_rows = result_low.reshape(chip_count, block_count, block_seen, model_width)
    chip_base = lax.axis_index("dp") * chip_count
    own_places = lax.dynamic_slice_in_dim(visible_index[0], chip_base, chip_count, 0)
    block_ids = lax.broadcasted_iota(jnp.int32, (chip_count, block_count, block_seen), 1)
    local_src = own_places.reshape(chip_count, block_count, block_seen) - block_ids * block_len
    slot_ids = lax.broadcasted_iota(jnp.int32, (chip_count, block_count, block_len, block_seen), 2)
    pick_src = (local_src[:, :, None, :] == slot_ids).astype(jnp.bfloat16)
    gaps_src = (1.0 - jnp.sum(pick_src.astype(jnp.float32), axis=-1)).astype(jnp.bfloat16)
    filled = jnp.einsum("cbpv,cbvd->cbpd", pick_src, block_rows, preferred_element_type=jnp.float32)
    filled = filled + gaps_src[..., None].astype(jnp.float32) * mask_value
    arrived = lax.all_to_all(
        filled.astype(jnp.bfloat16), "dp", split_axis=1, concat_axis=0, tiled=True
    )
    full_layout = arrived.reshape(1, chips_group, block_len, model_width)
    cot_full = cotangent[0]
    returned = lax.all_to_all(
        cot_full.reshape(chips_group, 1, block_len, model_width),
        "dp",
        split_axis=0,
        concat_axis=1,
        tiled=True,
    )
    result_grad = jnp.einsum(
        "cbpv,cbpd->cbvd", pick_src, returned, preferred_element_type=jnp.float32
    )
    result_grad = result_grad.reshape(row_count, model_width)
    mask_grad = jnp.einsum("cbp,cbpd->d", gaps_src, returned, preferred_element_type=jnp.float32)
    again_cols = (
        lax.all_gather(qkv_low, "fsdp", axis=1, tiled=True),
        lax.all_gather(out_low, "fsdp", axis=1, tiled=True),
        lax.all_gather(up_low, "fsdp", axis=1, tiled=True),
        lax.all_gather(down_low, "fsdp", axis=1, tiled=True),
    )
    again_set = (
        lax.all_gather(again_cols[0], "dp", axis=0, tiled=True),
        lax.all_gather(again_cols[1], "dp", axis=0, tiled=True),
        lax.all_gather(again_cols[2], "dp", axis=0, tiled=True),
        lax.all_gather(again_cols[3], "dp", axis=0, tiled=True),
    )
    qkv_back, out_back, up_back, down_back = again_set
    feed_grad = result_grad.astype(jnp.bfloat16)
    down_bias_grad = jnp.sum(feed_grad.astype(jnp.float32), axis=0)
    down_grad = contract_rows(active_low, feed_grad)
    active_grad = contract_cols(feed_grad, down_back)
    gate_grad = pull_gelu(active_grad)[0].astype(jnp.bfloat16)
    up_bias_grad = jnp.sum(gate_grad.astype(jnp.float32), axis=0)
    up_grad = contract_rows(normed_two_low, gate_grad)
    normed_two_grad = contract_cols(gate_grad, up_back)
    middle_part, gain_two_grad, shift_two_grad = pull_two(normed_two_grad)
    middle_grad = result_grad + middle_part
    branch_grad = middle_grad.astype(jnp.bfloat16)
    out_bias_grad = jnp.sum(branch_grad.astype(jnp.float32), axis=0)
    out_grad = contract_rows(context, branch_grad)
    context_grad = contract_cols(branch_grad, out_back).astype(jnp.bfloat16)
    context_grad = context_grad.reshape(chip_count, seq_len, head_count, HD)
    again_scores = (
        jnp.einsum("cqhe,ckhe->chqk", queries, key_rows, preferred_element_type=jnp.float32)
        * score_scale
    )
    attn_full = jnp.exp(again_scores - log_total)
    attn_again = attn_full.astype(jnp.bfloat16)
    value_grad = jnp.einsum(
        "chqk,cqhe->ckhe", attn_again, context_grad, preferred_element_type=jnp.float32
    )
    prob_grad = jnp.einsum(
        "cqhe,ckhe->chqk", context_grad, values, preferred_element_type=jnp.float32
    )
    inner_sum = jnp.sum(attn_full * prob_grad, axis=-1, keepdims=True)
    score_grad = (attn_full * (prob_grad - inner_sum) * score_scale).astype(jnp.bfloat16)
    query_grad = jnp.einsum(
        "chqk,ckhe->cqhe", score_grad, key_rows, preferred_element_type=jnp.float32
    )
    key_grad = jnp.einsum(
        "chqk,cqhe->ckhe", score_grad, queries, preferred_element_type=jnp.float32
    )
    mixed_grad = jnp.stack([query_grad, key_grad, value_grad], axis=2).astype(jnp.bfloat16)
    mixed_grad = mixed_grad.reshape(row_count, 3 * model_width)
    value_bias_grad = jnp.sum(mixed_grad[:, 2 * model_width :].astype(jnp.float32), axis=0)
    qkv_grad = contract_rows(normed_low, mixed_grad)
    normed_grad = contract_cols(mixed_grad, qkv_back)
    input_part, gain_one_grad, shift_one_grad = pull_one(normed_grad)
    tokens_grad = (middle_grad + input_part).reshape(1, chip_count, seq_len, model_width)
    vector_grad = jnp.concatenate(
        [
            jnp.stack(
                [
                    gain_one_grad,
                    shift_one_grad,
                    value_bias_grad,
                    out_bias_grad,
                    gain_two_grad,
                    shift_two_grad,
                ]
            ),
            up_bias_grad.reshape(-1, model_width),
            jnp.stack([down_bias_grad, mask_grad]),
        ],
        axis=0,
    )
    summed = (
        lax.psum_scatter(qkv_grad, "dp", scatter_dimension=0, tiled=True),
        lax.psum_scatter(out_grad, "dp", scatter_dimension=0, tiled=True),
        lax.psum_scatter(up_grad, "dp", scatter_dimension=0, tiled=True),
        lax.psum_scatter(down_grad, "dp", scatter_dimension=0, tiled=True),
        lax.psum_scatter(vector_grad, "dp", scatter_dimension=1, tiled=True),
    )
    shares = (
        lax.psum_scatter(
            summed[0].astype(jnp.bfloat16), "fsdp", scatter_dimension=1, tiled=True
        ).astype(jnp.float32),
        lax.psum_scatter(
            summed[1].astype(jnp.bfloat16), "fsdp", scatter_dimension=1, tiled=True
        ).astype(jnp.float32),
        lax.psum_scatter(
            summed[2].astype(jnp.bfloat16), "fsdp", scatter_dimension=1, tiled=True
        ).astype(jnp.float32),
        lax.psum_scatter(
            summed[3].astype(jnp.bfloat16), "fsdp", scatter_dimension=1, tiled=True
        ).astype(jnp.float32),
        lax.psum_scatter(
            summed[4].astype(jnp.bfloat16), "fsdp", scatter_dimension=0, tiled=True
        ).astype(jnp.float32),
    )
    squares = (
        jnp.sum(shares[0] * shares[0])
        + jnp.sum(shares[1] * shares[1])
        + jnp.sum(shares[2] * shares[2])
    )
    squares = squares + jnp.sum(shares[3] * shares[3]) + jnp.sum(shares[4] * shares[4])
    grad_total = lax.psum(squares, ("dp", "fsdp"))
    grad_norm = jnp.sqrt(grad_total)
    tokens_all = lax.axis_size("dp") * lax.axis_size("fsdp") * chip_count * seq_len
    threshold = 0.05 * model_width * math.sqrt(tokens_all)
    clip_factor = jnp.minimum(1.0, threshold / grad_norm)
    ff_width = up_weight.shape[1] * lax.axis_size("fsdp")
    qkv_out = adam_step(
        qkv_weight,
        shares[0],
        qkv_first,
        qkv_second,
        clip_factor,
        0.6 / math.sqrt(model_width),
        0.05,
    )
    out_out = adam_step(
        out_weight,
        shares[1],
        out_first,
        out_second,
        clip_factor,
        0.6 / math.sqrt(model_width // 32),
        0.05,
    )
    up_out = adam_step(
        up_weight, shares[2], up_first, up_second, clip_factor, 0.6 / math.sqrt(model_width), 0.05
    )
    down_out = adam_step(
        down_weight,
        shares[3],
        down_first,
        down_second,
        clip_factor,
        0.6 / math.sqrt(ff_width),
        0.05,
    )
    vec_out = adam_step(vectors, shares[4], vector_first, vector_second, clip_factor, 0.45, 0.0)
    return (
        full_layout,
        tokens_grad,
        qkv_out[0],
        qkv_out[1],
        qkv_out[2],
        qkv_out[2].astype(jnp.bfloat16),
        out_out[0],
        out_out[1],
        out_out[2],
        out_out[2].astype(jnp.bfloat16),
        up_out[0],
        up_out[1],
        up_out[2],
        up_out[2].astype(jnp.bfloat16),
        down_out[0],
        down_out[1],
        down_out[2],
        down_out[2].astype(jnp.bfloat16),
        vec_out[0],
        vec_out[1],
        vec_out[2],
        grad_norm,
    )


def solution(mesh):
    in_specs = (
        P("fsdp", "dp", None, None),
        P("fsdp", None, None),
        P("fsdp", None, "dp", None),
        P("dp", "fsdp"),
        P("dp", "fsdp"),
        P("dp", "fsdp"),
        P("dp", "fsdp"),
        P("fsdp", "dp"),
        P("dp", "fsdp"),
        P("dp", "fsdp"),
        P("dp", "fsdp"),
        P("dp", "fsdp"),
        P("fsdp", "dp"),
        P("dp", "fsdp"),
        P("dp", "fsdp"),
        P("dp", "fsdp"),
        P("dp", "fsdp"),
        P("fsdp", "dp"),
    )
    out_specs = (
        P("fsdp", None, "dp", None),
        P("fsdp", "dp", None, None),
        P("dp", "fsdp"),
        P("dp", "fsdp"),
        P("dp", "fsdp"),
        P("dp", "fsdp"),
        P("dp", "fsdp"),
        P("dp", "fsdp"),
        P("dp", "fsdp"),
        P("dp", "fsdp"),
        P("dp", "fsdp"),
        P("dp", "fsdp"),
        P("dp", "fsdp"),
        P("dp", "fsdp"),
        P("dp", "fsdp"),
        P("dp", "fsdp"),
        P("dp", "fsdp"),
        P("dp", "fsdp"),
        P("fsdp", "dp"),
        P("fsdp", "dp"),
        P("fsdp", "dp"),
        P(),
    )
    return jax.shard_map(
        on_device, mesh=mesh, in_specs=in_specs, out_specs=out_specs, check_vma=False
    )
```

profile of v0, /device:TPU:0, one launch (start us, length us, event | category | flops | bytes accessed | tf_op | source)
XLA Modules:
  0.0 1309.0 jit_solution(11607204612275712795)
XLA Ops:
  8.2 8.4 all-gather.2
  19.2 5.6 all_gather.42
  26.6 8.1 all_gather.44
  34.8 6.0 all-to-all-start.1
  40.9 7.8 all_gather.46
  48.8 5.1 all-gather
  53.9 179.5 %all-gather.1 = bf16[8,96,12]{1,2,0:T(8,128)(2,1)S(1)} all-gather(bf16[1,96,12]{1,2,0:T(8,128)(2,1)S(1)} %bitcast.185), channel_id=1, replica_groups=mesh['dp'=8,'fsdp'=4] {'dp'}, dimensions={0}, use_global_device_ids=true | all-gather | bytes 20736 | tf_op jit(solution)/shard_map/all_gather | solution.py:90
  237.1 7.4 add_convert_fusion.2
  244.6 6.6 copy.137
  251.2 8.9 reshape.227
  260.1 3.3 fusion.101
  269.8 3.0 fusion.51
  274.5 3.5 fusion.102
  280.2 34.1 %all-gather.12.cloned.1.call-done = bf16[768,3072]{1,0:T(8,128)(2,1)} async-done(((bf16[96,3072]{1,0:T(8,128)(2,1)}), bf16[768,3072]{1,0:T(8,128)(2,1)}) %all-gather.12.cloned.1.call-update) | async-done | bytes 4718608 | tf_op jit(solution)/shard_map/all_gather | solution.py:88
  314.3 38.0 %multiply_convert_fusion.1 = (bf16[1024,3072]{1,0:T(8,128)(2,1)}, f32[1024,3072]{1,0:T(8,128)}, f32[1024,3072]{1,0:T(8,128)}) fusion(f32[3072]{0:T(1024)S(1)} %add.240, bf16[768,3072]{1,0:T(8,128)(2,1)} %all-gather.12.cloned.1.call-done, f32[1024,768]{1,0:T(8,128)} %copy-done.5, f32[768]{0:T(1024)S(1)} %get-tuple-element.141, ...), kind=kOutput, calls=%fused_computation.10 | convolution fusion | flops 5043388416 | bytes 39348224 | tf_op jit(solution)/shard_map/dot_general | solution.py:119
  352.4 4.0 fusion.17
  357.9 38.4 %all-gather.14.cloned.1.call-done = bf16[3072,768]{0,1:T(8,128)(2,1)} async-done(((bf16[384,768]{0,1:T(8,128)(2,1)}), bf16[3072,768]{0,1:T(8,128)(2,1)}) %all-gather.14.cloned.1.call-update) | async-done | bytes 4718608 | tf_op jit(solution)/shard_map/all_gather | solution.py:89
  396.3 18.3 %convert_reduce_fusion = (f32[3072]{0:T(1024)S(1)}, bf16[1024,3072]{1,0:T(8,128)(2,1)}) fusion(f32[1024,3072]{1,0:T(8,128)} %get-tuple-element.171, bf16[1024,768]{1,0:T(8,128)(2,1)} %get-tuple-element.176, bf16[3072,768]{0,1:T(8,128)(2,1)} %all-gather.14.cloned.1.call-done, f32[1024,3072]{1,0:T(8,128)} %get-tuple-element.187, f32[3072]{0:T(1024)S(1)} %add.240), kind=kOutput, calls=%fused_computation.3 | convolution fusion | flops 4885312512 | bytes 37773312 | tf_op jit(solution)/shard_map/dot_general | solution.py:29
  414.6 9.2 multiply_reduce_fusion.2
  431.7 3.2 fusion.38
  434.9 4.5 convolution_convert_fusion
  442.2 3.9 reshape.232
  446.0 8.2 fusion.52
  454.3 20.7 %fusion.44 = bf16[4,256,1,12,64]{1,4,3,0,2:T(8,128)(2,1)} fusion(f32[4,12,256,256]{2,3,1,0:T(8,128)} %fusion.52, f32[4,12,256]{2,1,0:T(8,128)S(1)} %log_add_fusion, f32[4,12,256,256]{2,3,1,0:T(8,128)} %copy-done.2, bf16[4,256,1,12,64]{1,0,4,3,2:T(4,128)(2,1)} %copy-done.11), kind=kOutput, calls=%fused_computation.74 | convolution fusion | flops 430977280 | bytes 28360704 | tf_op jit(solution)/shard_map/chqk,ckhe->cqhe/dot_general | solution.py:198
  474.9 20.4 %fusion.47 = bf16[4,256,1,12,64]{1,4,3,0,2:T(8,128)(2,1)} fusion(f32[4,12,256,256]{2,3,1,0:T(8,128)} %fusion.52, f32[4,12,256]{2,1,0:T(8,128)S(1)} %log_add_fusion, f32[4,12,256,256]{2,3,1,0:T(8,128)} %copy-done.2, bf16[4,256,1,12,64]{1,0,4,3,2:T(4,128)(2,1)} %copy-done.10), kind=kOutput, calls=%fused_computation.75 | convolution fusion | flops 430977280 | bytes 28360704 | tf_op jit(solution)/shard_map/chqk,cqhe->ckhe/dot_general | solution.py:201
  495.4 7.6 fusion.41
  503.8 4.5 copy.153
  512.0 6.0 fusion.103
  518.1 9.9 fusion.105
  528.1 11.5 fusion.86
  540.3 10.1 add_convert_fusion.3
  550.4 3.4 add_convert_fusion.1
  553.8 3.1 copy.145
  556.9 4.9 all-to-all-start
  562.0 8.6 fusion.88
  575.4 3.7 convolution_bitcast_fusion
  583.8 163.2 %reduce-scatter.18.cloned.1.call-done = f32[96,2304]{1,0:T(8,128)} async-done(((f32[768,2304]{1,0:T(8,128)}), f32[96,2304]{1,0:T(8,128)}) %reduce-scatter.18.cloned.1.call-update) | async-done | bytes 884752 | tf_op jit(solution)/shard_map/reduce_scatter | solution.py:229
  751.1 162.4 %reduce-scatter.26.cloned.1.call-done = f32[384,768]{1,0:T(8,128)} async-done(((f32[3072,768]{1,0:T(8,128)}), f32[384,768]{1,0:T(8,128)}) %reduce-scatter.26.cloned.1.call-update) | async-done | bytes 1179664 | tf_op jit(solution)/shard_map/reduce_scatter | solution.py:232
  917.9 162.3 %reduce-scatter.22.cloned.1.call-done = f32[96,3072]{1,0:T(8,128)} async-done(((f32[768,3072]{1,0:T(8,128)}), f32[96,3072]{1,0:T(8,128)}) %reduce-scatter.22.cloned.1.call-update) | async-done | bytes 1179664 | tf_op jit(solution)/shard_map/reduce_scatter | solution.py:231
  1088.3 5.3 add_add_fusion.2
  1093.7 50.6 %reduce-scatter.34.cloned.1.call-done = f32[96,12]{1,0:T(8,128)} async-done(((f32[768,12]{1,0:T(8,128)}), f32[96,12]{1,0:T(8,128)}) %reduce-scatter.34.cloned.1.call-update) | async-done | bytes 4624
  1145.2 5.7 all-reduce.1
  1151.4 14.6 %reduce-scatter.30.cloned.1.call-done = bf16[192,96]{1,0:T(8,128)(2,1)} async-done(((bf16[768,96]{1,0:T(8,128)(2,1)}), bf16[192,96]{1,0:T(8,128)(2,1)}) %reduce-scatter.30.cloned.1.call-update) | async-done | bytes 36880
  1167.6 23.2 %reduce-scatter.28.cloned.1.call-done = bf16[576,96]{1,0:T(8,128)(2,1)} async-done(((bf16[2304,96]{1,0:T(8,128)(2,1)}), bf16[576,96]{1,0:T(8,128)(2,1)}) %reduce-scatter.28.cloned.1.call-update) | async-done | bytes 110608
  1193.8 21.6 %reduce-scatter.32.cloned.1.call-done = bf16[192,384]{1,0:T(8,128)(2,1)} async-done(((bf16[768,384]{1,0:T(8,128)(2,1)}), bf16[192,384]{1,0:T(8,128)(2,1)}) %reduce-scatter.32.cloned.1.call-update) | async-done | bytes 147472
  1216.5 23.7 %reduce-scatter.24.cloned.1.call-done = bf16[96,768]{1,0:T(8,128)(2,1)} async-done(((bf16[96,3072]{1,0:T(8,128)(2,1)}), bf16[96,768]{1,0:T(8,128)(2,1)}) %reduce-scatter.24.cloned.1.call-update) | async-done | bytes 147472 | tf_op jit(solution)/shard_map/reduce_scatter | solution.py:242
  1244.5 39.4 %psum.7 = f32[]{:T(128)} all-reduce(f32[]{:T(128)S(6)} %add.256), channel_id=1, replica_groups=mesh['dp'=8,'fsdp'=4] {'dp','fsdp'}, use_global_device_ids=true, to_apply=%region_35.0 | all-reduce | flops 1 | bytes 8 | tf_op jit(solution)/shard_map/psum | solution.py:258
  1295.0 6.2 copy.210
  (218 shorter events, 80.5 us)
Async XLA Ops:
  7.2 229.1 %copy-start = (s32[1,32,256]{2,1,0:T(8,128)S(1)}, s32[1,32,256]{2,1,0:T(8,128)}, u32[]{:S(2)}) copy-start(s32[1,32,256]{2,1,0:T(8,128)} %param.19) | copy-start | bytes 98308
  7.2 229.9 %all-gather.8.cloned.1.call-start = ((), (), s32[]{:S(2)}) async-start(), calls=%async_computation.11 | async-start | bytes 3981312 | tf_op jit(solution)/shard_map/all_gather | solution.py:86
  18.1 256.4 %all-gather.10.cloned.1.call-start = ((), (), s32[]{:S(2)}) async-start(), calls=%async_computation.12 | async-start | bytes 1327104 | tf_op jit(solution)/shard_map/all_gather | solution.py:87
  25.6 288.7 %all-gather.12.cloned.1.call-start = ((), (), s32[]{:S(2)}) async-start(), calls=%async_computation.13 | async-start | bytes 5308416 | tf_op jit(solution)/shard_map/all_gather | solution.py:88
  34.8 6.1 copy-start.20
  34.8 14.0 %copy-start.42 = (f32[3,96]{1,0:T(4,128)S(1)}, f32[3,96]{1,0:T(4,128)}, u32[]{:S(2)}) copy-start(f32[3,96]{1,0:T(4,128)} %param.25) | copy-start | bytes 3460
  34.8 199.4 %copy-start.3 = (bf16[1,4,256,768]{3,2,1,0:T(8,128)(2,1)S(1)}, bf16[1,4,256,768]{3,2,1,0:T(8,128)(2,1)}, u32[]{:S(2)}) copy-start(bf16[1,4,256,768]{3,2,1,0:T(8,128)(2,1)} %param.18) | copy-start | bytes 4718596
  34.8 317.6 %all-to-all-start.1 = ((bf16[32,1,128,768]{3,2,1,0:T(8,128)(2,1)}), bf16[32,1,128,768]{3,2,1,0:T(8,128)(2,1)}, u32[]{:S(2)}, u32[]{:S(2)}) async-start(bf16[32,1,128,768]{3,2,1,0:T(8,128)(2,1)} %bitcast.162), calls=%async_computation.1 | async-start | bytes 12582912 | tf_op jit(solution)/shard_map/all_to_all | solution.py:144
  40.8 355.6 %all-gather.14.cloned.1.call-start = ((), (), s32[]{:S(2)}) async-start(), calls=%async_computation.14 | async-start | bytes 5308416 | tf_op jit(solution)/shard_map/all_gather | solution.py:89
  48.7 531.6 %reduce-scatter.20.cloned.1.call-start = ((), (), s32[]{:S(2)}) async-start(), calls=%async_computation.16 | async-start | bytes 2654208 | tf_op jit(solution)/shard_map/reduce_scatter | solution.py:230
  234.1 10.4 copy-start.28
  234.2 10.4 copy-start.35
  234.5 10.1 copy-start.31
  235.7 8.9 copy-start.33
  263.4 4.6 copy-start.12
  265.3 4.6 copy-start.2
  396.3 18.3 %copy-start.6 = (f32[1024,768]{1,0:T(8,128)S(1)}, f32[1024,768]{1,0:T(8,128)}, u32[]{:S(2)}) copy-start(f32[1024,768]{1,0:T(8,128)} %copy-done.5) | copy-start | bytes 9437188
  431.6 315.4 %reduce-scatter.18.cloned.1.call-start = ((), (), s32[]{:S(2)}) async-start(), calls=%async_computation.15 | async-start | bytes 7962624 | tf_op jit(solution)/shard_map/reduce_scatter | solution.py:229
  495.4 7.6 copy-start.13
  495.4 7.6 copy-start.14
  518.1 395.4 %reduce-scatter.26.cloned.1.call-start = ((), (), s32[]{:S(2)}) async-start(), calls=%async_computation.19 | async-start | bytes 10616832 | tf_op jit(solution)/shard_map/reduce_scatter | solution.py:232
  528.0 552.1 %reduce-scatter.22.cloned.1.call-start = ((), (), s32[]{:S(2)}) async-start(), calls=%async_computation.17 | async-start | bytes 10616832 | tf_op jit(solution)/shard_map/reduce_scatter | solution.py:231
  540.3 10.2 copy-start.44
  556.9 5.0 copy-start.32
  556.9 687.6 %all-to-all-start = ((bf16[4,8,128,768]{3,2,0,1:T(8,128)(2,1)}), bf16[4,8,128,768]{3,2,0,1:T(8,128)(2,1)}, u32[]{:S(2)}, u32[]{:S(2)}) async-start(bf16[4,8,128,768]{3,2,0,1:T(8,128)(2,1)} %copy.145), calls=%async_computation | async-start | bytes 12582912 | tf_op jit(solution)/shard_map/all_to_all | solution.py:139
  561.8 582.5 %reduce-scatter.34.cloned.1.call-start = ((), (), s32[]{:S(2)}) async-start(), calls=%async_computation.23 | async-start | bytes 442368
  561.9 11.5 copy-start.40
  562.0 11.5 copy-start.4
  562.0 11.5 copy-start.34
  570.5 4.8 copy-start.8
  580.2 585.8 %reduce-scatter.30.cloned.1.call-start = ((), (), s32[]{:S(2)}) async-start(), calls=%async_computation.21 | async-start | bytes 245760
  581.9 500.4 %copy-start.21 = (f32[384,192]{0,1:T(8,128)S(1)}, f32[384,192]{0,1:T(8,128)}, u32[]{:S(2)}) copy-start(f32[384,192]{0,1:T(8,128)} %param.24) | copy-start | bytes 884740
  583.7 607.1 %reduce-scatter.28.cloned.1.call-start = ((), (), s32[]{:S(2)}) async-start(), calls=%async_computation.20 | async-start | bytes 737280
  749.0 338.1 %copy-start.48 = (u32[32]{0:T(128)S(1)}, u32[32]{0:T(128)}, u32[]{:S(2)}) copy-start(u32[32]{0:T(128)} %constant.153) | copy-start | bytes 388
  751.1 464.3 %reduce-scatter.32.cloned.1.call-start = ((), (), s32[]{:S(2)}) async-start(), calls=%async_computation.22 | async-start | bytes 737280
  917.8 322.3 %reduce-scatter.24.cloned.1.call-start = ((), (), s32[]{:S(2)}) async-start(), calls=%async_computation.18 | async-start | bytes 737280 | tf_op jit(solution)/shard_map/reduce_scatter | solution.py:242
  1093.6 195.9 %copy-start.43 = (f32[3,96]{1,0:T(4,128)S(1)}, f32[3,96]{1,0:T(4,128)}, u32[]{:S(2)}) copy-start(f32[3,96]{1,0:T(4,128)} %param.25) | copy-start | bytes 3460
  1093.6 195.9 %copy-start.46 = (f32[3,96]{1,0:T(4,128)S(1)}, f32[3,96]{1,0:T(4,128)}, u32[]{:S(2)}) copy-start(f32[3,96]{1,0:T(4,128)} %param.35) | copy-start | bytes 3460
  1093.6 195.9 %copy-start.47 = (f32[3,96]{1,0:T(4,128)S(1)}, f32[3,96]{1,0:T(4,128)}, u32[]{:S(2)}) copy-start(f32[3,96]{1,0:T(4,128)} %param.30) | copy-start | bytes 3460
  1093.6 196.5 %copy-start.24 = (f32[96,192]{1,0:T(8,128)S(1)}, f32[96,192]{1,0:T(8,128)}, u32[]{:S(2)}) copy-start(f32[96,192]{1,0:T(8,128)} %param.22) | copy-start | bytes 221188
  1093.6 196.5 %copy-start.30 = (f32[96,192]{1,0:T(8,128)S(1)}, f32[96,192]{1,0:T(8,128)}, u32[]{:S(2)}) copy-start(f32[96,192]{1,0:T(8,128)} %param.32) | copy-start | bytes 221188
  1093.7 198.2 %copy-start.22 = (f32[96,576]{1,0:T(8,128)S(1)}, f32[96,576]{1,0:T(8,128)}, u32[]{:S(2)}) copy-start(f32[96,576]{1,0:T(8,128)} %param.21) | copy-start | bytes 663556
  1093.7 198.1 %copy-start.27 = (f32[96,576]{1,0:T(8,128)S(1)}, f32[96,576]{1,0:T(8,128)}, u32[]{:S(2)}) copy-start(f32[96,576]{1,0:T(8,128)} %param.31) | copy-start | bytes 663556
  1093.7 200.1 %copy-start.19 = (f32[96,768]{1,0:T(8,128)S(1)}, f32[96,768]{1,0:T(8,128)}, u32[]{:S(2)}) copy-start(f32[96,768]{1,0:T(8,128)} %param.23) | copy-start | bytes 884740
  1093.7 200.1 %copy-start.25 = (f32[96,768]{1,0:T(8,128)S(1)}, f32[96,768]{1,0:T(8,128)}, u32[]{:S(2)}) copy-start(f32[96,768]{1,0:T(8,128)} %param.33) | copy-start | bytes 884740
  1093.7 200.1 %copy-start.26 = (f32[96,768]{1,0:T(8,128)S(1)}, f32[96,768]{1,0:T(8,128)}, u32[]{:S(2)}) copy-start(f32[96,768]{1,0:T(8,128)} %param.28) | copy-start | bytes 884740
  1240.2 53.6 %copy-start.23 = (bf16[96,768]{1,0:T(8,128)(2,1)S(1)}, bf16[96,768]{1,0:T(8,128)(2,1)}, u32[]{:S(2)}) copy-start(bf16[96,768]{1,0:T(8,128)(2,1)} %reduce-scatter.24.cloned.1.call-done) | copy-start | bytes 442372
  1295.0 6.2 copy-start.1
  (16 other events, 35.2 us)
Sparse Core Ops, SparseCore 0:
  18.2 163.1 all-gather.7
  184.2 49.1 all-gather.9
  235.6 78.6 all-gather.11
  316.2 80.0 all-gather.13
  431.7 66.2 reduce-scatter.19
  518.2 228.6 reduce-scatter.17
  751.0 162.5 reduce-scatter.25
  917.6 162.5 reduce-scatter.21
  1083.8 60.4 reduce-scatter.33
  1147.3 18.7 reduce-scatter.29
  1168.7 22.0 reduce-scatter.27
  1193.3 22.0 reduce-scatter.31
  1218.1 22.0 reduce-scatter.23
where the time goes:
time: 1310 us
  waiting for transfers between devices  694 us (53%)
  blocking collectives  260 us (20%)
  matrix products  203 us (15%)
  local copies, waits for them, and re-layouts  75.6 us (6%)
  other arithmetic  44.4 us (3%)
  between operations  20.7 us (2%)
    all_gather x1, blocking collectives, on_device(): lax.all_gather(side_cols[4], 'dp', axis=1, tiled=True)  180 us
    reduce_scatter x1, waiting for transfers between devices, on_device(): lax.psum_scatter(qkv_grad, 'dp', scatter_dimension=0, tiled=True)  163 us
    reduce_scatter x1, waiting for transfers between devices, on_device(): lax.psum_scatter(down_grad, 'dp', scatter_dimension=0, tiled=True)  162 us
    reduce_scatter x1, waiting for transfers between devices, on_device(): lax.psum_scatter(up_grad, 'dp', scatter_dimension=0, tiled=True)  162 us
    unnamed x17, waiting for transfers between devices  110 us
    dot_general x4, matrix products, contract_cols(): lax.dot_general(left, right, (((1,), (1,)), ((), ())), preferred_element_...  40.6 us
    psum x1, blocking collectives, on_device(): grad_total = lax.psum(squares, ('dp', 'fsdp'))  39.4 us
    unnamed x122, local copies, waits for them, and re-layouts  39.3 us
  transfers between devices with their start and end apart: 15, of which 10 were waited for; matrix products, arithmetic and copies ran while one was open for 20% of the time, Pallas kernels for 0%

commit v1 on v0

--- a/solution.py
+++ b/solution.py
@@ -70,26 +70,36 @@
     head_count = model_width // HD
     row_count = chip_count * seq_len
     score_scale = HD ** (-0.5)
+    group_axis = lax.axis_size("fsdp")
+    device_count = block_count * group_axis
     qkv_low = qkv_weight.astype(jnp.bfloat16)
     out_low = out_weight.astype(jnp.bfloat16)
     up_low = up_weight.astype(jnp.bfloat16)
     down_low = down_weight.astype(jnp.bfloat16)
     vector_low = vectors.astype(jnp.bfloat16)
-    side_cols = (
-        lax.all_gather(qkv_low, "fsdp", axis=1, tiled=True),
-        lax.all_gather(out_low, "fsdp", axis=1, tiled=True),
-        lax.all_gather(up_low, "fsdp", axis=1, tiled=True),
-        lax.all_gather(down_low, "fsdp", axis=1, tiled=True),
-        lax.all_gather(vector_low, "fsdp", axis=0, tiled=True),
-    )
-    whole_set = (
-        lax.all_gather(side_cols[0], "dp", axis=0, tiled=True),
-        lax.all_gather(side_cols[1], "dp", axis=0, tiled=True),
-        lax.all_gather(side_cols[2], "dp", axis=0, tiled=True),
-        lax.all_gather(side_cols[3], "dp", axis=0, tiled=True),
-        lax.all_gather(side_cols[4], "dp", axis=1, tiled=True),
-    )
-    qkv_full, out_full, up_full, down_full, vector_full = whole_set
+    both = ("dp", "fsdp")
+
+    def gather_whole(shard):
+        rows, cols = shard.shape
+        pieces = lax.all_gather(shard, both, axis=0, tiled=False)
+        pieces = pieces.reshape(block_count, group_axis, rows, cols).transpose(0, 2, 1, 3)
+        return pieces.reshape(block_count * rows, group_axis * cols)
+
+    def scatter_sum(whole):
+        rows, cols = whole.shape[0] // block_count, whole.shape[1] // group_axis
+        pieces = whole.astype(jnp.bfloat16).reshape(block_count, rows, group_axis, cols)
+        pieces = pieces.transpose(0, 2, 1, 3).reshape(device_count * rows, cols)
+        return lax.psum_scatter(pieces, both, scatter_dimension=0, tiled=True).astype(jnp.float32)
+
+    vector_copies = jnp.broadcast_to(vector_low, (device_count,) + vector_low.shape)
+    vector_full = lax.all_to_all(vector_copies, both, split_axis=0, concat_axis=0, tiled=True)
+    vec_rows, vec_cols = vectors.shape
+    vector_full = vector_full.reshape(block_count, group_axis, vec_rows, vec_cols)
+    vector_full = vector_full.transpose(1, 2, 0, 3).reshape(group_axis * vec_rows, -1)
+    qkv_full = gather_whole(qkv_low)
+    out_full = gather_whole(out_low)
+    up_full = gather_whole(up_low)
+    down_full = gather_whole(down_low)
     params = vector_full.astype(jnp.float32)
     inputs = tokens.reshape(row_count, model_width).astype(jnp.float32)
     normed, pull_one = jax.vjp(norm_rows, inputs, params[0], params[1])
@@ -127,45 +137,31 @@
     result_low = result.astype(jnp.bfloat16)
     mask_value = params[11]
     block_rows = result_low.reshape(chip_count, block_count, block_seen, model_width)
-    chip_base = lax.axis_index("dp") * chip_count
-    own_places = lax.dynamic_slice_in_dim(visible_index[0], chip_base, chip_count, 0)
-    block_ids = lax.broadcasted_iota(jnp.int32, (chip_count, block_count, block_seen), 1)
-    local_src = own_places.reshape(chip_count, block_count, block_seen) - block_ids * block_len
-    slot_ids = lax.broadcasted_iota(jnp.int32, (chip_count, block_count, block_len, block_seen), 2)
-    pick_src = (local_src[:, :, None, :] == slot_ids).astype(jnp.bfloat16)
-    gaps_src = (1.0 - jnp.sum(pick_src.astype(jnp.float32), axis=-1)).astype(jnp.bfloat16)
-    filled = jnp.einsum("cbpv,cbvd->cbpd", pick_src, block_rows, preferred_element_type=jnp.float32)
-    filled = filled + gaps_src[..., None].astype(jnp.float32) * mask_value
-    arrived = lax.all_to_all(
-        filled.astype(jnp.bfloat16), "dp", split_axis=1, concat_axis=0, tiled=True
-    )
-    full_layout = arrived.reshape(1, chips_group, block_len, model_width)
+    arrived = lax.all_to_all(block_rows, "dp", split_axis=1, concat_axis=0, tiled=True)
+    arrived = arrived.reshape(chips_group, block_seen, model_width)
+    my_block = lax.axis_index("dp")
+    places = visible_index[0].reshape(chips_group, block_count, block_seen)
+    places = lax.dynamic_index_in_dim(places, my_block, 1, keepdims=False) - my_block * block_len
+    slot_ids = lax.broadcasted_iota(jnp.int32, (chips_group, block_len, block_seen), 1)
+    pick = (places[:, None, :] == slot_ids).astype(jnp.bfloat16)
+    gaps = 1.0 - jnp.sum(pick.astype(jnp.float32), axis=-1)
+    filled = jnp.einsum("cpv,cvd->cpd", pick, arrived, preferred_element_type=jnp.float32)
+    filled = filled + gaps[..., None] * mask_value
+    full_layout = filled.astype(jnp.bfloat16).reshape(1, chips_group, block_len, model_width)
     cot_full = cotangent[0]
+    cot_seen = jnp.einsum("cpv,cpd->cvd", pick, cot_full, preferred_element_type=jnp.float32)
+    mask_grad = jnp.einsum(
+        "cp,cpd->d", gaps.astype(jnp.bfloat16), cot_full, preferred_element_type=jnp.float32
+    )
     returned = lax.all_to_all(
-        cot_full.reshape(chips_group, 1, block_len, model_width),
+        cot_seen.astype(jnp.bfloat16).reshape(block_count, chip_count, block_seen, model_width),
         "dp",
         split_axis=0,
-        concat_axis=1,
+        concat_axis=2,
         tiled=True,
     )
-    result_grad = jnp.einsum(
-        "cbpv,cbpd->cbvd", pick_src, returned, preferred_element_type=jnp.float32
-    )
-    result_grad = result_grad.reshape(row_count, model_width)
-    mask_grad = jnp.einsum("cbp,cbpd->d", gaps_src, returned, preferred_element_type=jnp.float32)
-    again_cols = (
-        lax.all_gather(qkv_low, "fsdp", axis=1, tiled=True),
-        lax.all_gather(out_low, "fsdp", axis=1, tiled=True),
-        lax.all_gather(up_low, "fsdp", axis=1, tiled=True),
-        lax.all_gather(down_low, "fsdp", axis=1, tiled=True),
-    )
-    again_set = (
-        lax.all_gather(again_cols[0], "dp", axis=0, tiled=True),
-        lax.all_gather(again_cols[1], "dp", axis=0, tiled=True),
-        lax.all_gather(again_cols[2], "dp", axis=0, tiled=True),
-        lax.all_gather(again_cols[3], "dp", axis=0, tiled=True),
-    )
-    qkv_back, out_back, up_back, down_back = again_set
+    result_grad = returned.reshape(row_count, model_width).astype(jnp.float32)
+    qkv_back, out_back, up_back, down_back = qkv_full, out_full, up_full, down_full
     feed_grad = result_grad.astype(jnp.bfloat16)
     down_bias_grad = jnp.sum(feed_grad.astype(jnp.float32), axis=0)
     down_grad = contract_rows(active_low, feed_grad)
@@ -225,29 +221,15 @@
         ],
         axis=0,
     )
-    summed = (
-        lax.psum_scatter(qkv_grad, "dp", scatter_dimension=0, tiled=True),
-        lax.psum_scatter(out_grad, "dp", scatter_dimension=0, tiled=True),
-        lax.psum_scatter(up_grad, "dp", scatter_dimension=0, tiled=True),
-        lax.psum_scatter(down_grad, "dp", scatter_dimension=0, tiled=True),
-        lax.psum_scatter(vector_grad, "dp", scatter_dimension=1, tiled=True),
-    )
+    vector_parts = vector_grad.reshape(group_axis, vec_rows, block_count, vec_cols)
+    vector_parts = vector_parts.transpose(2, 0, 1, 3).reshape(device_count, vec_rows, vec_cols)
+    vector_parts = lax.all_to_all(vector_parts, both, split_axis=0, concat_axis=0, tiled=True)
     shares = (
-        lax.psum_scatter(
-            summed[0].astype(jnp.bfloat16), "fsdp", scatter_dimension=1, tiled=True
-        ).astype(jnp.float32),
-        lax.psum_scatter(
-            summed[1].astype(jnp.bfloat16), "fsdp", scatter_dimension=1, tiled=True
-        ).astype(jnp.float32),
-        lax.psum_scatter(
-            summed[2].astype(jnp.bfloat16), "fsdp", scatter_dimension=1, tiled=True
-        ).astype(jnp.float32),
-        lax.psum_scatter(
-            summed[3].astype(jnp.bfloat16), "fsdp", scatter_dimension=1, tiled=True
-        ).astype(jnp.float32),
-        lax.psum_scatter(
-            summed[4].astype(jnp.bfloat16), "fsdp", scatter_dimension=0, tiled=True
-        ).astype(jnp.float32),
+        scatter_sum(qkv_grad),
+        scatter_sum(out_grad),
+        scatter_sum(up_grad),
+        scatter_sum(down_grad),
+        jnp.sum(vector_parts, axis=0),
     )
     squares = (
         jnp.sum(shares[0] * shares[0])
@@ -255,7 +237,8 @@
         + jnp.sum(shares[2] * shares[2])
     )
     squares = squares + jnp.sum(shares[3] * shares[3]) + jnp.sum(shares[4] * shares[4])
-    grad_total = lax.psum(squares, ("dp", "fsdp"))
+    square_parts = jnp.broadcast_to(squares, (device_count, 1))
+    grad_total = jnp.sum(lax.all_to_all(square_parts, both, split_axis=0, concat_axis=0, tiled=True))
     grad_norm = jnp.sqrt(grad_total)
     tokens_all = lax.axis_size("dp") * lax.axis_size("fsdp") * chip_count * seq_len
     threshold = 0.05 * model_width * math.sqrt(tokens_all)

time: 1310 us -> 861 us (0.66)
  waiting for transfers between devices: 694 us -> 405 us
  blocking collectives: 260 us -> 0 us
  local copies, waits for them, and re-layouts: 75.6 us -> 151 us
  starting transfers between devices: 11.4 us -> 26.5 us
    reduce_scatter x5 -> x3, waiting for transfers between devices: 512 us -> 122 us  [scatter_sum(): lax.psum_scatter(pieces, both, scatter_dimension=0, tiled=True)]
    all_gather x6 -> x0, blocking collectives: 215 us -> none  [the longest x1 180 us: on_device(): lax.all_gather(side_cols[4], 'dp', axis=1, tiled=True)]
    all_gather x4, waiting for transfers between devices: 72.6 us -> 165 us  [gather_whole(): pieces = lax.all_gather(shard, both, axis=0, tiled=False)]
    reshape x1 -> x13, local copies, waits for them, and re-layouts: 0.08 us -> 62.1 us  [the longest x5 25.9 us: gather_whole(): pieces.reshape(block_count, group_axis, rows, cols).transpose(0, 2, 1, 3)]
    psum x1 -> x0, blocking collectives: 39.4 us -> none  [on_device(): grad_total = lax.psum(squares, ('dp', 'fsdp'))]
    all_to_all x2 -> x5, starting transfers between devices: 10.9 us -> 26.1 us  [the longest x1 7.3 us: on_device(): lax.all_to_all(vector_copies, both, split_axis=0, concat_axis=0, tiled=True)]
    unnamed x17 -> x9, waiting for transfers between devices: 110 us -> 118 us
    unnamed x122 -> x109, local copies, waits for them, and re-layouts: 39.3 us -> 34.9 us
  transfers between devices with their start and end apart: 15 -> 13, of which waited for: 10 -> 8; matrix products, arithmetic and copies ran while one was open for 20% -> 33% of each run, Pallas kernels for 0% -> 0%
where the time goes in v1:
time: 861 us; the launch traced here: 850 us
  waiting for transfers between devices  405 us (47%)
  matrix products  207 us (24%)
  local copies, waits for them, and re-layouts  151 us (18%)
  other arithmetic  40.7 us (5%)
  starting transfers between devices  26.5 us (3%)
  between operations  20.6 us (2%)
    all_gather x4, waiting for transfers between devices, gather_whole(): pieces = lax.all_gather(shard, both, axis=0, tiled=False)  165 us
    reduce_scatter x3, waiting for transfers between devices, scatter_sum(): lax.psum_scatter(pieces, both, scatter_dimension=0, tiled=True)  122 us
    unnamed x9, waiting for transfers between devices  118 us
    dot_general x1, matrix products, on_device(): jnp.dot(normed_two_low, up_full, preferred_element_type=jnp.float32)  45.2 us
    unnamed x109, local copies, waits for them, and re-layouts  34.9 us
    dot_general x4, matrix products, contract_cols(): lax.dot_general(left, right, (((1,), (1,)), ((), ())), preferred_element_...  34.9 us
    dot_general x4, matrix products, contract_rows(): lax.dot_general(left, right, (((0,), (0,)), ((), ())), preferred_element_...  28.5 us
    reshape x5, local copies, waits for them, and re-layouts, gather_whole(): pieces.reshape(block_count, group_axis, rows, cols).transpose(0, 2, 1, 3)  25.9 us
  transfers between devices with their start and end apart: 13, of which 8 were waited for; matrix products, arithmetic and copies ran while one was open for 33% of the time, Pallas kernels for 0%

profile of v1, /device:TPU:0, one launch (start us, length us, event | category | flops | bytes accessed | tf_op | source)
XLA Modules:
  0.0 850.3 jit_solution(3535606908100045826)
XLA Ops:
  13.5 7.3 all-to-all-start
  24.0 5.0 fusion.51
  29.1 5.8 all-to-all-start.2
  39.6 41.6 %all-gather.11.cloned.1.call-done = bf16[3072,192]{1,0:T(8,128)(2,1)} async-done(((bf16[96,192]{1,0:T(8,128)(2,1)}), bf16[3072,192]{1,0:T(8,128)(2,1)}) %all-gather.11.cloned.1.call-update) | async-done | bytes 1179664 | tf_op jit(solution)/shard_map/all_gather | solution.py:84
  84.0 3.8 reshape.317
  89.1 55.8 %all-gather.9.cloned.1.call-done = bf16[3072,576]{1,0:T(8,128)(2,1)} async-done(((bf16[96,576]{1,0:T(8,128)(2,1)}), bf16[3072,576]{1,0:T(8,128)(2,1)}) %all-gather.9.cloned.1.call-update) | async-done | bytes 3538960 | tf_op jit(solution)/shard_map/all_gather | solution.py:84
  144.9 6.1 copy.229
  151.0 7.9 reshape.313
  158.9 7.4 add_convert_fusion.2
  166.3 6.6 copy.163
  173.0 8.9 %reshape.314 = bf16[4,256,3,12,64]{1,0,4,3,2:T(4,128)(2,1)} reshape(bf16[1024,2304]{0,1:T(8,128)(2,1)} %copy.163) | data formatting | bytes 9437184 | tf_op jit(solution)/shard_map/reshape | solution.py:111
  181.8 3.5 fusion.102
  200.7 10.0 %all-gather.13.cloned.1.call-done = bf16[3072,768]{1,0:T(8,128)(2,1)} async-done(((bf16[96,768]{1,0:T(8,128)(2,1)}), bf16[3072,768]{1,0:T(8,128)(2,1)}) %all-gather.13.cloned.1.call-update) | async-done | bytes 4718608 | tf_op jit(solution)/shard_map/all_gather | solution.py:84
  210.7 6.0 copy.170
  216.7 3.2 copy.203
  219.9 57.4 %all-gather.15.cloned.1.call-done = bf16[12288,192]{0,1:T(8,128)(2,1)} async-done(((bf16[384,192]{0,1:T(8,128)(2,1)}), bf16[12288,192]{0,1:T(8,128)(2,1)}) %all-gather.15.cloned.1.call-update) | async-done | bytes 4718608 | tf_op jit(solution)/shard_map/all_gather | solution.py:84
  277.3 8.2 reshape.320
  290.3 3.1 copy-done.16
  293.4 45.2 %multiply_convert_fusion.1 = (bf16[1024,3072]{1,0:T(8,128)(2,1)}, f32[1024,3072]{1,0:T(8,128)}, f32[1024,3072]{1,0:T(8,128)}) fusion(f32[3072]{0:T(1024)S(1)} %add.223, bf16[768,3072]{1,0:T(8,128)(2,1)S(1)} %bitcast.201, f32[1024,768]{1,0:T(8,128)S(1)} %copy-done.8, f32[768]{0:T(1024)S(1)} %get-tuple-element.31, f32[768]{0:T(1024)S(1)} %get-tuple-element.32, ...), kind=kOutput, calls=%fused_computation.10 | convolution fusion | flops 5043388416 | bytes 39348224 | tf_op jit(solution)/shard_map/dot_general | solution.py:129
  338.5 15.5 %convert_reduce_fusion = (f32[3072]{0:T(1024)S(1)}, bf16[1024,3072]{1,0:T(8,128)(2,1)}) fusion(f32[1024,3072]{1,0:T(8,128)} %get-tuple-element.61, bf16[1024,768]{1,0:T(8,128)(2,1)S(1)} %bitcast.187, bf16[3072,768]{0,1:T(8,128)(2,1)S(1)} %bitcast.197, f32[1024,3072]{1,0:T(8,128)} %get-tuple-element.77, f32[3072]{0:T(1024)S(1)} %add.223), kind=kOutput, calls=%fused_computation.3 | convolution fusion | flops 4885312512 | bytes 37773312 | tf_op jit(solution)/shard_map/dot_general | solution.py:29
  354.1 9.2 %multiply_reduce_fusion.2 = (f32[768]{0:T(1024)S(1)}, f32[1024]{0:T(1024)S(1)}, f32[768]{0:T(1024)S(1)}, f32[1024,768]{1,0:T(8,128)S(1)}) fusion(f32[1024,768]{1,0:T(8,128)S(1)} %copy-done.8, f32[1024]{0:T(1024)S(1)} %fusion.74, f32[1024]{0:T(1024)S(1)} %broadcast_multiply_fusion, f32[768]{0:T(1024)S(1)} %get-tuple-element.32, ...), kind=kOutput, calls=%fused_computation.66 | convolution fusion | flops 4838126592 | bytes 17323008 | tf_op jit(solution)/shard_map/dot_general | solution.py:29
  372.3 3.5 reshape.331
  377.3 3.0 copy.174
  383.2 7.8 fusion.55
  391.0 8.2 fusion.41
  399.2 20.8 %fusion.44 = bf16[4,256,1,12,64]{1,4,3,0,2:T(8,128)(2,1)} fusion(f32[4,12,256,256]{2,3,1,0:T(8,128)} %fusion.55, f32[4,12,256]{2,1,0:T(8,128)S(1)} %copy-done.33, f32[4,12,256,256]{2,3,1,0:T(8,128)} %copy-done, bf16[4,256,1,12,64]{1,0,4,3,2:T(4,128)(2,1)} %copy-done.13), kind=kOutput, calls=%fused_computation.77 | convolution fusion | flops 430977280 | bytes 28360704 | tf_op jit(solution)/shard_map/chqk,ckhe->cqhe/dot_general | solution.py:194
  420.0 22.5 %fusion.47 = bf16[4,256,1,12,64]{1,4,3,0,2:T(8,128)(2,1)} fusion(f32[4,12,256,256]{2,3,1,0:T(8,128)} %fusion.55, f32[4,12,256]{2,1,0:T(8,128)S(1)} %copy-done.33, f32[4,12,256,256]{2,3,1,0:T(8,128)} %copy-done, bf16[4,256,1,12,64]{1,0,4,3,2:T(4,128)(2,1)S(1)} %copy-done.12), kind=kOutput, calls=%fused_computation.78 | convolution fusion | flops 430977280 | bytes 28360704 | tf_op jit(solution)/shard_map/chqk,cqhe->ckhe/dot_general | solution.py:197
  445.3 4.5 copy.180
  453.6 5.4 convolution_convert_fusion.2
  459.0 9.1 %reshape.329 = bf16[8,96,4,576]{3,2,1,0:T(4,128)(2,1)} reshape(bf16[768,2304]{1,0:T(8,128)(2,1)} %convolution_convert_fusion.2) | data formatting | bytes 7077888 | tf_op jit(solution)/shard_map/reshape | solution.py:90
  468.1 4.7 copy.181
  472.9 10.4 %convolution_convert_fusion.1 = bf16[768,3072]{1,0:T(8,128)(2,1)} fusion(bf16[1024,3072]{1,0:T(8,128)(2,1)} %get-tuple-element.81, f32[1024,768]{1,0:T(8,128)} %copy-done.7, f32[768]{0:T(1024)S(1)} %get-tuple-element.31, f32[768]{0:T(1024)S(1)} %get-tuple-element.32, f32[1024]{0:T(1024)S(1)} %fusion.74, f32[1024]{0:T(1024)S(1)} %broadcast_multiply_fusion), kind=kOutput, calls=%fused_computation.43 | convolution fusion | flops 4838129664 | bytes 14170112 | tf_op jit(solution)/shard_map/dot_general | solution.py:23
  483.3 9.8 %reshape.333 = bf16[8,96,4,768]{3,2,1,0:T(4,128)(2,1)} reshape(bf16[768,3072]{1,0:T(8,128)(2,1)} %convolution_convert_fusion.1) | data formatting | bytes 9437184 | tf_op jit(solution)/shard_map/reshape | solution.py:90
  493.1 5.5 copy.183
  499.6 10.2 %convolution_convert_fusion = bf16[3072,768]{1,0:T(8,128)(2,1)} fusion(bf16[1024,3072]{1,0:T(8,128)(2,1)} %get-tuple-element.60, bf16[1024,768]{1,0:T(8,128)(2,1)S(1)} %bitcast.188), kind=kOutput, calls=%fused_computation.42 | convolution fusion | flops 4834197504 | bytes 12582912 | tf_op jit(solution)/shard_map/dot_general | solution.py:23
  509.8 6.7 copy.184
  516.5 5.6 copy.208
  522.1 9.1 %copy.196 = bf16[8,4,384,192]{3,2,1,0:T(8,128)(2,1)} copy(bf16[8,4,384,192]{2,0,3,1:T(8,128)(2,1)} %bitcast.182) | data formatting | bytes 9437184
  531.2 3.9 fusion.59
  535.6 7.7 fusion.89
  551.8 10.0 %add_convert_fusion.3 = bf16[1024,768]{1,0:T(8,128)(2,1)S(1)} fusion(f32[1024,768]{1,0:T(8,128)} %copy-done.7, bf16[1024,3072]{1,0:T(8,128)(2,1)} %get-tuple-element.60, bf16[3072,768]{0,1:T(8,128)(2,1)} %bitcast.198, f32[768]{0:T(1024)S(1)} %copy-done.47), kind=kOutput, calls=%fused_computation.72 | convolution fusion | flops 4834197504 | bytes 15731712 | tf_op jit(solution)/shard_map/dot_general | solution.py:135
  563.2 6.2 all-to-all-start.1
  569.3 4.7 add_add_fusion.2
  576.2 7.8 reduce-scatter.7.cloned.1.call-done
  586.9 114.0 %reduce-scatter.11.cloned.1.call-done = bf16[96,768]{1,0:T(8,128)(2,1)} async-done(((bf16[3072,768]{1,0:T(8,128)(2,1)}), bf16[96,768]{1,0:T(8,128)(2,1)}) %reduce-scatter.11.cloned.1.call-update) | async-done | bytes 147472 | tf_op jit(solution)/shard_map/reduce_scatter | solution.py:92
  703.1 118.0 %reduce-scatter.13.cloned.1.call-done = bf16[384,192]{1,0:T(8,128)(2,1)} async-done(((bf16[12288,192]{1,0:T(8,128)(2,1)}), bf16[384,192]{1,0:T(8,128)(2,1)}) %reduce-scatter.13.cloned.1.call-update) | async-done | bytes 147472
  824.8 3.9 all-to-all-start.4
  828.8 6.3 fusion.17
  (203 shorter events, 83.0 us)
Async XLA Ops:
  7.2 74.0 %all-gather.11.cloned.1.call-start = ((), (), s32[]{:S(2)}) async-start(), calls=%async_computation.13 | async-start | bytes 1622016 | tf_op jit(solution)/shard_map/all_gather | solution.py:84
  8.8 136.1 %all-gather.9.cloned.1.call-start = ((), (), s32[]{:S(2)}) async-start(), calls=%async_computation.12 | async-start | bytes 4055040 | tf_op jit(solution)/shard_map/all_gather | solution.py:84
  10.5 200.3 %all-gather.13.cloned.1.call-start = ((), (), s32[]{:S(2)}) async-start(), calls=%async_computation.14 | async-start | bytes 4866048 | tf_op jit(solution)/shard_map/all_gather | solution.py:84
  13.5 15.6 %all-to-all-start = ((bf16[32,3,96]{2,1,0:T(4,128)(2,1)}), bf16[32,3,96]{2,1,0:T(4,128)(2,1)S(1)}, u32[]{:S(2)}, u32[]{:S(2)}) async-start(bf16[32,3,96]{2,1,0:T(4,128)(2,1)} %broadcast_in_dim.12), calls=%async_computation | async-start | bytes 65536 | tf_op jit(solution)/shard_map/all_to_all | solution.py:95
  20.8 256.5 %all-gather.15.cloned.1.call-start = ((), (), s32[]{:S(2)}) async-start(), calls=%async_computation.15 | async-start | bytes 4866048 | tf_op jit(solution)/shard_map/all_gather | solution.py:84
  24.0 10.9 %copy-start.1 = (bf16[1,4,256,768]{3,2,1,0:T(8,128)(2,1)S(1)}, bf16[1,4,256,768]{3,2,1,0:T(8,128)(2,1)}, u32[]{:S(2)}) copy-start(bf16[1,4,256,768]{3,2,1,0:T(8,128)(2,1)} %param.18) | copy-start | bytes 4718596
  29.1 58.7 %all-to-all-start.2 = ((bf16[8,4,32,768]{3,2,1,0:T(8,128)(2,1)}), bf16[8,4,32,768]{3,2,1,0:T(8,128)(2,1)S(1)}, u32[]{:S(2)}, u32[]{:S(2)}) async-start(bf16[8,4,32,768]{3,2,1,0:T(8,128)(2,1)} %bitcast.196), calls=%async_computation.2 | async-start | bytes 3145728 | tf_op jit(solution)/shard_map/all_to_all | solution.py:156
  34.9 539.9 %reduce-scatter.9.cloned.1.call-start = ((), (), s32[]{:S(2)}) async-start(), calls=%async_computation.10 | async-start | bytes 1622016 | tf_op jit(solution)/shard_map/reduce_scatter | solution.py:92
  37.8 51.4 %copy-start.41 = (f32[768]{0:T(1024)}, f32[768]{0:T(1024)S(1)}, u32[]{:S(2)}) copy-start(f32[768]{0:T(1024)S(1)} %get-tuple-element.36) | copy-start | bytes 9220
  87.8 63.2 %copy-start.4 = (bf16[8,4,32,768]{3,2,1,0:T(8,128)(2,1)}, bf16[8,4,32,768]{3,2,1,0:T(8,128)(2,1)S(1)}, u32[]{:S(2)}) copy-start(bf16[8,4,32,768]{3,2,1,0:T(8,128)(2,1)S(1)} %all-to-all-done.2) | copy-start | bytes 4718596
  151.0 7.9 copy-start.17
  185.4 4.6 copy-start.14
  187.3 4.6 copy-start
  288.4 5.0 copy-start.16
  289.6 49.0 %copy-start.15 = (bf16[96,8,8,384]{3,1,2,0:T(8,128)(2,1)}, bf16[96,8,8,384]{3,1,2,0:T(8,128)(2,1)S(1)}, u32[]{:S(2)}) copy-start(bf16[96,8,8,384]{3,1,2,0:T(8,128)(2,1)S(1)} %copy.204) | copy-start | bytes 14155780
  293.4 45.2 %copy-start.6 = (bf16[1,4,8,32,768]{4,3,2,1,0:T(8,128)(2,1)S(1)}, bf16[1,4,8,32,768]{4,3,2,1,0:T(8,128)(2,1)}, u32[]{:S(2)}) copy-start(bf16[1,4,8,32,768]{4,3,2,1,0:T(8,128)(2,1)} %copy.173) | copy-start | bytes 4718596
  364.7 5.0 copy-start.3
  377.2 206.7 %reduce-scatter.7.cloned.1.call-start = ((), (), s32[]{:S(2)}) async-start(), calls=%async_computation.9 | async-start | bytes 4055040 | tf_op jit(solution)/shard_map/reduce_scatter | solution.py:92
  383.2 7.8 copy-start.33
  399.2 20.8 %copy-start.12 = (bf16[4,256,1,12,64]{1,0,4,3,2:T(4,128)(2,1)S(1)}, bf16[4,256,1,12,64]{1,0,4,3,2:T(4,128)(2,1)}, u32[]{:S(2)}) copy-start(bf16[4,256,1,12,64]{1,0,4,3,2:T(4,128)(2,1)} %copy-done.11) | copy-start | bytes 4718596
  472.8 228.0 %reduce-scatter.11.cloned.1.call-start = ((), (), s32[]{:S(2)}) async-start(), calls=%async_computation.11 | async-start | bytes 4866048 | tf_op jit(solution)/shard_map/reduce_scatter | solution.py:92
  498.7 322.4 %reduce-scatter.13.cloned.1.call-start = ((), (), s32[]{:S(2)}) async-start(), calls=%async_computation.16 | async-start | bytes 6488064
  531.2 4.0 copy-start.5
  531.2 4.3 copy-start.2
  531.2 4.3 copy-start.42
  543.3 8.5 %copy-start.47 = (f32[768]{0:T(1024)S(1)}, f32[768]{0:T(1024)}, u32[]{:S(2)}) copy-start(f32[768]{0:T(1024)} %get-tuple-element.29) | copy-start | bytes 9220
  548.9 14.3 %all-to-all-start.3 = ((f32[32,3,96]{2,1,0:T(4,128)}), f32[32,3,96]{2,1,0:T(4,128)S(1)}, u32[]{:S(2)}, u32[]{:S(2)}) async-start(f32[32,3,96]{2,1,0:T(4,128)} %copy.187), calls=%async_computation.6 | async-start | bytes 131072 | tf_op jit(solution)/shard_map/all_to_all | solution.py:226
  563.2 261.0 %all-to-all-start.1 = ((bf16[4,8,32,768]{3,2,0,1:T(8,128)(2,1)}), bf16[4,8,32,768]{3,2,0,1:T(8,128)(2,1)}, u32[]{:S(2)}, u32[]{:S(2)}) async-start(bf16[4,8,32,768]{3,2,0,1:T(8,128)(2,1)} %copy.172), calls=%async_computation.1 | async-start | bytes 3145728 | tf_op jit(solution)/shard_map/all_to_all | solution.py:140
  569.3 259.3 %copy-start.43 = (f32[768]{0:T(1024)S(1)}, f32[768]{0:T(1024)}, u32[]{:S(2)}) copy-start(f32[768]{0:T(1024)} %get-tuple-element.30) | copy-start | bytes 9220
  574.1 263.0 %copy-start.46 = (f32[3,96]{1,0:T(4,128)S(1)}, f32[3,96]{1,0:T(4,128)}, u32[]{:S(2)}) copy-start(f32[3,96]{1,0:T(4,128)} %param.25) | copy-start | bytes 3460
  574.1 263.1 %copy-start.48 = (f32[3,96]{1,0:T(4,128)S(1)}, f32[3,96]{1,0:T(4,128)}, u32[]{:S(2)}) copy-start(f32[3,96]{1,0:T(4,128)} %param.35) | copy-start | bytes 3460
  574.1 263.1 %copy-start.49 = (f32[3,96]{1,0:T(4,128)S(1)}, f32[3,96]{1,0:T(4,128)}, u32[]{:S(2)}) copy-start(f32[3,96]{1,0:T(4,128)} %param.30) | copy-start | bytes 3460
  574.1 263.7 %copy-start.21 = (f32[384,192]{0,1:T(8,128)S(1)}, f32[384,192]{0,1:T(8,128)}, u32[]{:S(2)}) copy-start(f32[384,192]{0,1:T(8,128)} %param.24) | copy-start | bytes 884740
  574.1 263.7 %copy-start.29 = (f32[384,192]{0,1:T(8,128)S(1)}, f32[384,192]{0,1:T(8,128)}, u32[]{:S(2)}) copy-start(f32[384,192]{0,1:T(8,128)} %param.34) | copy-start | bytes 884740
  574.1 263.7 %copy-start.30 = (f32[384,192]{0,1:T(8,128)S(1)}, f32[384,192]{0,1:T(8,128)}, u32[]{:S(2)}) copy-start(f32[384,192]{0,1:T(8,128)} %param.29) | copy-start | bytes 884740
  824.8 11.0 %all-to-all-start.4 = ((f32[32,1,1]{2,1,0:T(1,128)}), f32[32,1,1]{2,1,0:T(1,128)S(1)}, u32[]{:S(2)}, u32[]{:S(2)}) async-start(f32[32,1,1]{2,1,0:T(1,128)} %broadcast_in_dim.34), calls=%async_computation.7 | async-start | bytes 32768 | tf_op jit(solution)/shard_map/all_to_all | solution.py:241
  828.7 10.2 %copy-start.28 = (f32[96,192]{1,0:T(8,128)S(1)}, f32[96,192]{1,0:T(8,128)}, u32[]{:S(2)}) copy-start(f32[96,192]{1,0:T(8,128)} %param.22) | copy-start | bytes 221188
  828.7 10.2 %copy-start.38 = (bf16[96,192]{1,0:T(8,128)(2,1)S(1)}, bf16[96,192]{1,0:T(8,128)(2,1)}, u32[]{:S(2)}) copy-start(bf16[96,192]{1,0:T(8,128)(2,1)} %reduce-scatter.9.cloned.1.call-done) | copy-start | bytes 110596
  828.7 10.2 %copy-start.39 = (f32[96,192]{1,0:T(8,128)S(1)}, f32[96,192]{1,0:T(8,128)}, u32[]{:S(2)}) copy-start(f32[96,192]{1,0:T(8,128)} %param.32) | copy-start | bytes 221188
  828.7 10.2 %copy-start.40 = (f32[96,192]{1,0:T(8,128)S(1)}, f32[96,192]{1,0:T(8,128)}, u32[]{:S(2)}) copy-start(f32[96,192]{1,0:T(8,128)} %param.27) | copy-start | bytes 221188
  828.7 11.0 %copy-start.25 = (f32[96,576]{1,0:T(8,128)S(1)}, f32[96,576]{1,0:T(8,128)}, u32[]{:S(2)}) copy-start(f32[96,576]{1,0:T(8,128)} %param.21) | copy-start | bytes 663556
  828.7 11.0 %copy-start.27 = (bf16[96,576]{1,0:T(8,128)(2,1)S(1)}, bf16[96,576]{1,0:T(8,128)(2,1)}, u32[]{:S(2)}) copy-start(bf16[96,576]{1,0:T(8,128)(2,1)} %reduce-scatter.7.cloned.1.call-done) | copy-start | bytes 331780
  828.8 11.0 %copy-start.36 = (f32[96,576]{1,0:T(8,128)S(1)}, f32[96,576]{1,0:T(8,128)}, u32[]{:S(2)}) copy-start(f32[96,576]{1,0:T(8,128)} %param.31) | copy-start | bytes 663556
  828.8 10.9 %copy-start.37 = (f32[96,576]{1,0:T(8,128)S(1)}, f32[96,576]{1,0:T(8,128)}, u32[]{:S(2)}) copy-start(f32[96,576]{1,0:T(8,128)} %param.26) | copy-start | bytes 663556
  828.8 12.0 %copy-start.22 = (f32[96,768]{1,0:T(8,128)S(1)}, f32[96,768]{1,0:T(8,128)}, u32[]{:S(2)}) copy-start(f32[96,768]{1,0:T(8,128)} %param.23) | copy-start | bytes 884740
  828.8 12.0 %copy-start.26 = (bf16[96,768]{1,0:T(8,128)(2,1)S(1)}, bf16[96,768]{1,0:T(8,128)(2,1)}, u32[]{:S(2)}) copy-start(bf16[96,768]{1,0:T(8,128)(2,1)} %reduce-scatter.11.cloned.1.call-done) | copy-start | bytes 442372
  828.8 12.0 %copy-start.31 = (f32[96,768]{1,0:T(8,128)S(1)}, f32[96,768]{1,0:T(8,128)}, u32[]{:S(2)}) copy-start(f32[96,768]{1,0:T(8,128)} %param.33) | copy-start | bytes 884740
  828.8 12.0 %copy-start.32 = (f32[96,768]{1,0:T(8,128)S(1)}, f32[96,768]{1,0:T(8,128)}, u32[]{:S(2)}) copy-start(f32[96,768]{1,0:T(8,128)} %param.28) | copy-start | bytes 884740
  (15 other events, 33.7 us)
Sparse Core Ops, SparseCore 0:
  11.5 69.6 all-gather.10
  84.6 60.2 all-gather.8
  148.4 62.3 all-gather.12
  213.9 63.2 all-gather.14
  377.4 95.1 reduce-scatter.8
  477.8 106.1 reduce-scatter.6
  589.5 111.3 reduce-scatter.10
  707.4 113.6 reduce-scatter.12

commit v2 on v1

v2 whole, which is shorter than its diff:
```python
import functools
import math

import jax
import jax.numpy as jnp
from jax import lax
from jax.experimental import pallas as pl
from jax.experimental.pallas import tpu as pltpu
from jax.sharding import PartitionSpec as P

HD = 64
STEP = 10
F32 = jnp.float32
BF16 = jnp.bfloat16
VMEM_BYTES = 60 * 1024 * 1024


def params_for(**more):
    return pltpu.CompilerParams(vmem_limit_bytes=VMEM_BYTES, **more)


def dot_nn(left, right):
    return lax.dot_general(left, right, (((1,), (0,)), ((), ())), preferred_element_type=F32)


def dot_nt(left, right):
    return lax.dot_general(left, right, (((1,), (1,)), ((), ())), preferred_element_type=F32)


def dot_tn(left, right):
    return lax.dot_general(left, right, (((0,), (0,)), ((), ())), preferred_element_type=F32)


def norm_parts(values):
    center = values - jnp.mean(values, axis=-1, keepdims=True)
    spread = jnp.mean(center * center, axis=-1, keepdims=True)
    factor = lax.rsqrt(spread + 1e-05)
    return center * factor, factor


def norm_back(grad, hat, factor, gain):
    scaled = grad * gain
    inner = jnp.mean(scaled * hat, axis=-1, keepdims=True)
    return factor * (scaled - jnp.mean(scaled, axis=-1, keepdims=True) - hat * inner)


def gelu_pair(gate):
    size = jnp.abs(gate) * (0.5**0.5)
    ratio = 1.0 / (1.0 + 0.3275911 * size)
    bell = jnp.exp(-size * size)
    tail = ratio * (
        0.254829592
        + ratio * (-0.284496736 + ratio * (1.421413741 + ratio * (-1.453152027 + ratio * 1.061405429)))
    )
    half = 0.5 * tail * bell
    cdf = jnp.where(gate >= 0, 1.0 - half, half)
    return gate * cdf, cdf + gate * (bell * (0.5 / math.pi) ** 0.5)


def load_grid(table, refs, me_ref, dest, sems, rows, first=0):
    copies = []
    for ref, places in zip(refs, table):
        for pos, (rel_d, rel_f, off) in enumerate(places):
            d = rel_d ^ me_ref[0]
            f = rel_f ^ me_ref[1]
            height = ref.shape[1]
            start = pl.multiple_of(d * rows + off, 16)
            copy = pltpu.make_async_copy(
                ref.at[pos], dest.at[f, pl.ds(start, height)], sems.at[first + len(copies)]
            )
            copy.start()
            copies.append(copy)
    return copies


def load_down(table, refs, me_ref, dest, sems, share, first=0):
    copies = []
    for ref, places in zip(refs, table):
        for pos, (rel_d, rel_f, off) in enumerate(places):
            if share is None:
                pairs = [(ref.at[pos], dest)]
            else:
                half, wide = share
                d = rel_d ^ me_ref[0]
                f = rel_f ^ me_ref[1]
                lane = pl.multiple_of(d * wide, 128)
                pairs = []
                for k in range(2):
                    row = pl.multiple_of(f * (2 * half) + k * half + off, 16)
                    pairs.append(
                        (
                            ref.at[pos, :, pl.ds(k * wide, wide)],
                            dest.at[pl.ds(row, ref.shape[1]), pl.ds(lane, wide)],
                        )
                    )
            for src, dst in pairs:
                copy = pltpu.make_async_copy(src, dst, sems.at[first + len(copies)])
                copy.start()
                copies.append(copy)
    return copies


def any_specs(count):
    return [pl.BlockSpec(memory_space=pl.ANY)] * count


SMEM_SPEC = pl.BlockSpec(memory_space=pltpu.SMEM)


def full_spec(shape):
    return pl.BlockSpec(shape, lambda i: (0,) * len(shape))


def attend_body(table, rows, heads, wide, *refs):
    n = len(table)
    me_ref, x_ref, vec_ref, bias_ref = refs[:4]
    w_refs = refs[4 : 4 + n]
    normed_ref, mixed_ref, probs_ref, context_ref, weight, sems = refs[4 + n :]
    count = sum(len(t) for t in table)

    @pl.when(pl.program_id(0) == 0)
    def _():
        for copy in load_grid(table, w_refs, me_ref, weight, sems, rows):
            copy.wait()

    hat, _ = norm_parts(x_ref[0].astype(F32))
    normed = (hat * vec_ref[0:1, :] + vec_ref[1:2, :]).astype(BF16)
    normed_ref[0] = normed
    shares = weight.shape[0]
    for f in range(shares):
        mixed = dot_nn(normed, weight[f, :, :wide]) + bias_ref[f]
        mixed_ref[f, 0] = mixed.astype(BF16)
    per = wide // HD

    def part(which, head):
        g = which * heads + head
        return mixed_ref[g // per, 0, :, (g % per) * HD : (g % per + 1) * HD]

    for head in range(heads):
        scores = dot_nt(part(0, head) * jnp.asarray(HD ** (-0.5), BF16), part(1, head))
        peak = jnp.max(scores, axis=-1, keepdims=True)
        expo = jnp.exp(scores - peak)
        total = jnp.sum(expo, axis=-1, keepdims=True)
        probs = (expo * (1.0 / total)).astype(BF16)
        probs_ref[0, head] = probs
        context_ref[0, :, head * HD : (head + 1) * HD] = dot_nn(probs, part(2, head)).astype(BF16)


def attend_forward(me, x, vec, bias, table, arrays, rows, wide):
    chips, seq, model = x.shape
    heads = model // HD
    shares = bias.shape[0]
    cols = arrays[0].shape[-1]
    count = sum(len(t) for t in table)
    return pl.pallas_call(
        functools.partial(attend_body, table, rows, heads, wide),
        grid=(chips,),
        in_specs=[
            SMEM_SPEC,
            pl.BlockSpec((1, seq, model), lambda i: (i, 0, 0)),
            full_spec(vec.shape),
            full_spec(bias.shape),
        ]
        + any_specs(len(arrays)),
        out_specs=[
            pl.BlockSpec((1, seq, model), lambda i: (i, 0, 0)),
            pl.BlockSpec((shares, 1, seq, wide), lambda i: (0, i, 0, 0)),
            pl.BlockSpec((1, heads, seq, seq), lambda i: (i, 0, 0, 0)),
            pl.BlockSpec((1, seq, model), lambda i: (i, 0, 0)),
        ],
        out_shape=[
            jax.ShapeDtypeStruct((chips, seq, model), BF16),
            jax.ShapeDtypeStruct((shares, chips, seq, wide), BF16),
            jax.ShapeDtypeStruct((chips, heads, seq, seq), BF16),
            jax.ShapeDtypeStruct((chips, seq, model), BF16),
        ],
        scratch_shapes=[
            pltpu.VMEM((shares, model, cols), BF16),
            pltpu.SemaphoreType.DMA((count,)),
        ],
        compiler_params=params_for(),
        name="attend_forward",
    )(me, x, vec, bias, *arrays)


def feed_up_body(q_table, u_table, rows, wide, *refs):
    nq, nu = len(q_table), len(u_table)
    me_ref, x_ref, context_ref, vec_ref, bias_ref = refs[:5]
    q_refs = refs[5 : 5 + nq]
    u_refs = refs[5 + nq : 5 + nq + nu]
    (
        middle_ref,
        normed_ref,
        active_ref,
        slope_ref,
        out_ref,
        packed,
        up,
        sems,
    ) = refs[5 + nq + nu :]
    count = sum(len(t) for t in q_table)
    shares, _, cols = packed.shape
    slim = cols - wide

    @pl.when(pl.program_id(0) == 0)
    def _():
        first = load_grid(q_table, q_refs, me_ref, packed, sems, rows)
        second = load_grid(u_table, u_refs, me_ref, up, sems, rows, first=count)
        for copy in first:
            copy.wait()
        for f in range(shares):
            out_ref[:, f * slim : (f + 1) * slim] = packed[f, :, wide:]
        for copy in second:
            copy.wait()

    branch = dot_nn(context_ref[0], out_ref[...])
    middle = x_ref[0].astype(F32) + branch + vec_ref[3:4, :]
    middle_ref[0] = middle
    hat, _ = norm_parts(middle)
    normed = (hat * vec_ref[4:5, :] + vec_ref[5:6, :]).astype(BF16)
    normed_ref[0] = normed
    span = up.shape[2]
    for f in range(shares):
        gate = dot_nn(normed, up[f]) + bias_ref[:, f * span : (f + 1) * span]
        active, slope = gelu_pair(gate)
        active_ref[0, :, f * span : (f + 1) * span] = active.astype(BF16)
        slope_ref[0, :, f * span : (f + 1) * span] = slope.astype(BF16)


def feed_up(me, x, context, vec, bias, q_table, q_arrays, u_table, u_arrays, rows, wide):
    chips, seq, model = x.shape
    ff = bias.shape[1]
    cols = q_arrays[0].shape[-1]
    span = u_arrays[0].shape[-1]
    shares = ff // span
    count = sum(len(t) for t in q_table) + sum(len(t) for t in u_table)
    tile = lambda w: pl.BlockSpec((1, seq, w), lambda i: (i, 0, 0))
    return pl.pallas_call(
        functools.partial(feed_up_body, q_table, u_table, rows, wide),
        grid=(chips,),
        in_specs=[SMEM_SPEC, tile(model), tile(model), full_spec(vec.shape), full_spec(bias.shape)]
        + any_specs(len(q_arrays) + len(u_arrays)),
        out_specs=[tile(model), tile(model), tile(ff), tile(ff), full_spec((model, model))],
        out_shape=[
            jax.ShapeDtypeStruct((chips, seq, model), F32),
            jax.ShapeDtypeStruct((chips, seq, model), BF16),
            jax.ShapeDtypeStruct((chips, seq, ff), BF16),
            jax.ShapeDtypeStruct((chips, seq, ff), BF16),
            jax.ShapeDtypeStruct((model, model), BF16),
        ],
        scratch_shapes=[
            pltpu.VMEM((shares, model, cols), BF16),
            pltpu.VMEM((shares, model, span), BF16),
            pltpu.SemaphoreType.DMA((count,)),
        ],
        compiler_params=params_for(),
        name="feed_up",
    )(me, x, context, vec, bias, *q_arrays, *u_arrays)


def feed_down_body(u_table, d_table, rows, share, *refs):
    nu, nd = len(u_table), len(d_table)
    me_ref, grad_ref, middle_ref, active_ref, slope_ref, vec_ref, out_ref = refs[:7]
    u_refs = refs[7 : 7 + nu]
    d_refs = refs[7 + nu : 7 + nu + nd]
    (
        result_ref,
        gate_grad_ref,
        middle_grad_ref,
        branch_grad_ref,
        context_grad_ref,
        sums_ref,
        bias_sums_ref,
        up,
        down,
        sems,
    ) = refs[7 + nu + nd :]
    count = sum(len(t) for t in u_table)
    shares, model, span = up.shape
    step = pl.program_id(0)

    @pl.when(step == 0)
    def _():
        first = load_grid(u_table, u_refs, me_ref, up, sems, rows)
        second = load_down(d_table, d_refs, me_ref, down, sems, share, first=count)
        sums_ref[...] = jnp.zeros_like(sums_ref)
        bias_sums_ref[...] = jnp.zeros_like(bias_sums_ref)
        for copy in first + second:
            copy.wait()

    seq = middle_ref.shape[1]
    middle = middle_ref[0]
    feed_grad = grad_ref[:, 0].reshape(seq, model)
    result = middle + dot_nt(active_ref[0], down[...]) + vec_ref[10:11, :]
    result_ref[:, 0] = result.astype(BF16).reshape(result_ref.shape[0], -1, model)
    normed_grad = jnp.zeros((seq, model), F32)
    for f in range(shares):
        lanes = slice(f * span, (f + 1) * span)
        active_grad = dot_nn(feed_grad, down[:, lanes])
        gate_grad = (active_grad * slope_ref[0, :, lanes].astype(F32)).astype(BF16)
        gate_grad_ref[0, :, lanes] = gate_grad
        bias_sums_ref[:, lanes] += jnp.sum(gate_grad.astype(F32), axis=0, keepdims=True)
        normed_grad += dot_nt(gate_grad, up[f])
    hat, factor = norm_parts(middle)
    gain = vec_ref[4:5, :]
    grad_full = feed_grad.astype(F32)
    middle_grad = grad_full + norm_back(normed_grad, hat, factor, gain)
    middle_grad_ref[0] = middle_grad
    branch_grad = middle_grad.astype(BF16)
    branch_grad_ref[0] = branch_grad
    context_grad_ref[0] = dot_nt(branch_grad, out_ref[...]).astype(BF16)
    sums_ref[0:1, :] += jnp.sum(branch_grad.astype(F32), axis=0, keepdims=True)
    sums_ref[1:2, :] += jnp.sum(normed_grad * hat, axis=0, keepdims=True)
    sums_ref[2:3, :] += jnp.sum(normed_grad, axis=0, keepdims=True)
    sums_ref[3:4, :] += jnp.sum(grad_full, axis=0, keepdims=True)


def feed_down(
    me, grad, middle, active, slope, vec, out_whole, u_table, u_arrays, d_table, d_arrays, rows, share
):
    chips, seq, model = middle.shape
    ff = active.shape[2]
    blocks, _, seen, _ = grad.shape
    span = u_arrays[0].shape[-1]
    shares = ff // span
    count = sum(len(t) for t in u_table) + 2 * sum(len(t) for t in d_table)
    tile = lambda w: pl.BlockSpec((1, seq, w), lambda i: (i, 0, 0))
    spread = pl.BlockSpec((blocks, 1, seen, model), lambda i: (0, i, 0, 0))
    return pl.pallas_call(
        functools.partial(feed_down_body, u_table, d_table, rows, share),
        grid=(chips,),
        in_specs=[
            SMEM_SPEC,
            spread,
            tile(model),
            tile(ff),
            tile(ff),
            full_spec(vec.shape),
            full_spec(out_whole.shape),
        ]
        + any_specs(len(u_arrays) + len(d_arrays)),
        out_specs=[
            spread,
            tile(ff),
            tile(model),
            tile(model),
            tile(model),
            full_spec((8, model)),
            full_spec((1, ff)),
        ],
        out_shape=[
            jax.ShapeDtypeStruct(grad.shape, BF16),
            jax.ShapeDtypeStruct((chips, seq, ff), BF16),
            jax.ShapeDtypeStruct((chips, seq, model), F32),
            jax.ShapeDtypeStruct((chips, seq, model), BF16),
            jax.ShapeDtypeStruct((chips, seq, model), BF16),
            jax.ShapeDtypeStruct((8, model), F32),
            jax.ShapeDtypeStruct((1, ff), F32),
        ],
        scratch_shapes=[
            pltpu.VMEM((shares, model, span), BF16),
            pltpu.VMEM((model, ff), BF16),
            pltpu.SemaphoreType.DMA((count,)),
        ],
        compiler_params=params_for(),
        name="feed_down",
    )(me, grad, middle, active, slope, vec, out_whole, *u_arrays, *d_arrays)


def attend_back_body(heads, mixed_ref, probs_ref, context_ref, grad_ref, mixed_grad_ref, sums_ref):
    wide = mixed_ref.shape[3]
    per = wide // HD

    @pl.when(pl.program_id(0) == 0)
    def _():
        sums_ref[...] = jnp.zeros_like(sums_ref)

    def place(which, head):
        g = which * heads + head
        return g // per, slice((g % per) * HD, (g % per + 1) * HD)

    def part(which, head):
        f, lanes = place(which, head)
        return mixed_ref[f, 0, :, lanes]

    for head in range(heads):
        lanes = slice(head * HD, (head + 1) * HD)
        out_grad = grad_ref[0, :, lanes]
        probs = probs_ref[0, head]
        query, key, value = part(0, head), part(1, head), part(2, head)
        value_grad = dot_tn(probs, out_grad).astype(BF16)
        prob_grad = dot_nt(out_grad, value)
        inner = jnp.sum(
            out_grad.astype(F32) * context_ref[0, :, lanes].astype(F32), axis=-1, keepdims=True
        )
        score_grad = (probs.astype(F32) * ((prob_grad - inner) * HD ** (-0.5))).astype(BF16)
        grads = (dot_nn(score_grad, key).astype(BF16), dot_tn(score_grad, query).astype(BF16), value_grad)
        for which in range(3):
            f, spot = place(which, head)
            mixed_grad_ref[f, 0, :, spot] = grads[which]
        sums_ref[0:1, lanes] += jnp.sum(value_grad.astype(F32), axis=0, keepdims=True)


def attend_back(mixed, probs, context, context_grad):
    shares, chips, seq, wide = mixed.shape
    model = context.shape[2]
    heads = model // HD
    tile = pl.BlockSpec((1, seq, model), lambda i: (i, 0, 0))
    packed = pl.BlockSpec((shares, 1, seq, wide), lambda i: (0, i, 0, 0))
    return pl.pallas_call(
        functools.partial(attend_back_body, heads),
        grid=(chips,),
        in_specs=[packed, pl.BlockSpec((1, heads, seq, seq), lambda i: (i, 0, 0, 0)), tile, tile],
        out_specs=[packed, full_spec((8, model))],
        out_shape=[
            jax.ShapeDtypeStruct(mixed.shape, BF16),
            jax.ShapeDtypeStruct((8, model), F32),
        ],
        compiler_params=params_for(),
        name="attend_back",
    )(mixed, probs, context, context_grad)


def tokens_back_body(table, rows, *refs):
    n = len(table)
    me_ref, x_ref, grad_ref, mixed_grad_ref, vec_ref = refs[:5]
    w_refs = refs[5 : 5 + n]
    tokens_ref, sums_ref, weight, sems = refs[5 + n :]
    wide = mixed_grad_ref.shape[3]

    @pl.when(pl.program_id(0) == 0)
    def _():
        sums_ref[...] = jnp.zeros_like(sums_ref)
        for copy in load_grid(table, w_refs, me_ref, weight, sems, rows):
            copy.wait()

    normed_grad = dot_nt(mixed_grad_ref[0, 0], weight[0, :, :wide])
    for f in range(1, weight.shape[0]):
        normed_grad += dot_nt(mixed_grad_ref[f, 0], weight[f, :, :wide])
    hat, factor = norm_parts(x_ref[0].astype(F32))
    tokens_ref[0] = grad_ref[0] + norm_back(normed_grad, hat, factor, vec_ref[0:1, :])
    sums_ref[0:1, :] += jnp.sum(normed_grad * hat, axis=0, keepdims=True)
    sums_ref[1:2, :] += jnp.sum(normed_grad, axis=0, keepdims=True)


def tokens_back(me, x, middle_grad, mixed_grad, vec, table, arrays, rows):
    chips, seq, model = x.shape
    shares, _, _, wide = mixed_grad.shape
    cols = arrays[0].shape[-1]
    count = sum(len(t) for t in table)
    tile = pl.BlockSpec((1, seq, model), lambda i: (i, 0, 0))
    return pl.pallas_call(
        functools.partial(tokens_back_body, table, rows),
        grid=(chips,),
        in_specs=[
            SMEM_SPEC,
            tile,
            tile,
            pl.BlockSpec((shares, 1, seq, wide), lambda i: (0, i, 0, 0)),
            full_spec(vec.shape),
        ]
        + any_specs(len(arrays)),
        out_specs=[tile, full_spec((8, model))],
        out_shape=[
            jax.ShapeDtypeStruct((chips, seq, model), F32),
            jax.ShapeDtypeStruct((8, model), F32),
        ],
        scratch_shapes=[
            pltpu.VMEM((shares, model, cols), BF16),
            pltpu.SemaphoreType.DMA((count,)),
        ],
        compiler_params=params_for(),
        name="tokens_back",
    )(me, x, middle_grad, mixed_grad, vec, *arrays)


def place_of(order, rel_d, rel_f):
    pos = 0
    for is_dp, value in order:
        bit = ((rel_d if is_dp else rel_f) // value) % 2
        pos = pos * 2 + bit
    return pos


def up_grad_body(order, rows, me_ref, left_ref, right_ref, out_ref):
    f = pl.program_id(0)
    grad = dot_tn(left_ref[...], right_ref[...])
    if order is None:
        out_ref[f] = grad.astype(BF16)
    else:
        for d in range(grad.shape[0] // rows):
            pos = place_of(order, d ^ me_ref[0], f ^ me_ref[1])
            out_ref[pos] = grad[d * rows : (d + 1) * rows].astype(BF16)


def up_grad_blocks(me, left, right, order, rows, shares):
    tokens, model = left.shape
    span = right.shape[1] // shares
    shape = (shares, model, span) if order is None else (shares * model // rows, rows, span)
    return pl.pallas_call(
        functools.partial(up_grad_body, order, rows),
        grid=(shares,),
        in_specs=[
            SMEM_SPEC,
            full_spec(left.shape),
            pl.BlockSpec((tokens, span), lambda i: (0, i)),
        ],
        out_specs=full_spec(shape),
        out_shape=jax.ShapeDtypeStruct(shape, BF16),
        compiler_params=params_for(),
        name="up_grad",
    )(me, left, right)


def down_grad_body(order, half, me_ref, grad_ref, active_ref, out_ref):
    d = pl.program_id(0)
    grad_seen = grad_ref[...]
    whole = dot_tn(grad_seen, active_ref[...])
    if order is None:
        out_ref[...] = whole.astype(BF16)
    else:
        wide = whole.shape[1]
        for f in range(whole.shape[0] // (2 * half)):
            pos = place_of(order, d ^ me_ref[0], f ^ me_ref[1])
            for k in range(2):
                start = (2 * f + k) * half
                out_ref[pos, :, k * wide : (k + 1) * wide] = whole[start : start + half].astype(BF16)


def down_grad_blocks(me, grad, active, order, half, wide):
    tokens, model = grad.shape
    ff = active.shape[1]
    if order is None:
        steps, width, shape = 4, ff // 4, (model, ff)
        out_spec = pl.BlockSpec((model, width), lambda i: (0, i))
    else:
        steps, width = ff // wide, wide
        shape = (steps * model // (2 * half), half, 2 * wide)
        out_spec = full_spec(shape)
    return pl.pallas_call(
        functools.partial(down_grad_body, order, half),
        grid=(steps,),
        in_specs=[
            SMEM_SPEC,
            full_spec(grad.shape),
            pl.BlockSpec((tokens, width), lambda i: (0, i)),
        ],
        out_specs=out_spec,
        out_shape=jax.ShapeDtypeStruct(shape, BF16),
        compiler_params=params_for(),
        name="down_grad",
    )(me, grad, active)


def qkv_grad_body(order, rows, me_ref, normed_ref, mixed_grad_ref, context_ref, branch_ref, out_ref, slots):
    f = pl.program_id(0)
    shares = slots.shape[0]
    wide = mixed_grad_ref.shape[2]
    slim = slots.shape[2]

    @pl.when(f == 0)
    def _():
        whole = dot_tn(context_ref[...], branch_ref[...]).astype(BF16)
        for k in range(shares):
            slots[k] = whole[:, k * slim : (k + 1) * slim]

    grad = dot_tn(normed_ref[...], mixed_grad_ref[0]).astype(BF16)
    side = slots[f]
    if order is None:
        out_ref[f, :, :wide] = grad
        out_ref[f, :, wide:] = side
    else:
        for d in range(grad.shape[0] // rows):
            pos = place_of(order, d ^ me_ref[0], f ^ me_ref[1])
            out_ref[pos, :, :wide] = grad[d * rows : (d + 1) * rows]
            out_ref[pos, :, wide:] = side[d * rows : (d + 1) * rows]


def qkv_grad_blocks(me, normed, mixed_grad, context, branch_grad, order, rows):
    tokens, model = normed.shape
    shares, _, wide = mixed_grad.shape
    slim = model // shares
    cols = wide + slim
    shape = (shares, model, cols) if order is None else (shares * model // rows, rows, cols)
    return pl.pallas_call(
        functools.partial(qkv_grad_body, order, rows),
        grid=(shares,),
        in_specs=[
            SMEM_SPEC,
            full_spec(normed.shape),
            pl.BlockSpec((1, tokens, wide), lambda i: (i, 0, 0)),
            full_spec(context.shape),
            full_spec(branch_grad.shape),
        ],
        out_specs=full_spec(shape),
        out_shape=jax.ShapeDtypeStruct(shape, BF16),
        scratch_shapes=[pltpu.VMEM((shares, model, slim), BF16)],
        compiler_params=params_for(),
        name="qkv_grad",
    )(me, normed, mixed_grad, context, branch_grad)


DP, FSDP = "dp", "fsdp"


def swap(value, axis, bit):
    size = lax.axis_size(axis)
    return lax.ppermute(value, axis, [(i, i ^ bit) for i in range(size)])


def grow(value, step, dim=0):
    return jnp.concatenate([value, swap(value, *step)], axis=dim)


def add_low(left, right):
    return (left.astype(F32) + right.astype(F32)).astype(BF16)


def fold(value, step, dim=0, low=True):
    keep = lax.index_in_dim(value, 0, dim, keepdims=False)
    send = lax.index_in_dim(value, 1, dim, keepdims=False)
    arrived = swap(send, *step)
    if low:
        return add_low(keep, arrived)
    return keep.astype(F32) + arrived.astype(F32)


def rel_table(steps, last, off):
    places = []
    for pos in range(2 ** len(steps)):
        rel = {DP: 0, FSDP: 0}
        for k, (axis, bit) in enumerate(steps):
            if (pos >> k) & 1:
                rel[axis] ^= bit
        if last is not None:
            rel[last[0]] ^= last[1]
        places.append((rel[DP], rel[FSDP], off))
    return tuple(places)


CORE, XS, YS, Z_NEAR, Z_FAR = (FSDP, 1), (FSDP, 2), (DP, 1), (DP, 2), (DP, 4)
XY = [Z_FAR, Z_NEAR, XS, YS]
YX = [Z_FAR, Z_NEAR, YS, XS]


def grow_end(value, second):
    for step in second:
        value = grow(value, step)
    return value, swap(value, *CORE)


def order_of(steps):
    return [(axis == DP, bit) for axis, bit in steps]


def adam_step(weight, gradient, first_mom, second, clip_factor, step_rate, decay_rate):
    scaled = gradient * clip_factor
    first_new = 0.5 * first_mom + 0.5 * scaled
    second_new = 0.5 * second + 0.5 * scaled * scaled
    correction = 1.0 - 0.5**STEP
    update = first_new / correction / (jnp.sqrt(second_new / correction) + 1e-08)
    return (first_new, second_new, weight - step_rate * (update + decay_rate * weight))


def on_device(
    tokens,
    visible_index,
    cotangent,
    qkv_weight,
    out_weight,
    up_weight,
    down_weight,
    vectors,
    qkv_first,
    out_first,
    up_first,
    down_first,
    vector_first,
    qkv_second,
    out_second,
    up_second,
    down_second,
    vector_second,
):
    _, chip_count, seq_len, model_width = tokens.shape
    dp_size, fsdp_size = lax.axis_size(DP), lax.axis_size(FSDP)
    device_count = dp_size * fsdp_size
    both = (DP, FSDP)
    block_count = dp_size
    block_seen = seq_len // block_count
    block_len = cotangent.shape[2]
    chips_group = chip_count * block_count
    rows, wide = qkv_weight.shape
    slim = out_weight.shape[1]
    span = up_weight.shape[1]
    ff_width = span * fsdp_size
    half = slim // 2
    tall = down_weight.shape[0]
    folded = (dp_size, fsdp_size) == (8, 4)

    share_q = jnp.concatenate([qkv_weight, out_weight], axis=1).astype(BF16)
    share_u = up_weight.astype(BF16)
    down_turned = down_weight.astype(BF16).T

    vec_rows, vec_cols = vectors.shape
    vector_copies = jnp.broadcast_to(vectors.astype(BF16), (device_count, vec_rows, vec_cols))
    vec = lax.all_to_all(vector_copies, both, split_axis=0, concat_axis=0, tiled=True)
    vec = vec.reshape(dp_size, fsdp_size, vec_rows, vec_cols).transpose(1, 2, 0, 3)
    vec = vec.reshape(fsdp_size * vec_rows, model_width).astype(F32)

    if folded:
        me = jnp.stack([lax.axis_index(DP), lax.axis_index(FSDP)]).astype(jnp.int32)
        share_d = jnp.concatenate([down_turned[:half], down_turned[half:]], axis=1)
        cur = grow(grow(share_q[None], Z_FAR), Z_NEAR)
        cut = rows // 2
        q_arrays = grow_end(cur[:, :cut], [XS, YS]) + grow_end(cur[:, cut:], [YS, XS])
        q_table = (
            rel_table(XY, None, 0),
            rel_table(XY, CORE, 0),
            rel_table(YX, None, cut),
            rel_table(YX, CORE, cut),
        )
        cur = jnp.stack([share_u, share_d])[:, None]
        cur = grow(grow(cur, Z_FAR, 1), Z_NEAR, 1)
        u_arrays = grow_end(cur[0], [XS, YS])
        d_arrays = grow_end(cur[1], [YS, XS])
        u_table = (rel_table(XY, None, 0), rel_table(XY, CORE, 0))
        d_table = (rel_table(YX, None, 0), rel_table(YX, CORE, 0))
        order_d = [CORE, XS, YS, Z_NEAR, Z_FAR]
        order_u = [CORE, YS, XS, Z_NEAR, Z_FAR]
        q_order, u_order, d_order = order_of(order_d), order_of(order_u), order_of(order_d)
        down_share = (half, tall)
    else:
        me = jnp.zeros((2,), jnp.int32)

        def gather_whole(share):
            whole = lax.all_gather(share, both, axis=0, tiled=False)
            whole = whole.reshape((dp_size, fsdp_size) + share.shape).transpose(1, 0, 2, 3)
            return whole.reshape(fsdp_size, dp_size * share.shape[0], share.shape[1])

        q_arrays = (gather_whole(share_q),)
        u_arrays = (gather_whole(share_u),)
        down_whole = lax.all_gather(down_turned, both, axis=0, tiled=False)
        down_whole = down_whole.reshape(dp_size, fsdp_size, slim, tall).transpose(1, 2, 0, 3)
        d_arrays = (down_whole.reshape(1, model_width, ff_width),)
        q_table = u_table = (tuple((0, f, 0) for f in range(fsdp_size)),)
        d_table = (((0, 0, 0),),)
        q_order = u_order = d_order = None
        down_share = None

    my_block = lax.axis_index(DP)
    places = visible_index[0].reshape(chips_group, block_count, block_seen)
    places = lax.dynamic_index_in_dim(places, my_block, 1, keepdims=False) - my_block * block_len
    slot_ids = lax.broadcasted_iota(jnp.int32, (chips_group, block_len, block_seen), 1)
    pick = (places[:, None, :] == slot_ids).astype(BF16)
    gaps = 1.0 - jnp.sum(pick.astype(F32), axis=-1)
    cot = cotangent[0]
    cot_seen = jnp.einsum("cpv,cpd->cvd", pick, cot, preferred_element_type=F32).astype(BF16)
    cot_seen = cot_seen.reshape(block_count, chip_count, block_seen, model_width)
    mask_grad = jnp.einsum("cp,cpd->d", gaps.astype(BF16), cot, preferred_element_type=F32)
    grad = lax.all_to_all(cot_seen, DP, split_axis=0, concat_axis=0, tiled=True)
    whole_tiles = block_seen % 16 == 0
    if not whole_tiles:
        grad = grad.transpose(1, 0, 2, 3).reshape(1, chip_count, seq_len, model_width)

    x = tokens[0]
    value_bias = jnp.concatenate([jnp.zeros((2 * model_width,), F32), vec[2]])
    value_bias = value_bias.reshape(fsdp_size, 1, wide)
    up_bias = vec[6:10].reshape(1, ff_width)
    normed, mixed, probs, context = attend_forward(me, x, vec, value_bias, q_table, q_arrays, rows, wide)
    middle, normed_two, active, slope, out_whole = feed_up(
        me, x, context, vec, up_bias, q_table, q_arrays, u_table, u_arrays, rows, wide
    )
    result, gate_grad, middle_grad, branch_grad, context_grad, sums_two, up_sums = feed_down(
        me, grad, middle, active, slope, vec, out_whole, u_table, u_arrays, d_table, d_arrays, rows, down_share
    )
    token_count = chip_count * seq_len
    flat = lambda v: v.reshape(token_count, v.shape[-1])
    grad_rows = flat(grad.transpose(1, 0, 2, 3).reshape(chip_count, seq_len, model_width))
    down_blocks = down_grad_blocks(me, grad_rows, flat(active), d_order, half, tall)
    up_blocks = up_grad_blocks(me, flat(normed_two), flat(gate_grad), u_order, rows, fsdp_size)

    if not whole_tiles:
        result = result.reshape(chip_count, block_count, block_seen, model_width).transpose(1, 0, 2, 3)
    arrived = lax.all_to_all(result, DP, split_axis=0, concat_axis=0, tiled=True)
    arrived = arrived.reshape(chips_group, block_seen, model_width)

    mixed_grad, sums_value = attend_back(mixed, probs, context, context_grad)
    q_blocks = qkv_grad_blocks(
        me,
        flat(normed),
        mixed_grad.reshape(fsdp_size, token_count, wide),
        flat(context),
        flat(branch_grad),
        q_order,
        rows,
    )
    tokens_grad, sums_one = tokens_back(me, x, middle_grad, mixed_grad, vec, q_table, q_arrays, rows)

    filled = jnp.einsum("cpv,cvd->cpd", pick, arrived, preferred_element_type=F32)
    filled = filled + gaps[..., None] * vec[11]
    full_layout = filled.astype(BF16).reshape(1, chips_group, block_len, model_width)

    if folded:

        def fold_all(blocks, steps):
            for k, step in enumerate(steps):
                blocks = blocks.reshape((2, blocks.shape[0] // 2) + blocks.shape[1:])
                blocks = fold(blocks, step, 0, k < len(steps) - 1)
            return blocks[0]

        d_sum = fold_all(down_blocks, order_d)
        u_sum = fold_all(up_blocks, order_u)
        cur = fold(q_blocks.reshape((2, 16) + q_blocks.shape[1:]), CORE)
        cur = cur.reshape((2, 2, 4) + cur.shape[1:])
        left = fold(fold(cur[:, :, :, :cut], XS), YS)
        right = fold(fold(cur[:, :, :, cut:], YS, 1), XS)
        cur = jnp.concatenate([left, right], axis=1).reshape((2, 2) + share_q.shape)
        q_sum = fold(fold(cur, Z_NEAR), Z_FAR, 0, False)
        d_sum = jnp.concatenate([d_sum[:, :tall], d_sum[:, tall:]], axis=0).T
    else:

        def scatter_whole(whole):
            cols = whole.shape[2]
            pieces = whole.reshape(fsdp_size, dp_size, -1, cols).transpose(1, 0, 2, 3)
            pieces = pieces.reshape(-1, cols)
            return lax.psum_scatter(pieces, both, scatter_dimension=0, tiled=True).astype(F32)

        q_sum, u_sum = scatter_whole(q_blocks), scatter_whole(up_blocks)
        pieces = down_blocks.reshape(fsdp_size, slim, dp_size, tall).transpose(2, 0, 1, 3)
        pieces = pieces.reshape(device_count * slim, tall)
        d_sum = lax.psum_scatter(pieces, both, scatter_dimension=0, tiled=True).astype(F32).T

    vector_grad = jnp.concatenate(
        [
            sums_one[:2],
            sums_value[:1],
            sums_two[:3],
            up_sums.reshape(-1, model_width),
            sums_two[3:4],
            mask_grad[None],
        ],
        axis=0,
    )
    parts = vector_grad.reshape(fsdp_size, vec_rows, dp_size, vec_cols).transpose(2, 0, 1, 3)
    parts = parts.reshape(device_count, vec_rows, vec_cols)
    parts = lax.all_to_all(parts, both, split_axis=0, concat_axis=0, tiled=True)
    shares = (q_sum[:, :wide], q_sum[:, wide:], u_sum, d_sum, jnp.sum(parts, axis=0))
    squares = jnp.sum(q_sum * q_sum) + jnp.sum(u_sum * u_sum) + jnp.sum(d_sum * d_sum)
    squares = squares + jnp.sum(shares[4] * shares[4])
    square_parts = jnp.broadcast_to(squares, (device_count, 1))
    grad_total = jnp.sum(lax.all_to_all(square_parts, both, split_axis=0, concat_axis=0, tiled=True))
    grad_norm = jnp.sqrt(grad_total)
    tokens_all = device_count * chip_count * seq_len
    threshold = 0.05 * model_width * math.sqrt(tokens_all)
    clip = jnp.minimum(1.0, threshold / grad_norm)
    rate = 0.6 / math.sqrt(model_width)
    out_rate = 0.6 / math.sqrt(model_width // 32)
    down_rate = 0.6 / math.sqrt(ff_width)
    qkv_out = adam_step(qkv_weight, shares[0], qkv_first, qkv_second, clip, rate, 0.05)
    out_out = adam_step(out_weight, shares[1], out_first, out_second, clip, out_rate, 0.05)
    up_out = adam_step(up_weight, shares[2], up_first, up_second, clip, rate, 0.05)
    down_out = adam_step(down_weight, shares[3], down_first, down_second, clip, down_rate, 0.05)
    vec_out = adam_step(vectors, shares[4], vector_first, vector_second, clip, 0.45, 0.0)
    return (
        full_layout,
        tokens_grad[None],
        *qkv_out,
        qkv_out[2].astype(BF16),
        *out_out,
        out_out[2].astype(BF16),
        *up_out,
        up_out[2].astype(BF16),
        *down_out,
        down_out[2].astype(BF16),
        *vec_out,
        grad_norm,
    )


def solution(mesh):
    grid = P("dp", "fsdp")
    table = P("fsdp", "dp")
    weights = (grid, grid, grid, grid, table)
    in_specs = (
        P("fsdp", "dp", None, None),
        P("fsdp", None, None),
        P("fsdp", None, "dp", None),
        *weights,
        *weights,
        *weights,
    )
    out_specs = (
        P("fsdp", None, "dp", None),
        P("fsdp", "dp", None, None),
        *(grid,) * 16,
        *(table,) * 3,
        P(),
    )
    return jax.shard_map(
        on_device, mesh=mesh, in_specs=in_specs, out_specs=out_specs, check_vma=False
    )
```

time: 861 us -> 451 us (0.52)
  waiting for transfers between devices: 405 us -> 137 us
  matrix products: 207 us -> 12.1 us
  Pallas kernels: 0 us -> 147 us
  local copies, waits for them, and re-layouts: 151 us -> 37.2 us
  starting transfers between devices: 26.5 us -> 70 us
  between operations: 20.6 us -> 6.13 us
    dot_general x21 -> x3, matrix products: 207 us -> 12.1 us  [the longest x1 6.24 us: on_device(): jnp.einsum('cpv,cvd->cpd', pick, arrived, preferred_element_type=F32)]
    all_gather x4 -> x0, waiting for transfers between devices: 165 us -> none  [gather_whole(): pieces = lax.all_gather(shard, both, axis=0, tiled=False)]
    pallas_call x0 -> x8, Pallas kernels: none -> 147 us  [the longest x1 29.2 us: feed_down(): pl.pallas_call(functools.partial(feed_down_body, u_table, d_table, rows,...]
    ppermute x0 -> x33, waiting for transfers between devices: none -> 131 us  [swap(): return lax.ppermute(value, axis, [(i, i ^ bit) for i in range(size)])]
    reduce_scatter x3 -> x0, waiting for transfers between devices: 122 us -> none  [scatter_sum(): lax.psum_scatter(pieces, both, scatter_dimension=0, tiled=True)]
    unnamed x9 -> x0, waiting for transfers between devices: 118 us -> none
    reshape x20 -> x4, local copies, waits for them, and re-layouts: 73.9 us -> 3.36 us  [the longest x1 1.38 us: on_device(): value_bias = value_bias.reshape(fsdp_size, 1, wide)]
    ppermute x0 -> x33, starting transfers between devices: none -> 41.6 us  [swap(): return lax.ppermute(value, axis, [(i, i ^ bit) for i in range(size)])]
  transfers between devices with their start and end apart: 13 -> 38, of which waited for: 8 -> 16; matrix products, arithmetic and copies ran while one was open for 33% -> 17% of each run, Pallas kernels for 0% -> 18%
where the time goes in v2:
time: 451 us; the launch traced here: 446 us
  Pallas kernels  147 us (33%)
  waiting for transfers between devices  137 us (30%)
  starting transfers between devices  70 us (16%)
  local copies, waits for them, and re-layouts  37.2 us (8%)
  other arithmetic  37 us (8%)
  matrix products  12.1 us (3%)
  between operations  6.13 us (1%)
    ppermute x33, waiting for transfers between devices, swap(): return lax.ppermute(value, axis, [(i, i ^ bit) for i in range(size)])  131 us
    ppermute x33, starting transfers between devices, swap(): return lax.ppermute(value, axis, [(i, i ^ bit) for i in range(size)])  41.6 us
    pallas_call x1, Pallas kernels, feed_down(): pl.pallas_call(functools.partial(feed_down_body, u_table, d_table, rows,...  29.2 us
    pallas_call x1, Pallas kernels, feed_up(): pl.pallas_call(functools.partial(feed_up_body, q_table, u_table, rows, wi...  25.3 us
    pallas_call x1, Pallas kernels, attend_back(): pl.pallas_call(functools.partial(attend_back_body, heads), grid=(chips,),...  22.9 us
    pallas_call x1, Pallas kernels, attend_forward(): pl.pallas_call(functools.partial(attend_body, table, rows, heads, wide),...  21.8 us
    convert_element_type x13, other arithmetic, add_low(): return (left.astype(F32) + right.astype(F32)).astype(BF16)  16 us
    pallas_call x1, Pallas kernels, down_grad_blocks(): pl.pallas_call(functools.partial(down_grad_body, order, half), grid=(step...  12.8 us
  transfers between devices with their start and end apart: 38, of which 16 were waited for; matrix products, arithmetic and copies ran while one was open for 17% of the time, Pallas kernels for 18%

profile of v2, /device:TPU:0, one launch (start us, length us, event | category | flops | bytes accessed | tf_op | source)
XLA Modules:
  0.0 445.9 jit_solution(16199028922410560158)
XLA Ops:
  2.7 4.1 collective-permute-start.8
  6.8 13.3 %collective-permute-done.8 = bf16[2,1,96,768]{3,2,1,0:T(8,128)(2,1)S(1)} collective-permute-done((bf16[2,1,96,768]{3,2,1,0:T(8,128)(2,1)S(1)}, bf16[2,1,96,768]{3,2,1,0:T(8,128)(2,1)S(1)}, u32[]{:S(2)}, u32[]{:S(2)}) %collective-permute-start.8) | collective-permute-done | bytes 294944 | tf_op jit(solution)/shard_map/ppermute | solution.py:608
  21.0 13.8 %collective-permute-done.9 = bf16[2,2,96,768]{3,2,1,0:T(8,128)(2,1)S(1)} collective-permute-done((bf16[2,2,96,768]{3,2,1,0:T(8,128)(2,1)S(1)}, bf16[2,2,96,768]{3,2,1,0:T(8,128)(2,1)S(1)}, u32[]{:S(2)}, u32[]{:S(2)}) %collective-permute-start.9) | collective-permute-done | bytes 589856 | tf_op jit(solution)/shard_map/ppermute | solution.py:608
  37.9 10.8 %collective-permute-done.10 = bf16[4,96,768]{2,1,0:T(8,128)(2,1)S(1)} collective-permute-done((bf16[4,96,768]{2,1,0:T(8,128)(2,1)S(1)}, bf16[4,96,768]{2,1,0:T(8,128)(2,1)S(1)}, u32[]{:S(2)}, u32[]{:S(2)}) %collective-permute-start.10) | collective-permute-done | bytes 589856 | tf_op jit(solution)/shard_map/ppermute | solution.py:608
  51.3 4.5 %collective-permute-start = (bf16[1,96,768]{2,1,0:T(8,128)(2,1)S(1)}, bf16[1,96,768]{2,1,0:T(8,128)(2,1)S(1)}, u32[]{:S(2)}, u32[]{:S(2)}) collective-permute-start(bf16[1,96,768]{2,1,0:T(8,128)(2,1)S(1)} %pad_maximum_fusion.14), channel_id=1, source_target_pairs={{0,16},{4,20},{8,24},{12,28},{16,0},{20,4},{24,8},{28,12},{1,17},{... | collective-permute-start | bytes 442376 | tf_op jit(solution)/shard_map/ppermute | solution.py:608
  56.4 2.7 all-to-all-start.1
  60.5 1.8 collective-permute-start.14
  63.9 4.9 %fusion.5 = bf16[32,32,768]{2,1,0:T(8,128)(2,1)} fusion(bf16[1,32,128,768]{3,2,1,0:T(8,128)(2,1)} %param.20, s32[32,32]{1,0:T(8,128)S(1)} %bitcast.132), kind=kOutput, calls=%fused_computation.13 | convolution fusion | flops 202244096 | bytes 7868416 | tf_op jit(solution)/shard_map/cpv,cpd->cvd/dot_general | solution.py:758
  68.8 2.4 collective-permute-done.1
  71.3 4.5 %all-to-all-done.1 = bf16[32,3,96]{2,1,0:T(4,128)(2,1)S(1)} async-done(((bf16[32,3,96]{2,1,0:T(4,128)(2,1)}), bf16[32,3,96]{2,1,0:T(4,128)(2,1)S(1)}, u32[]{:S(2)}, u32[]{:S(2)}) %all-to-all-start.1) | async-done | bytes 18464 | tf_op jit(solution)/shard_map/all_to_all | solution.py:707
  75.9 8.4 %all-to-all-start = ((bf16[8,4,32,768]{3,2,1,0:T(8,128)(2,1)}), bf16[8,4,32,768]{3,2,1,0:T(8,128)(2,1)}, u32[]{:S(2)}, u32[]{:S(2)}) async-start(bf16[8,4,32,768]{3,2,1,0:T(8,128)(2,1)} %bitcast.4), calls=%async_computation | async-start | bytes 3145728 | tf_op jit(solution)/shard_map/all_to_all | solution.py:761
  84.3 2.1 collective-permute-start.5
  86.4 1.7 pad_maximum_fusion.refs_9_.refs_7_
  89.1 2.9 pad_maximum_fusion.1.refs_9_
  93.6 12.5 %collective-permute-done.5 = bf16[4,48,768]{2,1,0:T(8,128)(2,1)S(1)} collective-permute-done((bf16[4,48,768]{2,1,0:T(8,128)(2,1)S(1)}, bf16[4,48,768]{2,1,0:T(8,128)(2,1)S(1)}, u32[]{:S(2)}, u32[]{:S(2)}) %collective-permute-start.5) | collective-permute-done | bytes 294944 | tf_op jit(solution)/shard_map/ppermute | solution.py:608
  108.9 10.4 %collective-permute-done.6 = bf16[8,48,768]{2,1,0:T(8,128)(2,1)S(1)} collective-permute-done((bf16[8,48,768]{2,1,0:T(8,128)(2,1)S(1)}, bf16[8,48,768]{2,1,0:T(8,128)(2,1)S(1)}, u32[]{:S(2)}, u32[]{:S(2)}) %collective-permute-start.6) | collective-permute-done | bytes 589856 | tf_op jit(solution)/shard_map/ppermute | solution.py:608
  119.6 4.2 collective-permute-done.3
  133.2 21.8 %attend_forward.1 = (bf16[4,256,768]{2,1,0:T(8,128)(2,1)}, bf16[4,4,256,576]{3,2,1,0:T(8,128)(2,1)}, bf16[4,12,256,256]{3,2,1,0:T(8,128)(2,1)}, bf16[4,256,768]{2,1,0:T(8,128)(2,1)}) custom-call(s32[2]{0:T(128)} %pad_add_fusion.refs_0_.me_ref, bf16[4,256,768]{2,1,0:T(8,128)(2,1)} %bitcast.120, f32[12,768]{1,0:T(8,128)} %reshape.229.refs_2_.refs_3_.refs_5_.refs_4_, ...), custom_call_target="tpu_custom_call" | custom-call | tf_op jit(solution)/shard_map/attend_forward/pallas_call | solution.py:155
  155.1 25.3 %feed_up.1 = (f32[4,256,768]{2,1,0:T(8,128)}, bf16[4,256,768]{2,1,0:T(8,128)(2,1)}, bf16[4,256,3072]{2,1,0:T(8,128)(2,1)}, bf16[4,256,3072]{2,1,0:T(8,128)(2,1)}, bf16[768,768]{1,0:T(8,128)(2,1)}) custom-call(s32[2]{0:T(128)} %pad_add_fusion.refs_0_.me_ref, bf16[4,256,768]{2,1,0:T(8,128)(2,1)} %bitcast.121, ...), custom_call_target="tpu_custom_call" | custom-call | tf_op jit(solution)/shard_map/feed_up/pallas_call | solution.py:238
  180.4 29.2 %feed_down.1 = (bf16[8,4,32,768]{3,2,1,0:T(8,128)(2,1)}, bf16[4,256,3072]{2,1,0:T(8,128)(2,1)}, f32[4,256,768]{2,1,0:T(8,128)}, bf16[4,256,768]{2,1,0:T(8,128)(2...) custom-call(s32[2]{0:T(128)} %pad_add_fusion.refs_0_.me_ref, ...), custom_call_target="tpu_custom_call" | custom-call | tf_op jit(solution)/shard_map/feed_down/pallas_call | solution.py:329
  209.7 22.9 %attend_back.1 = (bf16[4,4,256,576]{3,2,1,0:T(8,128)(2,1)}, f32[8,768]{1,0:T(8,128)}) custom-call(bf16[4,4,256,576]{3,2,1,0:T(8,128)(2,1)} %get-tuple-element.49.mixed_ref, bf16[4,12,256,256]{3,2,1,0:T(8,128)(2,1)} %get-tuple-element.50.probs_ref, bf16[4,256,768]{2,1,0:T(8,128)(2,1)} %get-tuple-element.42.refs_2_.context_ref, ...), custom_call_target="tpu_custom_call" | custom-call | tf_op jit(solution)/shard_map/attend_back/pallas_call | solution.py:410
  232.6 12.3 %qkv_grad.1 = bf16[32,96,768]{2,1,0:T(8,128)(2,1)} custom-call(s32[2]{0:T(128)} %pad_add_fusion.refs_0_.me_ref, bf16[1024,768]{1,0:T(8,128)(2,1)} %bitcast.130, bf16[4,1024,576]{2,1,0:T(8,128)(2,1)} %bitcast.117, bf16[1024,768]{1,0:T(8,128)(2,1)} %bitcast.123, bf16[1024,768]{1,0:T(8,128)(2,1)} %bitcast.131), custom_call_target="tpu_custom_call" | custom-call | tf_op jit(solution)/shard_map/qkv_grad/pallas_call | solution.py:585
  244.9 1.8 slice.244
  247.3 2.7 copy.70
  249.9 12.8 %down_grad.1 = bf16[32,96,768]{2,1,0:T(8,128)(2,1)} custom-call(s32[2]{0:T(128)} %pad_add_fusion.refs_0_.me_ref, bf16[1024,768]{1,0:T(8,128)(2,1)} %bitcast.128, bf16[1024,3072]{1,0:T(8,128)(2,1)} %bitcast.116), custom_call_target="tpu_custom_call" | custom-call | tf_op jit(solution)/shard_map/down_grad/pallas_call | solution.py:540
  262.8 3.2 slice.269
  266.2 9.9 %up_grad.1 = bf16[32,96,768]{2,1,0:T(8,128)(2,1)} custom-call(s32[2]{0:T(128)} %pad_add_fusion.refs_0_.me_ref, bf16[1024,768]{1,0:T(8,128)(2,1)} %bitcast.129, bf16[1024,3072]{1,0:T(8,128)(2,1)} %bitcast.127), custom_call_target="tpu_custom_call" | custom-call | tf_op jit(solution)/shard_map/up_grad/pallas_call | solution.py:500
  276.1 3.4 slice.259
  280.7 3.2 add_convert_fusion.3
  286.7 1.9 collective-permute-start.19
  290.1 12.6 %tokens_back.1 = (f32[4,256,768]{2,1,0:T(8,128)}, f32[8,768]{1,0:T(8,128)}) custom-call(s32[2]{0:T(128)} %pad_add_fusion.refs_0_.me_ref, bf16[4,256,768]{2,1,0:T(8,128)(2,1)} %bitcast.122, f32[4,256,768]{2,1,0:T(8,128)} %get-tuple-element.48.refs_2_, bf16[4,4,256,576]{3,2,1,0:T(8,128)(2,1)} %get-tuple-element.52.refs_3_, ...), custom_call_target="tpu_custom_call" | custom-call | tf_op jit(solution)/shard_map/tokens_back/pallas_call | solution.py:452
  307.2 2.3 concatenate.91
  311.7 8.4 %all-to-all-start.3 = ((f32[32,3,96]{2,1,0:T(4,128)}), f32[32,3,96]{2,1,0:T(4,128)S(1)}, u32[]{:S(2)}, u32[]{:S(2)}) async-start(f32[32,3,96]{2,1,0:T(4,128)} %copy.72), calls=%async_computation.3 | async-start | bytes 131072 | tf_op jit(solution)/shard_map/all_to_all | solution.py:847
  320.1 3.2 add_convert_fusion.1
  324.5 1.8 collective-permute-start.29
  330.9 2.3 add_convert_fusion.2
  337.3 6.0 %all-to-all-start.2 = ((bf16[8,4,32,768]{3,2,1,0:T(8,128)(2,1)}), bf16[8,4,32,768]{3,2,1,0:T(8,128)(2,1)}, u32[]{:S(2)}, u32[]{:S(2)}) async-start(bf16[8,4,32,768]{3,2,1,0:T(8,128)(2,1)} %get-tuple-element.47), calls=%async_computation.2 | async-start | bytes 3145728 | tf_op jit(solution)/shard_map/all_to_all | solution.py:785
  344.4 14.9 %collective-permute-done.20 = bf16[4,48,768]{2,1,0:T(8,128)(2,1)} collective-permute-done((bf16[4,48,768]{2,1,0:T(8,128)(2,1)}, bf16[4,48,768]{2,1,0:T(8,128)(2,1)}, u32[]{:S(2)}, u32[]{:S(2)}) %collective-permute-start.20) | collective-permute-done | bytes 294944 | tf_op jit(solution)/shard_map/ppermute | solution.py:608
  360.3 1.7 collective-permute-start.21
  365.2 12.4 %collective-permute-done.24 = bf16[8,96,768]{2,1,0:T(8,128)(2,1)} collective-permute-done((bf16[8,96,768]{2,1,0:T(8,128)(2,1)}, bf16[8,96,768]{2,1,0:T(8,128)(2,1)}, u32[]{:S(2)}, u32[]{:S(2)}) %collective-permute-start.24) | collective-permute-done | bytes 1179680 | tf_op jit(solution)/shard_map/ppermute | solution.py:608
  377.6 1.6 add_convert_fusion.5
  380.5 12.6 %collective-permute-done.30 = bf16[4,96,768]{2,1,0:T(8,128)(2,1)S(1)} collective-permute-done((bf16[4,96,768]{2,1,0:T(8,128)(2,1)S(1)}, bf16[4,96,768]{2,1,0:T(8,128)(2,1)S(1)}, u32[]{:S(2)}, u32[]{:S(2)}) %collective-permute-start.30) | collective-permute-done | bytes 589856 | tf_op jit(solution)/shard_map/ppermute | solution.py:608
  395.7 2.5 collective-permute-start.22
  398.2 9.8 %collective-permute-done.31 = bf16[2,96,768]{2,1,0:T(8,128)(2,1)S(1)} collective-permute-done((bf16[2,96,768]{2,1,0:T(8,128)(2,1)S(1)}, bf16[2,96,768]{2,1,0:T(8,128)(2,1)S(1)}, u32[]{:S(2)}, u32[]{:S(2)}) %collective-permute-start.31) | collective-permute-done | bytes 294944 | tf_op jit(solution)/shard_map/ppermute | solution.py:608
  408.2 4.1 collective-permute-done.26
  414.6 9.0 %collective-permute-done.27 = bf16[1,96,768]{2,1,0:T(8,128)(2,1)S(1)} collective-permute-done((bf16[1,96,768]{2,1,0:T(8,128)(2,1)S(1)}, bf16[1,96,768]{2,1,0:T(8,128)(2,1)S(1)}, u32[]{:S(2)}, u32[]{:S(2)}) %collective-permute-start.27) | collective-permute-done | bytes 147488 | tf_op jit(solution)/shard_map/ppermute | solution.py:608
  428.2 3.0 all-to-all-start.4
  431.4 6.2 %fusion = bf16[1,32,128,768]{3,2,1,0:T(8,128)(2,1)} fusion(f32[768]{0:T(1024)S(1)} %copy-done.30, f32[32,128]{1,0:T(8,128)S(1)} %copy-done.26, bf16[32,32,768]{2,1,0:T(8,128)(2,1)} %bitcast.16, s32[32,32]{1,0:T(8,128)S(1)} %bitcast.134), kind=kOutput, calls=%fused_computation.1 | convolution fusion | flops 210894848 | bytes 7887872 | tf_op jit(solution)/shard_map/cpv,cvd->cpd/dot_general | solution.py:800
  (217 shorter events, 69.8 us)
Async XLA Ops:
  2.7 17.4 %collective-permute-start.8 = (bf16[2,1,96,768]{3,2,1,0:T(8,128)(2,1)S(1)}, bf16[2,1,96,768]{3,2,1,0:T(8,128)(2,1)S(1)}, u32[]{:S(2)}, u32[]{:S(2)}) collective-permute-start(bf16[2,1,96,768]{3,2,1,0:T(8,128)(2,1)S(1)} %maximum_bitcast_fusion), channel_id=1, source_target_pairs={{0,16},{4,20},{8,24},{12,28},{16,0},{20,4},{24,8},{28,12},{1,17},{... | collective-permute-start | bytes 884744 | tf_op jit(solution)/shard_map/ppermute | solution.py:608
  20.2 17.7 %copy-start.15 = (f32[96,192]{1,0:T(8,128)S(1)}, f32[96,192]{1,0:T(8,128)}, u32[]{:S(2)}) copy-start(f32[96,192]{1,0:T(8,128)} %param.22) | copy-start | bytes 221188
  20.2 17.7 %copy-start.12 = (f32[96,576]{1,0:T(8,128)S(1)}, f32[96,576]{1,0:T(8,128)}, u32[]{:S(2)}) copy-start(f32[96,576]{1,0:T(8,128)} %param.21) | copy-start | bytes 663556
  20.2 14.6 %collective-permute-start.9 = (bf16[2,2,96,768]{3,2,1,0:T(8,128)(2,1)S(1)}, bf16[2,2,96,768]{3,2,1,0:T(8,128)(2,1)S(1)}, u32[]{:S(2)}, u32[]{:S(2)}) collective-permute-start(bf16[2,2,96,768]{3,2,1,0:T(8,128)(2,1)S(1)} %pad_maximum_fusion.10), channel_id=1, source_target_pairs={{0,8},{4,12},{8,0},{12,4},{16,24},{20,28},{24,16},{28,20},{1,9},{5... | collective-permute-start | bytes 1769480 | tf_op jit(solution)/shard_map/ppermute | solution.py:608
  34.9 20.9 %copy-start.33 = (f32[3,96]{1,0:T(4,128)S(1)}, f32[3,96]{1,0:T(4,128)}, u32[]{:S(2)}) copy-start(f32[3,96]{1,0:T(4,128)} %param.25) | copy-start | bytes 3460
  34.9 24.2 %copy-start.27 = (s32[1,32,256]{2,1,0:T(8,128)S(1)}, s32[1,32,256]{2,1,0:T(8,128)}, u32[]{:S(2)}) copy-start(s32[1,32,256]{2,1,0:T(8,128)} %param.19) | copy-start | bytes 98308
  35.0 13.7 %collective-permute-start.10 = (bf16[4,96,768]{2,1,0:T(8,128)(2,1)S(1)}, bf16[4,96,768]{2,1,0:T(8,128)(2,1)S(1)}, u32[]{:S(2)}, u32[]{:S(2)}) collective-permute-start(bf16[4,96,768]{2,1,0:T(8,128)(2,1)S(1)} %get-tuple-element.86), channel_id=1, source_target_pairs={{0,2},{1,3},{2,0},{3,1},{4,6},{5,7},{6,4},{7,5},{8,10},{9,11},{10,... | collective-permute-start | bytes 1769480 | tf_op jit(solution)/shard_map/ppermute | solution.py:608
  36.3 22.9 %collective-permute-start.13 = (bf16[4,96,768]{2,1,0:T(8,128)(2,1)S(1)}, bf16[4,96,768]{2,1,0:T(8,128)(2,1)S(1)}, u32[]{:S(2)}, u32[]{:S(2)}) collective-permute-start(bf16[4,96,768]{2,1,0:T(8,128)(2,1)S(1)} %get-tuple-element.85), channel_id=1, source_target_pairs={{0,4},{4,0},{8,12},{12,8},{16,20},{20,16},{24,28},{28,24},{1,5},{5... | collective-permute-start | bytes 1769480 | tf_op jit(solution)/shard_map/ppermute | solution.py:608
  49.9 36.5 %collective-permute-start.11 = (bf16[8,96,768]{2,1,0:T(8,128)(2,1)}, bf16[8,96,768]{2,1,0:T(8,128)(2,1)}, u32[]{:S(2)}, u32[]{:S(2)}) collective-permute-start(bf16[8,96,768]{2,1,0:T(8,128)(2,1)} %pad_maximum_fusion.5), channel_id=1, source_target_pairs={{0,4},{4,0},{8,12},{12,8},{16,20},{20,16},{24,28},{28,24},{1,5},{5... | collective-permute-start | bytes 3538952 | tf_op jit(solution)/shard_map/ppermute | solution.py:608
  51.3 11.0 %collective-permute-start = (bf16[1,96,768]{2,1,0:T(8,128)(2,1)S(1)}, bf16[1,96,768]{2,1,0:T(8,128)(2,1)S(1)}, u32[]{:S(2)}, u32[]{:S(2)}) collective-permute-start(bf16[1,96,768]{2,1,0:T(8,128)(2,1)S(1)} %pad_maximum_fusion.14), channel_id=1, source_target_pairs={{0,16},{4,20},{8,24},{12,28},{16,0},{20,4},{24,8},{28,12},{1,17},{... | collective-permute-start | bytes 442376 | tf_op jit(solution)/shard_map/ppermute | solution.py:608
  56.4 19.4 %all-to-all-start.1 = ((bf16[32,3,96]{2,1,0:T(4,128)(2,1)}), bf16[32,3,96]{2,1,0:T(4,128)(2,1)S(1)}, u32[]{:S(2)}, u32[]{:S(2)}) async-start(bf16[32,3,96]{2,1,0:T(4,128)(2,1)} %broadcast_in_dim.19), calls=%async_computation.1 | async-start | bytes 65536 | tf_op jit(solution)/shard_map/all_to_all | solution.py:707
  60.5 28.6 %collective-permute-start.14 = (bf16[8,96,768]{2,1,0:T(8,128)(2,1)}, bf16[8,96,768]{2,1,0:T(8,128)(2,1)}, u32[]{:S(2)}, u32[]{:S(2)}) collective-permute-start(bf16[8,96,768]{2,1,0:T(8,128)(2,1)} %pad_maximum_fusion.6), channel_id=1, source_target_pairs={{0,2},{1,3},{2,0},{3,1},{4,6},{5,7},{6,4},{7,5},{8,10},{9,11},{10,... | collective-permute-start | bytes 3538952 | tf_op jit(solution)/shard_map/ppermute | solution.py:608
  62.4 8.8 %collective-permute-start.1 = (bf16[2,96,768]{2,1,0:T(8,128)(2,1)S(1)}, bf16[2,96,768]{2,1,0:T(8,128)(2,1)S(1)}, u32[]{:S(2)}, u32[]{:S(2)}) collective-permute-start(bf16[2,96,768]{2,1,0:T(8,128)(2,1)S(1)} %pad_maximum_fusion.12), channel_id=1, source_target_pairs={{0,8},{4,12},{8,0},{12,4},{16,24},{20,28},{24,16},{28,20},{1,9},{5... | collective-permute-start | bytes 884744 | tf_op jit(solution)/shard_map/ppermute | solution.py:608
  75.9 104.5 %all-to-all-start = ((bf16[8,4,32,768]{3,2,1,0:T(8,128)(2,1)}), bf16[8,4,32,768]{3,2,1,0:T(8,128)(2,1)}, u32[]{:S(2)}, u32[]{:S(2)}) async-start(bf16[8,4,32,768]{3,2,1,0:T(8,128)(2,1)} %bitcast.4), calls=%async_computation | async-start | bytes 3145728 | tf_op jit(solution)/shard_map/all_to_all | solution.py:761
  84.3 21.8 %collective-permute-start.5 = (bf16[4,48,768]{2,1,0:T(8,128)(2,1)S(1)}, bf16[4,48,768]{2,1,0:T(8,128)(2,1)S(1)}, u32[]{:S(2)}, u32[]{:S(2)}) collective-permute-start(bf16[4,48,768]{2,1,0:T(8,128)(2,1)S(1)} %get-tuple-element.87), channel_id=1, source_target_pairs={{0,4},{4,0},{8,12},{12,8},{16,20},{20,16},{24,28},{28,24},{1,5},{5... | collective-permute-start | bytes 884744 | tf_op jit(solution)/shard_map/ppermute | solution.py:608
  88.0 67.0 %collective-permute-start.12 = (bf16[16,96,768]{2,1,0:T(8,128)(2,1)S(1)}, bf16[16,96,768]{2,1,0:T(8,128)(2,1)}, u32[]{:S(2)}, u32[]{:S(2)}) collective-permute-start(bf16[16,96,768]{2,1,0:T(8,128)(2,1)S(1)} %pad_maximum_fusion.refs_9_.refs_7_), channel_id=1, source_target_pairs={{0,1},{1,0},{2,3},{3,2},{4,5},{5,4},{6,7},{7,6},{8,9},{9,8},{10,11... | collective-permute-start | bytes 7077896 | tf_op jit(solution)/shard_map/ppermute | solution.py:608
  92.0 88.4 %collective-permute-start.15 = (bf16[16,96,768]{2,1,0:T(8,128)(2,1)}, bf16[16,96,768]{2,1,0:T(8,128)(2,1)}, u32[]{:S(2)}, u32[]{:S(2)}) collective-permute-start(bf16[16,96,768]{2,1,0:T(8,128)(2,1)} %pad_maximum_fusion.1.refs_9_), channel_id=1, source_target_pairs={{0,1},{1,0},{2,3},{3,2},{4,5},{5,4},{6,7},{7,6},{8,9},{9,8},{10,11... | collective-permute-start | bytes 7077896 | tf_op jit(solution)/shard_map/ppermute | solution.py:608
  92.0 15.7 %collective-permute-start.2 = (bf16[4,48,768]{2,1,0:T(8,128)(2,1)S(1)}, bf16[4,48,768]{2,1,0:T(8,128)(2,1)S(1)}, u32[]{:S(2)}, u32[]{:S(2)}) collective-permute-start(bf16[4,48,768]{2,1,0:T(8,128)(2,1)S(1)} %get-tuple-element.88), channel_id=1, source_target_pairs={{0,2},{1,3},{2,0},{3,1},{4,6},{5,7},{6,4},{7,5},{8,10},{9,11},{10,... | collective-permute-start | bytes 884744 | tf_op jit(solution)/shard_map/ppermute | solution.py:608
  106.1 13.2 %collective-permute-start.6 = (bf16[8,48,768]{2,1,0:T(8,128)(2,1)S(1)}, bf16[8,48,768]{2,1,0:T(8,128)(2,1)S(1)}, u32[]{:S(2)}, u32[]{:S(2)}) collective-permute-start(bf16[8,48,768]{2,1,0:T(8,128)(2,1)S(1)} %pad_maximum_fusion.9), channel_id=1, source_target_pairs={{0,2},{1,3},{2,0},{3,1},{4,6},{5,7},{6,4},{7,5},{8,10},{9,11},{10,... | collective-permute-start | bytes 1769480 | tf_op jit(solution)/shard_map/ppermute | solution.py:608
  107.8 16.0 %collective-permute-start.3 = (bf16[8,48,768]{2,1,0:T(8,128)(2,1)S(1)}, bf16[8,48,768]{2,1,0:T(8,128)(2,1)S(1)}, u32[]{:S(2)}, u32[]{:S(2)}) collective-permute-start(bf16[8,48,768]{2,1,0:T(8,128)(2,1)S(1)} %pad_maximum_fusion.8), channel_id=1, source_target_pairs={{0,4},{4,0},{8,12},{12,8},{16,20},{20,16},{24,28},{28,24},{1,5},{5... | collective-permute-start | bytes 1769480 | tf_op jit(solution)/shard_map/ppermute | solution.py:608
  119.5 13.7 %collective-permute-start.7 = (bf16[16,48,768]{2,1,0:T(8,128)(2,1)S(1)}, bf16[16,48,768]{2,1,0:T(8,128)(2,1)}, u32[]{:S(2)}, u32[]{:S(2)}) collective-permute-start(bf16[16,48,768]{2,1,0:T(8,128)(2,1)S(1)} %pad_maximum_fusion.3.refs_6_.refs_7_), channel_id=1, source_target_pairs={{0,1},{1,0},{2,3},{3,2},{4,5},{5,4},{6,7},{7,6},{8,9},{9,8},{10,11... | collective-permute-start | bytes 3538952 | tf_op jit(solution)/shard_map/ppermute | solution.py:608
  125.0 8.3 %collective-permute-start.4 = (bf16[16,48,768]{2,1,0:T(8,128)(2,1)}, bf16[16,48,768]{2,1,0:T(8,128)(2,1)}, u32[]{:S(2)}, u32[]{:S(2)}) collective-permute-start(bf16[16,48,768]{2,1,0:T(8,128)(2,1)} %pad_maximum_fusion.2.refs_4_.refs_5_), channel_id=1, source_target_pairs={{0,1},{1,0},{2,3},{3,2},{4,5},{5,4},{6,7},{7,6},{8,9},{9,8},{10,11... | collective-permute-start | bytes 3538952 | tf_op jit(solution)/shard_map/ppermute | solution.py:608
  246.7 34.0 %collective-permute-start.16 = (bf16[16,96,768]{2,1,0:T(8,128)(2,1)S(1)}, bf16[16,96,768]{2,1,0:T(8,128)(2,1)}, u32[]{:S(2)}, u32[]{:S(2)}) collective-permute-start(bf16[16,96,768]{2,1,0:T(8,128)(2,1)S(1)} %slice.244), channel_id=1, source_target_pairs={{0,1},{1,0},{2,3},{3,2},{4,5},{5,4},{6,7},{7,6},{8,9},{9,8},{10,11... | collective-permute-start | bytes 7077896 | tf_op jit(solution)/shard_map/ppermute | solution.py:608
  266.0 54.1 %collective-permute-start.28 = (bf16[16,96,768]{2,1,0:T(8,128)(2,1)}, bf16[16,96,768]{2,1,0:T(8,128)(2,1)}, u32[]{:S(2)}, u32[]{:S(2)}) collective-permute-start(bf16[16,96,768]{2,1,0:T(8,128)(2,1)} %slice.269), channel_id=1, source_target_pairs={{0,1},{1,0},{2,3},{3,2},{4,5},{5,4},{6,7},{7,6},{8,9},{9,8},{10,11... | collective-permute-start | bytes 7077896 | tf_op jit(solution)/shard_map/ppermute | solution.py:608
  279.6 51.3 %collective-permute-start.23 = (bf16[16,96,768]{2,1,0:T(8,128)(2,1)}, bf16[16,96,768]{2,1,0:T(8,128)(2,1)}, u32[]{:S(2)}, u32[]{:S(2)}) collective-permute-start(bf16[16,96,768]{2,1,0:T(8,128)(2,1)} %slice.259), channel_id=1, source_target_pairs={{0,1},{1,0},{2,3},{3,2},{4,5},{5,4},{6,7},{7,6},{8,9},{9,8},{10,11... | collective-permute-start | bytes 7077896 | tf_op jit(solution)/shard_map/ppermute | solution.py:608
  284.7 41.5 %collective-permute-start.17 = (bf16[2,4,48,768]{3,2,1,0:T(8,128)(2,1)}, bf16[2,4,48,768]{3,2,1,0:T(8,128)(2,1)S(1)}, u32[]{:S(2)}, u32[]{:S(2)}) collective-permute-start(bf16[2,4,48,768]{3,2,1,0:T(8,128)(2,1)} %slice_bitcast_fusion.2), channel_id=1, source_target_pairs={{0,2},{1,3},{2,0},{3,1},{4,6},{5,7},{6,4},{7,5},{8,10},{9,11},{10,... | collective-permute-start | bytes 1769480 | tf_op jit(solution)/shard_map/ppermute | solution.py:608
  286.7 40.3 %collective-permute-start.19 = (bf16[2,4,48,768]{3,2,1,0:T(8,128)(2,1)}, bf16[2,4,48,768]{3,2,1,0:T(8,128)(2,1)}, u32[]{:S(2)}, u32[]{:S(2)}) collective-permute-start(bf16[2,4,48,768]{3,2,1,0:T(8,128)(2,1)} %slice_bitcast_fusion), channel_id=1, source_target_pairs={{0,4},{4,0},{8,12},{12,8},{16,20},{20,16},{24,28},{28,24},{1,5},{5... | collective-permute-start | bytes 1769480 | tf_op jit(solution)/shard_map/ppermute | solution.py:608
  307.2 23.7 %slice-start.2 = ((s8[4718592]{0:T(1024)(128)(4,1)}), s8[524288]{0:T(1024)(128)(4,1)S(1)}, s32[]{:S(2)}) async-start(s8[4718592]{0:T(1024)(128)(4,1)} %bitcast.118), calls=%async_computation.7 | async-start | bytes 1048576
  311.7 25.6 %all-to-all-start.3 = ((f32[32,3,96]{2,1,0:T(4,128)}), f32[32,3,96]{2,1,0:T(4,128)S(1)}, u32[]{:S(2)}, u32[]{:S(2)}) async-start(f32[32,3,96]{2,1,0:T(4,128)} %copy.72), calls=%async_computation.3 | async-start | bytes 131072 | tf_op jit(solution)/shard_map/all_to_all | solution.py:847
  324.5 37.6 %collective-permute-start.29 = (bf16[8,96,768]{2,1,0:T(8,128)(2,1)}, bf16[8,96,768]{2,1,0:T(8,128)(2,1)}, u32[]{:S(2)}, u32[]{:S(2)}) collective-permute-start(bf16[8,96,768]{2,1,0:T(8,128)(2,1)} %slice.271), channel_id=1, source_target_pairs={{0,2},{1,3},{2,0},{3,1},{4,6},{5,7},{6,4},{7,5},{8,10},{9,11},{10,... | collective-permute-start | bytes 3538952 | tf_op jit(solution)/shard_map/ppermute | solution.py:608
  329.4 13.9 %collective-permute-start.18 = (bf16[4,48,768]{2,1,0:T(8,128)(2,1)}, bf16[4,48,768]{2,1,0:T(8,128)(2,1)S(1)}, u32[]{:S(2)}, u32[]{:S(2)}) collective-permute-start(bf16[4,48,768]{2,1,0:T(8,128)(2,1)} %slice_bitcast_fusion.8), channel_id=1, source_target_pairs={{0,4},{4,0},{8,12},{12,8},{16,20},{20,16},{24,28},{28,24},{1,5},{5... | collective-permute-start | bytes 884744 | tf_op jit(solution)/shard_map/ppermute | solution.py:608
  335.7 41.8 %collective-permute-start.24 = (bf16[8,96,768]{2,1,0:T(8,128)(2,1)}, bf16[8,96,768]{2,1,0:T(8,128)(2,1)}, u32[]{:S(2)}, u32[]{:S(2)}) collective-permute-start(bf16[8,96,768]{2,1,0:T(8,128)(2,1)} %slice.261), channel_id=1, source_target_pairs={{0,4},{4,0},{8,12},{12,8},{16,20},{20,16},{24,28},{28,24},{1,5},{5... | collective-permute-start | bytes 3538952 | tf_op jit(solution)/shard_map/ppermute | solution.py:608
  337.0 22.2 %collective-permute-start.20 = (bf16[4,48,768]{2,1,0:T(8,128)(2,1)}, bf16[4,48,768]{2,1,0:T(8,128)(2,1)}, u32[]{:S(2)}, u32[]{:S(2)}) collective-permute-start(bf16[4,48,768]{2,1,0:T(8,128)(2,1)} %slice_bitcast_fusion.6), channel_id=1, source_target_pairs={{0,2},{1,3},{2,0},{3,1},{4,6},{5,7},{6,4},{7,5},{8,10},{9,11},{10,... | collective-permute-start | bytes 884744 | tf_op jit(solution)/shard_map/ppermute | solution.py:608
  337.3 24.8 %copy-start.3 = (bf16[16,96,768]{2,1,0:T(8,128)(2,1)S(1)}, bf16[16,96,768]{2,1,0:T(8,128)(2,1)}, u32[]{:S(2)}) copy-start(bf16[16,96,768]{2,1,0:T(8,128)(2,1)} %copy-done.2) | copy-start | bytes 7077892
  337.3 90.3 %all-to-all-start.2 = ((bf16[8,4,32,768]{3,2,1,0:T(8,128)(2,1)}), bf16[8,4,32,768]{3,2,1,0:T(8,128)(2,1)}, u32[]{:S(2)}, u32[]{:S(2)}) async-start(bf16[8,4,32,768]{3,2,1,0:T(8,128)(2,1)} %get-tuple-element.47), calls=%async_computation.2 | async-start | bytes 3145728 | tf_op jit(solution)/shard_map/all_to_all | solution.py:785
  343.3 36.5 %copy-start.28 = (f32[3,96]{1,0:T(4,128)}, f32[3,96]{1,0:T(4,128)S(1)}, u32[]{:S(2)}) copy-start(f32[3,96]{1,0:T(4,128)S(1)} %reduce_sum.67) | copy-start | bytes 3460
  360.3 17.3 %copy-start.5 = (bf16[16,96,768]{2,1,0:T(8,128)(2,1)S(1)}, bf16[16,96,768]{2,1,0:T(8,128)(2,1)}, u32[]{:S(2)}) copy-start(bf16[16,96,768]{2,1,0:T(8,128)(2,1)} %copy-done.4) | copy-start | bytes 7077892
  360.3 20.1 %collective-permute-start.21 = (bf16[2,96,768]{2,1,0:T(8,128)(2,1)S(1)}, bf16[2,96,768]{2,1,0:T(8,128)(2,1)S(1)}, u32[]{:S(2)}, u32[]{:S(2)}) collective-permute-start(bf16[2,96,768]{2,1,0:T(8,128)(2,1)S(1)} %pad_maximum_fusion.11), channel_id=1, source_target_pairs={{0,8},{4,12},{8,0},{12,4},{16,24},{20,28},{24,16},{28,20},{1,9},{5... | collective-permute-start | bytes 884744 | tf_op jit(solution)/shard_map/ppermute | solution.py:608
  363.7 29.5 %collective-permute-start.30 = (bf16[4,96,768]{2,1,0:T(8,128)(2,1)S(1)}, bf16[4,96,768]{2,1,0:T(8,128)(2,1)S(1)}, u32[]{:S(2)}, u32[]{:S(2)}) collective-permute-start(bf16[4,96,768]{2,1,0:T(8,128)(2,1)S(1)} %slice.273), channel_id=1, source_target_pairs={{0,4},{4,0},{8,12},{12,8},{16,20},{20,16},{24,28},{28,24},{1,5},{5... | collective-permute-start | bytes 1769480 | tf_op jit(solution)/shard_map/ppermute | solution.py:608
  379.2 15.7 %collective-permute-start.25 = (bf16[4,96,768]{2,1,0:T(8,128)(2,1)S(1)}, bf16[4,96,768]{2,1,0:T(8,128)(2,1)S(1)}, u32[]{:S(2)}, u32[]{:S(2)}) collective-permute-start(bf16[4,96,768]{2,1,0:T(8,128)(2,1)S(1)} %slice.263), channel_id=1, source_target_pairs={{0,2},{1,3},{2,0},{3,1},{4,6},{5,7},{6,4},{7,5},{8,10},{9,11},{10,... | collective-permute-start | bytes 1769480 | tf_op jit(solution)/shard_map/ppermute | solution.py:608
  393.3 14.7 %collective-permute-start.31 = (bf16[2,96,768]{2,1,0:T(8,128)(2,1)S(1)}, bf16[2,96,768]{2,1,0:T(8,128)(2,1)S(1)}, u32[]{:S(2)}, u32[]{:S(2)}) collective-permute-start(bf16[2,96,768]{2,1,0:T(8,128)(2,1)S(1)} %slice.275), channel_id=1, source_target_pairs={{0,8},{4,12},{8,0},{12,4},{16,24},{20,28},{24,16},{28,20},{1,9},{5... | collective-permute-start | bytes 884744 | tf_op jit(solution)/shard_map/ppermute | solution.py:608
  395.0 17.3 %collective-permute-start.26 = (bf16[2,96,768]{2,1,0:T(8,128)(2,1)S(1)}, bf16[2,96,768]{2,1,0:T(8,128)(2,1)S(1)}, u32[]{:S(2)}, u32[]{:S(2)}) collective-permute-start(bf16[2,96,768]{2,1,0:T(8,128)(2,1)S(1)} %slice.265), channel_id=1, source_target_pairs={{0,8},{4,12},{8,0},{12,4},{16,24},{20,28},{24,16},{28,20},{1,9},{5... | collective-permute-start | bytes 884744 | tf_op jit(solution)/shard_map/ppermute | solution.py:608
  395.7 35.5 %copy-start.26 = (f32[32,128]{1,0:T(8,128)S(1)}, f32[32,128]{1,0:T(8,128)}, u32[]{:S(2)}) copy-start(f32[32,128]{1,0:T(8,128)} %get-tuple-element.96) | copy-start | bytes 49156
  395.7 35.5 %copy-start.30 = (f32[768]{0:T(1024)S(1)}, f32[768]{0:T(1024)}, u32[]{:S(2)}) copy-start(f32[768]{0:T(1024)} %get-tuple-element.63) | copy-start | bytes 9220
  395.7 18.2 %collective-permute-start.22 = (bf16[96,768]{1,0:T(8,128)(2,1)S(1)}, bf16[96,768]{1,0:T(8,128)(2,1)S(1)}, u32[]{:S(2)}, u32[]{:S(2)}) collective-permute-start(bf16[96,768]{1,0:T(8,128)(2,1)S(1)} %slice_bitcast_fusion.10), channel_id=1, source_target_pairs={{0,16},{4,20},{8,24},{12,28},{16,0},{20,4},{24,8},{28,12},{1,17},{... | collective-permute-start | bytes 442376 | tf_op jit(solution)/shard_map/ppermute | solution.py:608
  408.1 17.4 %collective-permute-start.32 = (bf16[1,96,768]{2,1,0:T(8,128)(2,1)S(1)}, bf16[1,96,768]{2,1,0:T(8,128)(2,1)S(1)}, u32[]{:S(2)}, u32[]{:S(2)}) collective-permute-start(bf16[1,96,768]{2,1,0:T(8,128)(2,1)S(1)} %slice.277), channel_id=1, source_target_pairs={{0,16},{4,20},{8,24},{12,28},{16,0},{20,4},{24,8},{28,12},{1,17},{... | collective-permute-start | bytes 442376 | tf_op jit(solution)/shard_map/ppermute | solution.py:608
  412.4 11.2 %collective-permute-start.27 = (bf16[1,96,768]{2,1,0:T(8,128)(2,1)S(1)}, bf16[1,96,768]{2,1,0:T(8,128)(2,1)S(1)}, u32[]{:S(2)}, u32[]{:S(2)}) collective-permute-start(bf16[1,96,768]{2,1,0:T(8,128)(2,1)S(1)} %slice.267), channel_id=1, source_target_pairs={{0,16},{4,20},{8,24},{12,28},{16,0},{20,4},{24,8},{28,12},{1,17},{... | collective-permute-start | bytes 442376 | tf_op jit(solution)/shard_map/ppermute | solution.py:608
  428.2 10.1 %all-to-all-start.4 = ((f32[32,1,1]{2,1,0:T(1,128)}), f32[32,1,1]{2,1,0:T(1,128)S(1)}, u32[]{:S(2)}, u32[]{:S(2)}) async-start(f32[32,1,1]{2,1,0:T(1,128)} %broadcast_in_dim.23), calls=%async_computation.4 | async-start | bytes 32768 | tf_op jit(solution)/shard_map/all_to_all | solution.py:852
  (31 other events, 227.3 us)

commit v3 on v2

v3 whole, which is shorter than its diff:
```python
import functools
import math

import jax
import jax.numpy as jnp
from jax import lax
from jax.experimental import pallas as pl
from jax.experimental.pallas import tpu as pltpu
from jax.sharding import PartitionSpec as P

HD = 64
STEP = 10
F32 = jnp.float32
BF16 = jnp.bfloat16
VMEM_BYTES = 60 * 1024 * 1024


def params_for(**more):
    return pltpu.CompilerParams(vmem_limit_bytes=VMEM_BYTES, **more)


def busy_for(micros):
    return pl.CostEstimate(flops=micros * 10**9, bytes_accessed=micros * 3 * 10**6, transcendentals=0)


def dot_nn(left, right):
    return lax.dot_general(left, right, (((1,), (0,)), ((), ())), preferred_element_type=F32)


def dot_nt(left, right):
    return lax.dot_general(left, right, (((1,), (1,)), ((), ())), preferred_element_type=F32)


def dot_tn(left, right):
    return lax.dot_general(left, right, (((0,), (0,)), ((), ())), preferred_element_type=F32)


def norm_parts(values):
    center = values - jnp.mean(values, axis=-1, keepdims=True)
    spread = jnp.mean(center * center, axis=-1, keepdims=True)
    factor = lax.rsqrt(spread + 1e-05)
    return center * factor, factor


def norm_back(grad, hat, factor, gain):
    scaled = grad * gain
    inner = jnp.mean(scaled * hat, axis=-1, keepdims=True)
    return factor * (scaled - jnp.mean(scaled, axis=-1, keepdims=True) - hat * inner)


def gelu_pair(gate):
    cdf = 0.5 + 0.5 * lax.erf(gate * 0.5**0.5)
    bell = jnp.exp2(gate * gate * (-0.5 * math.log2(math.e))) * (0.5 / math.pi) ** 0.5
    return gate * cdf, cdf + gate * bell


def load_grid(table, refs, me_ref, dest, sems, rows, first=0):
    copies = []
    for ref, places in zip(refs, table):
        for pos, (rel_d, rel_f, off, turned) in enumerate(places):
            d = rel_d ^ me_ref[0] if turned else rel_d
            f = rel_f ^ me_ref[1] if turned else rel_f
            height = min(ref.shape[1], rows)
            start = pl.multiple_of(d * rows + off, 16)
            copy = pltpu.make_async_copy(
                ref.at[pos, pl.ds(0, height)], dest.at[f, pl.ds(start, height)], sems.at[first + len(copies)]
            )
            copy.start()
            copies.append(copy)
    return copies


def load_down(table, refs, me_ref, dest, sems, share, first=0):
    copies = []
    for ref, places in zip(refs, table):
        for pos, (rel_d, rel_f, off, turned) in enumerate(places):
            if share is None:
                pairs = [(ref.at[pos], dest)]
            else:
                half, wide = share
                d = rel_d ^ me_ref[0] if turned else rel_d
                f = rel_f ^ me_ref[1] if turned else rel_f
                lane = pl.multiple_of(d * wide, 128)
                pairs = []
                for k in range(2):
                    row = pl.multiple_of(f * (2 * half) + k * half + off, 16)
                    pairs.append(
                        (
                            ref.at[pos, :, pl.ds(k * wide, wide)],
                            dest.at[pl.ds(row, ref.shape[1]), pl.ds(lane, wide)],
                        )
                    )
            for src, dst in pairs:
                copy = pltpu.make_async_copy(src, dst, sems.at[first + len(copies)])
                copy.start()
                copies.append(copy)
    return copies


def any_specs(count):
    return [pl.BlockSpec(memory_space=pl.ANY)] * count


SMEM_SPEC = pl.BlockSpec(memory_space=pltpu.SMEM)


def full_spec(shape):
    return pl.BlockSpec(shape, lambda i: (0,) * len(shape))


def picked(places, length):
    lanes = places.shape[1]
    rows = lax.broadcasted_iota(jnp.int32, (length, lanes), 0)
    return (rows == places).astype(F32)


def seen_body(seen, cot_ref, places_ref, out_ref, sum_ref):
    count, length, _ = cot_ref.shape

    @pl.when(pl.program_id(0) == 0)
    def _():
        sum_ref[...] = jnp.zeros_like(sum_ref)

    for k in range(count):
        pick = picked(places_ref[k], length)
        gaps = 1.0 - jnp.sum(pick, axis=-1, keepdims=True)
        lane = lax.broadcasted_iota(jnp.int32, pick.shape, 1)
        rows = dot_tn(jnp.where(lane == seen, gaps, pick).astype(BF16), cot_ref[k])
        out_ref[k] = rows[:seen].astype(BF16)
        sum_ref[...] += rows[seen : seen + 1]


def seen_rows(cot, places, seen):
    chips, length, model = cot.shape
    step = 4
    return pl.pallas_call(
        functools.partial(seen_body, seen),
        grid=(chips // step,),
        in_specs=[
            pl.BlockSpec((step, length, model), lambda i: (i, 0, 0)),
            pl.BlockSpec((step, 1, places.shape[2]), lambda i: (i, 0, 0)),
        ],
        out_specs=[pl.BlockSpec((step, seen, model), lambda i: (i, 0, 0)), full_spec((1, model))],
        out_shape=[
            jax.ShapeDtypeStruct((chips, seen, model), BF16),
            jax.ShapeDtypeStruct((1, model), F32),
        ],
        compiler_params=params_for(),
        cost_estimate=busy_for(8),
        name="seen_rows",
    )(cot, places)


def lane_sides(seq):
    lane = lax.broadcasted_iota(jnp.int32, (seq, 2 * HD), 1)
    return lane, (lane < HD, lane >= HD)


def attend_body(table, rows, heads, wide, *refs):
    n = len(table)
    me_ref, x_ref, vec_ref = refs[:3]
    w_refs = refs[3 : 3 + n]
    normed_ref, mixed_ref, expo_ref, share_ref, context_ref, qkv_ref, out_ref, weight, sems = refs[3 + n :]
    shares, model, cols = weight.shape
    slim = cols - wide

    @pl.when(pl.program_id(0) == 0)
    def _():
        for copy in load_grid(table, w_refs, me_ref, weight, sems, rows):
            copy.wait()
        for f in range(shares):
            qkv_ref[:, f * wide : (f + 1) * wide] = weight[f, :, :wide]
            out_ref[:, f * slim : (f + 1) * slim] = weight[f, :, wide:]

    hat, _ = norm_parts(x_ref[0].astype(F32))
    normed = (hat * vec_ref[0:1, :] + vec_ref[1:2, :]).astype(BF16)
    normed_ref[0] = normed
    for part in range(3):
        lanes = slice(part * model, (part + 1) * model)
        mixed = dot_nn(normed, qkv_ref[:, lanes])
        if part == 2:
            mixed = mixed + vec_ref[2:3, :]
        mixed_ref[0, :, lanes] = mixed.astype(BF16)
    seq = normed.shape[0]
    _, sides = lane_sides(seq)
    one = jnp.ones((), BF16)
    for pair in range(heads // 2):
        query, key, value = (
            mixed_ref[0, :, part * model + 2 * HD * pair : part * model + 2 * HD * (pair + 1)]
            for part in range(3)
        )
        query = query * jnp.asarray(HD ** (-0.5), BF16)
        context = None
        for side in range(2):
            mine = sides[side]
            scores = dot_nt(key, jnp.where(mine, query, jnp.zeros_like(query)))
            expo = jnp.exp(scores - jnp.max(scores, axis=0, keepdims=True)).astype(BF16)
            expo_ref[0, 2 * pair + side] = expo
            rich = dot_tn(expo, jnp.where(mine, value, one))
            spot = HD * (1 - side)
            share = 1.0 / rich[:, spot : spot + 1]
            share_ref[0, :, 2 * pair + side : 2 * pair + side + 1] = share
            rich = rich * share
            context = rich if context is None else jnp.where(mine, rich, context)
        context_ref[0, :, 2 * HD * pair : 2 * HD * (pair + 1)] = context.astype(BF16)


def attend_forward(me, x, vec, table, arrays, rows, wide):
    chips, seq, model = x.shape
    heads = model // HD
    cols = arrays[0].shape[-1]
    shares = 3 * model // wide
    count = sum(len(t) for t in table)
    tile = lambda w: pl.BlockSpec((1, seq, w), lambda i: (i, 0, 0))
    return pl.pallas_call(
        functools.partial(attend_body, table, rows, heads, wide),
        grid=(chips,),
        in_specs=[SMEM_SPEC, tile(model), full_spec(vec.shape)] + any_specs(len(arrays)),
        out_specs=[
            tile(model),
            tile(3 * model),
            pl.BlockSpec((1, heads, seq, seq), lambda i: (i, 0, 0, 0)),
            tile(heads),
            tile(model),
            full_spec((model, 3 * model)),
            full_spec((model, model)),
        ],
        out_shape=[
            jax.ShapeDtypeStruct((chips, seq, model), BF16),
            jax.ShapeDtypeStruct((chips, seq, 3 * model), BF16),
            jax.ShapeDtypeStruct((chips, heads, seq, seq), BF16),
            jax.ShapeDtypeStruct((chips, seq, heads), F32),
            jax.ShapeDtypeStruct((chips, seq, model), BF16),
            jax.ShapeDtypeStruct((model, 3 * model), BF16),
            jax.ShapeDtypeStruct((model, model), BF16),
        ],
        scratch_shapes=[
            pltpu.VMEM((shares, model, cols), BF16),
            pltpu.SemaphoreType.DMA((count,)),
        ],
        compiler_params=params_for(),
        cost_estimate=busy_for(20),
        name="attend_forward",
    )(me, x, vec, *arrays)


def feed_up_body(table, rows, *refs):
    n = len(table)
    me_ref, x_ref, context_ref, vec_ref, bias_ref, out_ref = refs[:6]
    u_refs = refs[6 : 6 + n]
    middle_ref, normed_ref, active_ref, slope_ref, up, sems = refs[6 + n :]
    shares, _, span = up.shape

    @pl.when(pl.program_id(0) == 0)
    def _():
        for copy in load_grid(table, u_refs, me_ref, up, sems, rows):
            copy.wait()

    branch = dot_nn(context_ref[0], out_ref[...])
    middle = x_ref[0].astype(F32) + branch + vec_ref[3:4, :]
    middle_ref[0] = middle
    hat, _ = norm_parts(middle)
    normed = (hat * vec_ref[4:5, :] + vec_ref[5:6, :]).astype(BF16)
    normed_ref[0] = normed
    for f in range(shares):
        gate = dot_nn(normed, up[f]) + bias_ref[:, f * span : (f + 1) * span]
        active, slope = gelu_pair(gate)
        active_ref[0, :, f * span : (f + 1) * span] = active.astype(BF16)
        slope_ref[0, :, f * span : (f + 1) * span] = slope.astype(BF16)


def feed_up(me, x, context, vec, bias, out_whole, table, arrays, rows):
    chips, seq, model = x.shape
    ff = bias.shape[1]
    span = arrays[0].shape[-1]
    shares = ff // span
    count = sum(len(t) for t in table)
    tile = lambda w: pl.BlockSpec((1, seq, w), lambda i: (i, 0, 0))
    return pl.pallas_call(
        functools.partial(feed_up_body, table, rows),
        grid=(chips,),
        in_specs=[
            SMEM_SPEC,
            tile(model),
            tile(model),
            full_spec(vec.shape),
            full_spec(bias.shape),
            full_spec(out_whole.shape),
        ]
        + any_specs(len(arrays)),
        out_specs=[tile(model), tile(model), tile(ff), tile(ff)],
        out_shape=[
            jax.ShapeDtypeStruct((chips, seq, model), F32),
            jax.ShapeDtypeStruct((chips, seq, model), BF16),
            jax.ShapeDtypeStruct((chips, seq, ff), BF16),
            jax.ShapeDtypeStruct((chips, seq, ff), BF16),
        ],
        scratch_shapes=[
            pltpu.VMEM((shares, model, span), BF16),
            pltpu.SemaphoreType.DMA((count,)),
        ],
        compiler_params=params_for(),
        cost_estimate=busy_for(17),
        name="feed_up",
    )(me, x, context, vec, bias, out_whole, *arrays)


def feed_down_body(u_table, d_table, rows, share, *refs):
    nu, nd = len(u_table), len(d_table)
    me_ref, grad_ref, middle_ref, active_ref, slope_ref, vec_ref, out_ref = refs[:7]
    u_refs = refs[7 : 7 + nu]
    d_refs = refs[7 + nu : 7 + nu + nd]
    (
        result_ref,
        gate_grad_ref,
        middle_grad_ref,
        branch_grad_ref,
        context_grad_ref,
        sums_ref,
        bias_sums_ref,
        up,
        down,
        sems,
    ) = refs[7 + nu + nd :]
    count = sum(len(t) for t in u_table)
    shares, model, span = up.shape
    step = pl.program_id(0)

    @pl.when(step == 0)
    def _():
        first = load_grid(u_table, u_refs, me_ref, up, sems, rows)
        second = load_down(d_table, d_refs, me_ref, down, sems, share, first=count)
        sums_ref[...] = jnp.zeros_like(sums_ref)
        bias_sums_ref[...] = jnp.zeros_like(bias_sums_ref)
        for copy in first + second:
            copy.wait()

    seq = middle_ref.shape[1]
    middle = middle_ref[0]
    feed_grad = grad_ref[:, 0].reshape(seq, model)
    result = middle + dot_nt(active_ref[0], down[...]) + vec_ref[10:11, :]
    result_ref[:, 0] = result.astype(BF16).reshape(result_ref.shape[0], -1, model)
    normed_grad = jnp.zeros((seq, model), F32)
    for f in range(shares):
        lanes = slice(f * span, (f + 1) * span)
        active_grad = dot_nn(feed_grad, down[:, lanes])
        gate_grad = (active_grad * slope_ref[0, :, lanes].astype(F32)).astype(BF16)
        gate_grad_ref[0, :, lanes] = gate_grad
        bias_sums_ref[:, lanes] += jnp.sum(gate_grad.astype(F32), axis=0, keepdims=True)
        normed_grad += dot_nt(gate_grad, up[f])
    hat, factor = norm_parts(middle)
    gain = vec_ref[4:5, :]
    grad_full = feed_grad.astype(F32)
    middle_grad = grad_full + norm_back(normed_grad, hat, factor, gain)
    middle_grad_ref[0] = middle_grad
    branch_grad = middle_grad.astype(BF16)
    branch_grad_ref[0] = branch_grad
    context_grad_ref[0] = dot_nt(branch_grad, out_ref[...]).astype(BF16)
    sums_ref[0:1, :] += jnp.sum(branch_grad.astype(F32), axis=0, keepdims=True)
    sums_ref[1:2, :] += jnp.sum(normed_grad * hat, axis=0, keepdims=True)
    sums_ref[2:3, :] += jnp.sum(normed_grad, axis=0, keepdims=True)
    sums_ref[3:4, :] += jnp.sum(grad_full, axis=0, keepdims=True)


def feed_down(
    me, grad, middle, active, slope, vec, out_whole, u_table, u_arrays, d_table, d_arrays, rows, share
):
    chips, seq, model = middle.shape
    ff = active.shape[2]
    blocks, _, seen, _ = grad.shape
    span = u_arrays[0].shape[-1]
    shares = ff // span
    count = sum(len(t) for t in u_table) + 2 * sum(len(t) for t in d_table)
    tile = lambda w: pl.BlockSpec((1, seq, w), lambda i: (i, 0, 0))
    spread = pl.BlockSpec((blocks, 1, seen, model), lambda i: (0, i, 0, 0))
    return pl.pallas_call(
        functools.partial(feed_down_body, u_table, d_table, rows, share),
        grid=(chips,),
        in_specs=[
            SMEM_SPEC,
            spread,
            tile(model),
            tile(ff),
            tile(ff),
            full_spec(vec.shape),
            full_spec(out_whole.shape),
        ]
        + any_specs(len(u_arrays) + len(d_arrays)),
        out_specs=[
            spread,
            tile(ff),
            tile(model),
            tile(model),
            tile(model),
            full_spec((8, model)),
            full_spec((1, ff)),
        ],
        out_shape=[
            jax.ShapeDtypeStruct(grad.shape, BF16),
            jax.ShapeDtypeStruct((chips, seq, ff), BF16),
            jax.ShapeDtypeStruct((chips, seq, model), F32),
            jax.ShapeDtypeStruct((chips, seq, model), BF16),
            jax.ShapeDtypeStruct((chips, seq, model), BF16),
            jax.ShapeDtypeStruct((8, model), F32),
            jax.ShapeDtypeStruct((1, ff), F32),
        ],
        scratch_shapes=[
            pltpu.VMEM((shares, model, span), BF16),
            pltpu.VMEM((model, ff), BF16),
            pltpu.SemaphoreType.DMA((count,)),
        ],
        compiler_params=params_for(),
        cost_estimate=busy_for(20),
        name="feed_down",
    )(me, grad, middle, active, slope, vec, out_whole, *u_arrays, *d_arrays)


def attend_back_body(heads, mixed_ref, expo_ref, share_ref, context_ref, grad_ref, mixed_grad_ref, sums_ref):
    seq, model = context_ref.shape[1:]

    @pl.when(pl.program_id(0) == 0)
    def _():
        sums_ref[...] = jnp.zeros_like(sums_ref)

    lane, sides = lane_sides(seq)
    scale = jnp.asarray(HD ** (-0.5), BF16)
    for pair in range(heads // 2):
        spots = [
            slice(part * model + 2 * HD * pair, part * model + 2 * HD * (pair + 1)) for part in range(3)
        ]
        query, key, value = (mixed_ref[0, :, spot] for spot in spots)
        query, key = query * scale, key * scale
        nothing, one = jnp.zeros_like(query), jnp.ones((), BF16)
        out_grad = grad_ref[0, :, spots[0]].astype(F32)
        inner_parts = out_grad * context_ref[0, :, spots[0]].astype(F32)
        grads = [0.0, 0.0, 0.0]
        for side in range(2):
            mine, other = sides[side], HD * (1 - side)
            share = share_ref[0, :, 2 * pair + side : 2 * pair + side + 1]
            inner = -share * jnp.sum(jnp.where(mine, inner_parts, 0.0), axis=-1, keepdims=True)
            inner_high = inner.astype(BF16)
            inner_low = (inner - inner_high.astype(F32)).astype(BF16)
            scaled = jnp.where(mine, out_grad * share, 0.0).astype(BF16)
            rich = jnp.where(lane == other, inner_high, jnp.where(lane == other + 1, inner_low, scaled))
            prob_grad = dot_nt(jnp.where(mine, value, one), rich)
            expo = expo_ref[0, 2 * pair + side]
            score_grad = (expo.astype(F32) * prob_grad).astype(BF16)
            grads[0] += dot_tn(score_grad, jnp.where(mine, key, nothing))
            grads[1] += dot_nn(score_grad, jnp.where(mine, query, nothing))
            grads[2] += dot_nn(expo, scaled)
        for part in range(3):
            mixed_grad_ref[0, :, spots[part]] = grads[part].astype(BF16)
        sums_ref[0:1, spots[0]] += jnp.sum(grads[2].astype(BF16).astype(F32), axis=0, keepdims=True)


def attend_back(mixed, expo, share, context, context_grad):
    chips, seq, model = context.shape
    heads = model // HD
    tile = lambda w: pl.BlockSpec((1, seq, w), lambda i: (i, 0, 0))
    return pl.pallas_call(
        functools.partial(attend_back_body, heads),
        grid=(chips,),
        in_specs=[
            tile(3 * model),
            pl.BlockSpec((1, heads, seq, seq), lambda i: (i, 0, 0, 0)),
            tile(heads),
            tile(model),
            tile(model),
        ],
        out_specs=[tile(3 * model), full_spec((8, model))],
        out_shape=[
            jax.ShapeDtypeStruct(mixed.shape, BF16),
            jax.ShapeDtypeStruct((8, model), F32),
        ],
        compiler_params=params_for(),
        cost_estimate=busy_for(15),
        name="attend_back",
    )(mixed, expo, share, context, context_grad)


def tokens_back_body(x_ref, grad_ref, mixed_grad_ref, vec_ref, qkv_ref, tokens_ref, sums_ref):
    @pl.when(pl.program_id(0) == 0)
    def _():
        sums_ref[...] = jnp.zeros_like(sums_ref)

    normed_grad = dot_nt(mixed_grad_ref[0], qkv_ref[...])
    hat, factor = norm_parts(x_ref[0].astype(F32))
    tokens_ref[0] = grad_ref[0] + norm_back(normed_grad, hat, factor, vec_ref[0:1, :])
    sums_ref[0:1, :] += jnp.sum(normed_grad * hat, axis=0, keepdims=True)
    sums_ref[1:2, :] += jnp.sum(normed_grad, axis=0, keepdims=True)


def tokens_back(x, middle_grad, mixed_grad, vec, qkv_whole):
    chips, seq, model = x.shape
    tile = lambda w: pl.BlockSpec((1, seq, w), lambda i: (i, 0, 0))
    return pl.pallas_call(
        tokens_back_body,
        grid=(chips,),
        in_specs=[
            tile(model),
            tile(model),
            tile(3 * model),
            full_spec(vec.shape),
            full_spec(qkv_whole.shape),
        ],
        out_specs=[tile(model), full_spec((8, model))],
        out_shape=[
            jax.ShapeDtypeStruct((chips, seq, model), F32),
            jax.ShapeDtypeStruct((8, model), F32),
        ],
        compiler_params=params_for(),
        cost_estimate=busy_for(8),
        name="tokens_back",
    )(x, middle_grad, mixed_grad, vec, qkv_whole)


def store_block(order, refs, me_ref, d, f, *lanes_and_blocks):
    rel_d, rel_f = d ^ me_ref[0], f ^ me_ref[1]
    bits = [((rel_d if is_dp else rel_f) // value) % 2 for is_dp, value in order]
    pos = 0
    for bit in bits[1:]:
        pos = pos * 2 + bit
    for side, ref in enumerate(refs):

        @pl.when(bits[0] == side)
        def _():
            for lanes, block in lanes_and_blocks:
                ref[pos, :, lanes] = block


def up_grad_body(split, rows, left_ref, right_ref, out_ref):
    grad = dot_tn(left_ref[...], right_ref[...]).astype(BF16)
    if split:
        for d in range(grad.shape[0] // rows):
            out_ref[d, 0] = grad[d * rows : (d + 1) * rows]
    else:
        out_ref[0] = grad


def block_outs(order, whole, blocks):
    shapes = [whole] if order is None else [blocks, blocks]
    return [full_spec(s) for s in shapes], [jax.ShapeDtypeStruct(s, BF16) for s in shapes]


def up_grad_blocks(left, right, split, rows, shares):
    tokens, model = left.shape
    span = right.shape[1] // shares
    if split:
        shape = (model // rows, shares, rows, span)
        out_spec = pl.BlockSpec((model // rows, 1, rows, span), lambda i: (0, i, 0, 0))
    else:
        shape = (shares, model, span)
        out_spec = pl.BlockSpec((1, model, span), lambda i: (i, 0, 0))
    return pl.pallas_call(
        functools.partial(up_grad_body, split, rows),
        grid=(shares,),
        in_specs=[full_spec(left.shape), pl.BlockSpec((tokens, span), lambda i: (0, i))],
        out_specs=out_spec,
        out_shape=jax.ShapeDtypeStruct(shape, BF16),
        compiler_params=params_for(),
        cost_estimate=busy_for(8),
        name="up_grad",
    )(left, right)


def down_grad_body(order, half, me_ref, grad_ref, active_ref, *refs):
    d = pl.program_id(0)
    whole = dot_tn(grad_ref[...], active_ref[...]).astype(BF16)
    if order is None:
        refs[0][...] = whole
    else:
        wide = whole.shape[1]
        for f in range(whole.shape[0] // (2 * half)):
            parts = []
            for k in range(2):
                start = (2 * f + k) * half
                parts.append((slice(k * wide, (k + 1) * wide), whole[start : start + half]))
            store_block(order, refs, me_ref, d, f, *parts)


def down_grad_blocks(me, grad, active, order, half, wide):
    tokens, model = grad.shape
    ff = active.shape[1]
    steps, width = (4, ff // 4) if order is None else (ff // wide, wide)
    out_specs, out_shape = block_outs(order, (model, ff), (steps * model // (4 * half), half, 2 * wide))
    if order is None:
        out_specs = [pl.BlockSpec((model, width), lambda i: (0, i))]
    return pl.pallas_call(
        functools.partial(down_grad_body, order, half),
        grid=(steps,),
        in_specs=[
            SMEM_SPEC,
            full_spec(grad.shape),
            pl.BlockSpec((tokens, width), lambda i: (0, i)),
        ],
        out_specs=out_specs,
        out_shape=out_shape,
        compiler_params=params_for(),
        cost_estimate=busy_for(10),
        name="down_grad",
    )(me, grad, active)


def qkv_grad_body(order, rows, wide, me_ref, normed_ref, mixed_grad_ref, context_ref, branch_ref, *refs):
    step = pl.program_id(0)
    qkv, out = refs[-2:]
    parts, model, _ = qkv.shape
    shares = 3 * model // wide
    slim = model // shares

    qkv[step] = dot_tn(normed_ref[...], mixed_grad_ref[...]).astype(BF16)

    @pl.when(step == parts - 1)
    def _():
        out[...] = dot_tn(context_ref[...], branch_ref[...]).astype(BF16)

        def qkv_part(spot, f):
            pieces = []
            first, last = f * wide, (f + 1) * wide
            for part in range(parts):
                low, high = max(first, part * model), min(last, (part + 1) * model)
                if low < high:
                    pieces.append(
                        (slice(low - first, high - first), qkv[part, spot, low - part * model : high - part * model])
                    )
            return pieces + [(slice(wide, wide + slim), out[spot, f * slim : (f + 1) * slim])]

        for f in range(shares):
            if order is None:
                for lanes, block in qkv_part(slice(None), f):
                    refs[0][f, :, lanes] = block
            else:
                for d in range(model // rows):
                    store_block(order, refs[:-2], me_ref, d, f, *qkv_part(slice(d * rows, (d + 1) * rows), f))


def qkv_grad_blocks(me, normed, mixed_grad, context, branch_grad, order, rows, wide):
    tokens, model = normed.shape
    shares = 3 * model // wide
    cols = wide + model // shares
    out_specs, out_shape = block_outs(
        order, (shares, model, cols), (shares * model // rows // 2, rows, cols)
    )
    return pl.pallas_call(
        functools.partial(qkv_grad_body, order, rows, wide),
        grid=(3,),
        in_specs=[
            SMEM_SPEC,
            full_spec(normed.shape),
            pl.BlockSpec((tokens, model), lambda i: (0, i)),
            full_spec(context.shape),
            full_spec(branch_grad.shape),
        ],
        out_specs=out_specs,
        out_shape=out_shape,
        scratch_shapes=[pltpu.VMEM((3, model, model), BF16), pltpu.VMEM((model, model), BF16)],
        compiler_params=params_for(),
        cost_estimate=busy_for(10),
        name="qkv_grad",
    )(me, normed, mixed_grad, context, branch_grad)


DP, FSDP = "dp", "fsdp"


def swap(value, axis, bit):
    size = lax.axis_size(axis)
    return lax.ppermute(value, axis, [(i, i ^ bit) for i in range(size)])


def after(value, *others):
    return lax.optimization_barrier((value,) + others)[0]


def grow(value, step, *others):
    arrived = swap(value, *step)
    if others:
        arrived = after(arrived, *others)
    return jnp.concatenate([value, arrived], axis=0)


def fold_body(plan, count, *refs):
    sums = []
    for k in range(count):
        sums.append(refs[2 * k][...].astype(F32) + refs[2 * k + 1][...].astype(F32))
    for out_ref, takes in zip(refs[2 * count :], plan):
        start = 0
        for pair, spot in takes:
            part = sums[pair][spot].astype(out_ref.dtype)
            rows = part.shape[-2]
            out_ref[..., start : start + rows, :] = part
            start += rows


def fold_call(pairs, plan, in_blocks, out_blocks, out_shapes, steps, dtype=BF16):
    def spec(block, along):
        return pl.BlockSpec(block, lambda i: tuple(i if k == along else 0 for k in range(len(block))))

    arrays = [array for pair in pairs for array in pair]
    return pl.pallas_call(
        functools.partial(fold_body, plan, len(pairs)),
        grid=(steps,),
        in_specs=[spec(*in_blocks[k // 2]) for k in range(len(arrays))],
        out_specs=[spec(*b) for b in out_blocks],
        out_shape=[jax.ShapeDtypeStruct(shape, dtype) for shape in out_shapes],
        compiler_params=params_for(),
        cost_estimate=busy_for(2),
        name="fold_sums",
    )(*arrays)


class Fold:
    def __init__(self, keep, send):
        self.rows, self.cols = keep.shape[1:]
        self.keep, self.arrived = keep, swap(send, *CORE)
        self.stage = 0

    def step(self, *others):
        rows, cols = self.rows, self.cols
        cut, sizes = rows // 2, (2, 2, 4, rows, cols)
        upper, lower = slice(0, cut), slice(cut, rows)
        everything = slice(None)
        keep = after(self.keep, *others)
        if self.stage == 0:
            outs = fold_call(
                [(keep.reshape(sizes), self.arrived.reshape(sizes))],
                [
                    [(0, (0, everything, everything, upper))],
                    [(0, (1, everything, everything, upper))],
                    [(0, (everything, 0, everything, lower))],
                    [(0, (everything, 1, everything, lower))],
                ],
                [((2, 2, 1, rows, cols), 2)],
                [((2, 1, cut, cols), 1)] * 4,
                [(2, 4, cut, cols)] * 4,
                4,
            )
            self.keep, sent = (outs[0], outs[2]), (outs[1], outs[3])
            self.arrived = swap(sent[0], *XS), swap(sent[1], *YS)
        elif self.stage == 1:
            outs = fold_call(
                list(zip(keep, self.arrived)),
                [[(0, 0)], [(0, 1)], [(1, 0)], [(1, 1)]],
                [((2, 4, cut, cols), None)] * 2,
                [((4, cut, cols), None)] * 4,
                [(4, cut, cols)] * 4,
                1,
            )
            self.keep, sent = (outs[0], outs[2]), (outs[1], outs[3])
            self.arrived = swap(sent[0], *YS), swap(sent[1], *XS)
        elif self.stage == 2:
            near, far = slice(0, 2), slice(2, 4)
            self.keep, sent = fold_call(
                list(zip(keep, self.arrived)),
                [[(0, near), (1, near)], [(0, far), (1, far)]],
                [((4, cut, cols), None)] * 2,
                [((2, rows, cols), None)] * 2,
                [(2, rows, cols)] * 2,
                1,
            )
            self.arrived = swap(sent, *Z_NEAR)
        elif self.stage == 3:
            self.keep, sent = fold_call(
                [(keep, self.arrived)],
                [[(0, 0)], [(0, 1)]],
                [((2, rows, cols), None)],
                [((rows, cols), None)] * 2,
                [(rows, cols)] * 2,
                1,
            )
            self.arrived = swap(sent, *Z_FAR)
        else:
            return keep.astype(F32) + self.arrived.astype(F32)
        self.stage += 1
        return sent


def rel_table(steps, last, off):
    places = []
    for pos in range(2 ** len(steps)):
        rel = {DP: 0, FSDP: 0}
        for k, (axis, bit) in enumerate(steps):
            if (pos >> k) & 1:
                rel[axis] ^= bit
        if last is not None:
            rel[last[0]] ^= last[1]
        places.append((rel[DP], rel[FSDP], off, True))
    return tuple(places)


CORE, XS, YS, Z_NEAR, Z_FAR = (FSDP, 1), (FSDP, 2), (DP, 1), (DP, 2), (DP, 4)
XY = [Z_FAR, Z_NEAR, XS, YS]
YX = [Z_FAR, Z_NEAR, YS, XS]


def grow_end(value, second, *others):
    value = grow(value, second[0], *others)
    value = grow(value, second[1])
    return value, swap(value, *CORE)


def order_of(steps):
    return [(axis == DP, bit) for axis, bit in steps]


def adam_step(weight, gradient, first_mom, second, clip_factor, step_rate, decay_rate):
    scaled = gradient * clip_factor
    first_new = 0.5 * first_mom + 0.5 * scaled
    second_new = 0.5 * second + 0.5 * scaled * scaled
    correction = 1.0 - 0.5**STEP
    update = first_new / correction / (jnp.sqrt(second_new / correction) + 1e-08)
    return (first_new, second_new, weight - step_rate * (update + decay_rate * weight))


def on_device(
    tokens,
    visible_index,
    cotangent,
    qkv_weight,
    out_weight,
    up_weight,
    down_weight,
    vectors,
    qkv_first,
    out_first,
    up_first,
    down_first,
    vector_first,
    qkv_second,
    out_second,
    up_second,
    down_second,
    vector_second,
):
    _, chip_count, seq_len, model_width = tokens.shape
    dp_size, fsdp_size = lax.axis_size(DP), lax.axis_size(FSDP)
    device_count = dp_size * fsdp_size
    both = (DP, FSDP)
    block_count = dp_size
    block_seen = seq_len // block_count
    block_len = cotangent.shape[2]
    chips_group = chip_count * block_count
    rows, wide = qkv_weight.shape
    slim = out_weight.shape[1]
    span = up_weight.shape[1]
    ff_width = span * fsdp_size
    half = slim // 2
    tall = down_weight.shape[0]
    folded = (dp_size, fsdp_size) == (8, 4)

    share_q = jnp.concatenate([qkv_weight, out_weight], axis=1).astype(BF16)
    share_u = up_weight.astype(BF16)
    down_turned = down_weight.astype(BF16).T

    vec_rows, vec_cols = vectors.shape
    vector_copies = jnp.broadcast_to(vectors.astype(BF16), (device_count, vec_rows, vec_cols))
    vec_shares = lax.all_to_all(vector_copies, both, split_axis=0, concat_axis=0, tiled=True)
    vec = vec_shares.reshape(dp_size, fsdp_size, vec_rows, vec_cols).transpose(1, 2, 0, 3)
    vec = vec.reshape(fsdp_size * vec_rows, model_width).astype(F32)

    my_block = lax.axis_index(DP)
    places = visible_index[0].reshape(chips_group, block_count, block_seen)
    places = lax.dynamic_index_in_dim(places, my_block, 1, keepdims=False) - my_block * block_len
    seen_places = places
    cot = cotangent[0]
    whole_tiles = block_seen % 16 == 0
    if whole_tiles:
        places = jnp.pad(places, ((0, 0), (0, 128 - block_seen)), constant_values=-1)[:, None]
        cot_seen, mask_grad = seen_rows(cot, places, block_seen)
    else:
        slot_ids = lax.broadcasted_iota(jnp.int32, (chips_group, block_len, block_seen), 1)
        pick = (places[:, None, :] == slot_ids).astype(BF16)
        gaps = 1.0 - jnp.sum(pick.astype(F32), axis=-1)
        cot_seen = jnp.einsum("cpv,cpd->cvd", pick, cot, preferred_element_type=F32).astype(BF16)
        mask_grad = jnp.einsum("cp,cpd->d", gaps.astype(BF16), cot, preferred_element_type=F32)[None]
    if folded:
        me = jnp.stack([lax.axis_index(DP), lax.axis_index(FSDP)]).astype(jnp.int32)
        share_d = jnp.concatenate([down_turned[:half], down_turned[half:]], axis=1)
        cut = rows // 2
        cur = grow(grow(share_q[None], Z_FAR, vec_shares), Z_NEAR, cot_seen)
        d_cur = after(share_d[None], cur)
        q_upper, q_lower = grow(cur[:, :cut], XS), grow(cur[:, cut:], YS)
        d_cur = grow(d_cur, Z_FAR, q_upper, q_lower)
        q_upper, q_lower = grow(q_upper, YS), grow(q_lower, XS)
        q_arrays = (q_upper, swap(q_upper, *CORE), q_lower, swap(q_lower, *CORE))
        cot_seen = after(cot_seen, q_upper, q_lower)
        q_table = d_table = (
            rel_table(XY, None, 0),
            rel_table(XY, CORE, 0),
            rel_table(YX, None, cut),
            rel_table(YX, CORE, cut),
        )
        u_arrays = (lax.all_gather(share_u, both, axis=0, tiled=False),)
        u_table = (tuple((d, f, 0, False) for d in range(dp_size) for f in range(fsdp_size)),)
        q_order = d_order = order_of([CORE, XS, YS, Z_NEAR, Z_FAR])
        down_share = (half, tall)
        load_rows = rows
    else:
        me = jnp.zeros((2,), jnp.int32)

        def gather_whole(share):
            whole = lax.all_gather(share, both, axis=0, tiled=False)
            whole = whole.reshape((dp_size, fsdp_size) + share.shape).transpose(1, 0, 2, 3)
            return whole.reshape(fsdp_size, dp_size * share.shape[0], share.shape[1])

        q_arrays = (gather_whole(share_q),)
        u_arrays = (gather_whole(share_u),)
        down_whole = lax.all_gather(down_turned, both, axis=0, tiled=False)
        down_whole = down_whole.reshape(dp_size, fsdp_size, slim, tall).transpose(1, 2, 0, 3)
        d_arrays = (down_whole.reshape(1, model_width, ff_width),)
        q_table = u_table = (tuple((0, f, 0, False) for f in range(fsdp_size)),)
        d_table = (((0, 0, 0, False),),)
        q_order = d_order = None
        down_share = None
        load_rows = model_width

    cot_seen = cot_seen.reshape(block_count, chip_count, block_seen, model_width)
    grad = lax.all_to_all(cot_seen, DP, split_axis=0, concat_axis=0, tiled=True)
    if not whole_tiles:
        grad = grad.transpose(1, 0, 2, 3).reshape(1, chip_count, seq_len, model_width)

    x = tokens[0]
    up_bias = vec[6:10].reshape(1, ff_width)
    normed, mixed, expo, share, context, qkv_whole, out_whole = attend_forward(
        me, x, vec, q_table, q_arrays, load_rows, wide
    )
    if folded:
        d_cur = grow(d_cur, Z_NEAR, context)
        d_halves = d_cur[:, :cut], d_cur[:, cut:]
        context = after(context, *d_halves)
    middle, normed_two, active, slope = feed_up(
        me, x, context, vec, up_bias, out_whole, u_table, u_arrays, load_rows
    )
    if folded:
        d_halves = grow(d_halves[0], XS, active), grow(d_halves[1], YS, active)
        grad = after(grad, *d_halves)
    token_count = chip_count * seq_len
    flat = lambda v: v.reshape(token_count, v.shape[-1])
    grad_rows = flat(grad.transpose(1, 0, 2, 3).reshape(chip_count, seq_len, model_width))
    d_blocks = down_grad_blocks(me, grad_rows, flat(active), d_order, half, tall)
    if folded:
        upper, lower = grow(d_halves[0], YS, *d_blocks), grow(d_halves[1], XS, *d_blocks)
        d_arrays = (upper, swap(upper, *CORE), lower, swap(lower, *CORE))
    if folded:
        d_fold = Fold(*d_blocks)
        middle = after(middle, *d_blocks)
    result, gate_grad, middle_grad, branch_grad, context_grad, sums_two, up_sums = feed_down(
        me, grad, middle, active, slope, vec, out_whole, u_table, u_arrays, d_table, d_arrays, load_rows, down_share
    )
    if folded:
        normed_two = after(normed_two, d_fold.step(gate_grad))
    u_blocks = up_grad_blocks(flat(normed_two), flat(gate_grad), folded, rows, fsdp_size)
    if folded:
        u_sum = lax.psum_scatter(u_blocks.reshape(-1, span), both, scatter_dimension=0, tiled=True)
        context_grad = after(context_grad, d_fold.step(u_blocks), u_blocks)
        result = after(result, u_blocks)
    if not whole_tiles:
        result = result.reshape(chip_count, block_count, block_seen, model_width).transpose(1, 0, 2, 3)
    arrived = lax.all_to_all(result, DP, split_axis=0, concat_axis=0, tiled=True)
    arrived = arrived.reshape(chips_group, block_seen, model_width)
    mixed_grad, sums_value = attend_back(mixed, expo, share, context, context_grad)
    if folded:
        normed = after(normed, d_fold.step(mixed_grad))
    q_blocks = qkv_grad_blocks(
        me,
        flat(normed),
        flat(mixed_grad),
        flat(context),
        flat(branch_grad),
        q_order,
        rows,
        wide,
    )
    if folded:
        q_fold = Fold(*q_blocks)
        x = after(x, q_blocks, arrived)
    tokens_grad, sums_one = tokens_back(x, middle_grad, mixed_grad, vec, qkv_whole)

    slot_ids = lax.broadcasted_iota(jnp.int32, (chips_group, block_len, block_seen), 1)
    pick = (seen_places[:, None, :] == slot_ids).astype(BF16)
    gaps = 1.0 - jnp.sum(pick.astype(F32), axis=-1)
    filled = jnp.einsum("cpv,cvd->cpd", pick, arrived, preferred_element_type=F32)
    filled = filled + gaps[..., None] * vec[11]
    full_layout = filled.astype(BF16).reshape(1, chips_group, block_len, model_width)

    if folded:
        d_fold.step(tokens_grad)
        d_sum = d_fold.step()
        q_fold.step(tokens_grad)
        q_fold.step()
        q_fold.step()
        q_fold.step()
        q_sum = q_fold.step()
        u_sum = u_sum.astype(F32)
        d_sum = jnp.concatenate([d_sum[:, :tall], d_sum[:, tall:]], axis=0).T.astype(F32)
    else:

        def scatter_whole(whole):
            cols = whole.shape[2]
            pieces = whole.reshape(fsdp_size, dp_size, -1, cols).transpose(1, 0, 2, 3)
            pieces = pieces.reshape(-1, cols)
            return lax.psum_scatter(pieces, both, scatter_dimension=0, tiled=True).astype(F32)

        q_sum, u_sum = scatter_whole(q_blocks[0]), scatter_whole(u_blocks)
        pieces = d_blocks[0].reshape(fsdp_size, slim, dp_size, tall).transpose(2, 0, 1, 3)
        pieces = pieces.reshape(device_count * slim, tall)
        d_sum = lax.psum_scatter(pieces, both, scatter_dimension=0, tiled=True).astype(F32).T

    vector_grad = jnp.concatenate(
        [
            sums_one[:2],
            sums_value[:1],
            sums_two[:3],
            up_sums.reshape(-1, model_width),
            sums_two[3:4],
            mask_grad,
        ],
        axis=0,
    )
    parts = vector_grad.reshape(fsdp_size, vec_rows, dp_size, vec_cols).transpose(2, 0, 1, 3)
    parts = parts.reshape(device_count, vec_rows, vec_cols)
    parts = lax.all_to_all(parts, both, split_axis=0, concat_axis=0, tiled=True)
    shares = (q_sum[:, :wide], q_sum[:, wide:], u_sum, d_sum, jnp.sum(parts, axis=0))
    squares = jnp.sum(q_sum * q_sum) + jnp.sum(u_sum * u_sum) + jnp.sum(d_sum * d_sum)
    squares = squares + jnp.sum(shares[4] * shares[4])
    square_parts = jnp.broadcast_to(squares, (device_count, 1))
    grad_total = jnp.sum(lax.all_to_all(square_parts, both, split_axis=0, concat_axis=0, tiled=True))
    grad_norm = jnp.sqrt(grad_total)
    tokens_all = device_count * chip_count * seq_len
    threshold = 0.05 * model_width * math.sqrt(tokens_all)
    clip = jnp.minimum(1.0, threshold / grad_norm)
    rate = 0.6 / math.sqrt(model_width)
    out_rate = 0.6 / math.sqrt(model_width // 32)
    down_rate = 0.6 / math.sqrt(ff_width)
    qkv_out = adam_step(qkv_weight, shares[0], qkv_first, qkv_second, clip, rate, 0.05)
    out_out = adam_step(out_weight, shares[1], out_first, out_second, clip, out_rate, 0.05)
    up_out = adam_step(up_weight, shares[2], up_first, up_second, clip, rate, 0.05)
    down_out = adam_step(down_weight, shares[3], down_first, down_second, clip, down_rate, 0.05)
    vec_out = adam_step(vectors, shares[4], vector_first, vector_second, clip, 0.45, 0.0)
    return (
        full_layout,
        tokens_grad[None],
        *qkv_out,
        qkv_out[2].astype(BF16),
        *out_out,
        out_out[2].astype(BF16),
        *up_out,
        up_out[2].astype(BF16),
        *down_out,
        down_out[2].astype(BF16),
        *vec_out,
        grad_norm,
    )


def solution(mesh):
    grid = P("dp", "fsdp")
    table = P("fsdp", "dp")
    weights = (grid, grid, grid, grid, table)
    in_specs = (
        P("fsdp", "dp", None, None),
        P("fsdp", None, None),
        P("fsdp", None, "dp", None),
        *weights,
        *weights,
        *weights,
    )
    out_specs = (
        P("fsdp", None, "dp", None),
        P("fsdp", "dp", None, None),
        *(grid,) * 16,
        *(table,) * 3,
        P(),
    )
    return jax.shard_map(
        on_device, mesh=mesh, in_specs=in_specs, out_specs=out_specs, check_vma=False
    )
```

time: 451 us -> 372 us (0.82)
  waiting for transfers between devices: 137 us -> 90.8 us
  starting transfers between devices: 70 us -> 49.2 us
  local copies, waits for them, and re-layouts: 37.2 us -> 16.9 us
  Pallas kernels: 147 us -> 165 us
  other arithmetic: 37 us -> 23.8 us
  between operations: 6.13 us -> 19.2 us
  matrix products: 12.1 us -> 5.03 us
    ppermute x33 -> x30, waiting for transfers between devices: 131 us -> 79.1 us  [swap(): return lax.ppermute(value, axis, [(i, i ^ bit) for i in range(size)])]
    pallas_call x4 -> x13, Pallas kernels: 60.1 us -> 81.5 us  [the longest x8 22.3 us: fold_call(): pl.pallas_call(functools.partial(fold_body, plan, len(pairs)), grid=(step...]
    convert_element_type x14 -> x1, other arithmetic: 16.6 us -> 1.64 us  [on_device(): share_u = up_weight.astype(BF16)]
    ppermute x33 -> x30, starting transfers between devices: 41.6 us -> 28.4 us  [swap(): return lax.ppermute(value, axis, [(i, i ^ bit) for i in range(size)])]
    slice x14 -> x4, local copies, waits for them, and re-layouts: 12.3 us -> 0.85 us  [the longest x1 0.75 us: on_device(): filled = filled + gaps[..., None] * vec[11]]
    dot_general x2 -> x0, matrix products: 5.86 us -> none  [the longest x1 4.94 us: on_device(): jnp.einsum('cpv,cpd->cvd', pick, cot, preferred_element_type=F32)]
    unnamed x84 -> x76, local copies, waits for them, and re-layouts: 3.83 us -> 8.8 us
    all_to_all x1, starting transfers between devices: 8.35 us -> 3.75 us  [on_device(): grad = lax.all_to_all(cot_seen, DP, split_axis=0, concat_axis=0, tiled=True)]
  transfers between devices with their start and end apart: 38 -> 37, of which waited for: 16 -> 15; matrix products, arithmetic and copies ran while one was open for 17% -> 8% of each run, Pallas kernels for 18% -> 43%
where the time goes in v3:
time: 372 us; the launch traced here: 370 us
  Pallas kernels  165 us (44%)
  waiting for transfers between devices  90.8 us (24%)
  starting transfers between devices  49.2 us (13%)
  other arithmetic  23.8 us (6%)
  between operations  19.2 us (5%)
  local copies, waits for them, and re-layouts  16.9 us (5%)
  matrix products  5.03 us (1%)
    ppermute x30, waiting for transfers between devices, swap(): return lax.ppermute(value, axis, [(i, i ^ bit) for i in range(size)])  79.1 us
    pallas_call x1, Pallas kernels, feed_down(): pl.pallas_call(functools.partial(feed_down_body, u_table, d_table, rows,...  29.8 us
    ppermute x30, starting transfers between devices, swap(): return lax.ppermute(value, axis, [(i, i ^ bit) for i in range(size)])  28.4 us
    pallas_call x8, Pallas kernels, fold_call(): pl.pallas_call(functools.partial(fold_body, plan, len(pairs)), grid=(step...  22.3 us
    pallas_call x1, Pallas kernels, attend_forward(): pl.pallas_call(functools.partial(attend_body, table, rows, heads, wide),...  21.1 us
    pallas_call x1, Pallas kernels, attend_back(): pl.pallas_call(functools.partial(attend_back_body, heads), grid=(chips,),...  19.1 us
    pallas_call x1, Pallas kernels, feed_up(): pl.pallas_call(functools.partial(feed_up_body, table, rows), grid=(chips,...  17.1 us
    pallas_call x1, Pallas kernels, qkv_grad_blocks(): pl.pallas_call(functools.partial(qkv_grad_body, order, rows, wide), grid=...  14.6 us
  transfers between devices with their start and end apart: 37, of which 15 were waited for; matrix products, arithmetic and copies ran while one was open for 8% of the time, Pallas kernels for 43%

profile of v3, /device:TPU:0, one launch (start us, length us, event | category | flops | bytes accessed | tf_op | source)
XLA Modules:
  0.0 369.8 jit_solution(9901719092199483501)
XLA Ops:
  7.2 1.6 convert_element_type.68
  10.9 4.1 %collective-permute-start = (bf16[1,96,768]{2,1,0:T(8,128)(2,1)S(1)}, bf16[1,96,768]{2,1,0:T(8,128)(2,1)S(1)}, u32[]{:S(2)}, u32[]{:S(2)}) collective-permute-start(bf16[1,96,768]{2,1,0:T(8,128)(2,1)S(1)} %pad_maximum_fusion.12), channel_id=1, source_target_pairs={{0,16},{4,20},{8,24},{12,28},{16,0},{20,4},{24,8},{28,12},{1,17},{... | collective-permute-start | bytes 442376 | tf_op jit(solution)/shard_map/ppermute | solution.py:668
  16.3 3.8 %all-to-all-start = ((bf16[32,3,96]{2,1,0:T(4,128)(2,1)}), bf16[32,3,96]{2,1,0:T(4,128)(2,1)S(1)}, u32[]{:S(2)}, u32[]{:S(2)}) async-start(bf16[32,3,96]{2,1,0:T(4,128)(2,1)} %broadcast_in_dim.19), calls=%async_computation | async-start | bytes 65536 | tf_op jit(solution)/shard_map/all_to_all | solution.py:857
  21.6 5.7 %all-to-all-done = bf16[32,3,96]{2,1,0:T(4,128)(2,1)S(1)} async-done(((bf16[32,3,96]{2,1,0:T(4,128)(2,1)}), bf16[32,3,96]{2,1,0:T(4,128)(2,1)S(1)}, u32[]{:S(2)}, u32[]{:S(2)}) %all-to-all-start) | async-done | bytes 18464 | tf_op jit(solution)/shard_map/all_to_all | solution.py:857
  28.1 8.2 %seen_rows.1 = (bf16[32,32,768]{2,1,0:T(8,128)(2,1)}, f32[1,768]{1,0:T(1,128)}) custom-call(bf16[32,128,768]{2,1,0:T(8,128)(2,1)} %bitcast.64, s32[32,1,128]{2,1,0:T(1,128)} %bitcast.62), custom_call_target="tpu_custom_call" | custom-call | flops 8000000000 | bytes 24000000 | tf_op jit(solution)/shard_map/seen_rows/pallas_call | solution.py:136
  36.3 1.9 collective-permute-done.1
  40.0 9.2 %collective-permute-done.4 = bf16[4,48,768]{2,1,0:T(8,128)(2,1)S(1)} collective-permute-done((bf16[4,48,768]{2,1,0:T(8,128)(2,1)S(1)}, bf16[4,48,768]{2,1,0:T(8,128)(2,1)S(1)}, u32[]{:S(2)}, u32[]{:S(2)}) %collective-permute-start.4) | collective-permute-done | bytes 294944 | tf_op jit(solution)/shard_map/ppermute | solution.py:668
  50.1 2.5 collective-permute-done.2
  52.7 1.6 collective-permute-start.3
  54.3 12.6 %collective-permute-done.5 = bf16[8,48,768]{2,1,0:T(8,128)(2,1)} collective-permute-done((bf16[8,48,768]{2,1,0:T(8,128)(2,1)S(1)}, bf16[8,48,768]{2,1,0:T(8,128)(2,1)}, u32[]{:S(2)}, u32[]{:S(2)}) %collective-permute-start.5) | collective-permute-done | bytes 589856 | tf_op jit(solution)/shard_map/ppermute | solution.py:668
  66.9 2.2 pad_maximum_fusion.1.refs_5_
  69.1 2.9 collective-permute-done.3
  74.7 10.0 %collective-permute-done.6 = bf16[1,96,768]{2,1,0:T(8,128)(2,1)S(1)} collective-permute-done((bf16[1,96,768]{2,1,0:T(8,128)(2,1)S(1)}, bf16[1,96,768]{2,1,0:T(8,128)(2,1)S(1)}, u32[]{:S(2)}, u32[]{:S(2)}) %collective-permute-start.6) | collective-permute-done | bytes 147488 | tf_op jit(solution)/shard_map/ppermute | solution.py:668
  84.8 3.8 %all-to-all-start.1 = ((bf16[8,4,32,768]{3,2,1,0:T(8,128)(2,1)}), bf16[8,4,32,768]{3,2,1,0:T(8,128)(2,1)S(1)}, u32[]{:S(2)}, u32[]{:S(2)}) async-start(bf16[8,4,32,768]{3,2,1,0:T(8,128)(2,1)} %bitcast.7), calls=%async_computation.1 | async-start | bytes 3145728 | tf_op jit(solution)/shard_map/all_to_all | solution.py:918
  88.6 21.1 %attend_forward.1 = (bf16[4,256,768]{2,1,0:T(8,128)(2,1)}, bf16[4,256,2304]{2,1,0:T(8,128)(2,1)}, bf16[4,12,256,256]{3,2,1,0:T(8,128)(2,1)}, f32[4,256,12]{2,1,0...) custom-call(s32[2]{0:T(128)} %pad_add_fusion.refs_0_.me_ref, ...), custom_call_target="tpu_custom_call" | custom-call | flops 20000000000 | bytes 60000000 | tf_op jit(solution)/shard_map/attend_forward/pallas_call | solution.py:215
  109.8 2.1 collective-permute-start.11
  113.3 17.1 %feed_up.1 = (f32[4,256,768]{2,1,0:T(8,128)}, bf16[4,256,768]{2,1,0:T(8,128)(2,1)}, bf16[4,256,3072]{2,1,0:T(8,128)(2,1)}, bf16[4,256,3072]{2,1,0:T(8,128)(2,1)}) custom-call(s32[2]{0:T(128)} %pad_add_fusion.refs_0_.me_ref, bf16[4,256,768]{2,1,0:T(8,128)(2,1)} %bitcast.68, bf16[4,256,768]{2,1,0:T(8,128)(2,1)} %get-tuple-element.111.refs_2_.context_ref, ...), custom_call_target="tpu_custom_call" | custom-call | flops 16999999488 | bytes 51000000 | tf_op jit(solution)/shard_map/feed_up/pallas_call | solution.py:279
  134.5 13.3 %down_grad.1 = (bf16[16,96,768]{2,1,0:T(8,128)(2,1)}, bf16[16,96,768]{2,1,0:T(8,128)(2,1)}) custom-call(s32[2]{0:T(128)} %pad_add_fusion.refs_0_.me_ref, bf16[1024,768]{1,0:T(8,128)(2,1)} %bitcast.57, bf16[1024,3072]{1,0:T(8,128)(2,1)} %bitcast.70), custom_call_target="tpu_custom_call" | custom-call | flops 10000000000 | bytes 30000000 | tf_op jit(solution)/shard_map/down_grad/pallas_call | solution.py:588
  151.9 1.7 collective-permute-done.13.refs_9_
  154.7 29.8 %feed_down.1 = (bf16[8,4,32,768]{3,2,1,0:T(8,128)(2,1)}, bf16[4,256,3072]{2,1,0:T(8,128)(2,1)}, f32[4,256,768]{2,1,0:T(8,128)}, bf16[4,256,768]{2,1,0:T(8,128)(2...) custom-call(s32[2]{0:T(128)} %pad_add_fusion.refs_0_.me_ref, ...), custom_call_target="tpu_custom_call" | custom-call | flops 20000000000 | bytes 60000000 | tf_op jit(solution)/shard_map/feed_down/pallas_call | solution.py:376
  184.6 4.5 %fold_sums.8 = (bf16[2,4,48,768]{3,2,1,0:T(8,128)(2,1)}, bf16[2,4,48,768]{3,2,1,0:T(8,128)(2,1)}, bf16[2,4,48,768]{3,2,1,0:T(8,128)(2,1)}, bf16[2,4,48,768]{3,2,1,0:T(8,128)(2,1)}) custom-call(bf16[2,2,4,96,768]{4,3,2,1,0:T(8,128)(2,1)} %bitcast.74, bf16[2,2,4,96,768]{4,3,2,1,0:T(8,128)(2,1)} %bitcast.18.refs_1_), custom_call_target="tpu_custom_call" | custom-call | flops 2000000000 | bytes 6000000 | tf_op jit(solution)/shard_map/fold_sums/pallas_call | solution.py:700
  190.5 2.0 collective-permute-start.18
  192.4 9.2 %up_grad.1 = bf16[8,4,96,768]{3,2,1,0:T(8,128)(2,1)} custom-call(bf16[1024,768]{1,0:T(8,128)(2,1)} %bitcast.79, bf16[1024,3072]{1,0:T(8,128)(2,1)} %bitcast.71), custom_call_target="tpu_custom_call" | custom-call | flops 8000000000 | bytes 24000000 | tf_op jit(solution)/shard_map/up_grad/pallas_call | solution.py:554
  201.6 4.5 %all-to-all-start.2 = ((bf16[8,4,32,768]{3,2,1,0:T(8,128)(2,1)}), bf16[8,4,32,768]{3,2,1,0:T(8,128)(2,1)S(1)}, u32[]{:S(2)}, u32[]{:S(2)}) async-start(bf16[8,4,32,768]{3,2,1,0:T(8,128)(2,1)} %get-tuple-element.131), calls=%async_computation.2 | async-start | bytes 3145728 | tf_op jit(solution)/shard_map/all_to_all | solution.py:959
  208.6 2.7 fold_sums.9
  211.2 2.0 collective-permute-start.19
  213.8 19.1 %attend_back.1 = (bf16[4,256,2304]{2,1,0:T(8,128)(2,1)}, f32[8,768]{1,0:T(8,128)}) custom-call(bf16[4,256,2304]{2,1,0:T(8,128)(2,1)} %get-tuple-element.139.mixed_ref, bf16[4,12,256,256]{3,2,1,0:T(8,128)(2,1)} %get-tuple-element.140.expo_ref, f32[4,256,12]{2,1,0:T(8,128)} %get-tuple-element.141.share_ref, ...), custom_call_target="tpu_custom_call" | custom-call | flops 15000000512 | bytes 45000000 | tf_op jit(solution)/shard_map/attend_back/pallas_call | solution.py:460
  234.4 2.1 fold_sums.10
  236.5 14.6 %qkv_grad.1 = (bf16[16,96,768]{2,1,0:T(8,128)(2,1)}, bf16[16,96,768]{2,1,0:T(8,128)(2,1)}) custom-call(s32[2]{0:T(128)} %pad_add_fusion.refs_0_.me_ref, bf16[1024,768]{1,0:T(8,128)(2,1)} %bitcast.76, bf16[1024,2304]{1,0:T(8,128)(2,1)} %bitcast.72, bf16[1024,768]{1,0:T(8,128)(2,1)} %bitcast.77, bf16[1024,768]{1,0:T(8,128)(2,1)} %bitcast.78), custom_call_target="tpu_custom_call" | custom-call | flops 10000000000 | bytes 30000000 | tf_op jit(solution)/shard_map/qkv_grad/pallas_call | solution.py:644
  251.1 10.1 %tokens_back.1 = (f32[4,256,768]{2,1,0:T(8,128)}, f32[8,768]{1,0:T(8,128)}) custom-call(bf16[4,256,768]{2,1,0:T(8,128)(2,1)} %bitcast.69, f32[4,256,768]{2,1,0:T(8,128)} %get-tuple-element.155.grad_ref, bf16[4,256,2304]{2,1,0:T(8,128)(2,1)} %get-tuple-element.146.mixed_grad_ref, f32[12,768]{1,0:T(8,128)} %copy-done.17, ...), custom_call_target="tpu_custom_call" | custom-call | flops 8000000000 | bytes 24000000 | tf_op jit(solution)/shard_map/tokens_back/pallas_call | solution.py:496
  261.3 4.6 %fold_sums.11 = (bf16[2,4,48,768]{3,2,1,0:T(8,128)(2,1)}, bf16[2,4,48,768]{3,2,1,0:T(8,128)(2,1)}, bf16[2,4,48,768]{3,2,1,0:T(8,128)(2,1)}, bf16[2,4,48,768]{3,2,1,0:T(8,128)(2,1)}) custom-call(bf16[2,2,4,96,768]{4,3,2,1,0:T(8,128)(2,1)} %bitcast.75, bf16[2,2,4,96,768]{4,3,2,1,0:T(8,128)(2,1)} %bitcast.29.refs_1_), custom_call_target="tpu_custom_call" | custom-call | flops 2000000000 | bytes 6000000 | tf_op jit(solution)/shard_map/fold_sums/pallas_call | solution.py:700
  267.6 2.0 collective-permute-start.28
  269.7 18.2 %collective-permute-done.22.refs_1_ = bf16[2,4,48,768]{3,2,1,0:T(8,128)(2,1)S(1)} collective-permute-done((bf16[2,4,48,768]{3,2,1,0:T(8,128)(2,1)}, bf16[2,4,48,768]{3,2,1,0:T(8,128)(2,1)S(1)}, u32[]{:S(2)}, u32[]{:S(2)}) %collective-permute-start.22) | collective-permute-done | bytes 589856 | tf_op jit(solution)/shard_map/ppermute | solution.py:668
  289.5 2.7 fold_sums.12
  298.6 4.9 %all-to-all-start.3 = ((f32[32,3,96]{2,1,0:T(4,128)}), f32[32,3,96]{2,1,0:T(4,128)S(1)}, u32[]{:S(2)}, u32[]{:S(2)}) async-start(f32[32,3,96]{2,1,0:T(4,128)} %copy.64), calls=%async_computation.4 | async-start | bytes 131072 | tf_op jit(solution)/shard_map/all_to_all | solution.py:1022
  303.5 1.8 fold_sums.15
  305.3 2.4 collective-permute-start.29
  307.7 3.3 all-to-all-done.3
  312.5 2.1 fold_sums.13
  315.9 2.6 collective-permute-done.29
  318.5 7.3 %collective-permute-done.26.refs_1_ = bf16[2,96,768]{2,1,0:T(8,128)(2,1)S(1)} collective-permute-done((bf16[2,96,768]{2,1,0:T(8,128)(2,1)}, bf16[2,96,768]{2,1,0:T(8,128)(2,1)S(1)}, u32[]{:S(2)}, u32[]{:S(2)}) %collective-permute-start.26) | collective-permute-done | bytes 294944 | tf_op jit(solution)/shard_map/ppermute | solution.py:668
  326.5 1.8 fold_sums.14
  329.0 9.4 %collective-permute-done.27 = bf16[96,768]{1,0:T(8,128)(2,1)S(1)} collective-permute-done((bf16[96,768]{1,0:T(8,128)(2,1)}, bf16[96,768]{1,0:T(8,128)(2,1)S(1)}, u32[]{:S(2)}, u32[]{:S(2)}) %collective-permute-start.27) | collective-permute-done | bytes 147488 | tf_op jit(solution)/shard_map/ppermute | solution.py:668
  338.4 1.6 convert_add_fusion.1
  340.0 1.6 fusion.2
  344.8 3.7 %all-to-all-start.4 = ((f32[32,1,1]{2,1,0:T(1,128)}), f32[32,1,1]{2,1,0:T(1,128)S(1)}, u32[]{:S(2)}, u32[]{:S(2)}) async-start(f32[32,1,1]{2,1,0:T(1,128)} %broadcast_in_dim.22), calls=%async_computation.5 | async-start | bytes 32768 | tf_op jit(solution)/shard_map/all_to_all | solution.py:1027
  348.6 5.0 %fusion = bf16[1,32,128,768]{3,2,1,0:T(8,128)(2,1)} fusion(f32[768]{0:T(1024)S(1)} %slice_reduce_fusion, f32[32,128]{1,0:T(8,128)S(1)} %broadcast_subtract_fusion, bf16[32,32,768]{2,1,0:T(8,128)(2,1)S(1)} %bitcast.54, s32[32,32]{1,0:T(8,128)S(1)} %subtract_bitcast_fusion), kind=kOutput, calls=%fused_computation.1 | convolution fusion | flops 210894848 | bytes 7887872 | tf_op jit(solution)/shard_map/cpv,cvd->cpd/dot_general | solution.py:982
  353.7 1.9 all-to-all-done.4
  (183 shorter events, 47.5 us)
Async XLA Ops:
  7.2 106.1 %all-gather.3.cloned.1.call-start = ((), (), s32[]{:S(2)}) async-start(), calls=%async_computation.7 | async-start | bytes 4866048 | tf_op jit(solution)/shard_map/all_gather | solution.py:893
  10.9 16.5 %collective-permute-start = (bf16[1,96,768]{2,1,0:T(8,128)(2,1)S(1)}, bf16[1,96,768]{2,1,0:T(8,128)(2,1)S(1)}, u32[]{:S(2)}, u32[]{:S(2)}) collective-permute-start(bf16[1,96,768]{2,1,0:T(8,128)(2,1)S(1)} %pad_maximum_fusion.12), channel_id=1, source_target_pairs={{0,16},{4,20},{8,24},{12,28},{16,0},{20,4},{24,8},{28,12},{1,17},{... | collective-permute-start | bytes 442376 | tf_op jit(solution)/shard_map/ppermute | solution.py:668
  16.3 11.1 %all-to-all-start = ((bf16[32,3,96]{2,1,0:T(4,128)(2,1)}), bf16[32,3,96]{2,1,0:T(4,128)(2,1)S(1)}, u32[]{:S(2)}, u32[]{:S(2)}) async-start(bf16[32,3,96]{2,1,0:T(4,128)(2,1)} %broadcast_in_dim.19), calls=%async_computation | async-start | bytes 65536 | tf_op jit(solution)/shard_map/all_to_all | solution.py:857
  27.4 10.7 %collective-permute-start.1 = (bf16[2,96,768]{2,1,0:T(8,128)(2,1)S(1)}, bf16[2,96,768]{2,1,0:T(8,128)(2,1)S(1)}, u32[]{:S(2)}, u32[]{:S(2)}) collective-permute-start(bf16[2,96,768]{2,1,0:T(8,128)(2,1)S(1)} %pad_maximum_fusion.9), channel_id=1, source_target_pairs={{0,8},{4,12},{8,0},{12,4},{16,24},{20,28},{24,16},{28,20},{1,9},{5... | collective-permute-start | bytes 884744 | tf_op jit(solution)/shard_map/ppermute | solution.py:668
  38.3 16.0 %copy-start.1 = (f32[384,192]{0,1:T(8,128)S(1)}, f32[384,192]{0,1:T(8,128)}, u32[]{:S(2)}) copy-start(f32[384,192]{0,1:T(8,128)} %param.24) | copy-start | bytes 884740
  38.3 10.9 %collective-permute-start.4 = (bf16[4,48,768]{2,1,0:T(8,128)(2,1)S(1)}, bf16[4,48,768]{2,1,0:T(8,128)(2,1)S(1)}, u32[]{:S(2)}, u32[]{:S(2)}) collective-permute-start(bf16[4,48,768]{2,1,0:T(8,128)(2,1)S(1)} %get-tuple-element.205), channel_id=1, source_target_pairs={{0,4},{4,0},{8,12},{12,8},{16,20},{20,16},{24,28},{28,24},{1,5},{5... | collective-permute-start | bytes 884744 | tf_op jit(solution)/shard_map/ppermute | solution.py:668
  39.3 13.3 %collective-permute-start.2 = (bf16[4,48,768]{2,1,0:T(8,128)(2,1)S(1)}, bf16[4,48,768]{2,1,0:T(8,128)(2,1)S(1)}, u32[]{:S(2)}, u32[]{:S(2)}) collective-permute-start(bf16[4,48,768]{2,1,0:T(8,128)(2,1)S(1)} %get-tuple-element.206), channel_id=1, source_target_pairs={{0,2},{1,3},{2,0},{3,1},{4,6},{5,7},{6,4},{7,5},{8,10},{9,11},{10,... | collective-permute-start | bytes 884744 | tf_op jit(solution)/shard_map/ppermute | solution.py:668
  49.2 17.7 %collective-permute-start.5 = (bf16[8,48,768]{2,1,0:T(8,128)(2,1)S(1)}, bf16[8,48,768]{2,1,0:T(8,128)(2,1)}, u32[]{:S(2)}, u32[]{:S(2)}) collective-permute-start(bf16[8,48,768]{2,1,0:T(8,128)(2,1)S(1)} %pad_maximum_fusion.6), channel_id=1, source_target_pairs={{0,2},{1,3},{2,0},{3,1},{4,6},{5,7},{6,4},{7,5},{8,10},{9,11},{10,... | collective-permute-start | bytes 1769480 | tf_op jit(solution)/shard_map/ppermute | solution.py:668
  52.7 19.4 %collective-permute-start.3 = (bf16[8,48,768]{2,1,0:T(8,128)(2,1)S(1)}, bf16[8,48,768]{2,1,0:T(8,128)(2,1)S(1)}, u32[]{:S(2)}, u32[]{:S(2)}) collective-permute-start(bf16[8,48,768]{2,1,0:T(8,128)(2,1)S(1)} %pad_maximum_fusion.5), channel_id=1, source_target_pairs={{0,4},{4,0},{8,12},{12,8},{16,20},{20,16},{24,28},{28,24},{1,5},{5... | collective-permute-start | bytes 1769480 | tf_op jit(solution)/shard_map/ppermute | solution.py:668
  69.1 19.5 %collective-permute-start.9 = (bf16[16,48,768]{2,1,0:T(8,128)(2,1)}, bf16[16,48,768]{2,1,0:T(8,128)(2,1)}, u32[]{:S(2)}, u32[]{:S(2)}) collective-permute-start(bf16[16,48,768]{2,1,0:T(8,128)(2,1)} %pad_maximum_fusion.1.refs_5_), channel_id=1, source_target_pairs={{0,1},{1,0},{2,3},{3,2},{4,5},{5,4},{6,7},{7,6},{8,9},{9,8},{10,11... | collective-permute-start | bytes 3538952 | tf_op jit(solution)/shard_map/ppermute | solution.py:668
  73.2 15.4 %collective-permute-start.8 = (bf16[16,48,768]{2,1,0:T(8,128)(2,1)}, bf16[16,48,768]{2,1,0:T(8,128)(2,1)}, u32[]{:S(2)}, u32[]{:S(2)}) collective-permute-start(bf16[16,48,768]{2,1,0:T(8,128)(2,1)} %pad_maximum_fusion.refs_3_), channel_id=1, source_target_pairs={{0,1},{1,0},{2,3},{3,2},{4,5},{5,4},{6,7},{7,6},{8,9},{9,8},{10,11... | collective-permute-start | bytes 3538952 | tf_op jit(solution)/shard_map/ppermute | solution.py:668
  74.0 10.9 %copy-start.17 = (f32[12,768]{1,0:T(8,128)}, f32[12,768]{1,0:T(8,128)S(1)}, u32[]{:S(2)}) copy-start(f32[12,768]{1,0:T(8,128)S(1)} %reshape.166.refs_2_.refs_3_.refs_5_.vec_ref) | copy-start | bytes 110596
  74.0 10.7 %collective-permute-start.6 = (bf16[1,96,768]{2,1,0:T(8,128)(2,1)S(1)}, bf16[1,96,768]{2,1,0:T(8,128)(2,1)S(1)}, u32[]{:S(2)}, u32[]{:S(2)}) collective-permute-start(bf16[1,96,768]{2,1,0:T(8,128)(2,1)S(1)} %maximum_bitcast_fusion), channel_id=1, source_target_pairs={{0,16},{4,20},{8,24},{12,28},{16,0},{20,4},{24,8},{28,12},{1,17},{... | collective-permute-start | bytes 442376 | tf_op jit(solution)/shard_map/ppermute | solution.py:668
  84.7 25.0 %collective-permute-start.7 = (bf16[2,96,768]{2,1,0:T(8,128)(2,1)S(1)}, bf16[2,96,768]{2,1,0:T(8,128)(2,1)S(1)}, u32[]{:S(2)}, u32[]{:S(2)}) collective-permute-start(bf16[2,96,768]{2,1,0:T(8,128)(2,1)S(1)} %pad_maximum_fusion.10), channel_id=1, source_target_pairs={{0,8},{4,12},{8,0},{12,4},{16,24},{20,28},{24,16},{28,20},{1,9},{5... | collective-permute-start | bytes 884744 | tf_op jit(solution)/shard_map/ppermute | solution.py:668
  84.8 48.0 %all-to-all-start.1 = ((bf16[8,4,32,768]{3,2,1,0:T(8,128)(2,1)}), bf16[8,4,32,768]{3,2,1,0:T(8,128)(2,1)S(1)}, u32[]{:S(2)}, u32[]{:S(2)}) async-start(bf16[8,4,32,768]{3,2,1,0:T(8,128)(2,1)} %bitcast.7), calls=%async_computation.1 | async-start | bytes 3145728 | tf_op jit(solution)/shard_map/all_to_all | solution.py:918
  109.8 20.6 %collective-permute-start.11 = (bf16[4,48,768]{2,1,0:T(8,128)(2,1)S(1)}, bf16[4,48,768]{2,1,0:T(8,128)(2,1)S(1)}, u32[]{:S(2)}, u32[]{:S(2)}) collective-permute-start(bf16[4,48,768]{2,1,0:T(8,128)(2,1)S(1)} %get-tuple-element.203), channel_id=1, source_target_pairs={{0,4},{4,0},{8,12},{12,8},{16,20},{20,16},{24,28},{28,24},{1,5},{5... | collective-permute-start | bytes 884744 | tf_op jit(solution)/shard_map/ppermute | solution.py:668
  111.9 18.5 %collective-permute-start.10 = (bf16[4,48,768]{2,1,0:T(8,128)(2,1)S(1)}, bf16[4,48,768]{2,1,0:T(8,128)(2,1)S(1)}, u32[]{:S(2)}, u32[]{:S(2)}) collective-permute-start(bf16[4,48,768]{2,1,0:T(8,128)(2,1)S(1)} %get-tuple-element.204), channel_id=1, source_target_pairs={{0,2},{1,3},{2,0},{3,1},{4,6},{5,7},{6,4},{7,5},{8,10},{9,11},{10,... | collective-permute-start | bytes 884744 | tf_op jit(solution)/shard_map/ppermute | solution.py:668
  131.3 16.5 %collective-permute-start.14 = (bf16[8,48,768]{2,1,0:T(8,128)(2,1)}, bf16[8,48,768]{2,1,0:T(8,128)(2,1)}, u32[]{:S(2)}, u32[]{:S(2)}) collective-permute-start(bf16[8,48,768]{2,1,0:T(8,128)(2,1)} %pad_maximum_fusion.8), channel_id=1, source_target_pairs={{0,2},{1,3},{2,0},{3,1},{4,6},{5,7},{6,4},{7,5},{8,10},{9,11},{10,... | collective-permute-start | bytes 1769480 | tf_op jit(solution)/shard_map/ppermute | solution.py:668
  132.8 16.3 %collective-permute-start.12 = (bf16[8,48,768]{2,1,0:T(8,128)(2,1)}, bf16[8,48,768]{2,1,0:T(8,128)(2,1)}, u32[]{:S(2)}, u32[]{:S(2)}) collective-permute-start(bf16[8,48,768]{2,1,0:T(8,128)(2,1)} %pad_maximum_fusion.7), channel_id=1, source_target_pairs={{0,4},{4,0},{8,12},{12,8},{16,20},{20,16},{24,28},{28,24},{1,5},{5... | collective-permute-start | bytes 1769480 | tf_op jit(solution)/shard_map/ppermute | solution.py:668
  149.0 2.9 collective-permute-start.15
  150.7 3.0 collective-permute-start.13
  150.9 33.7 %collective-permute-start.16 = (bf16[16,96,768]{2,1,0:T(8,128)(2,1)}, bf16[16,96,768]{2,1,0:T(8,128)(2,1)}, u32[]{:S(2)}, u32[]{:S(2)}) collective-permute-start(bf16[16,96,768]{2,1,0:T(8,128)(2,1)} %get-tuple-element.119), channel_id=1, source_target_pairs={{0,1},{1,0},{2,3},{3,2},{4,5},{5,4},{6,7},{7,6},{8,9},{9,8},{10,11... | collective-permute-start | bytes 7077896 | tf_op jit(solution)/shard_map/ppermute | solution.py:668
  189.1 17.8 %collective-permute-start.17 = (bf16[2,4,48,768]{3,2,1,0:T(8,128)(2,1)}, bf16[2,4,48,768]{3,2,1,0:T(8,128)(2,1)S(1)}, u32[]{:S(2)}, u32[]{:S(2)}) collective-permute-start(bf16[2,4,48,768]{3,2,1,0:T(8,128)(2,1)} %get-tuple-element.128), channel_id=1, source_target_pairs={{0,2},{1,3},{2,0},{3,1},{4,6},{5,7},{6,4},{7,5},{8,10},{9,11},{10,... | collective-permute-start | bytes 1769480 | tf_op jit(solution)/shard_map/ppermute | solution.py:668
  190.5 16.4 %collective-permute-start.18 = (bf16[2,4,48,768]{3,2,1,0:T(8,128)(2,1)}, bf16[2,4,48,768]{3,2,1,0:T(8,128)(2,1)S(1)}, u32[]{:S(2)}, u32[]{:S(2)}) collective-permute-start(bf16[2,4,48,768]{3,2,1,0:T(8,128)(2,1)} %get-tuple-element.129), channel_id=1, source_target_pairs={{0,4},{4,0},{8,12},{12,8},{16,20},{20,16},{24,28},{28,24},{1,5},{5... | collective-permute-start | bytes 1769480 | tf_op jit(solution)/shard_map/ppermute | solution.py:668
  201.6 49.5 %all-to-all-start.2 = ((bf16[8,4,32,768]{3,2,1,0:T(8,128)(2,1)}), bf16[8,4,32,768]{3,2,1,0:T(8,128)(2,1)S(1)}, u32[]{:S(2)}, u32[]{:S(2)}) async-start(bf16[8,4,32,768]{3,2,1,0:T(8,128)(2,1)} %get-tuple-element.131), calls=%async_computation.2 | async-start | bytes 3145728 | tf_op jit(solution)/shard_map/all_to_all | solution.py:959
  206.2 133.9 %reduce-scatter.2.cloned.1.call-start = ((), (), s32[]{:S(2)}) async-start(), calls=%async_computation.6 | async-start | bytes 4866048 | tf_op jit(solution)/shard_map/reduce_scatter | solution.py:954
  211.2 21.7 %collective-permute-start.19 = (bf16[4,48,768]{2,1,0:T(8,128)(2,1)}, bf16[4,48,768]{2,1,0:T(8,128)(2,1)S(1)}, u32[]{:S(2)}, u32[]{:S(2)}) collective-permute-start(bf16[4,48,768]{2,1,0:T(8,128)(2,1)} %get-tuple-element.143), channel_id=1, source_target_pairs={{0,4},{4,0},{8,12},{12,8},{16,20},{20,16},{24,28},{28,24},{1,5},{5... | collective-permute-start | bytes 884744 | tf_op jit(solution)/shard_map/ppermute | solution.py:668
  213.2 19.7 %collective-permute-start.20 = (bf16[4,48,768]{2,1,0:T(8,128)(2,1)}, bf16[4,48,768]{2,1,0:T(8,128)(2,1)S(1)}, u32[]{:S(2)}, u32[]{:S(2)}) collective-permute-start(bf16[4,48,768]{2,1,0:T(8,128)(2,1)} %get-tuple-element.144), channel_id=1, source_target_pairs={{0,2},{1,3},{2,0},{3,1},{4,6},{5,7},{6,4},{7,5},{8,10},{9,11},{10,... | collective-permute-start | bytes 884744 | tf_op jit(solution)/shard_map/ppermute | solution.py:668
  251.1 10.1 %collective-permute-start.21 = (bf16[16,96,768]{2,1,0:T(8,128)(2,1)}, bf16[16,96,768]{2,1,0:T(8,128)(2,1)}, u32[]{:S(2)}, u32[]{:S(2)}) collective-permute-start(bf16[16,96,768]{2,1,0:T(8,128)(2,1)} %get-tuple-element.153), channel_id=1, source_target_pairs={{0,1},{1,0},{2,3},{3,2},{4,5},{5,4},{6,7},{7,6},{8,9},{9,8},{10,11... | collective-permute-start | bytes 7077896 | tf_op jit(solution)/shard_map/ppermute | solution.py:668
  265.9 21.9 %collective-permute-start.22 = (bf16[2,4,48,768]{3,2,1,0:T(8,128)(2,1)}, bf16[2,4,48,768]{3,2,1,0:T(8,128)(2,1)S(1)}, u32[]{:S(2)}, u32[]{:S(2)}) collective-permute-start(bf16[2,4,48,768]{3,2,1,0:T(8,128)(2,1)} %get-tuple-element.162), channel_id=1, source_target_pairs={{0,2},{1,3},{2,0},{3,1},{4,6},{5,7},{6,4},{7,5},{8,10},{9,11},{10,... | collective-permute-start | bytes 1769480 | tf_op jit(solution)/shard_map/ppermute | solution.py:668
  267.3 20.5 %collective-permute-start.23 = (bf16[2,4,48,768]{3,2,1,0:T(8,128)(2,1)}, bf16[2,4,48,768]{3,2,1,0:T(8,128)(2,1)S(1)}, u32[]{:S(2)}, u32[]{:S(2)}) collective-permute-start(bf16[2,4,48,768]{3,2,1,0:T(8,128)(2,1)} %get-tuple-element.164), channel_id=1, source_target_pairs={{0,4},{4,0},{8,12},{12,8},{16,20},{20,16},{24,28},{28,24},{1,5},{5... | collective-permute-start | bytes 1769480 | tf_op jit(solution)/shard_map/ppermute | solution.py:668
  267.6 35.8 %collective-permute-start.28 = (bf16[2,96,768]{2,1,0:T(8,128)(2,1)S(1)}, bf16[2,96,768]{2,1,0:T(8,128)(2,1)}, u32[]{:S(2)}, u32[]{:S(2)}) collective-permute-start(bf16[2,96,768]{2,1,0:T(8,128)(2,1)S(1)} %copy-done.30), channel_id=1, source_target_pairs={{0,8},{4,12},{8,0},{12,4},{16,24},{20,28},{24,16},{28,20},{1,9},{5... | collective-permute-start | bytes 884744 | tf_op jit(solution)/shard_map/ppermute | solution.py:668
  269.7 25.3 %copy-start.19 = (f32[8,768]{1,0:T(8,128)S(1)}, f32[8,768]{1,0:T(8,128)}, u32[]{:S(2)}) copy-start(f32[8,768]{1,0:T(8,128)} %get-tuple-element.181) | copy-start | bytes 73732
  269.7 25.8 %copy-start.18 = (f32[1,3072]{1,0:T(1,128)S(1)}, f32[1,3072]{1,0:T(1,128)}, u32[]{:S(2)}) copy-start(f32[1,3072]{1,0:T(1,128)} %get-tuple-element.182) | copy-start | bytes 36868
  269.7 28.0 %copy-start.21 = (f32[1,768]{1,0:T(1,128)S(1)}, f32[1,768]{1,0:T(1,128)}, u32[]{:S(2)}) copy-start(f32[1,768]{1,0:T(1,128)} %get-tuple-element.183) | copy-start | bytes 9220
  292.1 18.9 %collective-permute-start.24 = (bf16[4,48,768]{2,1,0:T(8,128)(2,1)}, bf16[4,48,768]{2,1,0:T(8,128)(2,1)S(1)}, u32[]{:S(2)}, u32[]{:S(2)}) collective-permute-start(bf16[4,48,768]{2,1,0:T(8,128)(2,1)} %get-tuple-element.168), channel_id=1, source_target_pairs={{0,4},{4,0},{8,12},{12,8},{16,20},{20,16},{24,28},{28,24},{1,5},{5... | collective-permute-start | bytes 884744 | tf_op jit(solution)/shard_map/ppermute | solution.py:668
  293.6 17.5 %collective-permute-start.25 = (bf16[4,48,768]{2,1,0:T(8,128)(2,1)}, bf16[4,48,768]{2,1,0:T(8,128)(2,1)S(1)}, u32[]{:S(2)}, u32[]{:S(2)}) collective-permute-start(bf16[4,48,768]{2,1,0:T(8,128)(2,1)} %get-tuple-element.170), channel_id=1, source_target_pairs={{0,2},{1,3},{2,0},{3,1},{4,6},{5,7},{6,4},{7,5},{8,10},{9,11},{10,... | collective-permute-start | bytes 884744 | tf_op jit(solution)/shard_map/ppermute | solution.py:668
  298.6 12.4 %all-to-all-start.3 = ((f32[32,3,96]{2,1,0:T(4,128)}), f32[32,3,96]{2,1,0:T(4,128)S(1)}, u32[]{:S(2)}, u32[]{:S(2)}) async-start(f32[32,3,96]{2,1,0:T(4,128)} %copy.64), calls=%async_computation.4 | async-start | bytes 131072 | tf_op jit(solution)/shard_map/all_to_all | solution.py:1022
  305.3 13.2 %collective-permute-start.29 = (bf16[96,768]{1,0:T(8,128)(2,1)}, bf16[96,768]{1,0:T(8,128)(2,1)S(1)}, u32[]{:S(2)}, u32[]{:S(2)}) collective-permute-start(bf16[96,768]{1,0:T(8,128)(2,1)} %get-tuple-element.178), channel_id=1, source_target_pairs={{0,16},{4,20},{8,24},{12,28},{16,0},{20,4},{24,8},{28,12},{1,17},{... | collective-permute-start | bytes 442376 | tf_op jit(solution)/shard_map/ppermute | solution.py:668
  311.1 7.4 %copy-start.14 = (bf16[96,768]{1,0:T(8,128)(2,1)S(1)}, bf16[96,768]{1,0:T(8,128)(2,1)}, u32[]{:S(2)}) copy-start(bf16[96,768]{1,0:T(8,128)(2,1)} %get-tuple-element.177) | copy-start | bytes 442372
  314.6 11.1 %collective-permute-start.26 = (bf16[2,96,768]{2,1,0:T(8,128)(2,1)}, bf16[2,96,768]{2,1,0:T(8,128)(2,1)S(1)}, u32[]{:S(2)}, u32[]{:S(2)}) collective-permute-start(bf16[2,96,768]{2,1,0:T(8,128)(2,1)} %get-tuple-element.172), channel_id=1, source_target_pairs={{0,8},{4,12},{8,0},{12,4},{16,24},{20,28},{24,16},{28,20},{1,9},{5... | collective-permute-start | bytes 884744 | tf_op jit(solution)/shard_map/ppermute | solution.py:668
  328.3 10.1 %collective-permute-start.27 = (bf16[96,768]{1,0:T(8,128)(2,1)}, bf16[96,768]{1,0:T(8,128)(2,1)S(1)}, u32[]{:S(2)}, u32[]{:S(2)}) collective-permute-start(bf16[96,768]{1,0:T(8,128)(2,1)} %get-tuple-element.174), channel_id=1, source_target_pairs={{0,16},{4,20},{8,24},{12,28},{16,0},{20,4},{24,8},{28,12},{1,17},{... | collective-permute-start | bytes 442376 | tf_op jit(solution)/shard_map/ppermute | solution.py:668
  344.8 10.8 %all-to-all-start.4 = ((f32[32,1,1]{2,1,0:T(1,128)}), f32[32,1,1]{2,1,0:T(1,128)S(1)}, u32[]{:S(2)}, u32[]{:S(2)}) async-start(f32[32,1,1]{2,1,0:T(1,128)} %broadcast_in_dim.22), calls=%async_computation.5 | async-start | bytes 32768 | tf_op jit(solution)/shard_map/all_to_all | solution.py:1027
  348.6 8.4 %copy-start.20 = (f32[3,96]{1,0:T(4,128)S(1)}, f32[3,96]{1,0:T(4,128)}, u32[]{:S(2)}) copy-start(f32[3,96]{1,0:T(4,128)} %param.25) | copy-start | bytes 3460
  348.6 8.4 %copy-start.22 = (f32[3,96]{1,0:T(4,128)S(1)}, f32[3,96]{1,0:T(4,128)}, u32[]{:S(2)}) copy-start(f32[3,96]{1,0:T(4,128)} %param.35) | copy-start | bytes 3460
  348.6 8.4 %copy-start.23 = (f32[3,96]{1,0:T(4,128)S(1)}, f32[3,96]{1,0:T(4,128)}, u32[]{:S(2)}) copy-start(f32[3,96]{1,0:T(4,128)} %param.30) | copy-start | bytes 3460
  348.6 9.0 %copy-start.8 = (f32[384,192]{0,1:T(8,128)S(1)}, f32[384,192]{0,1:T(8,128)}, u32[]{:S(2)}) copy-start(f32[384,192]{0,1:T(8,128)} %param.34) | copy-start | bytes 884740
  348.6 9.0 %copy-start.9 = (f32[384,192]{0,1:T(8,128)S(1)}, f32[384,192]{0,1:T(8,128)}, u32[]{:S(2)}) copy-start(f32[384,192]{0,1:T(8,128)} %param.29) | copy-start | bytes 884740
  (25 other events, 64.8 us)
Sparse Core Ops, SparseCore 0:
  11.5 73.5 all-gather.2
  212.5 124.5 reduce-scatter.1

commit v4 on v3

v4 whole, which is shorter than its diff:
```python
import functools
import math

import jax
import jax.numpy as jnp
from jax import lax
from jax.experimental import pallas as pl
from jax.experimental.pallas import tpu as pltpu
from jax.sharding import PartitionSpec as P

HD = 64
HEAD_GROUP = 6
STEP = 10
F32 = jnp.float32
BF16 = jnp.bfloat16
VMEM_BYTES = 66_900_000


def params_for(**more):
    return pltpu.CompilerParams(vmem_limit_bytes=VMEM_BYTES, **more)


def busy_for(micros):
    return pl.CostEstimate(flops=micros * 10**9, bytes_accessed=micros * 3 * 10**6, transcendentals=0)


def dot_nn(left, right):
    return lax.dot_general(left, right, (((1,), (0,)), ((), ())), preferred_element_type=F32)


def dot_nt(left, right):
    return lax.dot_general(left, right, (((1,), (1,)), ((), ())), preferred_element_type=F32)


def dot_tn(left, right):
    return lax.dot_general(left, right, (((0,), (0,)), ((), ())), preferred_element_type=F32)


def norm_parts(values):
    center = values - jnp.mean(values, axis=-1, keepdims=True)
    spread = jnp.mean(center * center, axis=-1, keepdims=True)
    factor = lax.rsqrt(spread + 1e-05)
    return center * factor, factor


def norm_back(grad, hat, factor, gain):
    scaled = grad * gain
    inner = jnp.mean(scaled * hat, axis=-1, keepdims=True)
    return factor * (scaled - jnp.mean(scaled, axis=-1, keepdims=True) - hat * inner)


def gelu_pair(gate):
    cdf = 0.5 + 0.5 * lax.erf(gate * 0.5**0.5)
    bell = jnp.exp2(gate * gate * (-0.5 * math.log2(math.e))) * (0.5 / math.pi) ** 0.5
    return gate * cdf, cdf + gate * bell


def load_grid(table, refs, me_ref, dest, sems, rows, first=0, start=True):
    copies = []
    for ref, places in zip(refs, table):
        for pos, (rel_d, rel_f, off, turned) in enumerate(places):
            d = rel_d ^ me_ref[0] if turned else rel_d
            f = rel_f ^ me_ref[1] if turned else rel_f
            height = min(ref.shape[1], rows)
            row = pl.multiple_of(d * rows + off, 16)
            copy = pltpu.make_async_copy(
                ref.at[pos, pl.ds(0, height)], dest.at[f, pl.ds(row, height)], sems.at[first + len(copies)]
            )
            if start:
                copy.start()
            copies.append(copy)
    return copies


def load_down(table, refs, me_ref, dest, sems, share, first=0, start=True):
    copies = []
    for ref, places in zip(refs, table):
        for pos, (rel_d, rel_f, off, turned) in enumerate(places):
            if share is None:
                pairs = [(ref.at[pos], dest)]
            else:
                half, wide = share
                d = rel_d ^ me_ref[0] if turned else rel_d
                f = rel_f ^ me_ref[1] if turned else rel_f
                lane = pl.multiple_of(d * wide, 128)
                pairs = []
                for k in range(2):
                    row = pl.multiple_of(f * (2 * half) + k * half + off, 16)
                    pairs.append(
                        (
                            ref.at[pos, pl.ds(ref.shape[1] - half, half), pl.ds(k * wide, wide)],
                            dest.at[pl.ds(row, half), pl.ds(lane, wide)],
                        )
                    )
            for src, dst in pairs:
                copy = pltpu.make_async_copy(src, dst, sems.at[first + len(copies)])
                if start:
                    copy.start()
                copies.append(copy)
    return copies


def any_specs(count):
    return [pl.BlockSpec(memory_space=pl.ANY)] * count


SMEM_SPEC = pl.BlockSpec(memory_space=pltpu.SMEM)


def full_spec(shape):
    return pl.BlockSpec(shape, lambda i: (0,) * len(shape))


def picked(places, length):
    lanes = places.shape[1]
    rows = lax.broadcasted_iota(jnp.int32, (length, lanes), 0)
    return (rows == places).astype(F32)


def seen_body(seen, cot_ref, places_ref, out_ref, sum_ref):
    count, length, _ = cot_ref.shape

    @pl.when(pl.program_id(0) == 0)
    def _():
        sum_ref[...] = jnp.zeros_like(sum_ref)

    for k in range(count):
        pick = picked(places_ref[k], length)
        gaps = 1.0 - jnp.sum(pick, axis=-1, keepdims=True)
        lane = lax.broadcasted_iota(jnp.int32, pick.shape, 1)
        rows = dot_tn(jnp.where(lane == seen, gaps, pick).astype(BF16), cot_ref[k])
        out_ref[k] = rows[:seen].astype(BF16)
        sum_ref[...] += rows[seen : seen + 1]


def seen_rows(cot, places, seen):
    chips, length, model = cot.shape
    step = 4
    return pl.pallas_call(
        functools.partial(seen_body, seen),
        grid=(chips // step,),
        in_specs=[
            pl.BlockSpec((step, length, model), lambda i: (i, 0, 0)),
            pl.BlockSpec((step, 1, places.shape[2]), lambda i: (i, 0, 0)),
        ],
        out_specs=[pl.BlockSpec((step, seen, model), lambda i: (i, 0, 0)), full_spec((1, model))],
        out_shape=[
            jax.ShapeDtypeStruct((chips, seen, model), BF16),
            jax.ShapeDtypeStruct((1, model), F32),
        ],
        compiler_params=params_for(),
        cost_estimate=busy_for(8),
        name="seen_rows",
    )(cot, places)


def attend_body(table, rows, heads, wide, *refs):
    n = len(table)
    me_ref, x_ref, vec_ref, bias_ref = refs[:4]
    w_refs = refs[4 : 4 + n]
    normed_ref, mixed_ref, expo_ref, share_ref, context_ref, qkv_out, out_out = refs[4 + n : 11 + n]
    qkv_ref, out_ref, weight, sems = refs[11 + n :]
    shares, model, cols = weight.shape
    slim = cols - wide
    step, last = pl.program_id(0), pl.num_programs(0) - 1
    count = sum(len(t) for t in table)
    saves = [
        pltpu.make_async_copy(qkv_ref, qkv_out, sems.at[count]),
        pltpu.make_async_copy(out_ref, out_out, sems.at[count + 1]),
    ]

    @pl.when(step == 0)
    def _():
        load_grid(table, w_refs, me_ref, weight, sems, rows)

    hat, _ = norm_parts(x_ref[0].astype(F32))
    normed = (hat * vec_ref[0:1, :] + vec_ref[1:2, :]).astype(BF16)
    normed_ref[...] = normed.T

    @pl.when(step == 0)
    def _():
        for copy in load_grid(table, w_refs, me_ref, weight, sems, rows, start=False):
            copy.wait()
        up_to = -(-wide // 128) * 128
        for f in range(shares):
            qkv_ref[f * wide : (f + 1) * wide, :] = weight[f, :, :up_to].T[:wide]
            out_ref[:, f * slim : (f + 1) * slim] = weight[f, :, wide:]
        for copy in saves:
            copy.start()

    for part in range(3):
        spot = slice(part * model, (part + 1) * model)
        mixed = dot_nt(qkv_ref[spot, :], normed)
        if part == 2:
            mixed = mixed + bias_ref[...]
        mixed_ref[spot, :] = mixed.astype(BF16)
    for first in range(0, heads, HEAD_GROUP):
        group = range(first, first + HEAD_GROUP)
        part = lambda which, head: mixed_ref[which * model + HD * head : which * model + HD * (head + 1), :]
        scores = [dot_tn(part(1, head), part(0, head) * jnp.asarray(HD ** (-0.5), BF16)) for head in group]
        expos = [jnp.exp(score - jnp.max(score, axis=0, keepdims=True)) for score in scores]
        shares = [1.0 / jnp.sum(expo, axis=0, keepdims=True) for expo in expos]
        expos = [expo.astype(BF16) for expo in expos]
        contexts = [dot_nn(part(2, head), expo) for head, expo in zip(group, expos)]
        for head, expo, share, context in zip(group, expos, shares, contexts):
            share_ref[head : head + 1, :] = share
            expo_ref[0, head] = expo
            context_ref[HD * head : HD * (head + 1), :] = (context * share).astype(BF16)

    @pl.when(step == last)
    def _():
        for copy in saves:
            copy.wait()


def attend_forward(me, x, vec, bias, table, arrays, rows, wide):
    chips, seq, model = x.shape
    heads = model // HD
    cols = arrays[0].shape[-1]
    shares = 3 * model // wide
    count = sum(len(t) for t in table)
    tall = lambda h: pl.BlockSpec((h, seq), lambda i: (0, i))
    tokens = chips * seq
    return pl.pallas_call(
        functools.partial(attend_body, table, rows, heads, wide),
        grid=(chips,),
        in_specs=[
            SMEM_SPEC,
            pl.BlockSpec((1, seq, model), lambda i: (i, 0, 0)),
            full_spec(vec.shape),
            full_spec(bias.shape),
        ]
        + any_specs(len(arrays)),
        out_specs=[
            tall(model),
            tall(3 * model),
            pl.BlockSpec((1, heads, seq, seq), lambda i: (i, 0, 0, 0)),
            tall(heads),
            tall(model),
        ]
        + any_specs(2),
        out_shape=[
            jax.ShapeDtypeStruct((model, tokens), BF16),
            jax.ShapeDtypeStruct((3 * model, tokens), BF16),
            jax.ShapeDtypeStruct((chips, heads, seq, seq), BF16),
            jax.ShapeDtypeStruct((heads, tokens), F32),
            jax.ShapeDtypeStruct((model, tokens), BF16),
            jax.ShapeDtypeStruct((3 * model, model), BF16),
            jax.ShapeDtypeStruct((model, model), BF16),
        ],
        scratch_shapes=[
            pltpu.VMEM((3 * model, model), BF16),
            pltpu.VMEM((model, model), BF16),
            pltpu.VMEM((shares, model, cols), BF16),
            pltpu.SemaphoreType.DMA((count + 2,)),
        ],
        compiler_params=params_for(),
        cost_estimate=busy_for(1),
        name="attend_forward",
    )(me, x, vec, bias, *arrays)


def feed_body(u_table, d_table, rows, share, *refs):
    nu, nd = len(u_table), len(d_table)
    me_ref, grad_ref, x_ref, context_ref, vec_ref, bias_ref, out_ref = refs[:7]
    u_refs = refs[7 : 7 + nu]
    d_refs = refs[7 + nu : 7 + nu + nd]
    (
        result_ref,
        normed_ref,
        active_ref,
        gate_grad_ref,
        feed_grad_ref,
        middle_grad_ref,
        branch_grad_ref,
        context_grad_ref,
        sums_ref,
        bias_sums_ref,
        up,
        down,
        sems,
    ) = refs[7 + nu + nd :]
    count = sum(len(t) for t in u_table)
    shares, model, span = up.shape
    seq = x_ref.shape[1]
    first_step = pl.program_id(0) == 0

    @pl.when(first_step)
    def _():
        load_grid(u_table, u_refs, me_ref, up, sems, rows)
        load_down(d_table, d_refs, me_ref, down, sems, share, first=count)
        sums_ref[...] = jnp.zeros_like(sums_ref)
        bias_sums_ref[...] = jnp.zeros_like(bias_sums_ref)

    feed_grad = grad_ref[:, 0].reshape(seq, model)
    feed_grad_ref[...] = feed_grad
    middle = x_ref[0].astype(F32) + dot_tn(context_ref[...], out_ref[...]) + vec_ref[3:4, :]
    hat, factor = norm_parts(middle)
    gain = vec_ref[4:5, :]
    normed = (hat * gain + vec_ref[5:6, :]).astype(BF16)
    normed_ref[...] = normed

    @pl.when(first_step)
    def _():
        copies = load_grid(u_table, u_refs, me_ref, up, sems, rows, start=False)
        copies += load_down(d_table, d_refs, me_ref, down, sems, share, first=count, start=False)
        for copy in copies:
            copy.wait()

    def fore(f):
        lanes = slice(f * span, (f + 1) * span)
        return dot_nn(normed, up[f]) + bias_ref[:, lanes], dot_nn(feed_grad, down[:, lanes])

    normed_grad = jnp.zeros((seq, model), F32)
    result = middle + vec_ref[10:11, :]
    ready = fore(0)
    for f in range(shares):
        lanes = slice(f * span, (f + 1) * span)
        gate, active_grad = ready
        if f + 1 < shares:
            ready = fore(f + 1)
        active, slope = gelu_pair(gate)
        active = active.astype(BF16)
        gate_grad = (active_grad * slope).astype(BF16)
        active_ref[:, lanes] = active
        gate_grad_ref[:, lanes] = gate_grad
        result += dot_nt(active, down[:, lanes])
        normed_grad += dot_nt(gate_grad, up[f])
        bias_sums_ref[:, lanes] += jnp.sum(gate_grad.astype(F32), axis=0, keepdims=True)
    result_ref[:, 0] = result.astype(BF16).reshape(result_ref.shape[0], -1, model)
    grad_full = feed_grad.astype(F32)
    middle_grad = grad_full + norm_back(normed_grad, hat, factor, gain)
    middle_grad_ref[0] = middle_grad
    branch_grad = middle_grad.astype(BF16)
    branch_grad_ref[...] = branch_grad
    context_grad_ref[...] = dot_nt(out_ref[...], branch_grad).astype(BF16)
    sums_ref[0:1, :] += jnp.sum(branch_grad.astype(F32), axis=0, keepdims=True)
    sums_ref[1:2, :] += jnp.sum(normed_grad * hat, axis=0, keepdims=True)
    sums_ref[2:3, :] += jnp.sum(normed_grad, axis=0, keepdims=True)
    sums_ref[3:4, :] += jnp.sum(grad_full, axis=0, keepdims=True)


def feed_forward_back(
    me, grad, x, context, vec, bias, out_whole, u_table, u_arrays, d_table, d_arrays, rows, share
):
    chips, seq, model = x.shape
    ff = bias.shape[1]
    blocks, _, seen, _ = grad.shape
    span = u_arrays[0].shape[-1]
    shares = ff // span
    tokens = chips * seq
    count = sum(len(t) for t in u_table) + 2 * sum(len(t) for t in d_table)
    tile = pl.BlockSpec((1, seq, model), lambda i: (i, 0, 0))
    flat = lambda w: pl.BlockSpec((seq, w), lambda i: (i, 0))
    tall = pl.BlockSpec((model, seq), lambda i: (0, i))
    spread = pl.BlockSpec((blocks, 1, seen, model), lambda i: (0, i, 0, 0))
    rows_of = lambda w: jax.ShapeDtypeStruct((tokens, w), BF16)
    return pl.pallas_call(
        functools.partial(feed_body, u_table, d_table, rows, share),
        grid=(chips,),
        in_specs=[
            SMEM_SPEC,
            spread,
            tile,
            tall,
            full_spec(vec.shape),
            full_spec(bias.shape),
            full_spec(out_whole.shape),
        ]
        + any_specs(len(u_arrays) + len(d_arrays)),
        out_specs=[
            spread,
            flat(model),
            flat(ff),
            flat(ff),
            flat(model),
            tile,
            flat(model),
            tall,
            full_spec((8, model)),
            full_spec((1, ff)),
        ],
        out_shape=[
            jax.ShapeDtypeStruct(grad.shape, BF16),
            rows_of(model),
            rows_of(ff),
            rows_of(ff),
            rows_of(model),
            jax.ShapeDtypeStruct((chips, seq, model), F32),
            rows_of(model),
            jax.ShapeDtypeStruct((model, tokens), BF16),
            jax.ShapeDtypeStruct((8, model), F32),
            jax.ShapeDtypeStruct((1, ff), F32),
        ],
        scratch_shapes=[
            pltpu.VMEM((shares, model, span), BF16),
            pltpu.VMEM((model, ff), BF16),
            pltpu.SemaphoreType.DMA((count,)),
        ],
        compiler_params=params_for(),
        cost_estimate=busy_for(10),
        name="feed_forward_back",
    )(me, grad, x, context, vec, bias, out_whole, *u_arrays, *d_arrays)


def attend_back_body(heads, mixed_ref, expo_ref, share_ref, grad_ref, mixed_grad_ref, sums_ref):
    model, seq = grad_ref.shape

    @pl.when(pl.program_id(0) == 0)
    def _():
        sums_ref[...] = jnp.zeros_like(sums_ref)

    scale = jnp.asarray(HD ** (-0.5), BF16)
    for first in range(0, heads, HEAD_GROUP):
        group = range(first, first + HEAD_GROUP)
        spot = lambda which, head: slice(which * model + HD * head, which * model + HD * (head + 1))
        shares = [share_ref[head : head + 1, :] for head in group]
        out_grads = [
            (grad_ref[spot(0, head), :].astype(F32) * share).astype(BF16) for head, share in zip(group, shares)
        ]
        prob_grads = [dot_tn(mixed_ref[spot(2, head), :], grad) for head, grad in zip(group, out_grads)]
        value_grads = [dot_nt(grad, expo_ref[0, head]) for head, grad in zip(group, out_grads)]
        score_grads = []
        for head, share, prob_grad in zip(group, shares, prob_grads):
            expo = expo_ref[0, head].astype(F32)
            weighted = expo * prob_grad
            inner = jnp.sum(weighted, axis=0, keepdims=True) * share
            score_grads.append((weighted - expo * inner).astype(BF16))
        query_grads = [dot_nn(mixed_ref[spot(1, head), :] * scale, grad) for head, grad in zip(group, score_grads)]
        key_grads = [dot_nt(mixed_ref[spot(0, head), :] * scale, grad) for head, grad in zip(group, score_grads)]
        for head, *grads in zip(group, query_grads, key_grads, value_grads):
            for which in range(3):
                mixed_grad_ref[spot(which, head), :] = grads[which].astype(BF16)
    sums_ref[...] += dot_nt(jnp.ones((8, seq), BF16), mixed_grad_ref[2 * model :, :])


def attend_back(mixed, expo, share, context_grad):
    model, tokens = context_grad.shape
    chips, heads, seq, _ = expo.shape
    tall = lambda h: pl.BlockSpec((h, seq), lambda i: (0, i))
    return pl.pallas_call(
        functools.partial(attend_back_body, heads),
        grid=(chips,),
        in_specs=[
            tall(3 * model),
            pl.BlockSpec((1, heads, seq, seq), lambda i: (i, 0, 0, 0)),
            tall(heads),
            tall(model),
        ],
        out_specs=[tall(3 * model), full_spec((8, model))],
        out_shape=[
            jax.ShapeDtypeStruct((3 * model, tokens), BF16),
            jax.ShapeDtypeStruct((8, model), F32),
        ],
        compiler_params=params_for(),
        cost_estimate=busy_for(30),
        name="attend_back",
    )(mixed, expo, share, context_grad)


def tokens_back_body(x_ref, grad_ref, mixed_grad_ref, vec_ref, qkv_ref, tokens_ref, sums_ref):
    @pl.when(pl.program_id(0) == 0)
    def _():
        sums_ref[...] = jnp.zeros_like(sums_ref)

    normed_grad = dot_tn(mixed_grad_ref[...], qkv_ref[...])
    hat, factor = norm_parts(x_ref[0].astype(F32))
    tokens_ref[0] = grad_ref[0] + norm_back(normed_grad, hat, factor, vec_ref[0:1, :])
    sums_ref[0:1, :] += jnp.sum(normed_grad * hat, axis=0, keepdims=True)
    sums_ref[1:2, :] += jnp.sum(normed_grad, axis=0, keepdims=True)


def tokens_back(x, middle_grad, mixed_grad, vec, qkv_whole):
    chips, seq, model = x.shape
    tile = pl.BlockSpec((1, seq, model), lambda i: (i, 0, 0))
    return pl.pallas_call(
        tokens_back_body,
        grid=(chips,),
        in_specs=[
            tile,
            tile,
            pl.BlockSpec((3 * model, seq), lambda i: (0, i)),
            full_spec(vec.shape),
            full_spec(qkv_whole.shape),
        ],
        out_specs=[tile, full_spec((8, model))],
        out_shape=[
            jax.ShapeDtypeStruct((chips, seq, model), F32),
            jax.ShapeDtypeStruct((8, model), F32),
        ],
        compiler_params=params_for(),
        cost_estimate=busy_for(40),
        name="tokens_back",
    )(x, middle_grad, mixed_grad, vec, qkv_whole)


def start_block(order, me_ref, d, f, sides, sem, source, *window):
    rel_d, rel_f = d ^ me_ref[0], f ^ me_ref[1]
    bits = [((rel_d if is_dp else rel_f) // value) % 2 for is_dp, value in order]
    pos = 0
    for bit in bits[1:]:
        pos = pos * 2 + bit
    for side, ref in enumerate(sides):

        @pl.when(bits[0] == side)
        def _():
            pltpu.make_async_copy(source, ref.at[(pos,) + window], sem).start()


def feed_grad_body(order, rows, half, wide, me_ref, normed_ref, gate_grad_ref, feed_grad_ref, active_ref, *refs):
    step = pl.program_id(0)
    if order is None:
        refs[0][0] = dot_tn(normed_ref[...], gate_grad_ref[...]).astype(BF16)
        refs[1][...] = dot_tn(feed_grad_ref[...], active_ref[...]).astype(BF16)
        return
    keep_ref, send_ref, up, down, sems = refs
    shares, model, span = up.shape
    count, fit = model // rows, span // wide
    sides = keep_ref, send_ref
    base = step * count * 2
    up[step] = dot_tn(normed_ref[...], gate_grad_ref[...]).astype(BF16)
    for d in range(count):
        source = up.at[step, pl.ds(d * rows, rows)]
        start_block(order, me_ref, d, step, sides, sems.at[step, d], source, pl.ds(0, rows))
    down[step] = dot_tn(feed_grad_ref[...], active_ref[...]).astype(BF16)
    sem = count
    for j in range(fit):
        for f in range(shares):
            for k in range(2):
                source = down.at[step, pl.ds((2 * f + k) * half, half), pl.ds(j * wide, wide)]
                window = pl.ds(rows, half), pl.ds(k * wide, wide)
                start_block(order, me_ref, step * fit + j, f, sides, sems.at[step, sem], source, *window)
                sem += 1

    @pl.when(step == shares - 1)
    def _():
        for s in range(shares):
            for d in range(count):
                pltpu.make_async_copy(
                    up.at[s, pl.ds(0, rows)], keep_ref.at[0, pl.ds(0, rows)], sems.at[s, d]
                ).wait()
            for k in range(count, sem):
                pltpu.make_async_copy(
                    down.at[s, pl.ds(0, half), pl.ds(0, wide)],
                    keep_ref.at[0, pl.ds(rows, half), pl.ds(0, wide)],
                    sems.at[s, k],
                ).wait()


def feed_grads(me, normed, gate_grad, feed_grad, active, order, rows, half, wide, shares):
    tokens, model = normed.shape
    ff = active.shape[1]
    span = ff // shares
    chunk = pl.BlockSpec((tokens, span), lambda i: (0, i))
    if order is None:
        out_specs = [
            pl.BlockSpec((1, model, span), lambda i: (i, 0, 0)),
            pl.BlockSpec((model, span), lambda i: (0, i)),
        ]
        shapes = [(shares, model, span), (model, ff)]
        scratch = []
    else:
        out_specs = any_specs(2)
        shapes = [(shares * model // rows // 2, rows + half, span)] * 2
        copies = model // rows + 2 * shares * (span // wide)
        scratch = [
            pltpu.VMEM((shares, model, span), BF16),
            pltpu.VMEM((shares, model, span), BF16),
            pltpu.SemaphoreType.DMA((shares, copies)),
        ]
    return pl.pallas_call(
        functools.partial(feed_grad_body, order, rows, half, wide),
        grid=(shares,),
        in_specs=[SMEM_SPEC, full_spec(normed.shape), chunk, full_spec(feed_grad.shape), chunk],
        out_specs=out_specs,
        out_shape=[jax.ShapeDtypeStruct(shape, BF16) for shape in shapes],
        scratch_shapes=scratch,
        compiler_params=params_for(),
        cost_estimate=busy_for(1),
        name="feed_grads",
    )(me, normed, gate_grad, feed_grad, active)


def qkv_grad_body(order, rows, me_ref, normed_ref, mixed_grad_ref, context_ref, branch_ref, *refs):
    f = pl.program_id(0)
    slots, packed = refs[-3:-1] if order is not None else refs[-2:]
    shares, model, slim = slots.shape
    wide = mixed_grad_ref.shape[0]

    @pl.when(f == 0)
    def _():
        whole = dot_nn(context_ref[...], branch_ref[...]).astype(BF16)
        for k in range(shares):
            slots[k] = whole[:, k * slim : (k + 1) * slim]

    packed[f, :, :wide] = dot_nt(normed_ref[...], mixed_grad_ref[...]).astype(BF16)
    packed[f, :, wide:] = slots[f]
    if order is None:
        refs[0][...] = packed[f]
        return
    sems = refs[-1]
    count = model // rows
    for d in range(count):
        source = packed.at[f, pl.ds(d * rows, rows)]
        start_block(order, me_ref, d, f, refs[:2], sems.at[f, d], source)

    @pl.when(f == shares - 1)
    def _():
        for s in range(shares):
            for d in range(count):
                pltpu.make_async_copy(packed.at[s, pl.ds(0, rows)], refs[0].at[0], sems.at[s, d]).wait()


def qkv_grads(me, normed, mixed_grad, context, branch_grad, order, rows, wide):
    model, tokens = normed.shape
    shares = 3 * model // wide
    slim = model // shares
    cols = wide + slim
    if order is None:
        out_specs = [pl.BlockSpec((model, cols), lambda i: (i, 0))]
        shapes = [(shares * model, cols)]
        sems = []
    else:
        out_specs = any_specs(2)
        shapes = [(shares * model // rows // 2, rows, cols)] * 2
        sems = [pltpu.SemaphoreType.DMA((shares, model // rows))]
    return pl.pallas_call(
        functools.partial(qkv_grad_body, order, rows),
        grid=(shares,),
        in_specs=[
            SMEM_SPEC,
            full_spec(normed.shape),
            pl.BlockSpec((wide, tokens), lambda i: (i, 0)),
            full_spec(context.shape),
            full_spec(branch_grad.shape),
        ],
        out_specs=out_specs,
        out_shape=[jax.ShapeDtypeStruct(shape, BF16) for shape in shapes],
        scratch_shapes=[pltpu.VMEM((shares, model, slim), BF16), pltpu.VMEM((shares, model, cols), BF16)] + sems,
        compiler_params=params_for(),
        cost_estimate=busy_for(30),
        name="qkv_grads",
    )(me, normed, mixed_grad, context, branch_grad)


DP, FSDP = "dp", "fsdp"


def swap(value, axis, bit):
    size = lax.axis_size(axis)
    return lax.ppermute(value, axis, [(i, i ^ bit) for i in range(size)])


def after(value, *others):
    return lax.optimization_barrier((value,) + others)[0]


def grow(value, step, *others):
    arrived = swap(value, *step)
    if others:
        arrived = after(arrived, *others)
    return jnp.concatenate([value, arrived], axis=0)


def fold_body(plan, count, *refs):
    sums = []
    for k in range(count):
        sums.append(refs[2 * k][...].astype(F32) + refs[2 * k + 1][...].astype(F32))
    for out_ref, takes in zip(refs[2 * count :], plan):
        start = 0
        for pair, spot in takes:
            part = sums[pair][spot].astype(out_ref.dtype)
            rows = part.shape[-2]
            out_ref[..., start : start + rows, :] = part
            start += rows


def fold_call(pairs, plan, in_blocks, out_blocks, out_shapes, steps, dtype=BF16):
    def spec(block, along):
        return pl.BlockSpec(block, lambda i: tuple(i if k == along else 0 for k in range(len(block))))

    arrays = [array for pair in pairs for array in pair]
    return pl.pallas_call(
        functools.partial(fold_body, plan, len(pairs)),
        grid=(steps,),
        in_specs=[spec(*in_blocks[k // 2]) for k in range(len(arrays))],
        out_specs=[spec(*b) for b in out_blocks],
        out_shape=[jax.ShapeDtypeStruct(shape, dtype) for shape in out_shapes],
        compiler_params=params_for(),
        cost_estimate=busy_for(2),
        name="fold_sums",
    )(*arrays)


class Fold:
    def __init__(self, keep, send):
        self.rows, self.cols = keep.shape[1:]
        self.keep, self.arrived = keep, swap(send, *CORE)
        self.stage = 0

    def step(self, *others):
        rows, cols = self.rows, self.cols
        cut, sizes = rows // 2, (2, 2, 4, rows, cols)
        upper, lower = slice(0, cut), slice(cut, rows)
        everything = slice(None)
        keep = after(self.keep, *others)
        if self.stage == 0:
            outs = fold_call(
                [(keep.reshape(sizes), self.arrived.reshape(sizes))],
                [
                    [(0, (0, everything, everything, upper))],
                    [(0, (1, everything, everything, upper))],
                    [(0, (everything, 0, everything, lower))],
                    [(0, (everything, 1, everything, lower))],
                ],
                [((2, 2, 1, rows, cols), 2)],
                [((2, 1, cut, cols), 1)] * 4,
                [(2, 4, cut, cols)] * 4,
                4,
            )
            self.keep, sent = (outs[0], outs[2]), (outs[1], outs[3])
            self.arrived = swap(sent[0], *XS), swap(sent[1], *YS)
        elif self.stage == 1:
            outs = fold_call(
                list(zip(keep, self.arrived)),
                [[(0, 0)], [(0, 1)], [(1, 0)], [(1, 1)]],
                [((2, 4, cut, cols), None)] * 2,
                [((4, cut, cols), None)] * 4,
                [(4, cut, cols)] * 4,
                1,
            )
            self.keep, sent = (outs[0], outs[2]), (outs[1], outs[3])
            self.arrived = swap(sent[0], *YS), swap(sent[1], *XS)
        elif self.stage == 2:
            near, far = slice(0, 2), slice(2, 4)
            self.keep, sent = fold_call(
                list(zip(keep, self.arrived)),
                [[(0, near), (1, near)], [(0, far), (1, far)]],
                [((4, cut, cols), None)] * 2,
                [((2, rows, cols), None)] * 2,
                [(2, rows, cols)] * 2,
                1,
            )
            self.arrived = swap(sent, *Z_NEAR)
        elif self.stage == 3:
            self.keep, sent = fold_call(
                [(keep, self.arrived)],
                [[(0, 0)], [(0, 1)]],
                [((2, rows, cols), None)],
                [((rows, cols), None)] * 2,
                [(rows, cols)] * 2,
                1,
            )
            self.arrived = swap(sent, *Z_FAR)
        else:
            return keep.astype(F32) + self.arrived.astype(F32)
        self.stage += 1
        return sent


def rel_table(steps, last, off):
    places = []
    for pos in range(2 ** len(steps)):
        rel = {DP: 0, FSDP: 0}
        for k, (axis, bit) in enumerate(steps):
            if (pos >> k) & 1:
                rel[axis] ^= bit
        if last is not None:
            rel[last[0]] ^= last[1]
        places.append((rel[DP], rel[FSDP], off, True))
    return tuple(places)


CORE, XS, YS, Z_NEAR, Z_FAR = (FSDP, 1), (FSDP, 2), (DP, 1), (DP, 2), (DP, 4)
XY = [Z_FAR, Z_NEAR, XS, YS]
YX = [Z_FAR, Z_NEAR, YS, XS]


def grow_end(value, second, *others):
    value = grow(value, second[0], *others)
    value = grow(value, second[1])
    return value, swap(value, *CORE)


def order_of(steps):
    return [(axis == DP, bit) for axis, bit in steps]


def adam_step(weight, gradient, first_mom, second, clip_factor, step_rate, decay_rate):
    scaled = gradient * clip_factor
    first_new = 0.5 * first_mom + 0.5 * scaled
    second_new = 0.5 * second + 0.5 * scaled * scaled
    correction = 1.0 - 0.5**STEP
    update = first_new / correction / (jnp.sqrt(second_new / correction) + 1e-08)
    return (first_new, second_new, weight - step_rate * (update + decay_rate * weight))


def on_device(
    tokens,
    visible_index,
    cotangent,
    qkv_weight,
    out_weight,
    up_weight,
    down_weight,
    vectors,
    qkv_first,
    out_first,
    up_first,
    down_first,
    vector_first,
    qkv_second,
    out_second,
    up_second,
    down_second,
    vector_second,
):
    _, chip_count, seq_len, model_width = tokens.shape
    dp_size, fsdp_size = lax.axis_size(DP), lax.axis_size(FSDP)
    device_count = dp_size * fsdp_size
    both = (DP, FSDP)
    block_count = dp_size
    block_seen = seq_len // block_count
    block_len = cotangent.shape[2]
    chips_group = chip_count * block_count
    rows, wide = qkv_weight.shape
    slim = out_weight.shape[1]
    span = up_weight.shape[1]
    ff_width = span * fsdp_size
    half = slim // 2
    tall = down_weight.shape[0]
    folded = (dp_size, fsdp_size) == (8, 4)

    share_q = jnp.concatenate([qkv_weight, out_weight], axis=1).astype(BF16)
    share_u = up_weight.astype(BF16)
    down_turned = down_weight.astype(BF16).T

    vec_rows, vec_cols = vectors.shape
    vector_copies = jnp.broadcast_to(vectors.astype(BF16), (device_count, vec_rows, vec_cols))
    vec_shares = lax.all_to_all(vector_copies, both, split_axis=0, concat_axis=0, tiled=True)
    vec = vec_shares.reshape(dp_size, fsdp_size, vec_rows, vec_cols).transpose(1, 2, 0, 3)
    vec = vec.reshape(fsdp_size * vec_rows, model_width).astype(F32)

    my_block = lax.axis_index(DP)
    places = visible_index[0].reshape(chips_group, block_count, block_seen)
    places = lax.dynamic_index_in_dim(places, my_block, 1, keepdims=False) - my_block * block_len
    seen_places = places
    cot = cotangent[0]
    whole_tiles = block_seen % 16 == 0
    if whole_tiles:
        places = jnp.pad(places, ((0, 0), (0, 128 - block_seen)), constant_values=-1)[:, None]
        cot_seen, mask_grad = seen_rows(cot, places, block_seen)
    else:
        slot_ids = lax.broadcasted_iota(jnp.int32, (chips_group, block_len, block_seen), 1)
        pick = (places[:, None, :] == slot_ids).astype(BF16)
        gaps = 1.0 - jnp.sum(pick.astype(F32), axis=-1)
        cot_seen = jnp.einsum("cpv,cpd->cvd", pick, cot, preferred_element_type=F32).astype(BF16)
        mask_grad = jnp.einsum("cp,cpd->d", gaps.astype(BF16), cot, preferred_element_type=F32)[None]
    if folded:
        me = jnp.stack([lax.axis_index(DP), lax.axis_index(FSDP)]).astype(jnp.int32)
        share_d = jnp.concatenate([down_turned[:half], down_turned[half:]], axis=1)
        cut = rows // 2
        cur = grow(grow(share_q[None], Z_FAR, cot_seen), Z_NEAR)
        q_upper, q_lower = grow(cur[:, :cut], XS, vec_shares), grow(cur[:, cut:], YS, vec_shares)
        q_upper, q_lower = grow(q_upper, YS), grow(q_lower, XS)
        q_arrays = (q_upper, swap(q_upper, *CORE), q_lower, swap(q_lower, *CORE))
        q_table = (
            rel_table(XY, None, 0),
            rel_table(XY, CORE, 0),
            rel_table(YX, None, cut),
            rel_table(YX, CORE, cut),
        )
        gathered = lax.all_gather(jnp.concatenate([share_u, share_d]), both, axis=0, tiled=False)
        u_arrays = d_arrays = (gathered,)
        u_table = d_table = (tuple((d, f, 0, False) for d in range(dp_size) for f in range(fsdp_size)),)
        order = order_of([CORE, XS, YS, Z_NEAR, Z_FAR])
        down_share = (half, tall)
        load_rows = rows
    else:
        me = jnp.zeros((2,), jnp.int32)

        def gather_whole(share):
            whole = lax.all_gather(share, both, axis=0, tiled=False)
            whole = whole.reshape((dp_size, fsdp_size) + share.shape).transpose(1, 0, 2, 3)
            return whole.reshape(fsdp_size, dp_size * share.shape[0], share.shape[1])

        q_arrays = (gather_whole(share_q),)
        u_arrays = (gather_whole(share_u),)
        down_whole = lax.all_gather(down_turned, both, axis=0, tiled=False)
        down_whole = down_whole.reshape(dp_size, fsdp_size, slim, tall).transpose(1, 2, 0, 3)
        d_arrays = (down_whole.reshape(1, model_width, ff_width),)
        q_table = u_table = (tuple((0, f, 0, False) for f in range(fsdp_size)),)
        d_table = (((0, 0, 0, False),),)
        order = None
        down_share = None
        load_rows = model_width

    cot_seen = cot_seen.reshape(block_count, chip_count, block_seen, model_width)
    grad = lax.all_to_all(cot_seen, DP, split_axis=0, concat_axis=0, tiled=True)
    if not whole_tiles:
        grad = grad.transpose(1, 0, 2, 3).reshape(1, chip_count, seq_len, model_width)

    x = tokens[0]
    up_bias = vec[6:10].reshape(1, ff_width)
    value_bias = vec[2].reshape(model_width, 1)
    normed, mixed, expo, share, context, qkv_whole, out_whole = attend_forward(
        me, x, vec, value_bias, q_table, q_arrays, load_rows, wide
    )
    if folded:
        context = after(context, grad)
    result, normed_two, active, gate_grad, feed_grad, middle_grad, branch_grad, context_grad, sums_two, up_sums = (
        feed_forward_back(
            me, grad, x, context, vec, up_bias, out_whole, u_table, u_arrays, d_table, d_arrays, load_rows, down_share
        )
    )
    feed_blocks = feed_grads(me, normed_two, gate_grad, feed_grad, active, order, rows, half, tall, fsdp_size)
    if folded:
        feed_fold = Fold(*feed_blocks)
        context_grad = after(context_grad, *feed_blocks)
    mixed_grad, sums_value = attend_back(mixed, expo, share, context_grad)
    if folded:
        normed = after(normed, feed_fold.step(mixed_grad))
    q_blocks = qkv_grads(me, normed, mixed_grad, context, branch_grad, order, rows, wide)
    if folded:
        result = after(result, *q_blocks)
    if not whole_tiles:
        result = result.reshape(chip_count, block_count, block_seen, model_width).transpose(1, 0, 2, 3)
    arrived = lax.all_to_all(result, DP, split_axis=0, concat_axis=0, tiled=True)
    arrived = arrived.reshape(chips_group, block_seen, model_width)
    if folded:
        q_fold = Fold(*q_blocks)
        x = after(x, *q_blocks)
    tokens_grad, sums_one = tokens_back(x, middle_grad, mixed_grad, vec, qkv_whole)

    slot_ids = lax.broadcasted_iota(jnp.int32, (chips_group, block_len, block_seen), 1)
    pick = (seen_places[:, None, :] == slot_ids).astype(BF16)
    gaps = 1.0 - jnp.sum(pick.astype(F32), axis=-1)
    filled = jnp.einsum("cpv,cvd->cpd", pick, arrived, preferred_element_type=F32)
    filled = filled + gaps[..., None] * vec[11]
    full_layout = filled.astype(BF16).reshape(1, chips_group, block_len, model_width)

    if folded:
        feed_fold.step(tokens_grad)
        q_fold.step(tokens_grad)
        feed_fold.step()
        q_fold.step(arrived)
        feed_fold.step()
        q_fold.step()
        feed_sum = feed_fold.step()
        u_sum, d_sum = feed_sum[:rows], feed_sum[rows:]
        q_fold.step()
        q_sum = q_fold.step()
        d_sum = jnp.concatenate([d_sum[:, :tall], d_sum[:, tall:]], axis=0).T
    else:

        def scatter_whole(whole):
            cols = whole.shape[2]
            pieces = whole.reshape(fsdp_size, dp_size, -1, cols).transpose(1, 0, 2, 3)
            pieces = pieces.reshape(-1, cols)
            return lax.psum_scatter(pieces, both, scatter_dimension=0, tiled=True).astype(F32)

        q_sum, u_sum = scatter_whole(q_blocks[0].reshape(fsdp_size, model_width, -1)), scatter_whole(feed_blocks[0])
        pieces = feed_blocks[1].reshape(fsdp_size, slim, dp_size, tall).transpose(2, 0, 1, 3)
        pieces = pieces.reshape(device_count * slim, tall)
        d_sum = lax.psum_scatter(pieces, both, scatter_dimension=0, tiled=True).astype(F32).T

    vector_grad = jnp.concatenate(
        [
            sums_one[:2],
            sums_value[:1],
            sums_two[:3],
            up_sums.reshape(-1, model_width),
            sums_two[3:4],
            mask_grad,
        ],
        axis=0,
    )
    parts = vector_grad.reshape(fsdp_size, vec_rows, dp_size, vec_cols).transpose(2, 0, 1, 3)
    parts = parts.reshape(device_count, vec_rows, vec_cols)
    parts = lax.all_to_all(parts, both, split_axis=0, concat_axis=0, tiled=True)
    shares = (q_sum[:, :wide], q_sum[:, wide:], u_sum, d_sum, jnp.sum(parts, axis=0))
    squares = jnp.sum(q_sum * q_sum) + jnp.sum(u_sum * u_sum) + jnp.sum(d_sum * d_sum)
    squares = squares + jnp.sum(shares[4] * shares[4])
    square_parts = jnp.broadcast_to(squares, (device_count, 1))
    grad_total = jnp.sum(lax.all_to_all(square_parts, both, split_axis=0, concat_axis=0, tiled=True))
    grad_norm = jnp.sqrt(grad_total)
    tokens_all = device_count * chip_count * seq_len
    threshold = 0.05 * model_width * math.sqrt(tokens_all)
    clip = jnp.minimum(1.0, threshold / grad_norm)
    rate = 0.6 / math.sqrt(model_width)
    out_rate = 0.6 / math.sqrt(model_width // 32)
    down_rate = 0.6 / math.sqrt(ff_width)
    qkv_out = adam_step(qkv_weight, shares[0], qkv_first, qkv_second, clip, rate, 0.05)
    out_out = adam_step(out_weight, shares[1], out_first, out_second, clip, out_rate, 0.05)
    up_out = adam_step(up_weight, shares[2], up_first, up_second, clip, rate, 0.05)
    down_out = adam_step(down_weight, shares[3], down_first, down_second, clip, down_rate, 0.05)
    vec_out = adam_step(vectors, shares[4], vector_first, vector_second, clip, 0.45, 0.0)
    return (
        full_layout,
        tokens_grad[None],
        *qkv_out,
        qkv_out[2].astype(BF16),
        *out_out,
        out_out[2].astype(BF16),
        *up_out,
        up_out[2].astype(BF16),
        *down_out,
        down_out[2].astype(BF16),
        *vec_out,
        grad_norm,
    )


def solution(mesh):
    grid = P("dp", "fsdp")
    table = P("fsdp", "dp")
    weights = (grid, grid, grid, grid, table)
    in_specs = (
        P("fsdp", "dp", None, None),
        P("fsdp", None, None),
        P("fsdp", None, "dp", None),
        *weights,
        *weights,
        *weights,
    )
    out_specs = (
        P("fsdp", None, "dp", None),
        P("fsdp", "dp", None, None),
        *(grid,) * 16,
        *(table,) * 3,
        P(),
    )
    return jax.shard_map(
        on_device, mesh=mesh, in_specs=in_specs, out_specs=out_specs, check_vma=False
    )
```

time: 372 us -> 343 us (0.922)
  Pallas kernels: 165 us -> 138 us
    pallas_call x6 -> x4, Pallas kernels: 94.2 us -> 75.1 us  [the longest x1 36.8 us: feed_forward_back(): pl.pallas_call(functools.partial(feed_body, u_table, d_table, rows, share...]
    pallas_call x1, Pallas kernels: 19.1 us -> 11.3 us  [attend_back(): pl.pallas_call(functools.partial(attend_back_body, heads), grid=(chips,),...]
    concatenate x11 -> x6, other arithmetic: 8.13 us -> 2.34 us  [grow(): return jnp.concatenate([value, arrived], axis=0)]
    ppermute x30 -> x22, waiting for transfers between devices: 79.1 us -> 84.5 us  [swap(): return lax.ppermute(value, axis, [(i, i ^ bit) for i in range(size)])]
    unnamed x76 -> x58, local copies, waits for them, and re-layouts: 8.8 us -> 3.76 us
    pallas_call x8, Pallas kernels: 22.3 us -> 26.4 us  [fold_call(): pl.pallas_call(functools.partial(fold_body, plan, len(pairs)), grid=(step...]
    ppermute x30 -> x22, starting transfers between devices: 28.4 us -> 26.9 us  [swap(): return lax.ppermute(value, axis, [(i, i ^ bit) for i in range(size)])]
  transfers between devices with their start and end apart: 37 -> 28, of which waited for: 15 -> 14; matrix products, arithmetic and copies ran while one was open for 8% -> 9% of each run, Pallas kernels for 43% -> 23%
where the time goes in v4:
time: 343 us; the launch traced here: 341 us
  Pallas kernels  138 us (40%)
  waiting for transfers between devices  89.5 us (26%)
  starting transfers between devices  51.4 us (15%)
  other arithmetic  20.1 us (6%)
  between operations  19.1 us (6%)
  local copies, waits for them, and re-layouts  16.2 us (5%)
  matrix products  6.26 us (2%)
    ppermute x22, waiting for transfers between devices, swap(): return lax.ppermute(value, axis, [(i, i ^ bit) for i in range(size)])  84.5 us
    pallas_call x1, Pallas kernels, feed_forward_back(): pl.pallas_call(functools.partial(feed_body, u_table, d_table, rows, share...  36.8 us
    ppermute x22, starting transfers between devices, swap(): return lax.ppermute(value, axis, [(i, i ^ bit) for i in range(size)])  26.9 us
    pallas_call x8, Pallas kernels, fold_call(): pl.pallas_call(functools.partial(fold_body, plan, len(pairs)), grid=(step...  26.4 us
    pallas_call x1, Pallas kernels, attend_forward(): pl.pallas_call(functools.partial(attend_body, table, rows, heads, wide),...  17.4 us
    pallas_call x1, Pallas kernels, feed_grads(): pl.pallas_call(functools.partial(feed_grad_body, order, rows, half, wide)...  16.6 us
    pallas_call x1, Pallas kernels, qkv_grads(): pl.pallas_call(functools.partial(qkv_grad_body, order, rows), grid=(share...  11.7 us
    pallas_call x1, Pallas kernels, attend_back(): pl.pallas_call(functools.partial(attend_back_body, heads), grid=(chips,),...  11.3 us
  transfers between devices with their start and end apart: 28, of which 14 were waited for; matrix products, arithmetic and copies ran while one was open for 9% of the time, Pallas kernels for 23%

profile of v4, /device:TPU:0, one launch (start us, length us, event | category | flops | bytes accessed | tf_op | source)
XLA Modules:
  0.0 340.9 jit_solution(2347554804660140874)
XLA Ops:
  11.5 4.0 %collective-permute-start = (bf16[1,96,768]{2,1,0:T(8,128)(2,1)}, bf16[1,96,768]{2,1,0:T(8,128)(2,1)}, u32[]{:S(2)}, u32[]{:S(2)}) collective-permute-start(bf16[1,96,768]{2,1,0:T(8,128)(2,1)} %pad_maximum_fusion.7), channel_id=1, source_target_pairs={{0,16},{4,20},{8,24},{12,28},{16,0},{20,4},{24,8},{28,12},{1,17},{... | collective-permute-start | bytes 442376 | tf_op jit(solution)/shard_map/ppermute | solution.py:651
  16.3 8.2 %seen_rows.1 = (bf16[32,32,768]{2,1,0:T(8,128)(2,1)}, f32[1,768]{1,0:T(1,128)}) custom-call(bf16[32,128,768]{2,1,0:T(8,128)(2,1)} %bitcast.56, s32[32,1,128]{2,1,0:T(1,128)} %bitcast.52), custom_call_target="tpu_custom_call" | custom-call | flops 8000000000 | bytes 24000000 | tf_op jit(solution)/shard_map/seen_rows/pallas_call | solution.py:139
  25.5 1.7 collective-permute-start.1
  28.5 3.1 all-to-all-start.1
  31.6 7.1 %collective-permute-done.1 = bf16[2,96,768]{2,1,0:T(8,128)(2,1)S(1)} collective-permute-done((bf16[2,96,768]{2,1,0:T(8,128)(2,1)S(1)}, bf16[2,96,768]{2,1,0:T(8,128)(2,1)S(1)}, u32[]{:S(2)}, u32[]{:S(2)}) %collective-permute-start.1) | collective-permute-done | bytes 294944 | tf_op jit(solution)/shard_map/ppermute | solution.py:651
  39.7 2.7 all-to-all-done.1
  43.0 4.3 %all-to-all-start = ((bf16[8,4,32,768]{3,2,1,0:T(8,128)(2,1)}), bf16[8,4,32,768]{3,2,1,0:T(8,128)(2,1)}, u32[]{:S(2)}, u32[]{:S(2)}) async-start(bf16[8,4,32,768]{3,2,1,0:T(8,128)(2,1)} %bitcast.5), calls=%async_computation | async-start | bytes 3145728 | tf_op jit(solution)/shard_map/all_to_all | solution.py:899
  47.4 2.0 collective-permute-start.5
  49.9 17.1 %collective-permute-done.5 = bf16[4,48,768]{2,1,0:T(8,128)(2,1)S(1)} collective-permute-done((bf16[4,48,768]{2,1,0:T(8,128)(2,1)S(1)}, bf16[4,48,768]{2,1,0:T(8,128)(2,1)S(1)}, u32[]{:S(2)}, u32[]{:S(2)}) %collective-permute-start.5) | collective-permute-done | bytes 294944 | tf_op jit(solution)/shard_map/ppermute | solution.py:651
  68.3 2.6 collective-permute-start.3
  70.9 10.3 %collective-permute-done.6 = bf16[8,48,768]{2,1,0:T(8,128)(2,1)S(1)} collective-permute-done((bf16[8,48,768]{2,1,0:T(8,128)(2,1)S(1)}, bf16[8,48,768]{2,1,0:T(8,128)(2,1)S(1)}, u32[]{:S(2)}, u32[]{:S(2)}) %collective-permute-start.6) | collective-permute-done | bytes 589856 | tf_op jit(solution)/shard_map/ppermute | solution.py:651
  81.4 14.5 %collective-permute-done.3 = bf16[8,48,768]{2,1,0:T(8,128)(2,1)S(1)} collective-permute-done((bf16[8,48,768]{2,1,0:T(8,128)(2,1)S(1)}, bf16[8,48,768]{2,1,0:T(8,128)(2,1)S(1)}, u32[]{:S(2)}, u32[]{:S(2)}) %collective-permute-start.3) | collective-permute-done | bytes 589856 | tf_op jit(solution)/shard_map/ppermute | solution.py:651
  98.2 1.5 reshape.134.refs_2_.refs_4_.vec_ref
  99.7 1.9 slice_bitcast_fusion.1
  101.6 1.6 copy.62.refs_3_
  105.7 17.4 %attend_forward.1 = (bf16[768,1024]{1,0:T(8,128)(2,1)}, bf16[2304,1024]{1,0:T(8,128)(2,1)}, bf16[4,12,256,256]{3,2,1,0:T(8,128)(2,1)}, f32[12,1024]{1,0:T(8,128)...) custom-call(s32[2]{0:T(128)} %pad_add_fusion.refs_0_.me_ref, ...), custom_call_target="tpu_custom_call" | custom-call | flops 1000000000 | bytes 3000000 | tf_op jit(solution)/shard_map/attend_forward/pallas_call | solution.py:224
  123.2 36.8 %feed_forward_back.1 = (bf16[8,4,32,768]{3,2,1,0:T(8,128)(2,1)}, bf16[1024,768]{1,0:T(8,128)(2,1)}, bf16[1024,3072]{1,0:T(8,128)(2,1)}, bf16[1024,3072]{1,0:T(8,...) custom-call(s32[2]{0:T(128)} %pad_add_fusion.refs_0_.me_ref, ...), custom_call_target="tpu_custom_call" | custom-call | flops 10000000000 | bytes 30000000 | tf_op jit(solution)/shard_map/feed_forward_back/pallas_call | solution.py:358
  159.9 16.6 %feed_grads.1 = (bf16[16,192,768]{2,1,0:T(8,128)(2,1)}, bf16[16,192,768]{2,1,0:T(8,128)(2,1)}) custom-call(s32[2]{0:T(128)} %pad_add_fusion.refs_0_.me_ref, bf16[1024,768]{1,0:T(8,128)(2,1)} %get-tuple-element.100.normed_ref, bf16[1024,3072]{1,0:T(8,128)(2,1)} %get-tuple-element.101.gate_grad_ref, bf16[1024,768]{1,0:T(8,128)(2,1)} %get-tuple-element.102.feed_grad_ref, ...), custom_call_target="tpu_custom_call" | custom-call | flops 1000000000 | bytes 3000000 | tf_op jit(solution)/shard_map/feed_grads/pallas_call | solution.py:571
  176.9 11.3 %attend_back.1 = (bf16[2304,1024]{1,0:T(8,128)(2,1)}, f32[8,768]{1,0:T(8,128)}) custom-call(bf16[2304,1024]{1,0:T(8,128)(2,1)} %get-tuple-element.105.mixed_ref, bf16[4,12,256,256]{3,2,1,0:T(8,128)(2,1)} %get-tuple-element.106.expo_ref, f32[12,1024]{1,0:T(8,128)} %get-tuple-element.107.share_ref, bf16[768,1024]{1,0:T(8,128)(2,1)} %get-tuple-element.110.grad_ref), custom_call_target="tpu_custom_call" | custom-call | flops 30000001024 | bytes 90000000 | tf_op jit(solution)/shard_map/attend_back/pallas_call | solution.py:441
  188.2 6.5 %fold_sums.8 = (bf16[2,4,96,768]{3,2,1,0:T(8,128)(2,1)}, bf16[2,4,96,768]{3,2,1,0:T(8,128)(2,1)}, bf16[2,4,96,768]{3,2,1,0:T(8,128)(2,1)}, bf16[2,4,96,768]{3,2,1,0:T(8,128)(2,1)}) custom-call(bf16[2,2,4,192,768]{4,3,2,1,0:T(8,128)(2,1)} %bitcast.44, bf16[2,2,4,192,768]{4,3,2,1,0:T(8,128)(2,1)} %bitcast.15.refs_1_), custom_call_target="tpu_custom_call" | custom-call | flops 2000000000 | bytes 6000000 | tf_op jit(solution)/shard_map/fold_sums/pallas_call | solution.py:683
  195.9 11.7 %qkv_grads.1 = (bf16[16,96,768]{2,1,0:T(8,128)(2,1)}, bf16[16,96,768]{2,1,0:T(8,128)(2,1)}) custom-call(s32[2]{0:T(128)} %pad_add_fusion.refs_0_.me_ref, bf16[768,1024]{1,0:T(8,128)(2,1)} %get-tuple-element.115.normed_ref, bf16[2304,1024]{1,0:T(8,128)(2,1)} %get-tuple-element.111.mixed_grad_ref, bf16[768,1024]{1,0:T(8,128)(2,1)} %get-tuple-element.96.refs_3_.context_ref, ...), custom_call_target="tpu_custom_call" | custom-call | flops 30000001024 | bytes 90000000 | tf_op jit(solution)/shard_map/qkv_grads/pallas_call | solution.py:627
  207.7 6.6 %all-to-all-start.2 = ((bf16[8,4,32,768]{3,2,1,0:T(8,128)(2,1)}), bf16[8,4,32,768]{3,2,1,0:T(8,128)(2,1)}, u32[]{:S(2)}, u32[]{:S(2)}) async-start(bf16[8,4,32,768]{3,2,1,0:T(8,128)(2,1)} %get-tuple-element.119), calls=%async_computation.2 | async-start | bytes 3145728 | tf_op jit(solution)/shard_map/all_to_all | solution.py:928
  214.3 10.1 %tokens_back.1 = (f32[4,256,768]{2,1,0:T(8,128)}, f32[8,768]{1,0:T(8,128)}) custom-call(bf16[4,256,768]{2,1,0:T(8,128)(2,1)} %bitcast.47, f32[4,256,768]{2,1,0:T(8,128)} %get-tuple-element.121.grad_ref, bf16[2304,1024]{1,0:T(8,128)(2,1)} %get-tuple-element.111.mixed_grad_ref, f32[12,768]{1,0:T(8,128)} %reshape.134.refs_2_.refs_4_.vec_ref, ...), custom_call_target="tpu_custom_call" | custom-call | flops 40000000000 | bytes 120000000 | tf_op jit(solution)/shard_map/tokens_back/pallas_call | solution.py:476
  224.4 7.3 %collective-permute-done.17.refs_3_ = bf16[2,4,96,768]{3,2,1,0:T(8,128)(2,1)} collective-permute-done((bf16[2,4,96,768]{3,2,1,0:T(8,128)(2,1)}, bf16[2,4,96,768]{3,2,1,0:T(8,128)(2,1)}, u32[]{:S(2)}, u32[]{:S(2)}) %collective-permute-start.17) | collective-permute-done | bytes 1179680 | tf_op jit(solution)/shard_map/ppermute | solution.py:651
  231.8 3.9 %fold_sums.13 = (bf16[4,96,768]{2,1,0:T(8,128)(2,1)}, bf16[4,96,768]{2,1,0:T(8,128)(2,1)}, bf16[4,96,768]{2,1,0:T(8,128)(2,1)}, bf16[4,96,768]{2,1,0:T(8,128)(2,1)}) custom-call(bf16[2,4,96,768]{3,2,1,0:T(8,128)(2,1)} %get-tuple-element.143.refs_0_, bf16[2,4,96,768]{3,2,1,0:T(8,128)(2,1)} %collective-permute-done.16.refs_1_, ...), custom_call_target="tpu_custom_call" | custom-call | flops 2000000000 | bytes 6000000 | tf_op jit(solution)/shard_map/fold_sums/pallas_call | solution.py:683
  235.7 2.8 collective-permute-start.18
  239.0 4.5 %fold_sums.9 = (bf16[2,4,48,768]{3,2,1,0:T(8,128)(2,1)}, bf16[2,4,48,768]{3,2,1,0:T(8,128)(2,1)}, bf16[2,4,48,768]{3,2,1,0:T(8,128)(2,1)}, bf16[2,4,48,768]{3,2,1,0:T(8,128)(2,1)}) custom-call(bf16[2,2,4,96,768]{4,3,2,1,0:T(8,128)(2,1)} %bitcast.58, bf16[2,2,4,96,768]{4,3,2,1,0:T(8,128)(2,1)} %bitcast.20.refs_1_), custom_call_target="tpu_custom_call" | custom-call | flops 2000000000 | bytes 6000000 | tf_op jit(solution)/shard_map/fold_sums/pallas_call | solution.py:683
  243.5 1.5 collective-permute-start.10
  245.0 10.6 %collective-permute-done.18.refs_1_ = bf16[4,96,768]{2,1,0:T(8,128)(2,1)} collective-permute-done((bf16[4,96,768]{2,1,0:T(8,128)(2,1)}, bf16[4,96,768]{2,1,0:T(8,128)(2,1)}, u32[]{:S(2)}, u32[]{:S(2)}) %collective-permute-start.18) | collective-permute-done | bytes 589856 | tf_op jit(solution)/shard_map/ppermute | solution.py:651
  255.7 2.8 fold_sums.14
  258.4 1.6 collective-permute-start.20
  263.9 5.6 %all-to-all-start.3 = ((f32[32,3,96]{2,1,0:T(4,128)}), f32[32,3,96]{2,1,0:T(4,128)S(1)}, u32[]{:S(2)}, u32[]{:S(2)}) async-start(f32[32,3,96]{2,1,0:T(4,128)} %copy.64), calls=%async_computation.3 | async-start | bytes 131072 | tf_op jit(solution)/shard_map/all_to_all | solution.py:980
  269.5 2.7 fold_sums.10
  272.2 1.6 collective-permute-start.12
  275.2 1.6 all-to-all-done.3
  276.9 2.1 fold_sums.15
  279.8 1.9 collective-permute-done.12.refs_1_
  282.9 2.1 fold_sums.11
  285.0 1.5 collective-permute-start.14
  287.1 7.9 %collective-permute-done.21 = bf16[192,768]{1,0:T(8,128)(2,1)} collective-permute-done((bf16[192,768]{1,0:T(8,128)(2,1)}, bf16[192,768]{1,0:T(8,128)(2,1)}, u32[]{:S(2)}, u32[]{:S(2)}) %collective-permute-start.21) | collective-permute-done | bytes 294944 | tf_op jit(solution)/shard_map/ppermute | solution.py:651
  295.0 1.9 convert_add_fusion
  296.9 2.5 collective-permute-done.14.refs_1_
  299.4 1.8 fold_sums.12
  304.3 1.6 multiply_reduce_fusion.1
  306.0 4.1 %collective-permute-done.15 = bf16[96,768]{1,0:T(8,128)(2,1)S(1)} collective-permute-done((bf16[96,768]{1,0:T(8,128)(2,1)}, bf16[96,768]{1,0:T(8,128)(2,1)S(1)}, u32[]{:S(2)}, u32[]{:S(2)}) %collective-permute-start.15) | collective-permute-done | bytes 147488 | tf_op jit(solution)/shard_map/ppermute | solution.py:651
  310.0 1.6 convert_add_fusion.1
  314.8 4.7 %all-to-all-start.4 = ((f32[32,1,1]{2,1,0:T(1,128)}), f32[32,1,1]{2,1,0:T(1,128)S(1)}, u32[]{:S(2)}, u32[]{:S(2)}) async-start(f32[32,1,1]{2,1,0:T(1,128)} %broadcast_in_dim.18), calls=%async_computation.4 | async-start | bytes 32768 | tf_op jit(solution)/shard_map/all_to_all | solution.py:985
  319.7 6.3 %fusion = bf16[1,32,128,768]{3,2,1,0:T(8,128)(2,1)} fusion(f32[768]{0:T(1024)S(1)} %copy-done.21, f32[32,128]{1,0:T(8,128)S(1)} %broadcast_subtract_fusion, bf16[32,32,768]{2,1,0:T(8,128)(2,1)} %bitcast.16, s32[32,32]{1,0:T(8,128)S(1)} %subtract_bitcast_fusion), kind=kOutput, calls=%fused_computation.1 | convolution fusion | flops 210894848 | bytes 7887872 | tf_op jit(solution)/shard_map/cpv,cvd->cpd/dot_general | solution.py:938
  (137 shorter events, 35.7 us)
Async XLA Ops:
  7.2 2.9 copy-start.9
  7.2 3.0 copy-start.6
  7.2 8.4 %copy-start.20 = (s32[1,32,256]{2,1,0:T(8,128)S(1)}, s32[1,32,256]{2,1,0:T(8,128)}, u32[]{:S(2)}) copy-start(s32[1,32,256]{2,1,0:T(8,128)} %param.19) | copy-start | bytes 98308
  7.2 115.9 %all-gather.3.cloned.1.call-start = ((), (), s32[]{:S(2)}) async-start(), calls=%async_computation.5 | async-start | bytes 9732096 | tf_op jit(solution)/shard_map/all_gather | solution.py:873
  11.5 13.0 %collective-permute-start = (bf16[1,96,768]{2,1,0:T(8,128)(2,1)}, bf16[1,96,768]{2,1,0:T(8,128)(2,1)}, u32[]{:S(2)}, u32[]{:S(2)}) collective-permute-start(bf16[1,96,768]{2,1,0:T(8,128)(2,1)} %pad_maximum_fusion.7), channel_id=1, source_target_pairs={{0,16},{4,20},{8,24},{12,28},{16,0},{20,4},{24,8},{28,12},{1,17},{... | collective-permute-start | bytes 442376 | tf_op jit(solution)/shard_map/ppermute | solution.py:651
  25.5 13.2 %collective-permute-start.1 = (bf16[2,96,768]{2,1,0:T(8,128)(2,1)S(1)}, bf16[2,96,768]{2,1,0:T(8,128)(2,1)S(1)}, u32[]{:S(2)}, u32[]{:S(2)}) collective-permute-start(bf16[2,96,768]{2,1,0:T(8,128)(2,1)S(1)} %pad_maximum_fusion.5), channel_id=1, source_target_pairs={{0,8},{4,12},{8,0},{12,4},{16,24},{20,28},{24,16},{28,20},{1,9},{5... | collective-permute-start | bytes 884744 | tf_op jit(solution)/shard_map/ppermute | solution.py:651
  28.5 13.9 %all-to-all-start.1 = ((bf16[32,3,96]{2,1,0:T(4,128)(2,1)}), bf16[32,3,96]{2,1,0:T(4,128)(2,1)S(1)}, u32[]{:S(2)}, u32[]{:S(2)}) async-start(bf16[32,3,96]{2,1,0:T(4,128)(2,1)} %broadcast_in_dim.16), calls=%async_computation.1 | async-start | bytes 65536 | tf_op jit(solution)/shard_map/all_to_all | solution.py:840
  43.0 80.1 %all-to-all-start = ((bf16[8,4,32,768]{3,2,1,0:T(8,128)(2,1)}), bf16[8,4,32,768]{3,2,1,0:T(8,128)(2,1)}, u32[]{:S(2)}, u32[]{:S(2)}) async-start(bf16[8,4,32,768]{3,2,1,0:T(8,128)(2,1)} %bitcast.5), calls=%async_computation | async-start | bytes 3145728 | tf_op jit(solution)/shard_map/all_to_all | solution.py:899
  47.4 19.5 %collective-permute-start.5 = (bf16[4,48,768]{2,1,0:T(8,128)(2,1)S(1)}, bf16[4,48,768]{2,1,0:T(8,128)(2,1)S(1)}, u32[]{:S(2)}, u32[]{:S(2)}) collective-permute-start(bf16[4,48,768]{2,1,0:T(8,128)(2,1)S(1)} %get-tuple-element.181), channel_id=1, source_target_pairs={{0,4},{4,0},{8,12},{12,8},{16,20},{20,16},{24,28},{28,24},{1,5},{5... | collective-permute-start | bytes 884744 | tf_op jit(solution)/shard_map/ppermute | solution.py:651
  49.4 18.8 %collective-permute-start.2 = (bf16[4,48,768]{2,1,0:T(8,128)(2,1)S(1)}, bf16[4,48,768]{2,1,0:T(8,128)(2,1)S(1)}, u32[]{:S(2)}, u32[]{:S(2)}) collective-permute-start(bf16[4,48,768]{2,1,0:T(8,128)(2,1)S(1)} %get-tuple-element.182), channel_id=1, source_target_pairs={{0,2},{1,3},{2,0},{3,1},{4,6},{5,7},{6,4},{7,5},{8,10},{9,11},{10,... | collective-permute-start | bytes 884744 | tf_op jit(solution)/shard_map/ppermute | solution.py:651
  67.0 14.2 %collective-permute-start.6 = (bf16[8,48,768]{2,1,0:T(8,128)(2,1)S(1)}, bf16[8,48,768]{2,1,0:T(8,128)(2,1)S(1)}, u32[]{:S(2)}, u32[]{:S(2)}) collective-permute-start(bf16[8,48,768]{2,1,0:T(8,128)(2,1)S(1)} %pad_maximum_fusion.4), channel_id=1, source_target_pairs={{0,2},{1,3},{2,0},{3,1},{4,6},{5,7},{6,4},{7,5},{8,10},{9,11},{10,... | collective-permute-start | bytes 1769480 | tf_op jit(solution)/shard_map/ppermute | solution.py:651
  68.3 27.6 %collective-permute-start.3 = (bf16[8,48,768]{2,1,0:T(8,128)(2,1)S(1)}, bf16[8,48,768]{2,1,0:T(8,128)(2,1)S(1)}, u32[]{:S(2)}, u32[]{:S(2)}) collective-permute-start(bf16[8,48,768]{2,1,0:T(8,128)(2,1)S(1)} %pad_maximum_fusion.3), channel_id=1, source_target_pairs={{0,4},{4,0},{8,12},{12,8},{16,20},{20,16},{24,28},{28,24},{1,5},{5... | collective-permute-start | bytes 1769480 | tf_op jit(solution)/shard_map/ppermute | solution.py:651
  81.3 23.4 %copy-start = (bf16[16,48,768]{2,1,0:T(8,128)(2,1)}, bf16[16,48,768]{2,1,0:T(8,128)(2,1)S(1)}, u32[]{:S(2)}) copy-start(bf16[16,48,768]{2,1,0:T(8,128)(2,1)S(1)} %pad_maximum_fusion.1.refs_6_) | copy-start | bytes 3538948
  81.3 23.4 %collective-permute-start.7 = (bf16[16,48,768]{2,1,0:T(8,128)(2,1)S(1)}, bf16[16,48,768]{2,1,0:T(8,128)(2,1)S(1)}, u32[]{:S(2)}, u32[]{:S(2)}) collective-permute-start(bf16[16,48,768]{2,1,0:T(8,128)(2,1)S(1)} %pad_maximum_fusion.1.refs_6_), channel_id=1, source_target_pairs={{0,1},{1,0},{2,3},{3,2},{4,5},{5,4},{6,7},{7,6},{8,9},{9,8},{10,11... | collective-permute-start | bytes 3538952 | tf_op jit(solution)/shard_map/ppermute | solution.py:651
  96.0 8.7 %copy-start.1 = (bf16[16,48,768]{2,1,0:T(8,128)(2,1)}, bf16[16,48,768]{2,1,0:T(8,128)(2,1)S(1)}, u32[]{:S(2)}) copy-start(bf16[16,48,768]{2,1,0:T(8,128)(2,1)S(1)} %pad_maximum_fusion.refs_4_) | copy-start | bytes 3538948
  96.0 8.7 %collective-permute-start.4 = (bf16[16,48,768]{2,1,0:T(8,128)(2,1)S(1)}, bf16[16,48,768]{2,1,0:T(8,128)(2,1)}, u32[]{:S(2)}, u32[]{:S(2)}) collective-permute-start(bf16[16,48,768]{2,1,0:T(8,128)(2,1)S(1)} %pad_maximum_fusion.refs_4_), channel_id=1, source_target_pairs={{0,1},{1,0},{2,3},{3,2},{4,5},{5,4},{6,7},{7,6},{8,9},{9,8},{10,11... | collective-permute-start | bytes 3538952 | tf_op jit(solution)/shard_map/ppermute | solution.py:651
  176.5 11.7 %collective-permute-start.8 = (bf16[16,192,768]{2,1,0:T(8,128)(2,1)}, bf16[16,192,768]{2,1,0:T(8,128)(2,1)}, u32[]{:S(2)}, u32[]{:S(2)}) collective-permute-start(bf16[16,192,768]{2,1,0:T(8,128)(2,1)} %get-tuple-element.109), channel_id=1, source_target_pairs={{0,1},{1,0},{2,3},{3,2},{4,5},{5,4},{6,7},{7,6},{8,9},{9,8},{10,11... | collective-permute-start | bytes 14155784 | tf_op jit(solution)/shard_map/ppermute | solution.py:651
  194.8 29.7 %collective-permute-start.16 = (bf16[2,4,96,768]{3,2,1,0:T(8,128)(2,1)}, bf16[2,4,96,768]{3,2,1,0:T(8,128)(2,1)}, u32[]{:S(2)}, u32[]{:S(2)}) collective-permute-start(bf16[2,4,96,768]{3,2,1,0:T(8,128)(2,1)} %get-tuple-element.113), channel_id=1, source_target_pairs={{0,2},{1,3},{2,0},{3,1},{4,6},{5,7},{6,4},{7,5},{8,10},{9,11},{10,... | collective-permute-start | bytes 3538952 | tf_op jit(solution)/shard_map/ppermute | solution.py:651
  195.9 35.8 %collective-permute-start.17 = (bf16[2,4,96,768]{3,2,1,0:T(8,128)(2,1)}, bf16[2,4,96,768]{3,2,1,0:T(8,128)(2,1)}, u32[]{:S(2)}, u32[]{:S(2)}) collective-permute-start(bf16[2,4,96,768]{3,2,1,0:T(8,128)(2,1)} %get-tuple-element.114), channel_id=1, source_target_pairs={{0,4},{4,0},{8,12},{12,8},{16,20},{20,16},{24,28},{28,24},{1,5},{5... | collective-permute-start | bytes 3538952 | tf_op jit(solution)/shard_map/ppermute | solution.py:651
  207.6 31.4 %collective-permute-start.9 = (bf16[16,96,768]{2,1,0:T(8,128)(2,1)}, bf16[16,96,768]{2,1,0:T(8,128)(2,1)}, u32[]{:S(2)}, u32[]{:S(2)}) collective-permute-start(bf16[16,96,768]{2,1,0:T(8,128)(2,1)} %get-tuple-element.118), channel_id=1, source_target_pairs={{0,1},{1,0},{2,3},{3,2},{4,5},{5,4},{6,7},{7,6},{8,9},{9,8},{10,11... | collective-permute-start | bytes 7077896 | tf_op jit(solution)/shard_map/ppermute | solution.py:651
  207.7 56.2 %all-to-all-start.2 = ((bf16[8,4,32,768]{3,2,1,0:T(8,128)(2,1)}), bf16[8,4,32,768]{3,2,1,0:T(8,128)(2,1)}, u32[]{:S(2)}, u32[]{:S(2)}) async-start(bf16[8,4,32,768]{3,2,1,0:T(8,128)(2,1)} %get-tuple-element.119), calls=%async_computation.2 | async-start | bytes 3145728 | tf_op jit(solution)/shard_map/all_to_all | solution.py:928
  235.7 20.0 %collective-permute-start.18 = (bf16[4,96,768]{2,1,0:T(8,128)(2,1)}, bf16[4,96,768]{2,1,0:T(8,128)(2,1)}, u32[]{:S(2)}, u32[]{:S(2)}) collective-permute-start(bf16[4,96,768]{2,1,0:T(8,128)(2,1)} %get-tuple-element.148), channel_id=1, source_target_pairs={{0,4},{4,0},{8,12},{12,8},{16,20},{20,16},{24,28},{28,24},{1,5},{5... | collective-permute-start | bytes 1769480 | tf_op jit(solution)/shard_map/ppermute | solution.py:651
  238.5 17.2 %collective-permute-start.19 = (bf16[4,96,768]{2,1,0:T(8,128)(2,1)}, bf16[4,96,768]{2,1,0:T(8,128)(2,1)}, u32[]{:S(2)}, u32[]{:S(2)}) collective-permute-start(bf16[4,96,768]{2,1,0:T(8,128)(2,1)} %get-tuple-element.150), channel_id=1, source_target_pairs={{0,2},{1,3},{2,0},{3,1},{4,6},{5,7},{6,4},{7,5},{8,10},{9,11},{10,... | collective-permute-start | bytes 1769480 | tf_op jit(solution)/shard_map/ppermute | solution.py:651
  243.5 26.0 %collective-permute-start.10 = (bf16[2,4,48,768]{3,2,1,0:T(8,128)(2,1)}, bf16[2,4,48,768]{3,2,1,0:T(8,128)(2,1)}, u32[]{:S(2)}, u32[]{:S(2)}) collective-permute-start(bf16[2,4,48,768]{3,2,1,0:T(8,128)(2,1)} %get-tuple-element.128), channel_id=1, source_target_pairs={{0,2},{1,3},{2,0},{3,1},{4,6},{5,7},{6,4},{7,5},{8,10},{9,11},{10,... | collective-permute-start | bytes 1769480 | tf_op jit(solution)/shard_map/ppermute | solution.py:651
  245.0 24.5 %collective-permute-start.11 = (bf16[2,4,48,768]{3,2,1,0:T(8,128)(2,1)}, bf16[2,4,48,768]{3,2,1,0:T(8,128)(2,1)}, u32[]{:S(2)}, u32[]{:S(2)}) collective-permute-start(bf16[2,4,48,768]{3,2,1,0:T(8,128)(2,1)} %get-tuple-element.130), channel_id=1, source_target_pairs={{0,4},{4,0},{8,12},{12,8},{16,20},{20,16},{24,28},{28,24},{1,5},{5... | collective-permute-start | bytes 1769480 | tf_op jit(solution)/shard_map/ppermute | solution.py:651
  245.0 15.2 %copy-start.23 = (f32[8,768]{1,0:T(8,128)S(1)}, f32[8,768]{1,0:T(8,128)}, u32[]{:S(2)}) copy-start(f32[8,768]{1,0:T(8,128)} %get-tuple-element.157) | copy-start | bytes 73732
  245.0 16.5 %copy-start.22 = (f32[1,3072]{1,0:T(1,128)S(1)}, f32[1,3072]{1,0:T(1,128)}, u32[]{:S(2)}) copy-start(f32[1,3072]{1,0:T(1,128)} %get-tuple-element.158) | copy-start | bytes 36868
  245.0 18.0 %copy-start.25 = (f32[1,768]{1,0:T(1,128)S(1)}, f32[1,768]{1,0:T(1,128)}, u32[]{:S(2)}) copy-start(f32[1,768]{1,0:T(1,128)} %get-tuple-element.159) | copy-start | bytes 9220
  258.4 18.4 %collective-permute-start.20 = (bf16[2,192,768]{2,1,0:T(8,128)(2,1)}, bf16[2,192,768]{2,1,0:T(8,128)(2,1)}, u32[]{:S(2)}, u32[]{:S(2)}) collective-permute-start(bf16[2,192,768]{2,1,0:T(8,128)(2,1)} %get-tuple-element.152), channel_id=1, source_target_pairs={{0,8},{4,12},{8,0},{12,4},{16,24},{20,28},{24,16},{28,20},{1,9},{5... | collective-permute-start | bytes 1769480 | tf_op jit(solution)/shard_map/ppermute | solution.py:651
  263.9 12.9 %all-to-all-start.3 = ((f32[32,3,96]{2,1,0:T(4,128)}), f32[32,3,96]{2,1,0:T(4,128)S(1)}, u32[]{:S(2)}, u32[]{:S(2)}) async-start(f32[32,3,96]{2,1,0:T(4,128)} %copy.64), calls=%async_computation.3 | async-start | bytes 131072 | tf_op jit(solution)/shard_map/all_to_all | solution.py:980
  272.2 9.5 %collective-permute-start.12 = (bf16[4,48,768]{2,1,0:T(8,128)(2,1)}, bf16[4,48,768]{2,1,0:T(8,128)(2,1)}, u32[]{:S(2)}, u32[]{:S(2)}) collective-permute-start(bf16[4,48,768]{2,1,0:T(8,128)(2,1)} %get-tuple-element.134), channel_id=1, source_target_pairs={{0,4},{4,0},{8,12},{12,8},{16,20},{20,16},{24,28},{28,24},{1,5},{5... | collective-permute-start | bytes 884744 | tf_op jit(solution)/shard_map/ppermute | solution.py:651
  273.8 9.1 %collective-permute-start.13 = (bf16[4,48,768]{2,1,0:T(8,128)(2,1)}, bf16[4,48,768]{2,1,0:T(8,128)(2,1)}, u32[]{:S(2)}, u32[]{:S(2)}) collective-permute-start(bf16[4,48,768]{2,1,0:T(8,128)(2,1)} %get-tuple-element.136), channel_id=1, source_target_pairs={{0,2},{1,3},{2,0},{3,1},{4,6},{5,7},{6,4},{7,5},{8,10},{9,11},{10,... | collective-permute-start | bytes 884744 | tf_op jit(solution)/shard_map/ppermute | solution.py:651
  279.0 16.0 %collective-permute-start.21 = (bf16[192,768]{1,0:T(8,128)(2,1)}, bf16[192,768]{1,0:T(8,128)(2,1)}, u32[]{:S(2)}, u32[]{:S(2)}) collective-permute-start(bf16[192,768]{1,0:T(8,128)(2,1)} %get-tuple-element.154), channel_id=1, source_target_pairs={{0,16},{4,20},{8,24},{12,28},{16,0},{20,4},{24,8},{28,12},{1,17},{... | collective-permute-start | bytes 884744 | tf_op jit(solution)/shard_map/ppermute | solution.py:651
  285.0 14.5 %collective-permute-start.14 = (bf16[2,96,768]{2,1,0:T(8,128)(2,1)}, bf16[2,96,768]{2,1,0:T(8,128)(2,1)}, u32[]{:S(2)}, u32[]{:S(2)}) collective-permute-start(bf16[2,96,768]{2,1,0:T(8,128)(2,1)} %get-tuple-element.138), channel_id=1, source_target_pairs={{0,8},{4,12},{8,0},{12,4},{16,24},{20,28},{24,16},{28,20},{1,9},{5... | collective-permute-start | bytes 884744 | tf_op jit(solution)/shard_map/ppermute | solution.py:651
  301.2 18.4 %copy-start.21 = (f32[768]{0:T(1024)S(1)}, f32[768]{0:T(1024)}, u32[]{:S(2)}) copy-start(f32[768]{0:T(1024)} %get-tuple-element.188) | copy-start | bytes 9220
  301.2 8.8 %collective-permute-start.15 = (bf16[96,768]{1,0:T(8,128)(2,1)}, bf16[96,768]{1,0:T(8,128)(2,1)S(1)}, u32[]{:S(2)}, u32[]{:S(2)}) collective-permute-start(bf16[96,768]{1,0:T(8,128)(2,1)} %get-tuple-element.140), channel_id=1, source_target_pairs={{0,16},{4,20},{8,24},{12,28},{16,0},{20,4},{24,8},{28,12},{1,17},{... | collective-permute-start | bytes 442376 | tf_op jit(solution)/shard_map/ppermute | solution.py:651
  314.8 11.8 %all-to-all-start.4 = ((f32[32,1,1]{2,1,0:T(1,128)}), f32[32,1,1]{2,1,0:T(1,128)S(1)}, u32[]{:S(2)}, u32[]{:S(2)}) async-start(f32[32,1,1]{2,1,0:T(1,128)} %broadcast_in_dim.18), calls=%async_computation.4 | async-start | bytes 32768 | tf_op jit(solution)/shard_map/all_to_all | solution.py:985
  319.6 8.4 %copy-start.24 = (f32[3,96]{1,0:T(4,128)S(1)}, f32[3,96]{1,0:T(4,128)}, u32[]{:S(2)}) copy-start(f32[3,96]{1,0:T(4,128)} %param.25) | copy-start | bytes 3460
  319.6 8.4 %copy-start.26 = (f32[3,96]{1,0:T(4,128)S(1)}, f32[3,96]{1,0:T(4,128)}, u32[]{:S(2)}) copy-start(f32[3,96]{1,0:T(4,128)} %param.35) | copy-start | bytes 3460
  319.6 8.4 %copy-start.27 = (f32[3,96]{1,0:T(4,128)S(1)}, f32[3,96]{1,0:T(4,128)}, u32[]{:S(2)}) copy-start(f32[3,96]{1,0:T(4,128)} %param.30) | copy-start | bytes 3460
  319.6 9.0 %copy-start.3 = (f32[384,192]{0,1:T(8,128)S(1)}, f32[384,192]{0,1:T(8,128)}, u32[]{:S(2)}) copy-start(f32[384,192]{0,1:T(8,128)} %param.24) | copy-start | bytes 884740
  319.7 9.0 %copy-start.11 = (f32[384,192]{0,1:T(8,128)S(1)}, f32[384,192]{0,1:T(8,128)}, u32[]{:S(2)}) copy-start(f32[384,192]{0,1:T(8,128)} %param.34) | copy-start | bytes 884740
  319.7 9.0 %copy-start.12 = (f32[384,192]{0,1:T(8,128)S(1)}, f32[384,192]{0,1:T(8,128)}, u32[]{:S(2)}) copy-start(f32[384,192]{0,1:T(8,128)} %param.29) | copy-start | bytes 884740
  325.9 3.9 %copy-start.2 = (f32[192,768]{1,0:T(8,128)S(1)}, f32[192,768]{1,0:T(8,128)}, u32[]{:S(2)}) copy-start(f32[192,768]{1,0:T(8,128)} %convert_add_fusion) | copy-start | bytes 1769476
  325.9 3.9 %copy-start.4 = (f32[96,768]{1,0:T(8,128)S(1)}, f32[96,768]{1,0:T(8,128)}, u32[]{:S(2)}) copy-start(f32[96,768]{1,0:T(8,128)} %param.23) | copy-start | bytes 884740
  325.9 3.9 %copy-start.13 = (f32[96,768]{1,0:T(8,128)S(1)}, f32[96,768]{1,0:T(8,128)}, u32[]{:S(2)}) copy-start(f32[96,768]{1,0:T(8,128)} %param.33) | copy-start | bytes 884740
  326.0 3.9 %copy-start.14 = (f32[96,768]{1,0:T(8,128)S(1)}, f32[96,768]{1,0:T(8,128)}, u32[]{:S(2)}) copy-start(f32[96,768]{1,0:T(8,128)} %param.28) | copy-start | bytes 884740
  329.9 2.0 copy-start.7
  (8 other events, 9.8 us)
Sparse Core Ops, SparseCore 0:
  11.5 111.5 all-gather.2

commit v5 on v4

--- a/solution.py
+++ b/solution.py
@@ -111,38 +111,36 @@
     return pl.BlockSpec(shape, lambda i: (0,) * len(shape))
 
 
-def picked(places, length):
-    lanes = places.shape[1]
-    rows = lax.broadcasted_iota(jnp.int32, (length, lanes), 0)
-    return (rows == places).astype(F32)
-
-
-def seen_body(seen, cot_ref, places_ref, out_ref, sum_ref):
-    count, length, _ = cot_ref.shape
+def seen_body(seen, *refs):
+    cot_refs, (places_ref, out_ref, sum_ref) = refs[:-3], refs[-3:]
+    count, length, _ = cot_refs[0].shape
+    depth = places_ref.shape[1]
 
     @pl.when(pl.program_id(0) == 0)
     def _():
         sum_ref[...] = jnp.zeros_like(sum_ref)
 
-    for k in range(count):
-        pick = picked(places_ref[k], length)
-        gaps = 1.0 - jnp.sum(pick, axis=-1, keepdims=True)
-        lane = lax.broadcasted_iota(jnp.int32, pick.shape, 1)
-        rows = dot_tn(jnp.where(lane == seen, gaps, pick).astype(BF16), cot_ref[k])
+    lane = lax.broadcasted_iota(jnp.int32, (depth, length), 1)
+    row = lax.broadcasted_iota(jnp.int32, (depth, length), 0)
+    for k in range(count * len(cot_refs)):
+        pick = jnp.where((lane == places_ref[k]) | (row == seen), 1.0, 0.0).astype(BF16)
+        rows = dot_nn(pick, cot_refs[k // count][k % count])
         out_ref[k] = rows[:seen].astype(BF16)
-        sum_ref[...] += rows[seen : seen + 1]
+        sum_ref[...] += rows[seen : seen + 1] - jnp.sum(rows[:seen], axis=0, keepdims=True)
 
 
 def seen_rows(cot, places, seen):
     chips, length, model = cot.shape
-    step = 4
+    streams, step = 4, 8
+
+    def stream(k):
+        return pl.BlockSpec((step // streams, length, model), lambda i: (i * streams + k, 0, 0))
+
     return pl.pallas_call(
         functools.partial(seen_body, seen),
         grid=(chips // step,),
-        in_specs=[
-            pl.BlockSpec((step, length, model), lambda i: (i, 0, 0)),
-            pl.BlockSpec((step, 1, places.shape[2]), lambda i: (i, 0, 0)),
-        ],
+        in_specs=[stream(k) for k in range(streams)]
+        + [pl.BlockSpec((step,) + places.shape[1:], lambda i: (i, 0, 0))],
         out_specs=[pl.BlockSpec((step, seen, model), lambda i: (i, 0, 0)), full_spec((1, model))],
         out_shape=[
             jax.ShapeDtypeStruct((chips, seen, model), BF16),
@@ -151,7 +149,7 @@
         compiler_params=params_for(),
         cost_estimate=busy_for(8),
         name="seen_rows",
-    )(cot, places)
+    )(*[cot] * streams, places)
 
 
 def attend_body(table, rows, heads, wide, *refs):
@@ -302,23 +300,30 @@
 
     @pl.when(first_step)
     def _():
-        copies = load_grid(u_table, u_refs, me_ref, up, sems, rows, start=False)
-        copies += load_down(d_table, d_refs, me_ref, down, sems, share, first=count, start=False)
-        for copy in copies:
+        for copy in load_grid(u_table, u_refs, me_ref, up, sems, rows, start=False):
             copy.wait()
 
-    def fore(f):
-        lanes = slice(f * span, (f + 1) * span)
-        return dot_nn(normed, up[f]) + bias_ref[:, lanes], dot_nn(feed_grad, down[:, lanes])
+    def gate_of(f):
+        return dot_nn(normed, up[f]) + bias_ref[:, f * span : (f + 1) * span]
+
+    gate = gate_of(0)
+
+    @pl.when(first_step)
+    def _():
+        for copy in load_down(d_table, d_refs, me_ref, down, sems, share, first=count, start=False):
+            copy.wait()
+
+    def active_grad_of(f):
+        return dot_nn(feed_grad, down[:, f * span : (f + 1) * span])
 
     normed_grad = jnp.zeros((seq, model), F32)
     result = middle + vec_ref[10:11, :]
-    ready = fore(0)
+    ready = gate, active_grad_of(0)
     for f in range(shares):
         lanes = slice(f * span, (f + 1) * span)
         gate, active_grad = ready
         if f + 1 < shares:
-            ready = fore(f + 1)
+            ready = gate_of(f + 1), active_grad_of(f + 1)
         active, slope = gelu_pair(gate)
         active = active.astype(BF16)
         gate_grad = (active_grad * slope).astype(BF16)
@@ -453,7 +458,7 @@
             jax.ShapeDtypeStruct((8, model), F32),
         ],
         compiler_params=params_for(),
-        cost_estimate=busy_for(30),
+        cost_estimate=busy_for(1),
         name="attend_back",
     )(mixed, expo, share, context_grad)
 
@@ -489,7 +494,7 @@
             jax.ShapeDtypeStruct((8, model), F32),
         ],
         compiler_params=params_for(),
-        cost_estimate=busy_for(40),
+        cost_estimate=busy_for(25),
         name="tokens_back",
     )(x, middle_grad, mixed_grad, vec, qkv_whole)
 
@@ -638,7 +643,7 @@
         out_shape=[jax.ShapeDtypeStruct(shape, BF16) for shape in shapes],
         scratch_shapes=[pltpu.VMEM((shares, model, slim), BF16), pltpu.VMEM((shares, model, cols), BF16)] + sems,
         compiler_params=params_for(),
-        cost_estimate=busy_for(30),
+        cost_estimate=busy_for(1),
         name="qkv_grads",
     )(me, normed, mixed_grad, context, branch_grad)
 
@@ -677,7 +682,7 @@
 
 def fold_call(pairs, plan, in_blocks, out_blocks, out_shapes, steps, dtype=BF16):
     def spec(block, along):
-        return pl.BlockSpec(block, lambda i: tuple(i if k == along else 0 for k in range(len(block))))
+        return pl.BlockSpec(block, lambda i: tuple(i if k in along else 0 for k in range(len(block))))
 
     arrays = [array for pair in pairs for array in pair]
     return pl.pallas_call(
@@ -713,8 +718,8 @@
                     [(0, (everything, 0, everything, lower))],
                     [(0, (everything, 1, everything, lower))],
                 ],
-                [((2, 2, 1, rows, cols), 2)],
-                [((2, 1, cut, cols), 1)] * 4,
+                [((2, 2, 1, rows, cols), (2,))],
+                [((2, 1, cut, cols), (1,))] * 4,
                 [(2, 4, cut, cols)] * 4,
                 4,
             )
@@ -724,20 +729,19 @@
             outs = fold_call(
                 list(zip(keep, self.arrived)),
                 [[(0, 0)], [(0, 1)], [(1, 0)], [(1, 1)]],
-                [((2, 4, cut, cols), None)] * 2,
-                [((4, cut, cols), None)] * 4,
+                [((2, 4, cut, cols), ())] * 2,
+                [((4, cut, cols), ())] * 4,
                 [(4, cut, cols)] * 4,
                 1,
             )
             self.keep, sent = (outs[0], outs[2]), (outs[1], outs[3])
             self.arrived = swap(sent[0], *YS), swap(sent[1], *XS)
         elif self.stage == 2:
-            near, far = slice(0, 2), slice(2, 4)
             self.keep, sent = fold_call(
-                list(zip(keep, self.arrived)),
-                [[(0, near), (1, near)], [(0, far), (1, far)]],
-                [((4, cut, cols), None)] * 2,
-                [((2, rows, cols), None)] * 2,
+                [[v.reshape(2, 2, cut, cols) for v in pair] for pair in zip(keep, self.arrived)],
+                [[(0, 0), (1, 0)], [(0, 1), (1, 1)]],
+                [((2, 2, cut, cols), ())] * 2,
+                [((2, rows, cols), ())] * 2,
                 [(2, rows, cols)] * 2,
                 1,
             )
@@ -746,16 +750,86 @@
             self.keep, sent = fold_call(
                 [(keep, self.arrived)],
                 [[(0, 0)], [(0, 1)]],
-                [((2, rows, cols), None)],
-                [((rows, cols), None)] * 2,
+                [((2, rows, cols), ())],
+                [((rows, cols), ())] * 2,
                 [(rows, cols)] * 2,
                 1,
             )
             self.arrived = swap(sent, *Z_FAR)
         else:
-            return keep.astype(F32) + self.arrived.astype(F32)
+            return keep, self.arrived
         self.stage += 1
         return sent
+
+
+def lane_sums(values):
+    rows = jnp.sum(values, axis=0, keepdims=True)
+    total = rows[:, :128]
+    for k in range(1, values.shape[1] // 128):
+        total += rows[:, 128 * k : 128 * (k + 1)]
+    return total
+
+
+def last_body(keep_ref, arrived_ref, squares_ref, small_ref, sum_ref, parts_ref):
+    total = keep_ref[...].astype(F32) + arrived_ref[...].astype(F32)
+    sum_ref[...] = total
+    small = small_ref[...]
+    lane = lax.broadcasted_iota(jnp.int32, (1, 128), 1)
+    squares = squares_ref[...] + lane_sums(total * total) + jnp.where(lane == 0, jnp.sum(small * small), 0.0)
+    parts_ref[...] = jnp.broadcast_to(squares[None], parts_ref.shape)
+
+
+def last_sum(keep, arrived, squares, small, copies):
+    whole = lambda shape: pl.BlockSpec(shape, lambda: (0,) * len(shape))
+    out = (copies, 1, 128)
+    return pl.pallas_call(
+        last_body,
+        in_specs=[whole(v.shape) for v in (keep, arrived, squares, small)],
+        out_specs=[whole(keep.shape), whole(out)],
+        out_shape=[jax.ShapeDtypeStruct(keep.shape, F32), jax.ShapeDtypeStruct(out, F32)],
+        compiler_params=params_for(),
+        cost_estimate=busy_for(2),
+        name="last_sum",
+    )(keep, arrived, squares, small)
+
+
+def adam_body(threshold, plan, *refs):
+    ins, outs = refs[: 4 + 3 * len(plan)], refs[4 + 3 * len(plan) :]
+    parts_ref, q_ref, feed_ref, small_ref = ins[:4]
+    norm = jnp.sqrt(jnp.sum(jnp.sum(parts_ref[...], axis=0), axis=-1, keepdims=True))
+    outs[-1][...] = norm
+    clip = jnp.minimum(1.0, threshold / norm)
+    spot = 0
+    for k, (which, windows, step_rate, decay_rate, low) in enumerate(plan):
+        source = (q_ref, feed_ref, small_ref)[which]
+        weight, first, second = (ref[...] for ref in ins[4 + 3 * k : 7 + 3 * k])
+        gradient = jnp.concatenate([source[rows, lanes] for rows, lanes in windows], axis=0)
+        results = adam_step(weight, gradient, first, second, clip, step_rate, decay_rate)
+        for value in results:
+            outs[spot][...] = value
+            spot += 1
+        if low:
+            outs[spot][...] = results[2].astype(BF16)
+            spot += 1
+
+
+def adam_all(threshold, plan, parts, q_sum, feed_sum, small, states):
+    whole = lambda shape: pl.BlockSpec(shape, lambda: (0,) * len(shape))
+    arrays = [parts, q_sum, feed_sum, small] + [v for state in states for v in state]
+    shapes = []
+    for (_, _, _, _, low), (weight, _, _) in zip(plan, states):
+        shapes += [jax.ShapeDtypeStruct(weight.shape, F32)] * 3
+        shapes += [jax.ShapeDtypeStruct(weight.shape, BF16)] if low else []
+    shapes.append(jax.ShapeDtypeStruct((1, 1), F32))
+    return pl.pallas_call(
+        functools.partial(adam_body, threshold, plan),
+        in_specs=[whole(v.shape) for v in arrays],
+        out_specs=[whole(v.shape) for v in shapes],
+        out_shape=shapes,
+        compiler_params=params_for(),
+        cost_estimate=busy_for(4),
+        name="adam_all",
+    )(*arrays)
 
 
 def rel_table(steps, last, off):
@@ -848,7 +922,7 @@
     cot = cotangent[0]
     whole_tiles = block_seen % 16 == 0
     if whole_tiles:
-        places = jnp.pad(places, ((0, 0), (0, 128 - block_seen)), constant_values=-1)[:, None]
+        places = jnp.pad(places, ((0, 0), (0, 16)), constant_values=-1)[:, :, None]
         cot_seen, mask_grad = seen_rows(cot, places, block_seen)
     else:
         slot_ids = lax.broadcasted_iota(jnp.int32, (chips_group, block_len, block_seen), 1)
@@ -921,8 +995,6 @@
     if folded:
         normed = after(normed, feed_fold.step(mixed_grad))
     q_blocks = qkv_grads(me, normed, mixed_grad, context, branch_grad, order, rows, wide)
-    if folded:
-        result = after(result, *q_blocks)
     if not whole_tiles:
         result = result.reshape(chip_count, block_count, block_seen, model_width).transpose(1, 0, 2, 3)
     arrived = lax.all_to_all(result, DP, split_axis=0, concat_axis=0, tiled=True)
@@ -931,38 +1003,6 @@
         q_fold = Fold(*q_blocks)
         x = after(x, *q_blocks)
     tokens_grad, sums_one = tokens_back(x, middle_grad, mixed_grad, vec, qkv_whole)
-
-    slot_ids = lax.broadcasted_iota(jnp.int32, (chips_group, block_len, block_seen), 1)
-    pick = (seen_places[:, None, :] == slot_ids).astype(BF16)
-    gaps = 1.0 - jnp.sum(pick.astype(F32), axis=-1)
-    filled = jnp.einsum("cpv,cvd->cpd", pick, arrived, preferred_element_type=F32)
-    filled = filled + gaps[..., None] * vec[11]
-    full_layout = filled.astype(BF16).reshape(1, chips_group, block_len, model_width)
-
-    if folded:
-        feed_fold.step(tokens_grad)
-        q_fold.step(tokens_grad)
-        feed_fold.step()
-        q_fold.step(arrived)
-        feed_fold.step()
-        q_fold.step()
-        feed_sum = feed_fold.step()
-        u_sum, d_sum = feed_sum[:rows], feed_sum[rows:]
-        q_fold.step()
-        q_sum = q_fold.step()
-        d_sum = jnp.concatenate([d_sum[:, :tall], d_sum[:, tall:]], axis=0).T
-    else:
-
-        def scatter_whole(whole):
-            cols = whole.shape[2]
-            pieces = whole.reshape(fsdp_size, dp_size, -1, cols).transpose(1, 0, 2, 3)
-            pieces = pieces.reshape(-1, cols)
-            return lax.psum_scatter(pieces, both, scatter_dimension=0, tiled=True).astype(F32)
-
-        q_sum, u_sum = scatter_whole(q_blocks[0].reshape(fsdp_size, model_width, -1)), scatter_whole(feed_blocks[0])
-        pieces = feed_blocks[1].reshape(fsdp_size, slim, dp_size, tall).transpose(2, 0, 1, 3)
-        pieces = pieces.reshape(device_count * slim, tall)
-        d_sum = lax.psum_scatter(pieces, both, scatter_dimension=0, tiled=True).astype(F32).T
 
     vector_grad = jnp.concatenate(
         [
@@ -977,35 +1017,88 @@
     )
     parts = vector_grad.reshape(fsdp_size, vec_rows, dp_size, vec_cols).transpose(2, 0, 1, 3)
     parts = parts.reshape(device_count, vec_rows, vec_cols)
-    parts = lax.all_to_all(parts, both, split_axis=0, concat_axis=0, tiled=True)
-    shares = (q_sum[:, :wide], q_sum[:, wide:], u_sum, d_sum, jnp.sum(parts, axis=0))
-    squares = jnp.sum(q_sum * q_sum) + jnp.sum(u_sum * u_sum) + jnp.sum(d_sum * d_sum)
-    squares = squares + jnp.sum(shares[4] * shares[4])
-    square_parts = jnp.broadcast_to(squares, (device_count, 1))
-    grad_total = jnp.sum(lax.all_to_all(square_parts, both, split_axis=0, concat_axis=0, tiled=True))
-    grad_norm = jnp.sqrt(grad_total)
+    small = jnp.sum(lax.all_to_all(parts, both, split_axis=0, concat_axis=0, tiled=True), axis=0)
+
+    slot_ids = lax.broadcasted_iota(jnp.int32, (chips_group, block_len, block_seen), 1)
+    pick = (seen_places[:, None, :] == slot_ids).astype(BF16)
+    gaps = 1.0 - jnp.sum(pick.astype(F32), axis=-1)
+    filled = jnp.einsum("cpv,cvd->cpd", pick, arrived, preferred_element_type=F32)
+    filled = filled + gaps[..., None] * vec[11]
+    full_layout = filled.astype(BF16).reshape(1, chips_group, block_len, model_width)
+
+    if folded:
+        feed_fold.step(tokens_grad, arrived)
+        q_fold.step(tokens_grad)
+        feed_fold.step()
+        q_fold.step()
+        feed_fold.step()
+        q_fold.step()
+        feed_sum, squares = last_sum(*feed_fold.step(), jnp.zeros((1, 128), F32), small, 1)
+        q_fold.step()
+        q_sum, squares = last_sum(*q_fold.step(), squares[0], jnp.zeros_like(small), device_count)
+    else:
+
+        def scatter_whole(whole):
+            cols = whole.shape[2]
+            pieces = whole.reshape(fsdp_size, dp_size, -1, cols).transpose(1, 0, 2, 3)
+            pieces = pieces.reshape(-1, cols)
+            return lax.psum_scatter(pieces, both, scatter_dimension=0, tiled=True).astype(F32)
+
+        q_sum, u_sum = scatter_whole(q_blocks[0].reshape(fsdp_size, model_width, -1)), scatter_whole(feed_blocks[0])
+        pieces = feed_blocks[1].reshape(fsdp_size, slim, dp_size, tall).transpose(2, 0, 1, 3)
+        pieces = pieces.reshape(device_count * slim, tall)
+        d_sum = lax.psum_scatter(pieces, both, scatter_dimension=0, tiled=True).astype(F32).T
+
     tokens_all = device_count * chip_count * seq_len
     threshold = 0.05 * model_width * math.sqrt(tokens_all)
-    clip = jnp.minimum(1.0, threshold / grad_norm)
     rate = 0.6 / math.sqrt(model_width)
     out_rate = 0.6 / math.sqrt(model_width // 32)
     down_rate = 0.6 / math.sqrt(ff_width)
-    qkv_out = adam_step(qkv_weight, shares[0], qkv_first, qkv_second, clip, rate, 0.05)
-    out_out = adam_step(out_weight, shares[1], out_first, out_second, clip, out_rate, 0.05)
-    up_out = adam_step(up_weight, shares[2], up_first, up_second, clip, rate, 0.05)
-    down_out = adam_step(down_weight, shares[3], down_first, down_second, clip, down_rate, 0.05)
-    vec_out = adam_step(vectors, shares[4], vector_first, vector_second, clip, 0.45, 0.0)
+    if folded:
+        squares = lax.all_to_all(squares, both, split_axis=0, concat_axis=0, tiled=True)
+        everything = slice(None)
+        plan = (
+            (0, ((everything, slice(0, wide)),), rate, 0.05, True),
+            (0, ((everything, slice(wide, wide + slim)),), out_rate, 0.05, True),
+            (1, ((slice(0, rows), everything),), rate, 0.05, True),
+            (1, ((slice(rows, rows + half), slice(0, tall)), (slice(rows, rows + half), slice(tall, 2 * tall))), down_rate, 0.05, True),
+            (2, ((everything, everything),), 0.45, 0.0, False),
+        )
+        states = (
+            (qkv_weight, qkv_first, qkv_second),
+            (out_weight, out_first, out_second),
+            (up_weight, up_first, up_second),
+            (down_weight.T, down_first.T, down_second.T),
+            (vectors, vector_first, vector_second),
+        )
+        news = adam_all(threshold, plan, squares, q_sum, feed_sum, small, states)
+        qkv_out, out_out, up_out = news[0:4], news[4:8], news[8:12]
+        down_out = [v.T for v in news[12:16]]
+        vec_out, grad_norm = news[16:19], news[19][0, 0]
+    else:
+        grads = (q_sum[:, :wide], q_sum[:, wide:], u_sum, d_sum, small)
+        squares = sum(jnp.sum(grad * grad) for grad in grads)
+        squares = jnp.broadcast_to(squares, (device_count, 1))
+        grad_total = jnp.sum(lax.all_to_all(squares, both, split_axis=0, concat_axis=0, tiled=True))
+        grad_norm = jnp.sqrt(grad_total)
+        clip = jnp.minimum(1.0, threshold / grad_norm)
+
+        def stepped(*state):
+            news = adam_step(*state)
+            return news + (news[2].astype(BF16),)
+
+        qkv_out = stepped(qkv_weight, grads[0], qkv_first, qkv_second, clip, rate, 0.05)
+        out_out = stepped(out_weight, grads[1], out_first, out_second, clip, out_rate, 0.05)
+        up_out = stepped(up_weight, grads[2], up_first, up_second, clip, rate, 0.05)
+        down_out = stepped(down_weight, grads[3], down_first, down_second, clip, down_rate, 0.05)
+        vec_out = adam_step(vectors, grads[4], vector_first, vector_second, clip, 0.45, 0.0)
     return (
         full_layout,
         tokens_grad[None],
         *qkv_out,
-        qkv_out[2].astype(BF16),
         *out_out,
-        out_out[2].astype(BF16),
         *up_out,
-        up_out[2].astype(BF16),
         *down_out,
-        down_out[2].astype(BF16),
         *vec_out,
         grad_norm,
     )

time: 343 us -> 335 us (0.977)
  other arithmetic: 20.1 us -> 8.87 us
  Pallas kernels: 138 us -> 144 us
  between operations: 19.1 us -> 14.5 us
    pallas_call x0 -> x3, Pallas kernels: none -> 8.01 us  [the longest x1 4.23 us: adam_all(): pl.pallas_call(functools.partial(adam_body, threshold, plan), in_specs=[w...]
    convert_element_type x4 -> x0, other arithmetic: 4.11 us -> none  [the longest x1 1.12 us: on_device(): down_out[2].astype(BF16)]
    add x2 -> x0, other arithmetic: 3.53 us -> none  [step(): return keep.astype(F32) + self.arrived.astype(F32)]
  transfers between devices with their start and end apart: 28 -> 28, of which waited for: 14 -> 14; matrix products, arithmetic and copies ran while one was open for 9% -> 8% of each run, Pallas kernels for 23% -> 25%
where the time goes in v5:
time: 335 us; the launch traced here: 334 us
  Pallas kernels  144 us (43%)
  waiting for transfers between devices  90.6 us (27%)
  starting transfers between devices  53.2 us (16%)
  local copies, waits for them, and re-layouts  16.7 us (5%)
  between operations  14.5 us (4%)
  other arithmetic  8.87 us (3%)
  matrix products  6.18 us (2%)
    ppermute x22, waiting for transfers between devices, swap(): return lax.ppermute(value, axis, [(i, i ^ bit) for i in range(size)])  86.9 us
    pallas_call x1, Pallas kernels, feed_forward_back(): pl.pallas_call(functools.partial(feed_body, u_table, d_table, rows, share...  36.9 us
    ppermute x22, starting transfers between devices, swap(): return lax.ppermute(value, axis, [(i, i ^ bit) for i in range(size)])  28.3 us
    pallas_call x8, Pallas kernels, fold_call(): pl.pallas_call(functools.partial(fold_body, plan, len(pairs)), grid=(step...  26.5 us
    pallas_call x1, Pallas kernels, attend_forward(): pl.pallas_call(functools.partial(attend_body, table, rows, heads, wide),...  17.5 us
    pallas_call x1, Pallas kernels, feed_grads(): pl.pallas_call(functools.partial(feed_grad_body, order, rows, half, wide)...  16.4 us
    pallas_call x1, Pallas kernels, qkv_grads(): pl.pallas_call(functools.partial(qkv_grad_body, order, rows), grid=(share...  11.7 us
    pallas_call x1, Pallas kernels, attend_back(): pl.pallas_call(functools.partial(attend_back_body, heads), grid=(chips,),...  11.3 us
  transfers between devices with their start and end apart: 28, of which 14 were waited for; matrix products, arithmetic and copies ran while one was open for 8% of the time, Pallas kernels for 25%

profile of v5, /device:TPU:0, one launch (start us, length us, event | category | flops | bytes accessed | tf_op | source)
XLA Modules:
  0.0 333.8 jit_solution(287436804840846887)
XLA Ops:
  11.5 4.0 %collective-permute-start = (bf16[1,96,768]{2,1,0:T(8,128)(2,1)}, bf16[1,96,768]{2,1,0:T(8,128)(2,1)}, u32[]{:S(2)}, u32[]{:S(2)}) collective-permute-start(bf16[1,96,768]{2,1,0:T(8,128)(2,1)} %pad_maximum_fusion.6), channel_id=1, source_target_pairs={{0,16},{4,20},{8,24},{12,28},{16,0},{20,4},{24,8},{28,12},{1,17},{... | collective-permute-start | bytes 442376 | tf_op jit(solution)/shard_map/ppermute | solution.py:656
  16.9 5.3 %seen_rows.1 = (bf16[32,32,768]{2,1,0:T(8,128)(2,1)}, f32[1,768]{1,0:T(1,128)}) custom-call(bf16[32,128,768]{2,1,0:T(8,128)(2,1)} %bitcast.69, bf16[32,128,768]{2,1,0:T(8,128)(2,1)} %bitcast.70, bf16[32,128,768]{2,1,0:T(8,128)(2,1)} %bitcast.71, bf16[32,128,768]{2,1,0:T(8,128)(2,1)} %bitcast.72, s32[32,48,1]{2,1,0:T(8,128)} %copy.47.refs_4_), custom_call_target="tpu_custom_call" | custom-call | flops 8000000000 | bytes 24000000 | tf_op jit(solution)/shard_map/seen_rows/pallas_call | solution.py:139
  26.2 5.4 %all-to-all-start.1 = ((bf16[32,3,96]{2,1,0:T(4,128)(2,1)}), bf16[32,3,96]{2,1,0:T(4,128)(2,1)S(1)}, u32[]{:S(2)}, u32[]{:S(2)}) async-start(bf16[32,3,96]{2,1,0:T(4,128)(2,1)} %broadcast_in_dim.19), calls=%async_computation.1 | async-start | bytes 65536 | tf_op jit(solution)/shard_map/all_to_all | solution.py:914
  31.6 7.0 %collective-permute-done.1 = bf16[2,96,768]{2,1,0:T(8,128)(2,1)S(1)} collective-permute-done((bf16[2,96,768]{2,1,0:T(8,128)(2,1)S(1)}, bf16[2,96,768]{2,1,0:T(8,128)(2,1)S(1)}, u32[]{:S(2)}, u32[]{:S(2)}) %collective-permute-start.1) | collective-permute-done | bytes 294944 | tf_op jit(solution)/shard_map/ppermute | solution.py:656
  39.6 2.8 all-to-all-done.1
  43.0 4.3 %all-to-all-start = ((bf16[8,4,32,768]{3,2,1,0:T(8,128)(2,1)}), bf16[8,4,32,768]{3,2,1,0:T(8,128)(2,1)}, u32[]{:S(2)}, u32[]{:S(2)}) async-start(bf16[8,4,32,768]{3,2,1,0:T(8,128)(2,1)} %bitcast.5), calls=%async_computation | async-start | bytes 3145728 | tf_op jit(solution)/shard_map/all_to_all | solution.py:973
  47.4 2.0 collective-permute-start.5
  49.8 17.1 %collective-permute-done.5 = bf16[4,48,768]{2,1,0:T(8,128)(2,1)S(1)} collective-permute-done((bf16[4,48,768]{2,1,0:T(8,128)(2,1)S(1)}, bf16[4,48,768]{2,1,0:T(8,128)(2,1)S(1)}, u32[]{:S(2)}, u32[]{:S(2)}) %collective-permute-start.5) | collective-permute-done | bytes 294944 | tf_op jit(solution)/shard_map/ppermute | solution.py:656
  68.3 2.6 collective-permute-start.3
  70.9 10.2 %collective-permute-done.6 = bf16[8,48,768]{2,1,0:T(8,128)(2,1)S(1)} collective-permute-done((bf16[8,48,768]{2,1,0:T(8,128)(2,1)S(1)}, bf16[8,48,768]{2,1,0:T(8,128)(2,1)S(1)}, u32[]{:S(2)}, u32[]{:S(2)}) %collective-permute-start.6) | collective-permute-done | bytes 589856 | tf_op jit(solution)/shard_map/ppermute | solution.py:656
  81.3 14.5 %collective-permute-done.3 = bf16[8,48,768]{2,1,0:T(8,128)(2,1)S(1)} collective-permute-done((bf16[8,48,768]{2,1,0:T(8,128)(2,1)S(1)}, bf16[8,48,768]{2,1,0:T(8,128)(2,1)S(1)}, u32[]{:S(2)}, u32[]{:S(2)}) %collective-permute-start.3) | collective-permute-done | bytes 589856 | tf_op jit(solution)/shard_map/ppermute | solution.py:656
  98.2 1.5 reshape.163.refs_2_.refs_4_.vec_ref
  99.7 1.9 slice_bitcast_fusion.1
  101.6 1.6 copy.50.refs_3_
  105.7 17.5 %attend_forward.1 = (bf16[768,1024]{1,0:T(8,128)(2,1)}, bf16[2304,1024]{1,0:T(8,128)(2,1)}, bf16[4,12,256,256]{3,2,1,0:T(8,128)(2,1)}, f32[12,1024]{1,0:T(8,128)...) custom-call(s32[2]{0:T(128)} %pad_add_fusion.refs_0_.me_ref, ...), custom_call_target="tpu_custom_call" | custom-call | flops 1000000000 | bytes 3000000 | tf_op jit(solution)/shard_map/attend_forward/pallas_call | solution.py:222
  123.2 36.9 %feed_forward_back.1 = (bf16[8,4,32,768]{3,2,1,0:T(8,128)(2,1)}, bf16[1024,768]{1,0:T(8,128)(2,1)}, bf16[1024,3072]{1,0:T(8,128)(2,1)}, bf16[1024,3072]{1,0:T(8,...) custom-call(s32[2]{0:T(128)} %pad_add_fusion.refs_0_.me_ref, ...), custom_call_target="tpu_custom_call" | custom-call | flops 10000000000 | bytes 30000000 | tf_op jit(solution)/shard_map/feed_forward_back/pallas_call | solution.py:363
  160.1 16.4 %feed_grads.1 = (bf16[16,192,768]{2,1,0:T(8,128)(2,1)}, bf16[16,192,768]{2,1,0:T(8,128)(2,1)}) custom-call(s32[2]{0:T(128)} %pad_add_fusion.refs_0_.me_ref, bf16[1024,768]{1,0:T(8,128)(2,1)} %get-tuple-element.123.normed_ref, bf16[1024,3072]{1,0:T(8,128)(2,1)} %get-tuple-element.124.gate_grad_ref, bf16[1024,768]{1,0:T(8,128)(2,1)} %get-tuple-element.125.feed_grad_ref, ...), custom_call_target="tpu_custom_call" | custom-call | flops 1000000000 | bytes 3000000 | tf_op jit(solution)/shard_map/feed_grads/pallas_call | solution.py:576
  176.9 5.6 %all-to-all-start.2 = ((bf16[8,4,32,768]{3,2,1,0:T(8,128)(2,1)}), bf16[8,4,32,768]{3,2,1,0:T(8,128)(2,1)}, u32[]{:S(2)}, u32[]{:S(2)}) async-start(bf16[8,4,32,768]{3,2,1,0:T(8,128)(2,1)} %get-tuple-element.121), calls=%async_computation.2 | async-start | bytes 3145728 | tf_op jit(solution)/shard_map/all_to_all | solution.py:1000
  182.5 11.3 %attend_back.1 = (bf16[2304,1024]{1,0:T(8,128)(2,1)}, f32[8,768]{1,0:T(8,128)}) custom-call(bf16[2304,1024]{1,0:T(8,128)(2,1)} %get-tuple-element.128.mixed_ref, bf16[4,12,256,256]{3,2,1,0:T(8,128)(2,1)} %get-tuple-element.129.expo_ref, f32[12,1024]{1,0:T(8,128)} %get-tuple-element.130.share_ref, bf16[768,1024]{1,0:T(8,128)(2,1)} %get-tuple-element.133.grad_ref), custom_call_target="tpu_custom_call" | custom-call | flops 1000000000 | bytes 3000000 | tf_op jit(solution)/shard_map/attend_back/pallas_call | solution.py:446
  193.9 6.5 %fold_sums.8 = (bf16[2,4,96,768]{3,2,1,0:T(8,128)(2,1)}, bf16[2,4,96,768]{3,2,1,0:T(8,128)(2,1)}, bf16[2,4,96,768]{3,2,1,0:T(8,128)(2,1)}, bf16[2,4,96,768]{3,2,1,0:T(8,128)(2,1)}) custom-call(bf16[2,2,4,192,768]{4,3,2,1,0:T(8,128)(2,1)} %bitcast.55, bf16[2,2,4,192,768]{4,3,2,1,0:T(8,128)(2,1)} %bitcast.17.refs_1_), custom_call_target="tpu_custom_call" | custom-call | flops 2000000000 | bytes 6000000 | tf_op jit(solution)/shard_map/fold_sums/pallas_call | solution.py:688
  201.0 2.0 collective-permute-start.17
  203.0 11.7 %qkv_grads.1 = (bf16[16,96,768]{2,1,0:T(8,128)(2,1)}, bf16[16,96,768]{2,1,0:T(8,128)(2,1)}) custom-call(s32[2]{0:T(128)} %pad_add_fusion.refs_0_.me_ref, bf16[768,1024]{1,0:T(8,128)(2,1)} %get-tuple-element.138.normed_ref, bf16[2304,1024]{1,0:T(8,128)(2,1)} %get-tuple-element.134.mixed_grad_ref, bf16[768,1024]{1,0:T(8,128)(2,1)} %get-tuple-element.119.refs_3_.context_ref, ...), custom_call_target="tpu_custom_call" | custom-call | flops 1000000000 | bytes 3000000 | tf_op jit(solution)/shard_map/qkv_grads/pallas_call | solution.py:632
  214.8 10.1 %tokens_back.1 = (f32[4,256,768]{2,1,0:T(8,128)}, f32[8,768]{1,0:T(8,128)}) custom-call(bf16[4,256,768]{2,1,0:T(8,128)(2,1)} %bitcast.58, f32[4,256,768]{2,1,0:T(8,128)} %get-tuple-element.143.grad_ref, bf16[2304,1024]{1,0:T(8,128)(2,1)} %get-tuple-element.134.mixed_grad_ref, f32[12,768]{1,0:T(8,128)} %reshape.163.refs_2_.refs_4_.vec_ref, ...), custom_call_target="tpu_custom_call" | custom-call | flops 24999999488 | bytes 75000000 | tf_op jit(solution)/shard_map/tokens_back/pallas_call | solution.py:481
  224.9 3.4 %collective-permute-done.16.refs_1_ = bf16[2,4,96,768]{3,2,1,0:T(8,128)(2,1)} collective-permute-done((bf16[2,4,96,768]{3,2,1,0:T(8,128)(2,1)}, bf16[2,4,96,768]{3,2,1,0:T(8,128)(2,1)}, u32[]{:S(2)}, u32[]{:S(2)}) %collective-permute-start.16) | collective-permute-done | bytes 1179680 | tf_op jit(solution)/shard_map/ppermute | solution.py:656
  228.3 4.7 %collective-permute-done.17.refs_3_ = bf16[2,4,96,768]{3,2,1,0:T(8,128)(2,1)} collective-permute-done((bf16[2,4,96,768]{3,2,1,0:T(8,128)(2,1)}, bf16[2,4,96,768]{3,2,1,0:T(8,128)(2,1)}, u32[]{:S(2)}, u32[]{:S(2)}) %collective-permute-start.17) | collective-permute-done | bytes 1179680 | tf_op jit(solution)/shard_map/ppermute | solution.py:656
  233.0 3.9 %fold_sums.13 = (bf16[4,96,768]{2,1,0:T(8,128)(2,1)}, bf16[4,96,768]{2,1,0:T(8,128)(2,1)}, bf16[4,96,768]{2,1,0:T(8,128)(2,1)}, bf16[4,96,768]{2,1,0:T(8,128)(2,1)}) custom-call(bf16[2,4,96,768]{3,2,1,0:T(8,128)(2,1)} %get-tuple-element.165.refs_0_, bf16[2,4,96,768]{3,2,1,0:T(8,128)(2,1)} %collective-permute-done.16.refs_1_, ...), custom_call_target="tpu_custom_call" | custom-call | flops 2000000000 | bytes 6000000 | tf_op jit(solution)/shard_map/fold_sums/pallas_call | solution.py:688
  238.9 4.6 %fold_sums.9 = (bf16[2,4,48,768]{3,2,1,0:T(8,128)(2,1)}, bf16[2,4,48,768]{3,2,1,0:T(8,128)(2,1)}, bf16[2,4,48,768]{3,2,1,0:T(8,128)(2,1)}, bf16[2,4,48,768]{3,2,1,0:T(8,128)(2,1)}) custom-call(bf16[2,2,4,96,768]{4,3,2,1,0:T(8,128)(2,1)} %bitcast.73, bf16[2,2,4,96,768]{4,3,2,1,0:T(8,128)(2,1)} %bitcast.20.refs_1_), custom_call_target="tpu_custom_call" | custom-call | flops 2000000000 | bytes 6000000 | tf_op jit(solution)/shard_map/fold_sums/pallas_call | solution.py:688
  243.5 1.4 collective-permute-start.10
  245.6 7.9 %collective-permute-done.18 = bf16[4,96,768]{2,1,0:T(8,128)(2,1)} collective-permute-done((bf16[4,96,768]{2,1,0:T(8,128)(2,1)}, bf16[4,96,768]{2,1,0:T(8,128)(2,1)}, u32[]{:S(2)}, u32[]{:S(2)}) %collective-permute-start.18) | collective-permute-done | bytes 589856 | tf_op jit(solution)/shard_map/ppermute | solution.py:656
  253.5 1.3 collective-permute-done.19
  254.8 2.8 fold_sums.14
  257.5 2.4 collective-permute-start.20
  259.9 4.6 %collective-permute-done.10.refs_1_ = bf16[2,4,48,768]{3,2,1,0:T(8,128)(2,1)} collective-permute-done((bf16[2,4,48,768]{3,2,1,0:T(8,128)(2,1)}, bf16[2,4,48,768]{3,2,1,0:T(8,128)(2,1)}, u32[]{:S(2)}, u32[]{:S(2)}) %collective-permute-start.10) | collective-permute-done | bytes 589856 | tf_op jit(solution)/shard_map/ppermute | solution.py:656
  264.5 2.7 fold_sums.10
  267.2 1.7 collective-permute-start.12
  273.8 5.4 %all-to-all-start.3 = ((f32[32,3,96]{2,1,0:T(4,128)}), f32[32,3,96]{2,1,0:T(4,128)S(1)}, u32[]{:S(2)}, u32[]{:S(2)}) async-start(f32[32,3,96]{2,1,0:T(4,128)} %copy.52), calls=%async_computation.3 | async-start | bytes 131072 | tf_op jit(solution)/shard_map/all_to_all | solution.py:1020
  279.2 2.1 fold_sums.11
  281.3 1.8 collective-permute-start.14
  283.2 2.1 fold_sums.15
  285.3 2.1 collective-permute-start.21
  288.1 6.7 %collective-permute-done.14.refs_1_ = bf16[2,96,768]{2,1,0:T(8,128)(2,1)} collective-permute-done((bf16[2,96,768]{2,1,0:T(8,128)(2,1)}, bf16[2,96,768]{2,1,0:T(8,128)(2,1)}, u32[]{:S(2)}, u32[]{:S(2)}) %collective-permute-start.14) | collective-permute-done | bytes 294944 | tf_op jit(solution)/shard_map/ppermute | solution.py:656
  294.8 1.8 fold_sums.12
  297.1 8.9 %collective-permute-done.21.arrived_ref = bf16[192,768]{1,0:T(8,128)(2,1)} collective-permute-done((bf16[192,768]{1,0:T(8,128)(2,1)}, bf16[192,768]{1,0:T(8,128)(2,1)}, u32[]{:S(2)}, u32[]{:S(2)}) %collective-permute-start.21) | collective-permute-done | bytes 294944 | tf_op jit(solution)/shard_map/ppermute | solution.py:656
  306.4 2.0 last_sum.2
  309.0 1.8 last_sum.3
  310.8 4.2 %all-to-all-start.4 = ((f32[32,1,128]{2,1,0:T(1,128)}), f32[32,1,128]{2,1,0:T(1,128)S(1)}, u32[]{:S(2)}, u32[]{:S(2)}) async-start(f32[32,1,128]{2,1,0:T(1,128)} %get-tuple-element.183), calls=%async_computation.4 | async-start | bytes 32768 | tf_op jit(solution)/shard_map/all_to_all | solution.py:1058
  315.1 6.2 %fusion = bf16[1,32,128,768]{3,2,1,0:T(8,128)(2,1)} fusion(f32[768]{0:T(1024)S(1)} %copy-done.8, f32[32,128]{1,0:T(8,128)S(1)} %broadcast_subtract_fusion, bf16[32,32,768]{2,1,0:T(8,128)(2,1)} %bitcast.14, s32[32,32]{1,0:T(8,128)S(1)} %bitcast.62), kind=kOutput, calls=%fused_computation.1 | convolution fusion | flops 210894848 | bytes 7887872 | tf_op jit(solution)/shard_map/cpv,cvd->cpd/dot_general | solution.py:1025
  322.7 4.2 %adam_all.1 = (f32[96,576]{1,0:T(8,128)}, f32[96,576]{1,0:T(8,128)}, f32[96,576]{1,0:T(8,128)}, bf16[96,576]{1,0:T(8,128)(2,1)}, f32[96,192]{1,0:T(8,128)}, /*in...) custom-call(f32[32,1,128]{2,1,0:T(1,128)} %copy-done.9, ...), custom_call_target="tpu_custom_call" | custom-call | flops 4000000000 | bytes 12000000 | tf_op jit(solution)/shard_map/adam_all/pallas_call | solution.py:824
  (99 shorter events, 30.5 us)
Async XLA Ops:
  7.2 2.9 copy-start.6
  7.2 3.0 copy-start.4
  7.2 8.4 %copy-start.7 = (s32[1,32,256]{2,1,0:T(8,128)S(1)}, s32[1,32,256]{2,1,0:T(8,128)}, u32[]{:S(2)}) copy-start(s32[1,32,256]{2,1,0:T(8,128)} %param.19) | copy-start | bytes 98308
  7.2 116.0 %all-gather.3.cloned.1.call-start = ((), (), s32[]{:S(2)}) async-start(), calls=%async_computation.5 | async-start | bytes 9732096 | tf_op jit(solution)/shard_map/all_gather | solution.py:947
  10.2 0.6 copy-start.3
  11.5 11.4 %collective-permute-start = (bf16[1,96,768]{2,1,0:T(8,128)(2,1)}, bf16[1,96,768]{2,1,0:T(8,128)(2,1)}, u32[]{:S(2)}, u32[]{:S(2)}) collective-permute-start(bf16[1,96,768]{2,1,0:T(8,128)(2,1)} %pad_maximum_fusion.6), channel_id=1, source_target_pairs={{0,16},{4,20},{8,24},{12,28},{16,0},{20,4},{24,8},{28,12},{1,17},{... | collective-permute-start | bytes 442376 | tf_op jit(solution)/shard_map/ppermute | solution.py:656
  23.9 14.7 %collective-permute-start.1 = (bf16[2,96,768]{2,1,0:T(8,128)(2,1)S(1)}, bf16[2,96,768]{2,1,0:T(8,128)(2,1)S(1)}, u32[]{:S(2)}, u32[]{:S(2)}) collective-permute-start(bf16[2,96,768]{2,1,0:T(8,128)(2,1)S(1)} %pad_maximum_fusion.5), channel_id=1, source_target_pairs={{0,8},{4,12},{8,0},{12,4},{16,24},{20,28},{24,16},{28,20},{1,9},{5... | collective-permute-start | bytes 884744 | tf_op jit(solution)/shard_map/ppermute | solution.py:656
  26.2 16.2 %all-to-all-start.1 = ((bf16[32,3,96]{2,1,0:T(4,128)(2,1)}), bf16[32,3,96]{2,1,0:T(4,128)(2,1)S(1)}, u32[]{:S(2)}, u32[]{:S(2)}) async-start(bf16[32,3,96]{2,1,0:T(4,128)(2,1)} %broadcast_in_dim.19), calls=%async_computation.1 | async-start | bytes 65536 | tf_op jit(solution)/shard_map/all_to_all | solution.py:914
  42.4 0.6 copy-start.5
  43.0 80.2 %all-to-all-start = ((bf16[8,4,32,768]{3,2,1,0:T(8,128)(2,1)}), bf16[8,4,32,768]{3,2,1,0:T(8,128)(2,1)}, u32[]{:S(2)}, u32[]{:S(2)}) async-start(bf16[8,4,32,768]{3,2,1,0:T(8,128)(2,1)} %bitcast.5), calls=%async_computation | async-start | bytes 3145728 | tf_op jit(solution)/shard_map/all_to_all | solution.py:973
  47.4 19.5 %collective-permute-start.5 = (bf16[4,48,768]{2,1,0:T(8,128)(2,1)S(1)}, bf16[4,48,768]{2,1,0:T(8,128)(2,1)S(1)}, u32[]{:S(2)}, u32[]{:S(2)}) collective-permute-start(bf16[4,48,768]{2,1,0:T(8,128)(2,1)S(1)} %get-tuple-element.206), channel_id=1, source_target_pairs={{0,4},{4,0},{8,12},{12,8},{16,20},{20,16},{24,28},{28,24},{1,5},{5... | collective-permute-start | bytes 884744 | tf_op jit(solution)/shard_map/ppermute | solution.py:656
  49.3 18.9 %collective-permute-start.2 = (bf16[4,48,768]{2,1,0:T(8,128)(2,1)S(1)}, bf16[4,48,768]{2,1,0:T(8,128)(2,1)S(1)}, u32[]{:S(2)}, u32[]{:S(2)}) collective-permute-start(bf16[4,48,768]{2,1,0:T(8,128)(2,1)S(1)} %get-tuple-element.207), channel_id=1, source_target_pairs={{0,2},{1,3},{2,0},{3,1},{4,6},{5,7},{6,4},{7,5},{8,10},{9,11},{10,... | collective-permute-start | bytes 884744 | tf_op jit(solution)/shard_map/ppermute | solution.py:656
  67.0 14.1 %collective-permute-start.6 = (bf16[8,48,768]{2,1,0:T(8,128)(2,1)S(1)}, bf16[8,48,768]{2,1,0:T(8,128)(2,1)S(1)}, u32[]{:S(2)}, u32[]{:S(2)}) collective-permute-start(bf16[8,48,768]{2,1,0:T(8,128)(2,1)S(1)} %pad_maximum_fusion.4), channel_id=1, source_target_pairs={{0,2},{1,3},{2,0},{3,1},{4,6},{5,7},{6,4},{7,5},{8,10},{9,11},{10,... | collective-permute-start | bytes 1769480 | tf_op jit(solution)/shard_map/ppermute | solution.py:656
  68.3 27.6 %collective-permute-start.3 = (bf16[8,48,768]{2,1,0:T(8,128)(2,1)S(1)}, bf16[8,48,768]{2,1,0:T(8,128)(2,1)S(1)}, u32[]{:S(2)}, u32[]{:S(2)}) collective-permute-start(bf16[8,48,768]{2,1,0:T(8,128)(2,1)S(1)} %pad_maximum_fusion.3), channel_id=1, source_target_pairs={{0,4},{4,0},{8,12},{12,8},{16,20},{20,16},{24,28},{28,24},{1,5},{5... | collective-permute-start | bytes 1769480 | tf_op jit(solution)/shard_map/ppermute | solution.py:656
  81.2 23.4 %copy-start = (bf16[16,48,768]{2,1,0:T(8,128)(2,1)}, bf16[16,48,768]{2,1,0:T(8,128)(2,1)S(1)}, u32[]{:S(2)}) copy-start(bf16[16,48,768]{2,1,0:T(8,128)(2,1)S(1)} %pad_maximum_fusion.1.refs_6_) | copy-start | bytes 3538948
  81.2 23.4 %collective-permute-start.7 = (bf16[16,48,768]{2,1,0:T(8,128)(2,1)S(1)}, bf16[16,48,768]{2,1,0:T(8,128)(2,1)S(1)}, u32[]{:S(2)}, u32[]{:S(2)}) collective-permute-start(bf16[16,48,768]{2,1,0:T(8,128)(2,1)S(1)} %pad_maximum_fusion.1.refs_6_), channel_id=1, source_target_pairs={{0,1},{1,0},{2,3},{3,2},{4,5},{5,4},{6,7},{7,6},{8,9},{9,8},{10,11... | collective-permute-start | bytes 3538952 | tf_op jit(solution)/shard_map/ppermute | solution.py:656
  96.0 8.7 %copy-start.1 = (bf16[16,48,768]{2,1,0:T(8,128)(2,1)}, bf16[16,48,768]{2,1,0:T(8,128)(2,1)S(1)}, u32[]{:S(2)}) copy-start(bf16[16,48,768]{2,1,0:T(8,128)(2,1)S(1)} %pad_maximum_fusion.refs_4_) | copy-start | bytes 3538948
  96.0 8.7 %collective-permute-start.4 = (bf16[16,48,768]{2,1,0:T(8,128)(2,1)S(1)}, bf16[16,48,768]{2,1,0:T(8,128)(2,1)}, u32[]{:S(2)}, u32[]{:S(2)}) collective-permute-start(bf16[16,48,768]{2,1,0:T(8,128)(2,1)S(1)} %pad_maximum_fusion.refs_4_), channel_id=1, source_target_pairs={{0,1},{1,0},{2,3},{3,2},{4,5},{5,4},{6,7},{7,6},{8,9},{9,8},{10,11... | collective-permute-start | bytes 3538952 | tf_op jit(solution)/shard_map/ppermute | solution.py:656
  104.7 1.0 copy-start.2
  176.5 17.3 %collective-permute-start.8 = (bf16[16,192,768]{2,1,0:T(8,128)(2,1)}, bf16[16,192,768]{2,1,0:T(8,128)(2,1)}, u32[]{:S(2)}, u32[]{:S(2)}) collective-permute-start(bf16[16,192,768]{2,1,0:T(8,128)(2,1)} %get-tuple-element.132), channel_id=1, source_target_pairs={{0,1},{1,0},{2,3},{3,2},{4,5},{5,4},{6,7},{7,6},{8,9},{9,8},{10,11... | collective-permute-start | bytes 14155784 | tf_op jit(solution)/shard_map/ppermute | solution.py:656
  176.9 48.0 %all-to-all-start.2 = ((bf16[8,4,32,768]{3,2,1,0:T(8,128)(2,1)}), bf16[8,4,32,768]{3,2,1,0:T(8,128)(2,1)}, u32[]{:S(2)}, u32[]{:S(2)}) async-start(bf16[8,4,32,768]{3,2,1,0:T(8,128)(2,1)} %get-tuple-element.121), calls=%async_computation.2 | async-start | bytes 3145728 | tf_op jit(solution)/shard_map/all_to_all | solution.py:1000
  200.4 27.9 %collective-permute-start.16 = (bf16[2,4,96,768]{3,2,1,0:T(8,128)(2,1)}, bf16[2,4,96,768]{3,2,1,0:T(8,128)(2,1)}, u32[]{:S(2)}, u32[]{:S(2)}) collective-permute-start(bf16[2,4,96,768]{3,2,1,0:T(8,128)(2,1)} %get-tuple-element.136), channel_id=1, source_target_pairs={{0,2},{1,3},{2,0},{3,1},{4,6},{5,7},{6,4},{7,5},{8,10},{9,11},{10,... | collective-permute-start | bytes 3538952 | tf_op jit(solution)/shard_map/ppermute | solution.py:656
  201.0 32.0 %collective-permute-start.17 = (bf16[2,4,96,768]{3,2,1,0:T(8,128)(2,1)}, bf16[2,4,96,768]{3,2,1,0:T(8,128)(2,1)}, u32[]{:S(2)}, u32[]{:S(2)}) collective-permute-start(bf16[2,4,96,768]{3,2,1,0:T(8,128)(2,1)} %get-tuple-element.137), channel_id=1, source_target_pairs={{0,4},{4,0},{8,12},{12,8},{16,20},{20,16},{24,28},{28,24},{1,5},{5... | collective-permute-start | bytes 3538952 | tf_op jit(solution)/shard_map/ppermute | solution.py:656
  214.7 24.2 %collective-permute-start.9 = (bf16[16,96,768]{2,1,0:T(8,128)(2,1)}, bf16[16,96,768]{2,1,0:T(8,128)(2,1)}, u32[]{:S(2)}, u32[]{:S(2)}) collective-permute-start(bf16[16,96,768]{2,1,0:T(8,128)(2,1)} %get-tuple-element.141), channel_id=1, source_target_pairs={{0,1},{1,0},{2,3},{3,2},{4,5},{5,4},{6,7},{7,6},{8,9},{9,8},{10,11... | collective-permute-start | bytes 7077896 | tf_op jit(solution)/shard_map/ppermute | solution.py:656
  236.9 16.6 %collective-permute-start.18 = (bf16[4,96,768]{2,1,0:T(8,128)(2,1)}, bf16[4,96,768]{2,1,0:T(8,128)(2,1)}, u32[]{:S(2)}, u32[]{:S(2)}) collective-permute-start(bf16[4,96,768]{2,1,0:T(8,128)(2,1)} %get-tuple-element.170), channel_id=1, source_target_pairs={{0,4},{4,0},{8,12},{12,8},{16,20},{20,16},{24,28},{28,24},{1,5},{5... | collective-permute-start | bytes 1769480 | tf_op jit(solution)/shard_map/ppermute | solution.py:656
  238.2 16.6 %collective-permute-start.19 = (bf16[4,96,768]{2,1,0:T(8,128)(2,1)}, bf16[4,96,768]{2,1,0:T(8,128)(2,1)}, u32[]{:S(2)}, u32[]{:S(2)}) collective-permute-start(bf16[4,96,768]{2,1,0:T(8,128)(2,1)} %get-tuple-element.172), channel_id=1, source_target_pairs={{0,2},{1,3},{2,0},{3,1},{4,6},{5,7},{6,4},{7,5},{8,10},{9,11},{10,... | collective-permute-start | bytes 1769480 | tf_op jit(solution)/shard_map/ppermute | solution.py:656
  243.5 21.0 %collective-permute-start.10 = (bf16[2,4,48,768]{3,2,1,0:T(8,128)(2,1)}, bf16[2,4,48,768]{3,2,1,0:T(8,128)(2,1)}, u32[]{:S(2)}, u32[]{:S(2)}) collective-permute-start(bf16[2,4,48,768]{3,2,1,0:T(8,128)(2,1)} %get-tuple-element.150), channel_id=1, source_target_pairs={{0,2},{1,3},{2,0},{3,1},{4,6},{5,7},{6,4},{7,5},{8,10},{9,11},{10,... | collective-permute-start | bytes 1769480 | tf_op jit(solution)/shard_map/ppermute | solution.py:656
  244.8 19.7 %collective-permute-start.11 = (bf16[2,4,48,768]{3,2,1,0:T(8,128)(2,1)}, bf16[2,4,48,768]{3,2,1,0:T(8,128)(2,1)}, u32[]{:S(2)}, u32[]{:S(2)}) collective-permute-start(bf16[2,4,48,768]{3,2,1,0:T(8,128)(2,1)} %get-tuple-element.152), channel_id=1, source_target_pairs={{0,4},{4,0},{8,12},{12,8},{16,20},{20,16},{24,28},{28,24},{1,5},{5... | collective-permute-start | bytes 1769480 | tf_op jit(solution)/shard_map/ppermute | solution.py:656
  257.5 25.6 %collective-permute-start.20 = (bf16[2,192,768]{2,1,0:T(8,128)(2,1)}, bf16[2,192,768]{2,1,0:T(8,128)(2,1)}, u32[]{:S(2)}, u32[]{:S(2)}) collective-permute-start(bf16[2,192,768]{2,1,0:T(8,128)(2,1)} %get-tuple-element.174), channel_id=1, source_target_pairs={{0,8},{4,12},{8,0},{12,4},{16,24},{20,28},{24,16},{28,20},{1,9},{5... | collective-permute-start | bytes 1769480 | tf_op jit(solution)/shard_map/ppermute | solution.py:656
  259.9 10.3 %copy-start.11 = (f32[8,768]{1,0:T(8,128)S(1)}, f32[8,768]{1,0:T(8,128)}, u32[]{:S(2)}) copy-start(f32[8,768]{1,0:T(8,128)} %get-tuple-element.179) | copy-start | bytes 73732
  259.9 11.6 %copy-start.10 = (f32[1,3072]{1,0:T(1,128)S(1)}, f32[1,3072]{1,0:T(1,128)}, u32[]{:S(2)}) copy-start(f32[1,3072]{1,0:T(1,128)} %get-tuple-element.180) | copy-start | bytes 36868
  259.9 13.0 %copy-start.12 = (f32[1,768]{1,0:T(1,128)S(1)}, f32[1,768]{1,0:T(1,128)}, u32[]{:S(2)}) copy-start(f32[1,768]{1,0:T(1,128)} %get-tuple-element.181) | copy-start | bytes 9220
  267.2 12.0 %collective-permute-start.12 = (bf16[4,48,768]{2,1,0:T(8,128)(2,1)}, bf16[4,48,768]{2,1,0:T(8,128)(2,1)}, u32[]{:S(2)}, u32[]{:S(2)}) collective-permute-start(bf16[4,48,768]{2,1,0:T(8,128)(2,1)} %get-tuple-element.156), channel_id=1, source_target_pairs={{0,4},{4,0},{8,12},{12,8},{16,20},{20,16},{24,28},{28,24},{1,5},{5... | collective-permute-start | bytes 884744 | tf_op jit(solution)/shard_map/ppermute | solution.py:656
  268.9 10.4 %collective-permute-start.13 = (bf16[4,48,768]{2,1,0:T(8,128)(2,1)}, bf16[4,48,768]{2,1,0:T(8,128)(2,1)}, u32[]{:S(2)}, u32[]{:S(2)}) collective-permute-start(bf16[4,48,768]{2,1,0:T(8,128)(2,1)} %get-tuple-element.158), channel_id=1, source_target_pairs={{0,2},{1,3},{2,0},{3,1},{4,6},{5,7},{6,4},{7,5},{8,10},{9,11},{10,... | collective-permute-start | bytes 884744 | tf_op jit(solution)/shard_map/ppermute | solution.py:656
  273.8 13.6 %all-to-all-start.3 = ((f32[32,3,96]{2,1,0:T(4,128)}), f32[32,3,96]{2,1,0:T(4,128)S(1)}, u32[]{:S(2)}, u32[]{:S(2)}) async-start(f32[32,3,96]{2,1,0:T(4,128)} %copy.52), calls=%async_computation.3 | async-start | bytes 131072 | tf_op jit(solution)/shard_map/all_to_all | solution.py:1020
  281.3 13.4 %collective-permute-start.14 = (bf16[2,96,768]{2,1,0:T(8,128)(2,1)}, bf16[2,96,768]{2,1,0:T(8,128)(2,1)}, u32[]{:S(2)}, u32[]{:S(2)}) collective-permute-start(bf16[2,96,768]{2,1,0:T(8,128)(2,1)} %get-tuple-element.160), channel_id=1, source_target_pairs={{0,8},{4,12},{8,0},{12,4},{16,24},{20,28},{24,16},{28,20},{1,9},{5... | collective-permute-start | bytes 884744 | tf_op jit(solution)/shard_map/ppermute | solution.py:656
  285.3 20.6 %collective-permute-start.21 = (bf16[192,768]{1,0:T(8,128)(2,1)}, bf16[192,768]{1,0:T(8,128)(2,1)}, u32[]{:S(2)}, u32[]{:S(2)}) collective-permute-start(bf16[192,768]{1,0:T(8,128)(2,1)} %get-tuple-element.176), channel_id=1, source_target_pairs={{0,16},{4,20},{8,24},{12,28},{16,0},{20,4},{24,8},{28,12},{1,17},{... | collective-permute-start | bytes 884744 | tf_op jit(solution)/shard_map/ppermute | solution.py:656
  296.6 11.9 %collective-permute-start.15 = (bf16[96,768]{1,0:T(8,128)(2,1)}, bf16[96,768]{1,0:T(8,128)(2,1)}, u32[]{:S(2)}, u32[]{:S(2)}) collective-permute-start(bf16[96,768]{1,0:T(8,128)(2,1)} %get-tuple-element.162), channel_id=1, source_target_pairs={{0,16},{4,20},{8,24},{12,28},{16,0},{20,4},{24,8},{28,12},{1,17},{... | collective-permute-start | bytes 442376 | tf_op jit(solution)/shard_map/ppermute | solution.py:656
  309.0 6.0 %copy-start.8 = (f32[768]{0:T(1024)S(1)}, f32[768]{0:T(1024)}, u32[]{:S(2)}) copy-start(f32[768]{0:T(1024)} %get-tuple-element.211) | copy-start | bytes 9220
  310.8 11.3 %all-to-all-start.4 = ((f32[32,1,128]{2,1,0:T(1,128)}), f32[32,1,128]{2,1,0:T(1,128)S(1)}, u32[]{:S(2)}, u32[]{:S(2)}) async-start(f32[32,1,128]{2,1,0:T(1,128)} %get-tuple-element.183), calls=%async_computation.4 | async-start | bytes 32768 | tf_op jit(solution)/shard_map/all_to_all | solution.py:1058
  322.1 0.6 copy-start.9
Sparse Core Ops, SparseCore 0:
  11.5 111.5 all-gather.2

commit v6 on v5

--- a/solution.py
+++ b/solution.py
@@ -914,6 +914,8 @@
     vec_shares = lax.all_to_all(vector_copies, both, split_axis=0, concat_axis=0, tiled=True)
     vec = vec_shares.reshape(dp_size, fsdp_size, vec_rows, vec_cols).transpose(1, 2, 0, 3)
     vec = vec.reshape(fsdp_size * vec_rows, model_width).astype(F32)
+    value_bias = vec[2].reshape(model_width, 1)
+    up_bias = vec[6:10].reshape(1, ff_width)
 
     my_block = lax.axis_index(DP)
     places = visible_index[0].reshape(chips_group, block_count, block_seen)
@@ -935,7 +937,8 @@
         share_d = jnp.concatenate([down_turned[:half], down_turned[half:]], axis=1)
         cut = rows // 2
         cur = grow(grow(share_q[None], Z_FAR, cot_seen), Z_NEAR)
-        q_upper, q_lower = grow(cur[:, :cut], XS, vec_shares), grow(cur[:, cut:], YS, vec_shares)
+        early = vec, value_bias, up_bias, me
+        q_upper, q_lower = grow(cur[:, :cut], XS, *early), grow(cur[:, cut:], YS, *early)
         q_upper, q_lower = grow(q_upper, YS), grow(q_lower, XS)
         q_arrays = (q_upper, swap(q_upper, *CORE), q_lower, swap(q_lower, *CORE))
         q_table = (
@@ -975,8 +978,6 @@
         grad = grad.transpose(1, 0, 2, 3).reshape(1, chip_count, seq_len, model_width)
 
     x = tokens[0]
-    up_bias = vec[6:10].reshape(1, ff_width)
-    value_bias = vec[2].reshape(model_width, 1)
     normed, mixed, expo, share, context, qkv_whole, out_whole = attend_forward(
         me, x, vec, value_bias, q_table, q_arrays, load_rows, wide
     )

time: 335 us -> 329 us (0.982)
  local copies, waits for them, and re-layouts: 16.7 us -> 12.6 us
  waiting for transfers between devices: 90.6 us -> 86.8 us
    ppermute x22, waiting for transfers between devices: 86.9 us -> 75.4 us  [swap(): return lax.ppermute(value, axis, [(i, i ^ bit) for i in range(size)])]
    all_gather x1, waiting for transfers between devices: 0.02 us -> 10.5 us  [on_device(): lax.all_gather(jnp.concatenate([share_u, share_d]), both, axis=0, tiled=F...]
    ppermute x22, starting transfers between devices: 28.3 us -> 32.9 us  [swap(): return lax.ppermute(value, axis, [(i, i ^ bit) for i in range(size)])]
  transfers between devices with their start and end apart: 28 -> 28, of which waited for: 14 -> 14; matrix products, arithmetic and copies ran while one was open for 8% -> 6% of each run, Pallas kernels for 25% -> 26%
where the time goes in v6:
time: 329 us; the launch traced here: 327 us
  Pallas kernels  144 us (44%)
  waiting for transfers between devices  86.8 us (26%)
  starting transfers between devices  55.6 us (17%)
  between operations  14.5 us (4%)
  local copies, waits for them, and re-layouts  12.6 us (4%)
  other arithmetic  8.05 us (2%)
  matrix products  6.19 us (2%)
    ppermute x22, waiting for transfers between devices, swap(): return lax.ppermute(value, axis, [(i, i ^ bit) for i in range(size)])  75.4 us
    pallas_call x1, Pallas kernels, feed_forward_back(): pl.pallas_call(functools.partial(feed_body, u_table, d_table, rows, share...  36.8 us
    ppermute x22, starting transfers between devices, swap(): return lax.ppermute(value, axis, [(i, i ^ bit) for i in range(size)])  32.9 us
    pallas_call x8, Pallas kernels, fold_call(): pl.pallas_call(functools.partial(fold_body, plan, len(pairs)), grid=(step...  26.4 us
    pallas_call x1, Pallas kernels, attend_forward(): pl.pallas_call(functools.partial(attend_body, table, rows, heads, wide),...  17.4 us
    pallas_call x1, Pallas kernels, feed_grads(): pl.pallas_call(functools.partial(feed_grad_body, order, rows, half, wide)...  16.4 us
    pallas_call x1, Pallas kernels, qkv_grads(): pl.pallas_call(functools.partial(qkv_grad_body, order, rows), grid=(share...  11.7 us
    pallas_call x1, Pallas kernels, attend_back(): pl.pallas_call(functools.partial(attend_back_body, heads), grid=(chips,),...  11.3 us
  transfers between devices with their start and end apart: 28, of which 14 were waited for; matrix products, arithmetic and copies ran while one was open for 6% of the time, Pallas kernels for 26%

profile of v6, /device:TPU:0, one launch (start us, length us, event | category | flops | bytes accessed | tf_op | source)
XLA Modules:
  0.0 327.4 jit_solution(9716616969499803827)
XLA Ops:
  11.5 4.0 %collective-permute-start = (bf16[1,96,768]{2,1,0:T(8,128)(2,1)}, bf16[1,96,768]{2,1,0:T(8,128)(2,1)}, u32[]{:S(2)}, u32[]{:S(2)}) collective-permute-start(bf16[1,96,768]{2,1,0:T(8,128)(2,1)} %pad_maximum_fusion.6), channel_id=1, source_target_pairs={{0,16},{4,20},{8,24},{12,28},{16,0},{20,4},{24,8},{28,12},{1,17},{... | collective-permute-start | bytes 442376 | tf_op jit(solution)/shard_map/ppermute | solution.py:656
  16.2 4.0 %all-to-all-start.1 = ((bf16[32,3,96]{2,1,0:T(4,128)(2,1)}), bf16[32,3,96]{2,1,0:T(4,128)(2,1)}, u32[]{:S(2)}, u32[]{:S(2)}) async-start(bf16[32,3,96]{2,1,0:T(4,128)(2,1)} %broadcast_in_dim.19), calls=%async_computation.1 | async-start | bytes 65536 | tf_op jit(solution)/shard_map/all_to_all | solution.py:914
  21.6 5.4 %seen_rows.1 = (bf16[32,32,768]{2,1,0:T(8,128)(2,1)}, f32[1,768]{1,0:T(1,128)}) custom-call(bf16[32,128,768]{2,1,0:T(8,128)(2,1)} %bitcast.70, bf16[32,128,768]{2,1,0:T(8,128)(2,1)} %bitcast.71, bf16[32,128,768]{2,1,0:T(8,128)(2,1)} %bitcast.72, bf16[32,128,768]{2,1,0:T(8,128)(2,1)} %bitcast.73, s32[32,48,1]{2,1,0:T(8,128)} %copy.47.refs_4_), custom_call_target="tpu_custom_call" | custom-call | flops 8000000000 | bytes 24000000 | tf_op jit(solution)/shard_map/seen_rows/pallas_call | solution.py:139
  27.9 1.8 collective-permute-start.1
  30.3 4.8 %all-to-all-start = ((bf16[8,4,32,768]{3,2,1,0:T(8,128)(2,1)}), bf16[8,4,32,768]{3,2,1,0:T(8,128)(2,1)}, u32[]{:S(2)}, u32[]{:S(2)}) async-start(bf16[8,4,32,768]{3,2,1,0:T(8,128)(2,1)} %bitcast.56), calls=%async_computation | async-start | bytes 3145728 | tf_op jit(solution)/shard_map/all_to_all | solution.py:976
  35.9 4.6 %collective-permute-done.1 = bf16[2,96,768]{2,1,0:T(8,128)(2,1)S(1)} collective-permute-done((bf16[2,96,768]{2,1,0:T(8,128)(2,1)S(1)}, bf16[2,96,768]{2,1,0:T(8,128)(2,1)S(1)}, u32[]{:S(2)}, u32[]{:S(2)}) %collective-permute-start.1) | collective-permute-done | bytes 294944 | tf_op jit(solution)/shard_map/ppermute | solution.py:656
  41.6 4.6 %collective-permute-start.5 = (bf16[4,48,768]{2,1,0:T(8,128)(2,1)S(1)}, bf16[4,48,768]{2,1,0:T(8,128)(2,1)S(1)}, u32[]{:S(2)}, u32[]{:S(2)}) collective-permute-start(bf16[4,48,768]{2,1,0:T(8,128)(2,1)S(1)} %get-tuple-element.206), channel_id=1, source_target_pairs={{0,4},{4,0},{8,12},{12,8},{16,20},{20,16},{24,28},{28,24},{1,5},{5... | collective-permute-start | bytes 884744 | tf_op jit(solution)/shard_map/ppermute | solution.py:656
  49.4 12.0 %collective-permute-done.5 = bf16[4,48,768]{2,1,0:T(8,128)(2,1)S(1)} collective-permute-done((bf16[4,48,768]{2,1,0:T(8,128)(2,1)S(1)}, bf16[4,48,768]{2,1,0:T(8,128)(2,1)S(1)}, u32[]{:S(2)}, u32[]{:S(2)}) %collective-permute-start.5) | collective-permute-done | bytes 294944 | tf_op jit(solution)/shard_map/ppermute | solution.py:656
  61.4 1.5 collective-permute-start.6
  63.0 2.5 collective-permute-start.3
  65.5 11.0 %collective-permute-done.6 = bf16[8,48,768]{2,1,0:T(8,128)(2,1)S(1)} collective-permute-done((bf16[8,48,768]{2,1,0:T(8,128)(2,1)S(1)}, bf16[8,48,768]{2,1,0:T(8,128)(2,1)S(1)}, u32[]{:S(2)}, u32[]{:S(2)}) %collective-permute-start.6) | collective-permute-done | bytes 589856 | tf_op jit(solution)/shard_map/ppermute | solution.py:656
  77.7 7.4 %collective-permute-done.3 = bf16[8,48,768]{2,1,0:T(8,128)(2,1)S(1)} collective-permute-done((bf16[8,48,768]{2,1,0:T(8,128)(2,1)S(1)}, bf16[8,48,768]{2,1,0:T(8,128)(2,1)S(1)}, u32[]{:S(2)}, u32[]{:S(2)}) %collective-permute-start.3) | collective-permute-done | bytes 589856 | tf_op jit(solution)/shard_map/ppermute | solution.py:656
  85.3 1.7 copy.50.refs_3_
  86.9 2.6 collective-permute-done.4.refs_5_
  89.5 17.4 %attend_forward.1 = (bf16[768,1024]{1,0:T(8,128)(2,1)}, bf16[2304,1024]{1,0:T(8,128)(2,1)}, bf16[4,12,256,256]{3,2,1,0:T(8,128)(2,1)}, f32[12,1024]{1,0:T(8,128)...) custom-call(s32[2]{0:T(128)} %pad_add_fusion.refs_0_.me_ref, ...), custom_call_target="tpu_custom_call" | custom-call | flops 1000000000 | bytes 3000000 | tf_op jit(solution)/shard_map/attend_forward/pallas_call | solution.py:222
  106.9 10.5 %all-gather.3.cloned.1.call-done = bf16[6144,768]{1,0:T(8,128)(2,1)} async-done(((bf16[192,768]{1,0:T(8,128)(2,1)}), bf16[6144,768]{1,0:T(8,128)(2,1)}) %all-gather.3.cloned.1.call-update) | async-done | bytes 9437200 | tf_op jit(solution)/shard_map/all_gather | solution.py:950
  117.4 36.8 %feed_forward_back.1 = (bf16[8,4,32,768]{3,2,1,0:T(8,128)(2,1)}, bf16[1024,768]{1,0:T(8,128)(2,1)}, bf16[1024,3072]{1,0:T(8,128)(2,1)}, bf16[1024,3072]{1,0:T(8,...) custom-call(s32[2]{0:T(128)} %pad_add_fusion.refs_0_.me_ref, ...), custom_call_target="tpu_custom_call" | custom-call | flops 10000000000 | bytes 30000000 | tf_op jit(solution)/shard_map/feed_forward_back/pallas_call | solution.py:363
  154.2 16.4 %feed_grads.1 = (bf16[16,192,768]{2,1,0:T(8,128)(2,1)}, bf16[16,192,768]{2,1,0:T(8,128)(2,1)}) custom-call(s32[2]{0:T(128)} %pad_add_fusion.refs_0_.me_ref, bf16[1024,768]{1,0:T(8,128)(2,1)} %get-tuple-element.123.normed_ref, bf16[1024,3072]{1,0:T(8,128)(2,1)} %get-tuple-element.124.gate_grad_ref, bf16[1024,768]{1,0:T(8,128)(2,1)} %get-tuple-element.125.feed_grad_ref, ...), custom_call_target="tpu_custom_call" | custom-call | flops 1000000000 | bytes 3000000 | tf_op jit(solution)/shard_map/feed_grads/pallas_call | solution.py:576
  171.0 4.3 %all-to-all-start.2 = ((bf16[8,4,32,768]{3,2,1,0:T(8,128)(2,1)}), bf16[8,4,32,768]{3,2,1,0:T(8,128)(2,1)}, u32[]{:S(2)}, u32[]{:S(2)}) async-start(bf16[8,4,32,768]{3,2,1,0:T(8,128)(2,1)} %get-tuple-element.121), calls=%async_computation.2 | async-start | bytes 3145728 | tf_op jit(solution)/shard_map/all_to_all | solution.py:1001
  175.3 11.3 %attend_back.1 = (bf16[2304,1024]{1,0:T(8,128)(2,1)}, f32[8,768]{1,0:T(8,128)}) custom-call(bf16[2304,1024]{1,0:T(8,128)(2,1)} %get-tuple-element.128.mixed_ref, bf16[4,12,256,256]{3,2,1,0:T(8,128)(2,1)} %get-tuple-element.129.expo_ref, f32[12,1024]{1,0:T(8,128)} %get-tuple-element.130.share_ref, bf16[768,1024]{1,0:T(8,128)(2,1)} %get-tuple-element.133.grad_ref), custom_call_target="tpu_custom_call" | custom-call | flops 1000000000 | bytes 3000000 | tf_op jit(solution)/shard_map/attend_back/pallas_call | solution.py:446
  186.6 6.5 %fold_sums.8 = (bf16[2,4,96,768]{3,2,1,0:T(8,128)(2,1)}, bf16[2,4,96,768]{3,2,1,0:T(8,128)(2,1)}, bf16[2,4,96,768]{3,2,1,0:T(8,128)(2,1)}, bf16[2,4,96,768]{3,2,1,0:T(8,128)(2,1)}) custom-call(bf16[2,2,4,192,768]{4,3,2,1,0:T(8,128)(2,1)} %bitcast.55, bf16[2,2,4,192,768]{4,3,2,1,0:T(8,128)(2,1)} %bitcast.17.refs_1_), custom_call_target="tpu_custom_call" | custom-call | flops 2000000000 | bytes 6000000 | tf_op jit(solution)/shard_map/fold_sums/pallas_call | solution.py:688
  194.5 1.9 collective-permute-start.17
  196.4 11.7 %qkv_grads.1 = (bf16[16,96,768]{2,1,0:T(8,128)(2,1)}, bf16[16,96,768]{2,1,0:T(8,128)(2,1)}) custom-call(s32[2]{0:T(128)} %pad_add_fusion.refs_0_.me_ref, bf16[768,1024]{1,0:T(8,128)(2,1)} %get-tuple-element.138.normed_ref, bf16[2304,1024]{1,0:T(8,128)(2,1)} %get-tuple-element.134.mixed_grad_ref, bf16[768,1024]{1,0:T(8,128)(2,1)} %get-tuple-element.119.refs_3_.context_ref, ...), custom_call_target="tpu_custom_call" | custom-call | flops 1000000000 | bytes 3000000 | tf_op jit(solution)/shard_map/qkv_grads/pallas_call | solution.py:632
  208.2 10.1 %tokens_back.1 = (f32[4,256,768]{2,1,0:T(8,128)}, f32[8,768]{1,0:T(8,128)}) custom-call(bf16[4,256,768]{2,1,0:T(8,128)(2,1)} %bitcast.59, f32[4,256,768]{2,1,0:T(8,128)} %get-tuple-element.143.grad_ref, bf16[2304,1024]{1,0:T(8,128)(2,1)} %get-tuple-element.134.mixed_grad_ref, f32[12,768]{1,0:T(8,128)} %copy-done.5, bf16[2304,768]{1,0:T(8,128)(2,1)} %get-tuple-element.144.qkv_ref), custom_call_target="tpu_custom_call" | custom-call | flops 24999999488 | bytes 75000000 | tf_op jit(solution)/shard_map/tokens_back/pallas_call | solution.py:481
  218.3 3.3 collective-permute-done.16.refs_1_
  221.6 5.3 %collective-permute-done.17.refs_3_ = bf16[2,4,96,768]{3,2,1,0:T(8,128)(2,1)} collective-permute-done((bf16[2,4,96,768]{3,2,1,0:T(8,128)(2,1)}, bf16[2,4,96,768]{3,2,1,0:T(8,128)(2,1)}, u32[]{:S(2)}, u32[]{:S(2)}) %collective-permute-start.17) | collective-permute-done | bytes 1179680 | tf_op jit(solution)/shard_map/ppermute | solution.py:656
  226.9 3.9 %fold_sums.13 = (bf16[4,96,768]{2,1,0:T(8,128)(2,1)}, bf16[4,96,768]{2,1,0:T(8,128)(2,1)}, bf16[4,96,768]{2,1,0:T(8,128)(2,1)}, bf16[4,96,768]{2,1,0:T(8,128)(2,1)}) custom-call(bf16[2,4,96,768]{3,2,1,0:T(8,128)(2,1)} %get-tuple-element.165.refs_0_, bf16[2,4,96,768]{3,2,1,0:T(8,128)(2,1)} %collective-permute-done.16.refs_1_, ...), custom_call_target="tpu_custom_call" | custom-call | flops 2000000000 | bytes 6000000 | tf_op jit(solution)/shard_map/fold_sums/pallas_call | solution.py:688
  232.0 4.6 %fold_sums.9 = (bf16[2,4,48,768]{3,2,1,0:T(8,128)(2,1)}, bf16[2,4,48,768]{3,2,1,0:T(8,128)(2,1)}, bf16[2,4,48,768]{3,2,1,0:T(8,128)(2,1)}, bf16[2,4,48,768]{3,2,1,0:T(8,128)(2,1)}) custom-call(bf16[2,2,4,96,768]{4,3,2,1,0:T(8,128)(2,1)} %bitcast.74, bf16[2,2,4,96,768]{4,3,2,1,0:T(8,128)(2,1)} %bitcast.20.refs_1_), custom_call_target="tpu_custom_call" | custom-call | flops 2000000000 | bytes 6000000 | tf_op jit(solution)/shard_map/fold_sums/pallas_call | solution.py:688
  238.0 1.5 collective-permute-start.11
  239.4 7.9 %collective-permute-done.18 = bf16[4,96,768]{2,1,0:T(8,128)(2,1)} collective-permute-done((bf16[4,96,768]{2,1,0:T(8,128)(2,1)}, bf16[4,96,768]{2,1,0:T(8,128)(2,1)}, u32[]{:S(2)}, u32[]{:S(2)}) %collective-permute-start.18) | collective-permute-done | bytes 589856 | tf_op jit(solution)/shard_map/ppermute | solution.py:656
  247.9 2.8 fold_sums.14
  250.7 2.7 collective-permute-start.20
  253.5 5.2 %collective-permute-done.10.refs_1_ = bf16[2,4,48,768]{3,2,1,0:T(8,128)(2,1)} collective-permute-done((bf16[2,4,48,768]{3,2,1,0:T(8,128)(2,1)}, bf16[2,4,48,768]{3,2,1,0:T(8,128)(2,1)}, u32[]{:S(2)}, u32[]{:S(2)}) %collective-permute-start.10) | collective-permute-done | bytes 589856 | tf_op jit(solution)/shard_map/ppermute | solution.py:656
  258.6 2.7 fold_sums.10
  261.3 1.7 collective-permute-start.12
  267.2 5.5 %all-to-all-start.3 = ((f32[32,3,96]{2,1,0:T(4,128)}), f32[32,3,96]{2,1,0:T(4,128)S(1)}, u32[]{:S(2)}, u32[]{:S(2)}) async-start(f32[32,3,96]{2,1,0:T(4,128)} %copy.52), calls=%async_computation.3 | async-start | bytes 131072 | tf_op jit(solution)/shard_map/all_to_all | solution.py:1021
  272.8 2.1 fold_sums.11
  274.9 1.9 collective-permute-start.14
  276.8 2.1 fold_sums.15
  278.9 2.1 collective-permute-start.21
  281.6 6.7 %collective-permute-done.14.refs_1_ = bf16[2,96,768]{2,1,0:T(8,128)(2,1)} collective-permute-done((bf16[2,96,768]{2,1,0:T(8,128)(2,1)}, bf16[2,96,768]{2,1,0:T(8,128)(2,1)}, u32[]{:S(2)}, u32[]{:S(2)}) %collective-permute-start.14) | collective-permute-done | bytes 294944 | tf_op jit(solution)/shard_map/ppermute | solution.py:656
  288.3 1.8 fold_sums.12
  290.6 8.9 %collective-permute-done.21.arrived_ref = bf16[192,768]{1,0:T(8,128)(2,1)} collective-permute-done((bf16[192,768]{1,0:T(8,128)(2,1)}, bf16[192,768]{1,0:T(8,128)(2,1)}, u32[]{:S(2)}, u32[]{:S(2)}) %collective-permute-start.21) | collective-permute-done | bytes 294944 | tf_op jit(solution)/shard_map/ppermute | solution.py:656
  300.0 2.0 last_sum.2
  302.6 1.8 last_sum.3
  304.4 4.2 %all-to-all-start.4 = ((f32[32,1,128]{2,1,0:T(1,128)}), f32[32,1,128]{2,1,0:T(1,128)S(1)}, u32[]{:S(2)}, u32[]{:S(2)}) async-start(f32[32,1,128]{2,1,0:T(1,128)} %get-tuple-element.183), calls=%async_computation.4 | async-start | bytes 32768 | tf_op jit(solution)/shard_map/all_to_all | solution.py:1059
  308.6 6.2 %fusion = bf16[1,32,128,768]{3,2,1,0:T(8,128)(2,1)} fusion(f32[768]{0:T(1024)S(1)} %copy-done.9, f32[32,128]{1,0:T(8,128)S(1)} %broadcast_subtract_fusion, bf16[32,32,768]{2,1,0:T(8,128)(2,1)} %bitcast.14, s32[32,32]{1,0:T(8,128)S(1)} %bitcast.63), kind=kOutput, calls=%fused_computation.1 | convolution fusion | flops 210894848 | bytes 7887872 | tf_op jit(solution)/shard_map/cpv,cvd->cpd/dot_general | solution.py:1026
  316.3 4.2 %adam_all.1 = (f32[96,576]{1,0:T(8,128)}, f32[96,576]{1,0:T(8,128)}, f32[96,576]{1,0:T(8,128)}, bf16[96,576]{1,0:T(8,128)(2,1)}, f32[96,192]{1,0:T(8,128)}, /*in...) custom-call(f32[32,1,128]{2,1,0:T(1,128)} %copy-done.10, ...), custom_call_target="tpu_custom_call" | custom-call | flops 4000000000 | bytes 12000000 | tf_op jit(solution)/shard_map/adam_all/pallas_call | solution.py:824
  (103 shorter events, 27.1 us)
Async XLA Ops:
  7.2 3.0 copy-start.7
  7.2 3.0 copy-start.6
  7.2 8.4 %copy-start.14 = (f32[3,96]{1,0:T(4,128)S(1)}, f32[3,96]{1,0:T(4,128)}, u32[]{:S(2)}) copy-start(f32[3,96]{1,0:T(4,128)} %refs_16_.1) | copy-start | bytes 3460
  7.2 13.0 %copy-start.8 = (s32[1,32,256]{2,1,0:T(8,128)S(1)}, s32[1,32,256]{2,1,0:T(8,128)}, u32[]{:S(2)}) copy-start(s32[1,32,256]{2,1,0:T(8,128)} %param.19) | copy-start | bytes 98308
  7.2 110.1 %all-gather.3.cloned.1.call-start = ((), (), s32[]{:S(2)}) async-start(), calls=%async_computation.5 | async-start | bytes 9732096 | tf_op jit(solution)/shard_map/all_gather | solution.py:950
  10.2 0.6 copy-start.3
  11.5 15.4 %collective-permute-start = (bf16[1,96,768]{2,1,0:T(8,128)(2,1)}, bf16[1,96,768]{2,1,0:T(8,128)(2,1)}, u32[]{:S(2)}, u32[]{:S(2)}) collective-permute-start(bf16[1,96,768]{2,1,0:T(8,128)(2,1)} %pad_maximum_fusion.6), channel_id=1, source_target_pairs={{0,16},{4,20},{8,24},{12,28},{16,0},{20,4},{24,8},{28,12},{1,17},{... | collective-permute-start | bytes 442376 | tf_op jit(solution)/shard_map/ppermute | solution.py:656
  16.2 14.1 %all-to-all-start.1 = ((bf16[32,3,96]{2,1,0:T(4,128)(2,1)}), bf16[32,3,96]{2,1,0:T(4,128)(2,1)}, u32[]{:S(2)}, u32[]{:S(2)}) async-start(bf16[32,3,96]{2,1,0:T(4,128)(2,1)} %broadcast_in_dim.19), calls=%async_computation.1 | async-start | bytes 65536 | tf_op jit(solution)/shard_map/all_to_all | solution.py:914
  27.9 12.6 %collective-permute-start.1 = (bf16[2,96,768]{2,1,0:T(8,128)(2,1)S(1)}, bf16[2,96,768]{2,1,0:T(8,128)(2,1)S(1)}, u32[]{:S(2)}, u32[]{:S(2)}) collective-permute-start(bf16[2,96,768]{2,1,0:T(8,128)(2,1)S(1)} %pad_maximum_fusion.5), channel_id=1, source_target_pairs={{0,8},{4,12},{8,0},{12,4},{16,24},{20,28},{24,16},{28,20},{1,9},{5... | collective-permute-start | bytes 884744 | tf_op jit(solution)/shard_map/ppermute | solution.py:656
  30.3 10.2 %copy-start.4 = (bf16[1,96,192]{2,1,0:T(8,128)(2,1)S(1)}, bf16[1,96,192]{2,1,0:T(8,128)(2,1)}, u32[]{:S(2)}) copy-start(bf16[1,96,192]{2,1,0:T(8,128)(2,1)} %copy-done.3) | copy-start | bytes 110596
  30.3 76.6 %all-to-all-start = ((bf16[8,4,32,768]{3,2,1,0:T(8,128)(2,1)}), bf16[8,4,32,768]{3,2,1,0:T(8,128)(2,1)}, u32[]{:S(2)}, u32[]{:S(2)}) async-start(bf16[8,4,32,768]{3,2,1,0:T(8,128)(2,1)} %bitcast.56), calls=%async_computation | async-start | bytes 3145728 | tf_op jit(solution)/shard_map/all_to_all | solution.py:976
  35.9 25.5 %copy-start.5 = (f32[12,768]{1,0:T(8,128)}, f32[12,768]{1,0:T(8,128)S(1)}, u32[]{:S(2)}) copy-start(f32[12,768]{1,0:T(8,128)S(1)} %reshape.163.refs_2_.refs_4_.vec_ref) | copy-start | bytes 110596
  41.6 19.8 %collective-permute-start.5 = (bf16[4,48,768]{2,1,0:T(8,128)(2,1)S(1)}, bf16[4,48,768]{2,1,0:T(8,128)(2,1)S(1)}, u32[]{:S(2)}, u32[]{:S(2)}) collective-permute-start(bf16[4,48,768]{2,1,0:T(8,128)(2,1)S(1)} %get-tuple-element.206), channel_id=1, source_target_pairs={{0,4},{4,0},{8,12},{12,8},{16,20},{20,16},{24,28},{28,24},{1,5},{5... | collective-permute-start | bytes 884744 | tf_op jit(solution)/shard_map/ppermute | solution.py:656
  46.8 16.1 %collective-permute-start.2 = (bf16[4,48,768]{2,1,0:T(8,128)(2,1)S(1)}, bf16[4,48,768]{2,1,0:T(8,128)(2,1)S(1)}, u32[]{:S(2)}, u32[]{:S(2)}) collective-permute-start(bf16[4,48,768]{2,1,0:T(8,128)(2,1)S(1)} %get-tuple-element.207), channel_id=1, source_target_pairs={{0,2},{1,3},{2,0},{3,1},{4,6},{5,7},{6,4},{7,5},{8,10},{9,11},{10,... | collective-permute-start | bytes 884744 | tf_op jit(solution)/shard_map/ppermute | solution.py:656
  61.4 15.1 %collective-permute-start.6 = (bf16[8,48,768]{2,1,0:T(8,128)(2,1)S(1)}, bf16[8,48,768]{2,1,0:T(8,128)(2,1)S(1)}, u32[]{:S(2)}, u32[]{:S(2)}) collective-permute-start(bf16[8,48,768]{2,1,0:T(8,128)(2,1)S(1)} %pad_maximum_fusion.4), channel_id=1, source_target_pairs={{0,2},{1,3},{2,0},{3,1},{4,6},{5,7},{6,4},{7,5},{8,10},{9,11},{10,... | collective-permute-start | bytes 1769480 | tf_op jit(solution)/shard_map/ppermute | solution.py:656
  63.0 22.1 %collective-permute-start.3 = (bf16[8,48,768]{2,1,0:T(8,128)(2,1)S(1)}, bf16[8,48,768]{2,1,0:T(8,128)(2,1)S(1)}, u32[]{:S(2)}, u32[]{:S(2)}) collective-permute-start(bf16[8,48,768]{2,1,0:T(8,128)(2,1)S(1)} %pad_maximum_fusion.3), channel_id=1, source_target_pairs={{0,4},{4,0},{8,12},{12,8},{16,20},{20,16},{24,28},{28,24},{1,5},{5... | collective-permute-start | bytes 1769480 | tf_op jit(solution)/shard_map/ppermute | solution.py:656
  76.6 1.0 copy-start
  77.7 9.3 %collective-permute-start.7 = (bf16[16,48,768]{2,1,0:T(8,128)(2,1)S(1)}, bf16[16,48,768]{2,1,0:T(8,128)(2,1)S(1)}, u32[]{:S(2)}, u32[]{:S(2)}) collective-permute-start(bf16[16,48,768]{2,1,0:T(8,128)(2,1)S(1)} %pad_maximum_fusion.1.refs_6_), channel_id=1, source_target_pairs={{0,1},{1,0},{2,3},{3,2},{4,5},{5,4},{6,7},{7,6},{8,9},{9,8},{10,11... | collective-permute-start | bytes 3538952 | tf_op jit(solution)/shard_map/ppermute | solution.py:656
  85.2 1.8 copy-start.1
  85.2 4.3 %collective-permute-start.4 = (bf16[16,48,768]{2,1,0:T(8,128)(2,1)S(1)}, bf16[16,48,768]{2,1,0:T(8,128)(2,1)}, u32[]{:S(2)}, u32[]{:S(2)}) collective-permute-start(bf16[16,48,768]{2,1,0:T(8,128)(2,1)S(1)} %pad_maximum_fusion.refs_4_), channel_id=1, source_target_pairs={{0,1},{1,0},{2,3},{3,2},{4,5},{5,4},{6,7},{7,6},{8,9},{9,8},{10,11... | collective-permute-start | bytes 3538952 | tf_op jit(solution)/shard_map/ppermute | solution.py:656
  86.9 2.6 copy-start.2
  170.7 15.9 %collective-permute-start.8 = (bf16[16,192,768]{2,1,0:T(8,128)(2,1)}, bf16[16,192,768]{2,1,0:T(8,128)(2,1)}, u32[]{:S(2)}, u32[]{:S(2)}) collective-permute-start(bf16[16,192,768]{2,1,0:T(8,128)(2,1)} %get-tuple-element.132), channel_id=1, source_target_pairs={{0,1},{1,0},{2,3},{3,2},{4,5},{5,4},{6,7},{7,6},{8,9},{9,8},{10,11... | collective-permute-start | bytes 14155784 | tf_op jit(solution)/shard_map/ppermute | solution.py:656
  171.0 47.3 %all-to-all-start.2 = ((bf16[8,4,32,768]{3,2,1,0:T(8,128)(2,1)}), bf16[8,4,32,768]{3,2,1,0:T(8,128)(2,1)}, u32[]{:S(2)}, u32[]{:S(2)}) async-start(bf16[8,4,32,768]{3,2,1,0:T(8,128)(2,1)} %get-tuple-element.121), calls=%async_computation.2 | async-start | bytes 3145728 | tf_op jit(solution)/shard_map/all_to_all | solution.py:1001
  193.1 28.5 %collective-permute-start.16 = (bf16[2,4,96,768]{3,2,1,0:T(8,128)(2,1)}, bf16[2,4,96,768]{3,2,1,0:T(8,128)(2,1)}, u32[]{:S(2)}, u32[]{:S(2)}) collective-permute-start(bf16[2,4,96,768]{3,2,1,0:T(8,128)(2,1)} %get-tuple-element.136), channel_id=1, source_target_pairs={{0,2},{1,3},{2,0},{3,1},{4,6},{5,7},{6,4},{7,5},{8,10},{9,11},{10,... | collective-permute-start | bytes 3538952 | tf_op jit(solution)/shard_map/ppermute | solution.py:656
  194.5 32.4 %collective-permute-start.17 = (bf16[2,4,96,768]{3,2,1,0:T(8,128)(2,1)}, bf16[2,4,96,768]{3,2,1,0:T(8,128)(2,1)}, u32[]{:S(2)}, u32[]{:S(2)}) collective-permute-start(bf16[2,4,96,768]{3,2,1,0:T(8,128)(2,1)} %get-tuple-element.137), channel_id=1, source_target_pairs={{0,4},{4,0},{8,12},{12,8},{16,20},{20,16},{24,28},{28,24},{1,5},{5... | collective-permute-start | bytes 3538952 | tf_op jit(solution)/shard_map/ppermute | solution.py:656
  208.1 23.9 %collective-permute-start.9 = (bf16[16,96,768]{2,1,0:T(8,128)(2,1)}, bf16[16,96,768]{2,1,0:T(8,128)(2,1)}, u32[]{:S(2)}, u32[]{:S(2)}) collective-permute-start(bf16[16,96,768]{2,1,0:T(8,128)(2,1)} %get-tuple-element.141), channel_id=1, source_target_pairs={{0,1},{1,0},{2,3},{3,2},{4,5},{5,4},{6,7},{7,6},{8,9},{9,8},{10,11... | collective-permute-start | bytes 7077896 | tf_op jit(solution)/shard_map/ppermute | solution.py:656
  230.8 16.6 %collective-permute-start.18 = (bf16[4,96,768]{2,1,0:T(8,128)(2,1)}, bf16[4,96,768]{2,1,0:T(8,128)(2,1)}, u32[]{:S(2)}, u32[]{:S(2)}) collective-permute-start(bf16[4,96,768]{2,1,0:T(8,128)(2,1)} %get-tuple-element.170), channel_id=1, source_target_pairs={{0,4},{4,0},{8,12},{12,8},{16,20},{20,16},{24,28},{28,24},{1,5},{5... | collective-permute-start | bytes 1769480 | tf_op jit(solution)/shard_map/ppermute | solution.py:656
  231.4 16.6 %collective-permute-start.19 = (bf16[4,96,768]{2,1,0:T(8,128)(2,1)}, bf16[4,96,768]{2,1,0:T(8,128)(2,1)}, u32[]{:S(2)}, u32[]{:S(2)}) collective-permute-start(bf16[4,96,768]{2,1,0:T(8,128)(2,1)} %get-tuple-element.172), channel_id=1, source_target_pairs={{0,2},{1,3},{2,0},{3,1},{4,6},{5,7},{6,4},{7,5},{8,10},{9,11},{10,... | collective-permute-start | bytes 1769480 | tf_op jit(solution)/shard_map/ppermute | solution.py:656
  236.6 22.1 %collective-permute-start.10 = (bf16[2,4,48,768]{3,2,1,0:T(8,128)(2,1)}, bf16[2,4,48,768]{3,2,1,0:T(8,128)(2,1)}, u32[]{:S(2)}, u32[]{:S(2)}) collective-permute-start(bf16[2,4,48,768]{3,2,1,0:T(8,128)(2,1)} %get-tuple-element.150), channel_id=1, source_target_pairs={{0,2},{1,3},{2,0},{3,1},{4,6},{5,7},{6,4},{7,5},{8,10},{9,11},{10,... | collective-permute-start | bytes 1769480 | tf_op jit(solution)/shard_map/ppermute | solution.py:656
  238.0 20.6 %collective-permute-start.11 = (bf16[2,4,48,768]{3,2,1,0:T(8,128)(2,1)}, bf16[2,4,48,768]{3,2,1,0:T(8,128)(2,1)}, u32[]{:S(2)}, u32[]{:S(2)}) collective-permute-start(bf16[2,4,48,768]{3,2,1,0:T(8,128)(2,1)} %get-tuple-element.152), channel_id=1, source_target_pairs={{0,4},{4,0},{8,12},{12,8},{16,20},{20,16},{24,28},{28,24},{1,5},{5... | collective-permute-start | bytes 1769480 | tf_op jit(solution)/shard_map/ppermute | solution.py:656
  250.7 26.1 %collective-permute-start.20 = (bf16[2,192,768]{2,1,0:T(8,128)(2,1)}, bf16[2,192,768]{2,1,0:T(8,128)(2,1)}, u32[]{:S(2)}, u32[]{:S(2)}) collective-permute-start(bf16[2,192,768]{2,1,0:T(8,128)(2,1)} %get-tuple-element.174), channel_id=1, source_target_pairs={{0,8},{4,12},{8,0},{12,4},{16,24},{20,28},{24,16},{28,20},{1,9},{5... | collective-permute-start | bytes 1769480 | tf_op jit(solution)/shard_map/ppermute | solution.py:656
  253.4 10.1 %copy-start.12 = (f32[8,768]{1,0:T(8,128)S(1)}, f32[8,768]{1,0:T(8,128)}, u32[]{:S(2)}) copy-start(f32[8,768]{1,0:T(8,128)} %get-tuple-element.179) | copy-start | bytes 73732
  253.4 11.4 %copy-start.11 = (f32[1,3072]{1,0:T(1,128)S(1)}, f32[1,3072]{1,0:T(1,128)}, u32[]{:S(2)}) copy-start(f32[1,3072]{1,0:T(1,128)} %get-tuple-element.180) | copy-start | bytes 36868
  253.4 12.8 %copy-start.13 = (f32[1,768]{1,0:T(1,128)S(1)}, f32[1,768]{1,0:T(1,128)}, u32[]{:S(2)}) copy-start(f32[1,768]{1,0:T(1,128)} %get-tuple-element.181) | copy-start | bytes 9220
  261.3 11.5 %collective-permute-start.12 = (bf16[4,48,768]{2,1,0:T(8,128)(2,1)}, bf16[4,48,768]{2,1,0:T(8,128)(2,1)}, u32[]{:S(2)}, u32[]{:S(2)}) collective-permute-start(bf16[4,48,768]{2,1,0:T(8,128)(2,1)} %get-tuple-element.156), channel_id=1, source_target_pairs={{0,4},{4,0},{8,12},{12,8},{16,20},{20,16},{24,28},{28,24},{1,5},{5... | collective-permute-start | bytes 884744 | tf_op jit(solution)/shard_map/ppermute | solution.py:656
  263.0 9.7 %collective-permute-start.13 = (bf16[4,48,768]{2,1,0:T(8,128)(2,1)}, bf16[4,48,768]{2,1,0:T(8,128)(2,1)}, u32[]{:S(2)}, u32[]{:S(2)}) collective-permute-start(bf16[4,48,768]{2,1,0:T(8,128)(2,1)} %get-tuple-element.158), channel_id=1, source_target_pairs={{0,2},{1,3},{2,0},{3,1},{4,6},{5,7},{6,4},{7,5},{8,10},{9,11},{10,... | collective-permute-start | bytes 884744 | tf_op jit(solution)/shard_map/ppermute | solution.py:656
  267.2 13.8 %all-to-all-start.3 = ((f32[32,3,96]{2,1,0:T(4,128)}), f32[32,3,96]{2,1,0:T(4,128)S(1)}, u32[]{:S(2)}, u32[]{:S(2)}) async-start(f32[32,3,96]{2,1,0:T(4,128)} %copy.52), calls=%async_computation.3 | async-start | bytes 131072 | tf_op jit(solution)/shard_map/all_to_all | solution.py:1021
  274.9 13.4 %collective-permute-start.14 = (bf16[2,96,768]{2,1,0:T(8,128)(2,1)}, bf16[2,96,768]{2,1,0:T(8,128)(2,1)}, u32[]{:S(2)}, u32[]{:S(2)}) collective-permute-start(bf16[2,96,768]{2,1,0:T(8,128)(2,1)} %get-tuple-element.160), channel_id=1, source_target_pairs={{0,8},{4,12},{8,0},{12,4},{16,24},{20,28},{24,16},{28,20},{1,9},{5... | collective-permute-start | bytes 884744 | tf_op jit(solution)/shard_map/ppermute | solution.py:656
  278.9 20.6 %collective-permute-start.21 = (bf16[192,768]{1,0:T(8,128)(2,1)}, bf16[192,768]{1,0:T(8,128)(2,1)}, u32[]{:S(2)}, u32[]{:S(2)}) collective-permute-start(bf16[192,768]{1,0:T(8,128)(2,1)} %get-tuple-element.176), channel_id=1, source_target_pairs={{0,16},{4,20},{8,24},{12,28},{16,0},{20,4},{24,8},{28,12},{1,17},{... | collective-permute-start | bytes 884744 | tf_op jit(solution)/shard_map/ppermute | solution.py:656
  290.1 12.0 %collective-permute-start.15 = (bf16[96,768]{1,0:T(8,128)(2,1)}, bf16[96,768]{1,0:T(8,128)(2,1)}, u32[]{:S(2)}, u32[]{:S(2)}) collective-permute-start(bf16[96,768]{1,0:T(8,128)(2,1)} %get-tuple-element.162), channel_id=1, source_target_pairs={{0,16},{4,20},{8,24},{12,28},{16,0},{20,4},{24,8},{28,12},{1,17},{... | collective-permute-start | bytes 442376 | tf_op jit(solution)/shard_map/ppermute | solution.py:656
  302.6 6.0 %copy-start.9 = (f32[768]{0:T(1024)S(1)}, f32[768]{0:T(1024)}, u32[]{:S(2)}) copy-start(f32[768]{0:T(1024)} %get-tuple-element.211) | copy-start | bytes 9220
  304.4 11.3 %all-to-all-start.4 = ((f32[32,1,128]{2,1,0:T(1,128)}), f32[32,1,128]{2,1,0:T(1,128)S(1)}, u32[]{:S(2)}, u32[]{:S(2)}) async-start(f32[32,1,128]{2,1,0:T(1,128)} %get-tuple-element.183), calls=%async_computation.4 | async-start | bytes 32768 | tf_op jit(solution)/shard_map/all_to_all | solution.py:1059
  315.7 0.6 copy-start.10
Sparse Core Ops, SparseCore 0:
  11.5 105.7 all-gather.2
